TPU v7x, 1024 devices: a whole 4x4x32 slice. The times are simulated.
1024 devices in a mesh: blk: 32 (over y, z_lo), dp: 32 (over z_hi, x, core).
Axes of the slice: x: 4, y: 4, z: 32 (z_hi: 4, z_lo: 8; z = z_hi * 8 + z_lo), core: 2. Of those that a mesh axis runs over, the one named last changes fastest.
Arguments:
- image_emb: bfloat16 [16384, 1024], P(('blk', 'dp')), may hold values from -2 to 2
- text_emb: bfloat16 [16384, 1024], P(('blk', 'dp')), may hold values from -2 to 2
Outputs:
- grad_image: float32 [16384, 1024], P(('blk', 'dp'))
- grad_text: float32 [16384, 1024], P(('blk', 'dp'))
- row_loss: float32 [16384], P(('blk', 'dp'))
All inputs are finite; a program needn't handle non-finite values.
Results may differ from a plain program's by a relative error of at most 0.0029.
Values may be sent and summed in bfloat16 or wider, within the bound.
No kernel may reach another device: no remote copies, remote signals or barrier semaphores. Data moves between devices by JAX's collectives and lax.ppermute only.
A program may use at most 32 MiB of HBM per device.

v0:
```python
import jax
import jax.numpy as jnp
from jax import lax
from jax.sharding import PartitionSpec as P

logit_scale = 100.0


def combined_all(shard, axis, combine):
    everything = jax.tree.map(lambda part: lax.all_gather(part, axis), shard)
    first = jax.tree.map(lambda part: part[0], everything)

    def step(k, so_far):
        return combine(so_far, jax.tree.map(lambda part: part[k], everything))

    return lax.fori_loop(1, lax.axis_size(axis), step, first)


def combine(first, second):
    top = jnp.maximum(first[0], second[0])
    total = first[1] * jnp.exp(first[0] - top) + second[1] * jnp.exp(second[0] - top)
    return (top, total)


def body(image_emb, text_emb):
    own_rows = image_emb.shape[0]
    img_rows = lax.all_gather(image_emb, "dp", axis=0, tiled=True)
    txt_cols = lax.all_gather(text_emb, "blk", axis=0, tiled=True)
    scores = logit_scale * jnp.dot(img_rows, txt_cols.T, preferred_element_type=jnp.float32)
    row_top = jnp.max(scores, axis=1)
    row_total = jnp.sum(jnp.exp(scores - row_top[:, None]), axis=1)
    row_top, row_total = combined_all((row_top, row_total), "dp", combine)
    col_top = jnp.max(scores, axis=0)
    col_total = jnp.sum(jnp.exp(scores - col_top[None, :]), axis=0)
    col_top, col_total = combined_all((col_top, col_total), "blk", combine)
    row_lse = row_top + jnp.log(row_total)
    col_lse = col_top + jnp.log(col_total)
    weights = (
        0.5 * (jnp.exp(scores - row_lse[:, None]) + jnp.exp(scores - col_lse[None, :]))
    ).astype(jnp.bfloat16)
    image_sum = lax.psum_scatter(
        jnp.dot(weights, txt_cols, preferred_element_type=jnp.float32),
        "dp",
        scatter_dimension=0,
        tiled=True,
    )
    text_sum = lax.psum_scatter(
        lax.dot_general(
            weights, img_rows, (((0,), (0,)), ((), ())), preferred_element_type=jnp.float32
        ),
        "blk",
        scatter_dimension=0,
        tiled=True,
    )
    grad_image = logit_scale * image_sum - logit_scale * text_emb.astype(jnp.float32)
    grad_text = logit_scale * text_sum - logit_scale * image_emb.astype(jnp.float32)
    own_row_lse = lax.dynamic_slice_in_dim(row_lse, lax.axis_index("dp") * own_rows, own_rows, 0)
    own_col_lse = lax.dynamic_slice_in_dim(col_lse, lax.axis_index("blk") * own_rows, own_rows, 0)
    diag = logit_scale * jnp.sum(
        image_emb.astype(jnp.float32) * text_emb.astype(jnp.float32), axis=1
    )
    row_loss = 0.5 * (own_row_lse + own_col_lse) - diag
    return (grad_image, grad_text, row_loss)


def solution(mesh):
    placed = (P(("blk", "dp"), None), P(("blk", "dp"), None))
    return jax.shard_map(
        body,
        mesh=mesh,
        in_specs=placed,
        out_specs=(P(("blk", "dp"), None), P(("blk", "dp"), None), P(("blk", "dp"))),
        check_vma=False,
    )
```

profile of v0, /device:TPU:2, one launch (start us, length us, event | category | flops | bytes accessed | tf_op | source)
XLA Modules:
  0.0 1173.8 jit_solution(3582258444423698690)
XLA Ops:
  7.2 0.0 all-gather.11.cloned.1.call-start
  7.2 0.7 all-gather.11.cloned.1.call-update
  7.9 0.0 all-gather.13.cloned.1.call-start
  7.9 0.7 all-gather.13.cloned.1.call-update
  8.6 0.0 reduce-scatter.3.cloned.1.call-start
  8.7 124.6 %all-gather.11.cloned.1.call-done = bf16[512,1024]{1,0:T(8,128)(2,1)} async-done(((bf16[16,1024]{1,0:T(8,128)(2,1)}), bf16[512,1024]{1,0:T(8,128)(2,1)}) %all-gather.11.cloned.1.call-update) | async-done | bytes 1048592 | tf_op jit(solution)/shard_map/all_gather | solution.py:27
  133.3 226.0 %all-gather.13.cloned.1.call-done = bf16[512,1024]{1,0:T(8,128)(2,1)} async-done(((bf16[16,1024]{1,0:T(8,128)(2,1)}), bf16[512,1024]{1,0:T(8,128)(2,1)}) %all-gather.13.cloned.1.call-update) | async-done | bytes 1048592 | tf_op jit(solution)/shard_map/all_gather | solution.py:28
  359.3 2.4 fusion.5
  361.6 0.0 copy-start.3
  361.7 0.4 exponential_reduce_fusion.1
  362.0 67.9 %all-gather.5 = f32[32,1,512]{2,1,0:T(1,128)S(1)} all-gather(f32[1,1,512]{2,1,0:T(1,128)S(1)} %bitcast.51), channel_id=3, replica_groups=mesh['blk'=32,'dp'=32] {'dp'}, dimensions={0}, use_global_device_ids=true | all-gather | bytes 67584 | tf_op jit(solution)/shard_map/all_gather | solution.py:10
  430.0 77.5 %all-gather.4 = f32[32,1,512]{2,1,0:T(1,128)S(1)} all-gather(f32[1,1,512]{2,1,0:T(1,128)S(1)} %bitcast.49), channel_id=2, replica_groups=mesh['blk'=32,'dp'=32] {'dp'}, dimensions={0}, use_global_device_ids=true | all-gather | bytes 67584 | tf_op jit(solution)/shard_map/all_gather | solution.py:10
  507.5 115.0 %all-gather.7 = f32[32,1,512]{2,1,0:T(1,128)S(1)} all-gather(f32[1,1,512]{2,1,0:T(1,128)S(1)} %bitcast.50), channel_id=5, replica_groups=mesh['blk'=32,'dp'=32] {'blk'}, dimensions={0}, use_global_device_ids=true | all-gather | bytes 67584 | tf_op jit(solution)/shard_map/all_gather | solution.py:10
  622.4 111.7 %all-gather.6 = f32[32,1,512]{2,1,0:T(1,128)S(1)} all-gather(f32[1,1,512]{2,1,0:T(1,128)S(1)} %bitcast.48), channel_id=4, replica_groups=mesh['blk'=32,'dp'=32] {'blk'}, dimensions={0}, use_global_device_ids=true | all-gather | bytes 67584 | tf_op jit(solution)/shard_map/all_gather | solution.py:10
  734.1 1.8 while.34
  736.0 1.8 while.35
  737.8 0.0 copy-done.3
  737.8 2.2 fusion.4
  740.0 0.0 copy-start.2
  740.0 0.0 reduce-scatter.3.cloned.1.call-update
  740.0 0.0 reduce-scatter.5.cloned.1.call-start
  740.1 1.1 copy-done.2
  741.2 2.2 fusion.3
  743.5 0.0 copy-start
  743.5 0.0 copy-start.1
  743.5 0.0 reduce-scatter.5.cloned.1.call-update
  743.5 172.6 %reduce-scatter.3.cloned.1.call-done = f32[16,1024]{1,0:T(8,128)} async-done(((f32[512,1024]{1,0:T(8,128)}), f32[16,1024]{1,0:T(8,128)}) %reduce-scatter.3.cloned.1.call-update) | async-done | bytes 65552 | tf_op jit(solution)/shard_map/reduce_scatter | solution.py:41
  916.1 249.0 %reduce-scatter.5.cloned.1.call-done = f32[16,1024]{1,0:T(8,128)} async-done(((f32[512,1024]{1,0:T(8,128)}), f32[16,1024]{1,0:T(8,128)}) %reduce-scatter.5.cloned.1.call-update) | async-done | bytes 65552 | tf_op jit(solution)/shard_map/reduce_scatter | solution.py:47
  1165.0 0.0 copy-done
  1165.0 0.0 copy-done.1
  1165.1 1.7 fusion.2
  1166.7 0.6 multiply_subtract_fusion
  (133 shorter events, 2.1 us)
Async XLA Ops:
  7.2 126.1 %all-gather.11.cloned.1.call-start = ((), (), s32[]{:S(2)}) async-start(), calls=%async_computation.2 | async-start | bytes 1081344 | tf_op jit(solution)/shard_map/all_gather | solution.py:27
  7.9 351.4 %all-gather.13.cloned.1.call-start = ((), (), s32[]{:S(2)}) async-start(), calls=%async_computation.3 | async-start | bytes 1081344 | tf_op jit(solution)/shard_map/all_gather | solution.py:28
  8.6 907.4 %reduce-scatter.3.cloned.1.call-start = ((), (), s32[]{:S(2)}) async-start(), calls=%async_computation.4 | async-start | bytes 2162688 | tf_op jit(solution)/shard_map/reduce_scatter | solution.py:41
  361.6 376.2 %copy-start.3 = (bf16[512,1024]{1,0:T(8,128)(2,1)S(1)}, bf16[512,1024]{1,0:T(8,128)(2,1)}, u32[]{:S(2)}) copy-start(bf16[512,1024]{1,0:T(8,128)(2,1)} %all-gather.13.cloned.1.call-done) | copy-start | bytes 3145732
  740.0 1.2 copy-start.2
  740.0 425.0 %reduce-scatter.5.cloned.1.call-start = ((), (), s32[]{:S(2)}) async-start(), calls=%async_computation.5 | async-start | bytes 2162688 | tf_op jit(solution)/shard_map/reduce_scatter | solution.py:47
  743.5 421.6 %copy-start = (bf16[16,1024]{1,0:T(8,128)(2,1)S(1)}, bf16[16,1024]{1,0:T(8,128)(2,1)}, u32[]{:S(2)}) copy-start(bf16[16,1024]{1,0:T(8,128)(2,1)} %param.7) | copy-start | bytes 98308
  743.5 421.6 %copy-start.1 = (bf16[16,1024]{1,0:T(8,128)(2,1)S(1)}, bf16[16,1024]{1,0:T(8,128)(2,1)}, u32[]{:S(2)}) copy-start(bf16[16,1024]{1,0:T(8,128)(2,1)} %param.6) | copy-start | bytes 98308
Sparse Core Ops, SparseCore 0:
  12.3 120.9 all-gather.10
  136.0 223.2 all-gather.12
  740.2 175.8 reduce-scatter.2
  919.3 245.7 reduce-scatter.4
where the time goes:
time: 1170 us
  waiting for transfers between devices  774 us (66%)
  blocking collectives  372 us (32%)
  between operations  13.8 us (1%)
    all_gather x4, blocking collectives, combined_all(): everything = jax.tree.map(lambda part: lax.all_gather(part, axis), shard)  372 us
    reduce_scatter x1, waiting for transfers between devices, body(): lax.psum_scatter(lax.dot_general(weights, img_rows, (((0,), (0,)), ((), (...  249 us
    all_gather x1, waiting for transfers between devices, body(): txt_cols = lax.all_gather(text_emb, 'blk', axis=0, tiled=True)  226 us
    reduce_scatter x1, waiting for transfers between devices, body(): lax.psum_scatter(jnp.dot(weights, txt_cols, preferred_element_type=jnp.fl...  173 us
    all_gather x1, waiting for transfers between devices, body(): img_rows = lax.all_gather(image_emb, 'dp', axis=0, tiled=True)  125 us
  transfers between devices with their start and end apart: 4, of which 4 were waited for; matrix products, arithmetic and copies ran while one was open for 0% of the time, Pallas kernels for 0%

commit v1 on v0

v1 whole, which is shorter than its diff:
```python
import jax
import jax.numpy as jnp
from jax import lax
from jax.sharding import Mesh, PartitionSpec as P

logit_scale = 100.0

fine = {"y": 4, "zl": 8, "zh": 4, "x": 4, "core": 2}
chip = ("x", "core")
dp = ("zh", "x", "core")
blk = ("y", "zl")
everything = ("y", "zl", "zh", "x", "core")


def gather(rows, axis):
    copies = jnp.broadcast_to(rows[None], (lax.axis_size(axis),) + rows.shape)
    return lax.all_to_all(copies, axis, 0, 0)


def lse_all(scores, dim, axis):
    top = jnp.max(scores, axis=dim, keepdims=True)
    own = jnp.squeeze(top, dim) + jnp.log(jnp.sum(jnp.exp(scores - top), axis=dim))
    every = gather(own, axis)
    top = jnp.max(every, axis=0)
    return top + jnp.log(jnp.sum(jnp.exp(every - top[None]), axis=0))


def scatter_sum(parts, axis):
    return jnp.sum(
        lax.all_to_all(parts.astype(jnp.bfloat16), axis, 0, 0).astype(jnp.float32), axis=0
    )


def body(image_emb, text_emb):
    own_rows, width = image_emb.shape
    img_rows = gather(gather(image_emb, "zh"), chip).reshape(-1, width)
    txt_cols = gather(gather(text_emb, "zl"), "y").reshape(-1, width)
    scores = logit_scale * jnp.dot(img_rows, txt_cols.T, preferred_element_type=jnp.float32)
    row_lse = lse_all(scores, 1, dp)
    col_lse = lse_all(scores, 0, blk)
    weights = (
        0.5 * (jnp.exp(scores - row_lse[:, None]) + jnp.exp(scores - col_lse[None, :]))
    ).astype(jnp.bfloat16)
    image_part = jnp.dot(weights, txt_cols, preferred_element_type=jnp.float32)
    image_part = image_part.reshape(lax.axis_size(chip), lax.axis_size("zh"), own_rows, width)
    image_sum = scatter_sum(scatter_sum(image_part, chip), "zh")
    text_part = lax.dot_general(
        weights, img_rows, (((0,), (0,)), ((), ())), preferred_element_type=jnp.float32
    )
    text_part = text_part.reshape(lax.axis_size("y"), lax.axis_size("zl"), own_rows, width)
    text_sum = scatter_sum(scatter_sum(text_part, "y"), "zl")
    grad_image = logit_scale * image_sum - logit_scale * text_emb.astype(jnp.float32)
    grad_text = logit_scale * text_sum - logit_scale * image_emb.astype(jnp.float32)
    own_row = lax.axis_index(chip) * lax.axis_size("zh") + lax.axis_index("zh")
    own_row_lse = lax.dynamic_slice_in_dim(row_lse, own_row * own_rows, own_rows, 0)
    own_col_lse = lax.dynamic_slice_in_dim(col_lse, lax.axis_index(blk) * own_rows, own_rows, 0)
    diag = logit_scale * jnp.sum(
        image_emb.astype(jnp.float32) * text_emb.astype(jnp.float32), axis=1
    )
    row_loss = 0.5 * (own_row_lse + own_col_lse) - diag
    return (grad_image, grad_text, row_loss)


def solution(mesh):
    mesh = Mesh(mesh.devices.reshape(tuple(fine.values())), tuple(fine))
    placed = P(everything, None)
    return jax.shard_map(
        body,
        mesh=mesh,
        in_specs=(placed, placed),
        out_specs=(placed, placed, P(everything)),
        check_vma=False,
    )
```

time: 1170 us -> 264 us (0.23)
  the two profiles are of different devices: /device:TPU:2 before, /device:TPU:32 now
where the time goes in v1:
time: 264 us; the launch traced here: 263 us
  blocking collectives  113 us (43%)
  waiting for transfers between devices  105 us (40%)
  starting transfers between devices  32.2 us (12%)
  other arithmetic  4.48 us (2%)
  matrix products  4.28 us (2%)
  local copies, waits for them, and re-layouts  3.58 us (1%)
    all_to_all x4, blocking collectives, gather(): return lax.all_to_all(copies, axis, 0, 0)  113 us
    all_to_all x4, waiting for transfers between devices, scatter_sum(): lax.all_to_all(parts.astype(jnp.bfloat16), axis, 0, 0).astype(jnp.float32)  66.5 us
    all_to_all x2, waiting for transfers between devices, gather(): return lax.all_to_all(copies, axis, 0, 0)  38.6 us
    all_to_all x2, starting transfers between devices, gather(): return lax.all_to_all(copies, axis, 0, 0)  16.6 us
    all_to_all x4, starting transfers between devices, scatter_sum(): lax.all_to_all(parts.astype(jnp.bfloat16), axis, 0, 0).astype(jnp.float32)  15.6 us
  transfers between devices with their start and end apart: 6, of which 6 were waited for; matrix products, arithmetic and copies ran while one was open for 2% of the time, Pallas kernels for 0%

profile of v1, /device:TPU:32, one launch (start us, length us, event | category | flops | bytes accessed | tf_op | source)
XLA Modules:
  0.0 263.0 jit_solution(13643906678040802604)
XLA Ops:
  0.6 0.8 broadcast_in_dim.12
  1.4 58.2 %all_to_all.58 = bf16[4,16,1024]{2,1,0:T(8,128)(2,1)S(1)} all-to-all(bf16[4,16,1024]{2,1,0:T(8,128)(2,1)S(1)} %broadcast_in_dim.12), channel_id=1, replica_groups=mesh['y'=4,'zl'=8,'zh'=4,'x'=4,'core'=2] {'zh'}, dimensions={0} | all-to-all | bytes 262144 | tf_op jit(solution)/shard_map/all_to_all | solution.py:17
  59.7 20.2 %all_to_all.59 = bf16[8,4,16,1024]{3,2,1,0:T(8,128)(2,1)S(1)} all-to-all(bf16[8,4,16,1024]{3,2,1,0:T(8,128)(2,1)S(1)} %broadcast_in_dim.13), channel_id=1, replica_groups=mesh['y'=4,'zl'=8,'zh'=4,'x'=4,'core'=2] {'x','core'}, dimensions={0} | all-to-all | bytes 2097152 | tf_op jit(solution)/shard_map/all_to_all | solution.py:17
  79.9 19.1 %all_to_all.60 = bf16[8,16,1024]{2,1,0:T(8,128)(2,1)S(1)} all-to-all(bf16[8,16,1024]{2,1,0:T(8,128)(2,1)S(1)} %broadcast_in_dim.14), channel_id=1, replica_groups=mesh['y'=4,'zl'=8,'zh'=4,'x'=4,'core'=2] {'zl'}, dimensions={0} | all-to-all | bytes 524288 | tf_op jit(solution)/shard_map/all_to_all | solution.py:17
  99.0 0.1 broadcast_in_dim.15
  99.2 15.2 %all_to_all.61 = bf16[4,8,16,1024]{3,2,1,0:T(8,128)(2,1)S(1)} all-to-all(bf16[4,8,16,1024]{3,2,1,0:T(8,128)(2,1)S(1)} %broadcast_in_dim.15), channel_id=1, replica_groups=mesh['y'=4,'zl'=8,'zh'=4,'x'=4,'core'=2] {'y'}, dimensions={0} | all-to-all | bytes 2097152 | tf_op jit(solution)/shard_map/all_to_all | solution.py:17
  114.3 0.8 fusion.7
  115.2 0.4 exponential_reduce_fusion.1
  115.5 0.7 broadcast_in_dim.17
  116.2 10.0 %all-to-all-start.5 = ((f32[32,1,512]{2,1,0:T(1,128)}), f32[32,1,512]{2,1,0:T(1,128)S(1)}, u32[]{:S(2)}, u32[]{:S(2)}) async-start(f32[32,1,512]{2,1,0:T(1,128)} %broadcast_in_dim.17), calls=%async_computation.5 | async-start | bytes 131072 | tf_op jit(solution)/shard_map/all_to_all | solution.py:17
  126.2 11.7 %all-to-all-done.5 = f32[32,1,512]{2,1,0:T(1,128)S(1)} async-done(((f32[32,1,512]{2,1,0:T(1,128)}), f32[32,1,512]{2,1,0:T(1,128)S(1)}, u32[]{:S(2)}, u32[]{:S(2)}) %all-to-all-start.5) | async-done | bytes 65568 | tf_op jit(solution)/shard_map/all_to_all | solution.py:17
  137.9 0.7 broadcast_in_dim.16
  138.6 6.6 %all-to-all-start.4 = ((f32[32,1,512]{2,1,0:T(1,128)}), f32[32,1,512]{2,1,0:T(1,128)S(1)}, u32[]{:S(2)}, u32[]{:S(2)}) async-start(f32[32,1,512]{2,1,0:T(1,128)} %broadcast_in_dim.16), calls=%async_computation.4 | async-start | bytes 131072 | tf_op jit(solution)/shard_map/all_to_all | solution.py:17
  145.3 26.9 %all-to-all-done.4 = f32[32,1,512]{2,1,0:T(1,128)S(1)} async-done(((f32[32,1,512]{2,1,0:T(1,128)}), f32[32,1,512]{2,1,0:T(1,128)S(1)}, u32[]{:S(2)}, u32[]{:S(2)}) %all-to-all-start.4) | async-done | bytes 65568 | tf_op jit(solution)/shard_map/all_to_all | solution.py:17
  172.3 0.3 multiply_convert_fusion
  172.7 1.8 convolution_convert_fusion.1
  174.4 4.0 %all-to-all-start.6 = ((bf16[8,4,16,1024]{3,2,1,0:T(8,128)(2,1)}), bf16[8,4,16,1024]{3,2,1,0:T(8,128)(2,1)S(1)}, u32[]{:S(2)}, u32[]{:S(2)}) async-start(bf16[8,4,16,1024]{3,2,1,0:T(8,128)(2,1)} %convolution_convert_fusion.1), calls=%async_computation.6 | async-start | bytes 2097152 | tf_op jit(solution)/shard_map/all_to_all | solution.py:30
  178.5 0.3 fusion.14
  178.8 0.2 copy.10
  179.0 1.0 copy-done.1
  180.0 1.7 convolution_convert_fusion
  181.7 12.7 %all-to-all-done.6 = bf16[8,4,16,1024]{3,2,1,0:T(8,128)(2,1)S(1)} async-done(((bf16[8,4,16,1024]{3,2,1,0:T(8,128)(2,1)}), bf16[8,4,16,1024]{3,2,1,0:T(8,128)(2,1)S(1)}, u32[]{:S(2)}, u32[]{:S(2)}) %all-to-all-start.6) | async-done | bytes 1048608 | tf_op jit(solution)/shard_map/all_to_all | solution.py:30
  194.4 3.5 %all-to-all-start.8 = ((bf16[4,8,16,1024]{3,2,1,0:T(8,128)(2,1)}), bf16[4,8,16,1024]{3,2,1,0:T(8,128)(2,1)S(1)}, u32[]{:S(2)}, u32[]{:S(2)}) async-start(bf16[4,8,16,1024]{3,2,1,0:T(8,128)(2,1)} %convolution_convert_fusion), calls=%async_computation.8 | async-start | bytes 2097152 | tf_op jit(solution)/shard_map/all_to_all | solution.py:30
  198.0 0.8 reduce_sum.91
  198.8 14.3 %all-to-all-done.8 = bf16[4,8,16,1024]{3,2,1,0:T(8,128)(2,1)S(1)} async-done(((bf16[4,8,16,1024]{3,2,1,0:T(8,128)(2,1)}), bf16[4,8,16,1024]{3,2,1,0:T(8,128)(2,1)S(1)}, u32[]{:S(2)}, u32[]{:S(2)}) %all-to-all-start.8) | async-done | bytes 1048608 | tf_op jit(solution)/shard_map/all_to_all | solution.py:30
  213.1 3.3 %all-to-all-start.7 = ((bf16[4,16,1024]{2,1,0:T(8,128)(2,1)}), bf16[4,16,1024]{2,1,0:T(8,128)(2,1)S(1)}, u32[]{:S(2)}, u32[]{:S(2)}) async-start(bf16[4,16,1024]{2,1,0:T(8,128)(2,1)} %reduce_sum.91), calls=%async_computation.7 | async-start | bytes 262144 | tf_op jit(solution)/shard_map/all_to_all | solution.py:30
  216.4 0.9 reduce_sum.93
  217.4 24.5 %all-to-all-done.7 = bf16[4,16,1024]{2,1,0:T(8,128)(2,1)S(1)} async-done(((bf16[4,16,1024]{2,1,0:T(8,128)(2,1)}), bf16[4,16,1024]{2,1,0:T(8,128)(2,1)S(1)}, u32[]{:S(2)}, u32[]{:S(2)}) %all-to-all-start.7) | async-done | bytes 131104 | tf_op jit(solution)/shard_map/all_to_all | solution.py:30
  241.9 4.7 %all-to-all-start.9 = ((bf16[8,16,1024]{2,1,0:T(8,128)(2,1)}), bf16[8,16,1024]{2,1,0:T(8,128)(2,1)S(1)}, u32[]{:S(2)}, u32[]{:S(2)}) async-start(bf16[8,16,1024]{2,1,0:T(8,128)(2,1)} %reduce_sum.93), calls=%async_computation.9 | async-start | bytes 524288 | tf_op jit(solution)/shard_map/all_to_all | solution.py:30
  246.6 15.0 %all-to-all-done.9 = bf16[8,16,1024]{2,1,0:T(8,128)(2,1)S(1)} async-done(((bf16[8,16,1024]{2,1,0:T(8,128)(2,1)}), bf16[8,16,1024]{2,1,0:T(8,128)(2,1)S(1)}, u32[]{:S(2)}, u32[]{:S(2)}) %all-to-all-start.9) | async-done | bytes 262176 | tf_op jit(solution)/shard_map/all_to_all | solution.py:30
  261.6 0.8 fusion.2
  262.4 0.6 multiply_subtract_fusion
  (19 shorter events, 0.4 us)
Async XLA Ops:
  59.7 20.2 %copy-start.2 = (bf16[16,1024]{1,0:T(8,128)(2,1)S(1)}, bf16[16,1024]{1,0:T(8,128)(2,1)}, u32[]{:S(2)}) copy-start(bf16[16,1024]{1,0:T(8,128)(2,1)} %param.3) | copy-start | bytes 98308
  79.9 34.4 %copy-start = (bf16[8,4,16,1024]{3,2,1,0:T(8,128)(2,1)}, bf16[8,4,16,1024]{3,2,1,0:T(8,128)(2,1)S(1)}, u32[]{:S(2)}) copy-start(bf16[8,4,16,1024]{3,2,1,0:T(8,128)(2,1)S(1)} %all_to_all.59) | copy-start | bytes 3145732
  116.2 21.7 %all-to-all-start.5 = ((f32[32,1,512]{2,1,0:T(1,128)}), f32[32,1,512]{2,1,0:T(1,128)S(1)}, u32[]{:S(2)}, u32[]{:S(2)}) async-start(f32[32,1,512]{2,1,0:T(1,128)} %broadcast_in_dim.17), calls=%async_computation.5 | async-start | bytes 131072 | tf_op jit(solution)/shard_map/all_to_all | solution.py:17
  138.6 33.6 %all-to-all-start.4 = ((f32[32,1,512]{2,1,0:T(1,128)}), f32[32,1,512]{2,1,0:T(1,128)S(1)}, u32[]{:S(2)}, u32[]{:S(2)}) async-start(f32[32,1,512]{2,1,0:T(1,128)} %broadcast_in_dim.16), calls=%async_computation.4 | async-start | bytes 131072 | tf_op jit(solution)/shard_map/all_to_all | solution.py:17
  174.4 20.0 %all-to-all-start.6 = ((bf16[8,4,16,1024]{3,2,1,0:T(8,128)(2,1)}), bf16[8,4,16,1024]{3,2,1,0:T(8,128)(2,1)S(1)}, u32[]{:S(2)}, u32[]{:S(2)}) async-start(bf16[8,4,16,1024]{3,2,1,0:T(8,128)(2,1)} %convolution_convert_fusion.1), calls=%async_computation.6 | async-start | bytes 2097152 | tf_op jit(solution)/shard_map/all_to_all | solution.py:30
  178.8 1.2 copy-start.1
  194.4 18.7 %all-to-all-start.8 = ((bf16[4,8,16,1024]{3,2,1,0:T(8,128)(2,1)}), bf16[4,8,16,1024]{3,2,1,0:T(8,128)(2,1)S(1)}, u32[]{:S(2)}, u32[]{:S(2)}) async-start(bf16[4,8,16,1024]{3,2,1,0:T(8,128)(2,1)} %convolution_convert_fusion), calls=%async_computation.8 | async-start | bytes 2097152 | tf_op jit(solution)/shard_map/all_to_all | solution.py:30
  213.1 28.8 %all-to-all-start.7 = ((bf16[4,16,1024]{2,1,0:T(8,128)(2,1)}), bf16[4,16,1024]{2,1,0:T(8,128)(2,1)S(1)}, u32[]{:S(2)}, u32[]{:S(2)}) async-start(bf16[4,16,1024]{2,1,0:T(8,128)(2,1)} %reduce_sum.91), calls=%async_computation.7 | async-start | bytes 262144 | tf_op jit(solution)/shard_map/all_to_all | solution.py:30
  216.4 45.2 %copy-start.3 = (bf16[16,1024]{1,0:T(8,128)(2,1)S(1)}, bf16[16,1024]{1,0:T(8,128)(2,1)}, u32[]{:S(2)}) copy-start(bf16[16,1024]{1,0:T(8,128)(2,1)} %param.2) | copy-start | bytes 98308
  241.9 19.7 %all-to-all-start.9 = ((bf16[8,16,1024]{2,1,0:T(8,128)(2,1)}), bf16[8,16,1024]{2,1,0:T(8,128)(2,1)S(1)}, u32[]{:S(2)}, u32[]{:S(2)}) async-start(bf16[8,16,1024]{2,1,0:T(8,128)(2,1)} %reduce_sum.93), calls=%async_computation.9 | async-start | bytes 524288 | tf_op jit(solution)/shard_map/all_to_all | solution.py:30

commit v2 on v1

v2 whole, which is shorter than its diff:
```python
import functools

import jax
import jax.numpy as jnp
from jax import lax
from jax.sharding import Mesh, PartitionSpec as P

logit_scale = 100.0

fine = {"y": 4, "zl": 8, "zh": 4, "x": 4, "core": 2}
chip = ("x", "core")
dp = ("zh", "x", "core")
blk = ("y", "zl")
everything = ("y", "zl", "zh", "x", "core")


def gather(rows, axis):
    copies = jnp.broadcast_to(rows[None], (lax.axis_size(axis),) + rows.shape)
    return lax.all_to_all(copies, axis, 0, 0)


def swap(value, axis, step):
    return lax.ppermute(value, axis, [(i, i ^ step) for i in range(lax.axis_size(axis))])


def gather_by_swaps(rows, axis):
    me = lax.axis_index(axis)
    came = [rows] + [swap(rows, axis, p) for p in range(1, lax.axis_size(axis))]
    return jnp.stack([lax.select_n(me ^ k, *came) for k in range(len(came))])


def scatter_sum(parts, axis):
    return jnp.sum(
        lax.all_to_all(parts.astype(jnp.bfloat16), axis, 0, 0).astype(jnp.float32), axis=0
    )


def scatter_sum_by_swaps(parts, axis):
    me = lax.axis_index(axis)
    parts = parts.astype(jnp.bfloat16)
    own = [lax.dynamic_index_in_dim(parts, me ^ p, 0, False) for p in range(parts.shape[0])]
    came = own[:1] + [swap(own[p], axis, p) for p in range(1, parts.shape[0])]
    return sum(part.astype(jnp.float32) for part in came)


def lse(values, dim):
    top = jnp.max(values, axis=dim, keepdims=True)
    return jnp.squeeze(top, dim) + jnp.log(jnp.sum(jnp.exp(values - top), axis=dim))


def lse_of(*values):
    top = functools.reduce(jnp.maximum, values)
    return top + jnp.log(sum(jnp.exp(value - top) for value in values))


def lse_rows(scores):
    return lse(gather(lse(scores, 1), dp), 0)


def lse_cols(scores):
    total = lse(scores, 0)
    total = lse_of(total, *(swap(total, "y", step) for step in (1, 2, 3)))
    total = lse_of(total, *(swap(total, "zl", step) for step in (1, 2, 3)))
    return lse_of(total, swap(total, "zl", 4))


def body(image_emb, text_emb):
    own_rows, width = image_emb.shape
    img_rows = gather(gather_by_swaps(image_emb, "zh"), chip)
    txt_cols = gather_by_swaps(gather(text_emb, "zl"), "y")
    row_lanes, col_lanes = img_rows.shape[:-1], txt_cols.shape[:-1]
    img_rows, txt_cols = img_rows.reshape(-1, width), txt_cols.reshape(-1, width)
    scores = logit_scale * jnp.dot(img_rows, txt_cols.T, preferred_element_type=jnp.float32)
    row_lse = lse_rows(scores)
    col_lse = lse_cols(scores)
    weights = (
        0.5 * (jnp.exp(scores - row_lse[:, None]) + jnp.exp(scores - col_lse[None, :]))
    ).astype(jnp.bfloat16)
    image_part = jnp.dot(weights, txt_cols, preferred_element_type=jnp.float32)
    image_part = image_part.reshape(row_lanes + (width,))
    image_sum = scatter_sum_by_swaps(scatter_sum(image_part, chip), "zh")
    text_part = lax.dot_general(
        weights, img_rows, (((0,), (0,)), ((), ())), preferred_element_type=jnp.float32
    )
    text_part = text_part.reshape(col_lanes + (width,))
    text_sum = scatter_sum(scatter_sum_by_swaps(text_part, "y"), "zl")
    grad_image = logit_scale * image_sum - logit_scale * text_emb.astype(jnp.float32)
    grad_text = logit_scale * text_sum - logit_scale * image_emb.astype(jnp.float32)
    own_row = lax.axis_index(chip) * row_lanes[1] + lax.axis_index("zh")
    own_row_lse = lax.dynamic_slice_in_dim(row_lse, own_row * own_rows, own_rows, 0)
    own_col_lse = lax.dynamic_slice_in_dim(col_lse, lax.axis_index(blk) * own_rows, own_rows, 0)
    diag = logit_scale * jnp.sum(
        image_emb.astype(jnp.float32) * text_emb.astype(jnp.float32), axis=1
    )
    row_loss = 0.5 * (own_row_lse + own_col_lse) - diag
    return (grad_image, grad_text, row_loss)


def solution(mesh):
    mesh = Mesh(mesh.devices.reshape(tuple(fine.values())), tuple(fine))
    placed = P(everything, None)
    return jax.shard_map(
        body,
        mesh=mesh,
        in_specs=(placed, placed),
        out_specs=(placed, placed, P(everything)),
        check_vma=False,
    )
```

time: 264 us -> 228 us (0.86)
  the two profiles are of different devices: /device:TPU:32 before, /device:TPU:2 now
where the time goes in v2:
time: 228 us; the launch traced here: 227 us
  starting transfers between devices  149 us (65%)
  waiting for transfers between devices  62.2 us (27%)
  other arithmetic  5.71 us (3%)
  local copies, waits for them, and re-layouts  4.91 us (2%)
  matrix products  4.27 us (2%)
    ppermute x19, starting transfers between devices, swap(): lax.ppermute(value, axis, [(i, i ^ step) for i in range(lax.axis_size(axi...  103 us
    ppermute x19, waiting for transfers between devices, swap(): lax.ppermute(value, axis, [(i, i ^ step) for i in range(lax.axis_size(axi...  59.9 us
    all_to_all x3, starting transfers between devices, gather(): return lax.all_to_all(copies, axis, 0, 0)  32.4 us
    all_to_all x2, starting transfers between devices, scatter_sum(): lax.all_to_all(parts.astype(jnp.bfloat16), axis, 0, 0).astype(jnp.float32)  13.2 us
  transfers between devices with their start and end apart: 24, of which 12 were waited for; matrix products, arithmetic and copies ran while one was open for 3% of the time, Pallas kernels for 0%

profile of v2, /device:TPU:2, one launch (start us, length us, event | category | flops | bytes accessed | tf_op | source)
XLA Modules:
  0.0 226.9 jit_solution(18188893471816090080)
XLA Ops:
  2.1 12.5 %all-to-all-start.1 = ((bf16[8,16,1024]{2,1,0:T(8,128)(2,1)}), bf16[8,16,1024]{2,1,0:T(8,128)(2,1)S(1)}, u32[]{:S(2)}, u32[]{:S(2)}) async-start(bf16[8,16,1024]{2,1,0:T(8,128)(2,1)} %broadcast_in_dim.7), calls=%async_computation.1 | async-start | bytes 524288 | tf_op jit(solution)/shard_map/all_to_all | solution.py:19
  14.6 21.5 %collective-permute-start.1 = (bf16[16,1024]{1,0:T(8,128)(2,1)}, bf16[16,1024]{1,0:T(8,128)(2,1)S(1)}, u32[]{:S(2)}, u32[]{:S(2)}) collective-permute-start(bf16[16,1024]{1,0:T(8,128)(2,1)} %param.2), channel_id=1, source_target_pairs={{0,16},{8,24},{16,0},{24,8},{1,17},{9,25},{17,1},{25,9},{2,18},{10... | collective-permute-start | bytes 98312 | tf_op jit(solution)/shard_map/ppermute | solution.py:23
  36.1 6.1 %collective-permute-start = (bf16[16,1024]{1,0:T(8,128)(2,1)}, bf16[16,1024]{1,0:T(8,128)(2,1)S(1)}, u32[]{:S(2)}, u32[]{:S(2)}) collective-permute-start(bf16[16,1024]{1,0:T(8,128)(2,1)} %param.2), channel_id=1, source_target_pairs={{0,8},{8,0},{16,24},{24,16},{1,9},{9,1},{17,25},{25,17},{2,10},{10... | collective-permute-start | bytes 98312 | tf_op jit(solution)/shard_map/ppermute | solution.py:23
  42.2 2.1 collective-permute-start.2
  44.4 7.5 %collective-permute-done = bf16[16,1024]{1,0:T(8,128)(2,1)S(1)} collective-permute-done((bf16[16,1024]{1,0:T(8,128)(2,1)}, bf16[16,1024]{1,0:T(8,128)(2,1)S(1)}, u32[]{:S(2)}, u32[]{:S(2)}) %collective-permute-start) | collective-permute-done | bytes 32800 | tf_op jit(solution)/shard_map/ppermute | solution.py:23
  51.9 7.4 %collective-permute-done.2 = bf16[16,1024]{1,0:T(8,128)(2,1)S(1)} collective-permute-done((bf16[16,1024]{1,0:T(8,128)(2,1)}, bf16[16,1024]{1,0:T(8,128)(2,1)S(1)}, u32[]{:S(2)}, u32[]{:S(2)}) %collective-permute-start.2) | collective-permute-done | bytes 32800 | tf_op jit(solution)/shard_map/ppermute | solution.py:23
  61.3 4.8 %all-to-all-start = ((bf16[8,4,16,1024]{3,2,1,0:T(8,128)(2,1)}), bf16[8,4,16,1024]{3,2,1,0:T(8,128)(2,1)S(1)}, u32[]{:S(2)}, u32[]{:S(2)}) async-start(bf16[8,4,16,1024]{3,2,1,0:T(8,128)(2,1)} %broadcast_in_dim.6), calls=%async_computation | async-start | bytes 2097152 | tf_op jit(solution)/shard_map/all_to_all | solution.py:19
  66.1 4.9 %collective-permute-start.5 = (bf16[8,16,1024]{2,1,0:T(8,128)(2,1)S(1)}, bf16[8,16,1024]{2,1,0:T(8,128)(2,1)S(1)}, u32[]{:S(2)}, u32[]{:S(2)}) collective-permute-start(bf16[8,16,1024]{2,1,0:T(8,128)(2,1)S(1)} %all-to-all-done.1), channel_id=1, source_target_pairs={{0,768},{256,512},{512,256},{768,0},{1,769},{257,513},{513,257},{7... | collective-permute-start | bytes 786440 | tf_op jit(solution)/shard_map/ppermute | solution.py:23
  71.0 2.5 %collective-permute-start.4 = (bf16[8,16,1024]{2,1,0:T(8,128)(2,1)S(1)}, bf16[8,16,1024]{2,1,0:T(8,128)(2,1)S(1)}, u32[]{:S(2)}, u32[]{:S(2)}) collective-permute-start(bf16[8,16,1024]{2,1,0:T(8,128)(2,1)S(1)} %all-to-all-done.1), channel_id=1, source_target_pairs={{0,512},{256,768},{512,0},{768,256},{1,513},{257,769},{513,1},{769... | collective-permute-start | bytes 786440 | tf_op jit(solution)/shard_map/ppermute | solution.py:23
  73.6 2.4 %collective-permute-start.3 = (bf16[8,16,1024]{2,1,0:T(8,128)(2,1)S(1)}, bf16[8,16,1024]{2,1,0:T(8,128)(2,1)S(1)}, u32[]{:S(2)}, u32[]{:S(2)}) collective-permute-start(bf16[8,16,1024]{2,1,0:T(8,128)(2,1)S(1)} %all-to-all-done.1), channel_id=1, source_target_pairs={{0,256},{256,0},{512,768},{768,512},{1,257},{257,1},{513,769},{769... | collective-permute-start | bytes 786440 | tf_op jit(solution)/shard_map/ppermute | solution.py:23
  76.0 6.9 %collective-permute-done.5 = bf16[8,16,1024]{2,1,0:T(8,128)(2,1)S(1)} collective-permute-done((bf16[8,16,1024]{2,1,0:T(8,128)(2,1)S(1)}, bf16[8,16,1024]{2,1,0:T(8,128)(2,1)S(1)}, u32[]{:S(2)}, u32[]{:S(2)}) %collective-permute-start.5) | collective-permute-done | bytes 262176 | tf_op jit(solution)/shard_map/ppermute | solution.py:23
  83.6 2.2 collective-permute-done.3
  87.4 4.8 %collective-permute-start.8 = (f32[512]{0:T(512)S(1)}, f32[512]{0:T(512)S(1)}, u32[]{:S(2)}, u32[]{:S(2)}) collective-permute-start(f32[512]{0:T(512)S(1)} %log_add_fusion.3), channel_id=1, source_target_pairs={{0,768},{256,512},{512,256},{768,0},{1,769},{257,513},{513,257},{7... | collective-permute-start | bytes 6152 | tf_op jit(solution)/shard_map/ppermute | solution.py:23
  92.3 2.5 %collective-permute-start.7 = (f32[512]{0:T(512)S(1)}, f32[512]{0:T(512)S(1)}, u32[]{:S(2)}, u32[]{:S(2)}) collective-permute-start(f32[512]{0:T(512)S(1)} %log_add_fusion.3), channel_id=1, source_target_pairs={{0,512},{256,768},{512,0},{768,256},{1,513},{257,769},{513,1},{769... | collective-permute-start | bytes 6152 | tf_op jit(solution)/shard_map/ppermute | solution.py:23
  94.8 2.4 %collective-permute-start.6 = (f32[512]{0:T(512)S(1)}, f32[512]{0:T(512)S(1)}, u32[]{:S(2)}, u32[]{:S(2)}) collective-permute-start(f32[512]{0:T(512)S(1)} %log_add_fusion.3), channel_id=1, source_target_pairs={{0,256},{256,0},{512,768},{768,512},{1,257},{257,1},{513,769},{769... | collective-permute-start | bytes 6152 | tf_op jit(solution)/shard_map/ppermute | solution.py:23
  97.9 15.1 %all-to-all-start.2 = ((f32[32,1,512]{2,1,0:T(1,128)}), f32[32,1,512]{2,1,0:T(1,128)S(1)}, u32[]{:S(2)}, u32[]{:S(2)}) async-start(f32[32,1,512]{2,1,0:T(1,128)} %broadcast_in_dim.8), calls=%async_computation.2 | async-start | bytes 131072 | tf_op jit(solution)/shard_map/all_to_all | solution.py:19
  113.1 6.1 %collective-permute-start.11 = (f32[512]{0:T(512)S(1)}, f32[512]{0:T(512)S(1)}, u32[]{:S(2)}, u32[]{:S(2)}) collective-permute-start(f32[512]{0:T(512)S(1)} %log_add_fusion.2), channel_id=1, source_target_pairs={{0,96},{32,64},{64,32},{96,0},{128,224},{160,192},{192,160},{224,1... | collective-permute-start | bytes 6152 | tf_op jit(solution)/shard_map/ppermute | solution.py:23
  121.1 2.5 %collective-permute-start.9 = (f32[512]{0:T(512)S(1)}, f32[512]{0:T(512)S(1)}, u32[]{:S(2)}, u32[]{:S(2)}) collective-permute-start(f32[512]{0:T(512)S(1)} %log_add_fusion.2), channel_id=1, source_target_pairs={{0,32},{32,0},{64,96},{96,64},{128,160},{160,128},{192,224},{224,1... | collective-permute-start | bytes 6152 | tf_op jit(solution)/shard_map/ppermute | solution.py:23
  123.6 2.0 collective-permute-done.10
  126.6 6.6 %collective-permute-start.12 = (f32[512]{0:T(512)S(1)}, f32[512]{0:T(512)S(1)}, u32[]{:S(2)}, u32[]{:S(2)}) collective-permute-start(f32[512]{0:T(512)S(1)} %log_add_fusion.1), channel_id=1, source_target_pairs={{0,128},{32,160},{64,192},{96,224},{128,0},{160,32},{192,64},{224,... | collective-permute-start | bytes 6152 | tf_op jit(solution)/shard_map/ppermute | solution.py:23
  133.2 2.8 %collective-permute-done.12 = f32[512]{0:T(512)S(1)} collective-permute-done((f32[512]{0:T(512)S(1)}, f32[512]{0:T(512)S(1)}, u32[]{:S(2)}, u32[]{:S(2)}) %collective-permute-start.12) | collective-permute-done | bytes 2080 | tf_op jit(solution)/shard_map/ppermute | solution.py:23
  136.0 2.3 %all-to-all-done.2 = f32[32,1,512]{2,1,0:T(1,128)S(1)} async-done(((f32[32,1,512]{2,1,0:T(1,128)}), f32[32,1,512]{2,1,0:T(1,128)S(1)}, u32[]{:S(2)}, u32[]{:S(2)}) %all-to-all-start.2) | async-done | bytes 65568 | tf_op jit(solution)/shard_map/all_to_all | solution.py:19
  142.2 5.1 %all-to-all-start.3 = ((bf16[8,4,16,1024]{3,2,1,0:T(8,128)(2,1)}), bf16[8,4,16,1024]{3,2,1,0:T(8,128)(2,1)S(1)}, u32[]{:S(2)}, u32[]{:S(2)}) async-start(bf16[8,4,16,1024]{3,2,1,0:T(8,128)(2,1)} %convolution_convert_fusion.1), calls=%async_computation.3 | async-start | bytes 2097152 | tf_op jit(solution)/shard_map/all_to_all | solution.py:34
  149.1 3.4 %collective-permute-start.16 = (bf16[8,16,1024]{2,1,0:T(8,128)(2,1)S(1)}, bf16[8,16,1024]{2,1,0:T(8,128)(2,1)S(1)}, u32[]{:S(2)}, u32[]{:S(2)}) collective-permute-start(bf16[8,16,1024]{2,1,0:T(8,128)(2,1)S(1)} %get-tuple-element.7), channel_id=1, source_target_pairs={{0,256},{256,0},{512,768},{768,512},{1,257},{257,1},{513,769},{769... | collective-permute-start | bytes 786440 | tf_op jit(solution)/shard_map/ppermute | solution.py:23
  152.5 4.1 %collective-permute-start.18 = (bf16[8,16,1024]{2,1,0:T(8,128)(2,1)S(1)}, bf16[8,16,1024]{2,1,0:T(8,128)(2,1)S(1)}, u32[]{:S(2)}, u32[]{:S(2)}) collective-permute-start(bf16[8,16,1024]{2,1,0:T(8,128)(2,1)S(1)} %get-tuple-element.8), channel_id=1, source_target_pairs={{0,768},{256,512},{512,256},{768,0},{1,769},{257,513},{513,257},{7... | collective-permute-start | bytes 786440 | tf_op jit(solution)/shard_map/ppermute | solution.py:23
  156.6 2.6 %collective-permute-start.17 = (bf16[8,16,1024]{2,1,0:T(8,128)(2,1)S(1)}, bf16[8,16,1024]{2,1,0:T(8,128)(2,1)}, u32[]{:S(2)}, u32[]{:S(2)}) collective-permute-start(bf16[8,16,1024]{2,1,0:T(8,128)(2,1)S(1)} %get-tuple-element.9), channel_id=1, source_target_pairs={{0,512},{256,768},{512,0},{768,256},{1,513},{257,769},{513,1},{769... | collective-permute-start | bytes 786440 | tf_op jit(solution)/shard_map/ppermute | solution.py:23
  159.4 10.0 %collective-permute-done.18 = bf16[8,16,1024]{2,1,0:T(8,128)(2,1)S(1)} collective-permute-done((bf16[8,16,1024]{2,1,0:T(8,128)(2,1)S(1)}, bf16[8,16,1024]{2,1,0:T(8,128)(2,1)S(1)}, u32[]{:S(2)}, u32[]{:S(2)}) %collective-permute-start.18) | collective-permute-done | bytes 262176 | tf_op jit(solution)/shard_map/ppermute | solution.py:23
  171.2 8.1 %all-to-all-start.4 = ((bf16[8,16,1024]{2,1,0:T(8,128)(2,1)}), bf16[8,16,1024]{2,1,0:T(8,128)(2,1)S(1)}, u32[]{:S(2)}, u32[]{:S(2)}) async-start(bf16[8,16,1024]{2,1,0:T(8,128)(2,1)} %fusion.2), calls=%async_computation.4 | async-start | bytes 524288 | tf_op jit(solution)/shard_map/all_to_all | solution.py:34
  179.5 9.0 %collective-permute-start.13 = (bf16[16,1024]{1,0:T(8,128)(2,1)S(1)}, bf16[16,1024]{1,0:T(8,128)(2,1)S(1)}, u32[]{:S(2)}, u32[]{:S(2)}) collective-permute-start(bf16[16,1024]{1,0:T(8,128)(2,1)S(1)} %get-tuple-element.14), channel_id=1, source_target_pairs={{0,8},{8,0},{16,24},{24,16},{1,9},{9,1},{17,25},{25,17},{2,10},{10... | collective-permute-start | bytes 98312 | tf_op jit(solution)/shard_map/ppermute | solution.py:23
  188.5 12.1 %collective-permute-start.15 = (bf16[16,1024]{1,0:T(8,128)(2,1)S(1)}, bf16[16,1024]{1,0:T(8,128)(2,1)S(1)}, u32[]{:S(2)}, u32[]{:S(2)}) collective-permute-start(bf16[16,1024]{1,0:T(8,128)(2,1)S(1)} %get-tuple-element.15), channel_id=1, source_target_pairs={{0,24},{8,16},{16,8},{24,0},{1,25},{9,17},{17,9},{25,1},{2,26},{10... | collective-permute-start | bytes 98312 | tf_op jit(solution)/shard_map/ppermute | solution.py:23
  200.6 5.5 %collective-permute-start.14 = (bf16[16,1024]{1,0:T(8,128)(2,1)S(1)}, bf16[16,1024]{1,0:T(8,128)(2,1)S(1)}, u32[]{:S(2)}, u32[]{:S(2)}) collective-permute-start(bf16[16,1024]{1,0:T(8,128)(2,1)S(1)} %get-tuple-element.16), channel_id=1, source_target_pairs={{0,16},{8,24},{16,0},{24,8},{1,17},{9,25},{17,1},{25,9},{2,18},{10... | collective-permute-start | bytes 98312 | tf_op jit(solution)/shard_map/ppermute | solution.py:23
  206.2 19.3 %collective-permute-done.14 = bf16[16,1024]{1,0:T(8,128)(2,1)S(1)} collective-permute-done((bf16[16,1024]{1,0:T(8,128)(2,1)S(1)}, bf16[16,1024]{1,0:T(8,128)(2,1)S(1)}, u32[]{:S(2)}, u32[]{:S(2)}) %collective-permute-start.14) | collective-permute-done | bytes 32800 | tf_op jit(solution)/shard_map/ppermute | solution.py:23
  (53 shorter events, 18.7 us)
Async XLA Ops:
  2.1 58.0 %all-to-all-start.1 = ((bf16[8,16,1024]{2,1,0:T(8,128)(2,1)}), bf16[8,16,1024]{2,1,0:T(8,128)(2,1)S(1)}, u32[]{:S(2)}, u32[]{:S(2)}) async-start(bf16[8,16,1024]{2,1,0:T(8,128)(2,1)} %broadcast_in_dim.7), calls=%async_computation.1 | async-start | bytes 524288 | tf_op jit(solution)/shard_map/all_to_all | solution.py:19
  14.6 29.8 %collective-permute-start.1 = (bf16[16,1024]{1,0:T(8,128)(2,1)}, bf16[16,1024]{1,0:T(8,128)(2,1)S(1)}, u32[]{:S(2)}, u32[]{:S(2)}) collective-permute-start(bf16[16,1024]{1,0:T(8,128)(2,1)} %param.2), channel_id=1, source_target_pairs={{0,16},{8,24},{16,0},{24,8},{1,17},{9,25},{17,1},{25,9},{2,18},{10... | collective-permute-start | bytes 98312 | tf_op jit(solution)/shard_map/ppermute | solution.py:23
  36.1 15.8 %collective-permute-start = (bf16[16,1024]{1,0:T(8,128)(2,1)}, bf16[16,1024]{1,0:T(8,128)(2,1)S(1)}, u32[]{:S(2)}, u32[]{:S(2)}) collective-permute-start(bf16[16,1024]{1,0:T(8,128)(2,1)} %param.2), channel_id=1, source_target_pairs={{0,8},{8,0},{16,24},{24,16},{1,9},{9,1},{17,25},{25,17},{2,10},{10... | collective-permute-start | bytes 98312 | tf_op jit(solution)/shard_map/ppermute | solution.py:23
  42.2 17.1 %collective-permute-start.2 = (bf16[16,1024]{1,0:T(8,128)(2,1)}, bf16[16,1024]{1,0:T(8,128)(2,1)S(1)}, u32[]{:S(2)}, u32[]{:S(2)}) collective-permute-start(bf16[16,1024]{1,0:T(8,128)(2,1)} %param.2), channel_id=1, source_target_pairs={{0,24},{8,16},{16,8},{24,0},{1,25},{9,17},{17,9},{25,1},{2,26},{10... | collective-permute-start | bytes 98312 | tf_op jit(solution)/shard_map/ppermute | solution.py:23
  61.3 24.8 %all-to-all-start = ((bf16[8,4,16,1024]{3,2,1,0:T(8,128)(2,1)}), bf16[8,4,16,1024]{3,2,1,0:T(8,128)(2,1)S(1)}, u32[]{:S(2)}, u32[]{:S(2)}) async-start(bf16[8,4,16,1024]{3,2,1,0:T(8,128)(2,1)} %broadcast_in_dim.6), calls=%async_computation | async-start | bytes 2097152 | tf_op jit(solution)/shard_map/all_to_all | solution.py:19
  66.1 16.8 %collective-permute-start.5 = (bf16[8,16,1024]{2,1,0:T(8,128)(2,1)S(1)}, bf16[8,16,1024]{2,1,0:T(8,128)(2,1)S(1)}, u32[]{:S(2)}, u32[]{:S(2)}) collective-permute-start(bf16[8,16,1024]{2,1,0:T(8,128)(2,1)S(1)} %all-to-all-done.1), channel_id=1, source_target_pairs={{0,768},{256,512},{512,256},{768,0},{1,769},{257,513},{513,257},{7... | collective-permute-start | bytes 786440 | tf_op jit(solution)/shard_map/ppermute | solution.py:23
  71.0 12.6 %collective-permute-start.4 = (bf16[8,16,1024]{2,1,0:T(8,128)(2,1)S(1)}, bf16[8,16,1024]{2,1,0:T(8,128)(2,1)S(1)}, u32[]{:S(2)}, u32[]{:S(2)}) collective-permute-start(bf16[8,16,1024]{2,1,0:T(8,128)(2,1)S(1)} %all-to-all-done.1), channel_id=1, source_target_pairs={{0,512},{256,768},{512,0},{768,256},{1,513},{257,769},{513,1},{769... | collective-permute-start | bytes 786440 | tf_op jit(solution)/shard_map/ppermute | solution.py:23
  73.6 12.2 %collective-permute-start.3 = (bf16[8,16,1024]{2,1,0:T(8,128)(2,1)S(1)}, bf16[8,16,1024]{2,1,0:T(8,128)(2,1)S(1)}, u32[]{:S(2)}, u32[]{:S(2)}) collective-permute-start(bf16[8,16,1024]{2,1,0:T(8,128)(2,1)S(1)} %all-to-all-done.1), channel_id=1, source_target_pairs={{0,256},{256,0},{512,768},{768,512},{1,257},{257,1},{513,769},{769... | collective-permute-start | bytes 786440 | tf_op jit(solution)/shard_map/ppermute | solution.py:23
  86.1 1.0 copy-start
  87.4 25.6 %collective-permute-start.8 = (f32[512]{0:T(512)S(1)}, f32[512]{0:T(512)S(1)}, u32[]{:S(2)}, u32[]{:S(2)}) collective-permute-start(f32[512]{0:T(512)S(1)} %log_add_fusion.3), channel_id=1, source_target_pairs={{0,768},{256,512},{512,256},{768,0},{1,769},{257,513},{513,257},{7... | collective-permute-start | bytes 6152 | tf_op jit(solution)/shard_map/ppermute | solution.py:23
  92.3 20.8 %collective-permute-start.7 = (f32[512]{0:T(512)S(1)}, f32[512]{0:T(512)S(1)}, u32[]{:S(2)}, u32[]{:S(2)}) collective-permute-start(f32[512]{0:T(512)S(1)} %log_add_fusion.3), channel_id=1, source_target_pairs={{0,512},{256,768},{512,0},{768,256},{1,513},{257,769},{513,1},{769... | collective-permute-start | bytes 6152 | tf_op jit(solution)/shard_map/ppermute | solution.py:23
  94.8 18.2 %collective-permute-start.6 = (f32[512]{0:T(512)S(1)}, f32[512]{0:T(512)S(1)}, u32[]{:S(2)}, u32[]{:S(2)}) collective-permute-start(f32[512]{0:T(512)S(1)} %log_add_fusion.3), channel_id=1, source_target_pairs={{0,256},{256,0},{512,768},{768,512},{1,257},{257,1},{513,769},{769... | collective-permute-start | bytes 6152 | tf_op jit(solution)/shard_map/ppermute | solution.py:23
  97.9 40.3 %all-to-all-start.2 = ((f32[32,1,512]{2,1,0:T(1,128)}), f32[32,1,512]{2,1,0:T(1,128)S(1)}, u32[]{:S(2)}, u32[]{:S(2)}) async-start(f32[32,1,512]{2,1,0:T(1,128)} %broadcast_in_dim.8), calls=%async_computation.2 | async-start | bytes 131072 | tf_op jit(solution)/shard_map/all_to_all | solution.py:19
  113.1 10.5 %collective-permute-start.11 = (f32[512]{0:T(512)S(1)}, f32[512]{0:T(512)S(1)}, u32[]{:S(2)}, u32[]{:S(2)}) collective-permute-start(f32[512]{0:T(512)S(1)} %log_add_fusion.2), channel_id=1, source_target_pairs={{0,96},{32,64},{64,32},{96,0},{128,224},{160,192},{192,160},{224,1... | collective-permute-start | bytes 6152 | tf_op jit(solution)/shard_map/ppermute | solution.py:23
  119.1 6.4 %collective-permute-start.10 = (f32[512]{0:T(512)S(1)}, f32[512]{0:T(512)S(1)}, u32[]{:S(2)}, u32[]{:S(2)}) collective-permute-start(f32[512]{0:T(512)S(1)} %log_add_fusion.2), channel_id=1, source_target_pairs={{0,64},{32,96},{64,0},{96,32},{128,192},{160,224},{192,128},{224,1... | collective-permute-start | bytes 6152 | tf_op jit(solution)/shard_map/ppermute | solution.py:23
  121.1 5.5 %collective-permute-start.9 = (f32[512]{0:T(512)S(1)}, f32[512]{0:T(512)S(1)}, u32[]{:S(2)}, u32[]{:S(2)}) collective-permute-start(f32[512]{0:T(512)S(1)} %log_add_fusion.2), channel_id=1, source_target_pairs={{0,32},{32,0},{64,96},{96,64},{128,160},{160,128},{192,224},{224,1... | collective-permute-start | bytes 6152 | tf_op jit(solution)/shard_map/ppermute | solution.py:23
  126.6 9.4 %collective-permute-start.12 = (f32[512]{0:T(512)S(1)}, f32[512]{0:T(512)S(1)}, u32[]{:S(2)}, u32[]{:S(2)}) collective-permute-start(f32[512]{0:T(512)S(1)} %log_add_fusion.1), channel_id=1, source_target_pairs={{0,128},{32,160},{64,192},{96,224},{128,0},{160,32},{192,64},{224,... | collective-permute-start | bytes 6152 | tf_op jit(solution)/shard_map/ppermute | solution.py:23
  139.1 1.4 copy-start.1
  142.2 29.0 %all-to-all-start.3 = ((bf16[8,4,16,1024]{3,2,1,0:T(8,128)(2,1)}), bf16[8,4,16,1024]{3,2,1,0:T(8,128)(2,1)S(1)}, u32[]{:S(2)}, u32[]{:S(2)}) async-start(bf16[8,4,16,1024]{3,2,1,0:T(8,128)(2,1)} %convolution_convert_fusion.1), calls=%async_computation.3 | async-start | bytes 2097152 | tf_op jit(solution)/shard_map/all_to_all | solution.py:34
  149.1 10.3 %collective-permute-start.16 = (bf16[8,16,1024]{2,1,0:T(8,128)(2,1)S(1)}, bf16[8,16,1024]{2,1,0:T(8,128)(2,1)S(1)}, u32[]{:S(2)}, u32[]{:S(2)}) collective-permute-start(bf16[8,16,1024]{2,1,0:T(8,128)(2,1)S(1)} %get-tuple-element.7), channel_id=1, source_target_pairs={{0,256},{256,0},{512,768},{768,512},{1,257},{257,1},{513,769},{769... | collective-permute-start | bytes 786440 | tf_op jit(solution)/shard_map/ppermute | solution.py:23
  152.5 16.8 %collective-permute-start.18 = (bf16[8,16,1024]{2,1,0:T(8,128)(2,1)S(1)}, bf16[8,16,1024]{2,1,0:T(8,128)(2,1)S(1)}, u32[]{:S(2)}, u32[]{:S(2)}) collective-permute-start(bf16[8,16,1024]{2,1,0:T(8,128)(2,1)S(1)} %get-tuple-element.8), channel_id=1, source_target_pairs={{0,768},{256,512},{512,256},{768,0},{1,769},{257,513},{513,257},{7... | collective-permute-start | bytes 786440 | tf_op jit(solution)/shard_map/ppermute | solution.py:23
  156.6 12.7 %collective-permute-start.17 = (bf16[8,16,1024]{2,1,0:T(8,128)(2,1)S(1)}, bf16[8,16,1024]{2,1,0:T(8,128)(2,1)}, u32[]{:S(2)}, u32[]{:S(2)}) collective-permute-start(bf16[8,16,1024]{2,1,0:T(8,128)(2,1)S(1)} %get-tuple-element.9), channel_id=1, source_target_pairs={{0,512},{256,768},{512,0},{768,256},{1,513},{257,769},{513,1},{769... | collective-permute-start | bytes 786440 | tf_op jit(solution)/shard_map/ppermute | solution.py:23
  171.2 54.4 %copy-start.2 = (bf16[16,1024]{1,0:T(8,128)(2,1)S(1)}, bf16[16,1024]{1,0:T(8,128)(2,1)}, u32[]{:S(2)}) copy-start(bf16[16,1024]{1,0:T(8,128)(2,1)} %param.3) | copy-start | bytes 98308
  171.2 54.4 %copy-start.3 = (bf16[16,1024]{1,0:T(8,128)(2,1)S(1)}, bf16[16,1024]{1,0:T(8,128)(2,1)}, u32[]{:S(2)}) copy-start(bf16[16,1024]{1,0:T(8,128)(2,1)} %param.2) | copy-start | bytes 98308
  171.2 35.0 %all-to-all-start.4 = ((bf16[8,16,1024]{2,1,0:T(8,128)(2,1)}), bf16[8,16,1024]{2,1,0:T(8,128)(2,1)S(1)}, u32[]{:S(2)}, u32[]{:S(2)}) async-start(bf16[8,16,1024]{2,1,0:T(8,128)(2,1)} %fusion.2), calls=%async_computation.4 | async-start | bytes 524288 | tf_op jit(solution)/shard_map/all_to_all | solution.py:34
  179.5 26.7 %collective-permute-start.13 = (bf16[16,1024]{1,0:T(8,128)(2,1)S(1)}, bf16[16,1024]{1,0:T(8,128)(2,1)S(1)}, u32[]{:S(2)}, u32[]{:S(2)}) collective-permute-start(bf16[16,1024]{1,0:T(8,128)(2,1)S(1)} %get-tuple-element.14), channel_id=1, source_target_pairs={{0,8},{8,0},{16,24},{24,16},{1,9},{9,1},{17,25},{25,17},{2,10},{10... | collective-permute-start | bytes 98312 | tf_op jit(solution)/shard_map/ppermute | solution.py:23
  188.5 17.7 %collective-permute-start.15 = (bf16[16,1024]{1,0:T(8,128)(2,1)S(1)}, bf16[16,1024]{1,0:T(8,128)(2,1)S(1)}, u32[]{:S(2)}, u32[]{:S(2)}) collective-permute-start(bf16[16,1024]{1,0:T(8,128)(2,1)S(1)} %get-tuple-element.15), channel_id=1, source_target_pairs={{0,24},{8,16},{16,8},{24,0},{1,25},{9,17},{17,9},{25,1},{2,26},{10... | collective-permute-start | bytes 98312 | tf_op jit(solution)/shard_map/ppermute | solution.py:23
  200.6 24.9 %collective-permute-start.14 = (bf16[16,1024]{1,0:T(8,128)(2,1)S(1)}, bf16[16,1024]{1,0:T(8,128)(2,1)S(1)}, u32[]{:S(2)}, u32[]{:S(2)}) collective-permute-start(bf16[16,1024]{1,0:T(8,128)(2,1)S(1)} %get-tuple-element.16), channel_id=1, source_target_pairs={{0,16},{8,24},{16,0},{24,8},{1,17},{9,25},{17,1},{25,9},{2,18},{10... | collective-permute-start | bytes 98312 | tf_op jit(solution)/shard_map/ppermute | solution.py:23

commit v3 on v2

--- a/solution.py
+++ b/solution.py
@@ -1,5 +1,3 @@
-import functools
-
 import jax
 import jax.numpy as jnp
 from jax import lax
@@ -9,9 +7,12 @@
 
 fine = {"y": 4, "zl": 8, "zh": 4, "x": 4, "core": 2}
 chip = ("x", "core")
-dp = ("zh", "x", "core")
-blk = ("y", "zl")
+bits = (4, 2, 1)
 everything = ("y", "zl", "zh", "x", "core")
+
+
+def axes(axis):
+    return axis if isinstance(axis, tuple) else (axis,)
 
 
 def gather(rows, axis):
@@ -48,47 +49,62 @@
     return jnp.squeeze(top, dim) + jnp.log(jnp.sum(jnp.exp(values - top), axis=dim))
 
 
-def lse_of(*values):
-    top = functools.reduce(jnp.maximum, values)
-    return top + jnp.log(sum(jnp.exp(value - top) for value in values))
+def gather_by_doubling(rows, axis, steps):
+    for step in steps:
+        other = swap(rows, axis, step)
+        upper = (lax.axis_index(axis) & step) != 0
+        rows = jnp.stack([jnp.where(upper, other, rows), jnp.where(upper, rows, other)])
+    return rows
 
 
-def lse_rows(scores):
-    return lse(gather(lse(scores, 1), dp), 0)
+def scatter_sum_by_halving(parts, axis, steps):
+    for step in reversed(steps):
+        upper = jnp.where((lax.axis_index(axis) & step) != 0, 1, 0)
+        given = swap(lax.dynamic_index_in_dim(parts, 1 - upper, 0, False), axis, step)
+        parts = lax.dynamic_index_in_dim(parts, upper, 0, False) + given
+    return parts
 
 
-def lse_cols(scores):
-    total = lse(scores, 0)
-    total = lse_of(total, *(swap(total, "y", step) for step in (1, 2, 3)))
-    total = lse_of(total, *(swap(total, "zl", step) for step in (1, 2, 3)))
-    return lse_of(total, swap(total, "zl", 4))
+def lse_over(row, col, row_axis, col_axis):
+    n_row, n_col = lax.axis_size(row_axis), lax.axis_size(col_axis)
+    here, there = lax.axis_index(col_axis), lax.axis_index(row_axis)
+    same = (jnp.arange(n_col) == here)[:, None, None]
+    sent = jnp.broadcast_to(jnp.where(same, row, col), (n_col, n_row, row.shape[0]))
+    came = lax.all_to_all(sent.reshape(-1, row.shape[0]), axes(col_axis) + axes(row_axis), 0, 0)
+    came = came.reshape(sent.shape)
+    rows = lax.dynamic_index_in_dim(came, here, 0, False)
+    cols = lax.dynamic_index_in_dim(came, there, 1, False)
+    cols = jnp.where((jnp.arange(n_col) == here)[:, None], col, cols)
+    return lse(rows, 0), lse(cols, 0)
 
 
 def body(image_emb, text_emb):
     own_rows, width = image_emb.shape
-    img_rows = gather(gather_by_swaps(image_emb, "zh"), chip)
-    txt_cols = gather_by_swaps(gather(text_emb, "zl"), "y")
+    img_rows = gather(gather(image_emb, "zh"), chip)
+    txt_cols = gather_by_swaps(gather_by_doubling(text_emb, "zl", bits), "y")
     row_lanes, col_lanes = img_rows.shape[:-1], txt_cols.shape[:-1]
     img_rows, txt_cols = img_rows.reshape(-1, width), txt_cols.reshape(-1, width)
     scores = logit_scale * jnp.dot(img_rows, txt_cols.T, preferred_element_type=jnp.float32)
-    row_lse = lse_rows(scores)
-    col_lse = lse_cols(scores)
+    row_lse, col_lse = lse_over(lse(scores, 1), lse(scores, 0), chip, "y")
+    row_lse, col_lse = lse_over(row_lse, col_lse, "zh", "zl")
     weights = (
         0.5 * (jnp.exp(scores - row_lse[:, None]) + jnp.exp(scores - col_lse[None, :]))
     ).astype(jnp.bfloat16)
     image_part = jnp.dot(weights, txt_cols, preferred_element_type=jnp.float32)
     image_part = image_part.reshape(row_lanes + (width,))
-    image_sum = scatter_sum_by_swaps(scatter_sum(image_part, chip), "zh")
+    image_sum = scatter_sum(scatter_sum(image_part, chip), "zh")
     text_part = lax.dot_general(
         weights, img_rows, (((0,), (0,)), ((), ())), preferred_element_type=jnp.float32
     )
     text_part = text_part.reshape(col_lanes + (width,))
-    text_sum = scatter_sum(scatter_sum_by_swaps(text_part, "y"), "zl")
+    text_sum = scatter_sum_by_halving(scatter_sum_by_swaps(text_part, "y"), "zl", bits)
     grad_image = logit_scale * image_sum - logit_scale * text_emb.astype(jnp.float32)
     grad_text = logit_scale * text_sum - logit_scale * image_emb.astype(jnp.float32)
     own_row = lax.axis_index(chip) * row_lanes[1] + lax.axis_index("zh")
     own_row_lse = lax.dynamic_slice_in_dim(row_lse, own_row * own_rows, own_rows, 0)
-    own_col_lse = lax.dynamic_slice_in_dim(col_lse, lax.axis_index(blk) * own_rows, own_rows, 0)
+    zl = lax.axis_index("zl")
+    own_col = lax.axis_index("y") * 8 + (zl & 1) * 4 + (zl & 2) + (zl >> 2)
+    own_col_lse = lax.dynamic_slice_in_dim(col_lse, own_col * own_rows, own_rows, 0)
     diag = logit_scale * jnp.sum(
         image_emb.astype(jnp.float32) * text_emb.astype(jnp.float32), axis=1
     )

time: 228 us -> 217 us (0.952)
  the two profiles are of different devices: /device:TPU:2 before, /device:TPU:4 now
where the time goes in v3:
time: 217 us; the launch traced here: 215 us
  starting transfers between devices  110 us (51%)
  waiting for transfers between devices  87.2 us (40%)
  other arithmetic  7.19 us (3%)
  local copies, waits for them, and re-layouts  5.59 us (3%)
  matrix products  4.28 us (2%)
    ppermute x12, starting transfers between devices, swap(): lax.ppermute(value, axis, [(i, i ^ step) for i in range(lax.axis_size(axi...  49.1 us
    ppermute x12, waiting for transfers between devices, swap(): lax.ppermute(value, axis, [(i, i ^ step) for i in range(lax.axis_size(axi...  46.2 us
    all_to_all x2, waiting for transfers between devices, lse_over(): lax.all_to_all(sent.reshape(-1, row.shape[0]), axes(col_axis) + axes(row_...  28.7 us
    all_to_all x2, starting transfers between devices, gather(): return lax.all_to_all(copies, axis, 0, 0)  28.3 us
    all_to_all x2, starting transfers between devices, lse_over(): lax.all_to_all(sent.reshape(-1, row.shape[0]), axes(col_axis) + axes(row_...  22.5 us
    all_to_all x2, starting transfers between devices, scatter_sum(): lax.all_to_all(parts.astype(jnp.bfloat16), axis, 0, 0).astype(jnp.float32)  10.1 us
    all_to_all x2, waiting for transfers between devices, gather(): return lax.all_to_all(copies, axis, 0, 0)  7.76 us
    all_to_all x2, waiting for transfers between devices, scatter_sum(): lax.all_to_all(parts.astype(jnp.bfloat16), axis, 0, 0).astype(jnp.float32)  4.5 us
  transfers between devices with their start and end apart: 18, of which 13 were waited for; matrix products, arithmetic and copies ran while one was open for 3% of the time, Pallas kernels for 0%

profile of v3, /device:TPU:4, one launch (start us, length us, event | category | flops | bytes accessed | tf_op | source)
XLA Modules:
  0.0 215.3 jit_solution(15409727335822128484)
XLA Ops:
  0.6 9.1 %collective-permute-start = (bf16[16,1024]{1,0:T(8,128)(2,1)}, bf16[16,1024]{1,0:T(8,128)(2,1)S(1)}, u32[]{:S(2)}, u32[]{:S(2)}) collective-permute-start(bf16[16,1024]{1,0:T(8,128)(2,1)} %param.3), channel_id=1, source_target_pairs={{0,128},{32,160},{64,192},{96,224},{128,0},{160,32},{192,64},{224,... | collective-permute-start | bytes 98312 | tf_op jit(solution)/shard_map/ppermute | solution.py:24
  9.7 1.4 broadcast_in_dim.52
  11.1 23.5 %all-to-all-start = ((bf16[4,16,1024]{2,1,0:T(8,128)(2,1)}), bf16[4,16,1024]{2,1,0:T(8,128)(2,1)S(1)}, u32[]{:S(2)}, u32[]{:S(2)}) async-start(bf16[4,16,1024]{2,1,0:T(8,128)(2,1)} %broadcast_in_dim.52), calls=%async_computation | async-start | bytes 262144 | tf_op jit(solution)/shard_map/all_to_all | solution.py:20
  35.5 3.4 %collective-permute-start.1 = (bf16[2,16,1024]{2,1,0:T(8,128)(2,1)S(1)}, bf16[2,16,1024]{2,1,0:T(8,128)(2,1)S(1)}, u32[]{:S(2)}, u32[]{:S(2)}) collective-permute-start(bf16[2,16,1024]{2,1,0:T(8,128)(2,1)S(1)} %pad_maximum_fusion.3), channel_id=1, source_target_pairs={{0,64},{32,96},{64,0},{96,32},{128,192},{160,224},{192,128},{224,1... | collective-permute-start | bytes 196616 | tf_op jit(solution)/shard_map/ppermute | solution.py:24
  38.8 8.1 %collective-permute-done.1 = bf16[2,16,1024]{2,1,0:T(8,128)(2,1)S(1)} collective-permute-done((bf16[2,16,1024]{2,1,0:T(8,128)(2,1)S(1)}, bf16[2,16,1024]{2,1,0:T(8,128)(2,1)S(1)}, u32[]{:S(2)}, u32[]{:S(2)}) %collective-permute-start.1) | collective-permute-done | bytes 65568 | tf_op jit(solution)/shard_map/ppermute | solution.py:24
  47.0 1.9 collective-permute-start.2
  49.0 6.7 %collective-permute-done.2 = bf16[2,2,16,1024]{3,2,1,0:T(8,128)(2,1)S(1)} collective-permute-done((bf16[2,2,16,1024]{3,2,1,0:T(8,128)(2,1)S(1)}, bf16[2,2,16,1024]{3,2,1,0:T(8,128)(2,1)S(1)}, u32[]{:S(2)}, u32[]{:S(2)}) %collective-permute-start.2) | collective-permute-done | bytes 131104 | tf_op jit(solution)/shard_map/ppermute | solution.py:24
  55.7 7.8 %all-to-all-done = bf16[4,16,1024]{2,1,0:T(8,128)(2,1)S(1)} async-done(((bf16[4,16,1024]{2,1,0:T(8,128)(2,1)}), bf16[4,16,1024]{2,1,0:T(8,128)(2,1)S(1)}, u32[]{:S(2)}, u32[]{:S(2)}) %all-to-all-start) | async-done | bytes 131104 | tf_op jit(solution)/shard_map/all_to_all | solution.py:20
  63.4 1.2 broadcast_in_dim.53
  64.6 4.8 %all-to-all-start.1 = ((bf16[8,4,16,1024]{3,2,1,0:T(8,128)(2,1)}), bf16[8,4,16,1024]{3,2,1,0:T(8,128)(2,1)S(1)}, u32[]{:S(2)}, u32[]{:S(2)}) async-start(bf16[8,4,16,1024]{3,2,1,0:T(8,128)(2,1)} %broadcast_in_dim.53), calls=%async_computation.1 | async-start | bytes 2097152 | tf_op jit(solution)/shard_map/all_to_all | solution.py:20
  69.4 5.1 %collective-permute-start.4 = (bf16[2,2,2,16,1024]{4,3,2,1,0:T(8,128)(2,1)S(1)}, bf16[2,2,2,16,1024]{4,3,2,1,0:T(8,128)(2,1)S(1)}, u32[]{:S(2)}, u32[]{:S(2)}) collective-permute-start(bf16[2,2,2,16,1024]{4,3,2,1,0:T(8,128)(2,1)S(1)} %pad_maximum_fusion.1), channel_id=1, source_target_pairs={{0,512},{256,768},{512,0},{768,256},{1,513},{257,769},{513,1},{769... | collective-permute-start | bytes 786440 | tf_op jit(solution)/shard_map/ppermute | solution.py:24
  74.5 3.0 %collective-permute-start.5 = (bf16[2,2,2,16,1024]{4,3,2,1,0:T(8,128)(2,1)S(1)}, bf16[2,2,2,16,1024]{4,3,2,1,0:T(8,128)(2,1)S(1)}, u32[]{:S(2)}, u32[]{:S(2)}) collective-permute-start(bf16[2,2,2,16,1024]{4,3,2,1,0:T(8,128)(2,1)S(1)} %pad_maximum_fusion.1), channel_id=1, source_target_pairs={{0,768},{256,512},{512,256},{768,0},{1,769},{257,513},{513,257},{7... | collective-permute-start | bytes 786440 | tf_op jit(solution)/shard_map/ppermute | solution.py:24
  77.5 1.9 collective-permute-start.3
  79.5 1.8 collective-permute-done.4
  81.3 5.5 %collective-permute-done.5 = bf16[2,2,2,16,1024]{4,3,2,1,0:T(8,128)(2,1)S(1)} collective-permute-done((bf16[2,2,2,16,1024]{4,3,2,1,0:T(8,128)(2,1)S(1)}, bf16[2,2,2,16,1024]{4,3,2,1,0:T(8,128)(2,1)S(1)}, u32[]{:S(2)}, u32[]{:S(2)}) %collective-permute-start.5) | collective-permute-done | bytes 262176 | tf_op jit(solution)/shard_map/ppermute | solution.py:24
  89.7 7.2 %all-to-all-start.2 = ((f32[32,1,512]{2,1,0:T(1,128)}), f32[32,1,512]{2,1,0:T(1,128)S(1)}, u32[]{:S(2)}, u32[]{:S(2)}) async-start(f32[32,1,512]{2,1,0:T(1,128)} %all_to_all.26), calls=%async_computation.2 | async-start | bytes 131072 | tf_op jit(solution)/shard_map/all_to_all | solution.py:73
  96.9 5.3 %all-to-all-done.2 = f32[32,1,512]{2,1,0:T(1,128)S(1)} async-done(((f32[32,1,512]{2,1,0:T(1,128)}), f32[32,1,512]{2,1,0:T(1,128)S(1)}, u32[]{:S(2)}, u32[]{:S(2)}) %all-to-all-start.2) | async-done | bytes 65568 | tf_op jit(solution)/shard_map/all_to_all | solution.py:73
  103.3 15.3 %all-to-all-start.3 = ((f32[32,1,512]{2,1,0:T(1,128)}), f32[32,1,512]{2,1,0:T(1,128)S(1)}, u32[]{:S(2)}, u32[]{:S(2)}) async-start(f32[32,1,512]{2,1,0:T(1,128)} %all_to_all.28), calls=%async_computation.3 | async-start | bytes 131072 | tf_op jit(solution)/shard_map/all_to_all | solution.py:73
  118.6 23.4 %all-to-all-done.3 = f32[32,1,512]{2,1,0:T(1,128)S(1)} async-done(((f32[32,1,512]{2,1,0:T(1,128)}), f32[32,1,512]{2,1,0:T(1,128)S(1)}, u32[]{:S(2)}, u32[]{:S(2)}) %all-to-all-start.3) | async-done | bytes 65568 | tf_op jit(solution)/shard_map/all_to_all | solution.py:73
  145.2 1.7 convolution_convert_fusion.1
  146.9 5.9 %all-to-all-start.4 = ((bf16[8,4,16,1024]{3,2,1,0:T(8,128)(2,1)}), bf16[8,4,16,1024]{3,2,1,0:T(8,128)(2,1)S(1)}, u32[]{:S(2)}, u32[]{:S(2)}) async-start(bf16[8,4,16,1024]{3,2,1,0:T(8,128)(2,1)} %convolution_convert_fusion.1), calls=%async_computation.4 | async-start | bytes 2097152 | tf_op jit(solution)/shard_map/all_to_all | solution.py:35
  152.8 1.8 convolution_convert_fusion
  154.7 2.5 %collective-permute-start.6 = (bf16[2,2,2,16,1024]{4,3,2,1,0:T(8,128)(2,1)S(1)}, bf16[2,2,2,16,1024]{4,3,2,1,0:T(8,128)(2,1)S(1)}, u32[]{:S(2)}, u32[]{:S(2)}) collective-permute-start(bf16[2,2,2,16,1024]{4,3,2,1,0:T(8,128)(2,1)S(1)} %get-tuple-element.7), channel_id=1, source_target_pairs={{0,256},{256,0},{512,768},{768,512},{1,257},{257,1},{513,769},{769... | collective-permute-start | bytes 786440 | tf_op jit(solution)/shard_map/ppermute | solution.py:24
  157.2 3.1 %collective-permute-start.8 = (bf16[2,2,2,16,1024]{4,3,2,1,0:T(8,128)(2,1)S(1)}, bf16[2,2,2,16,1024]{4,3,2,1,0:T(8,128)(2,1)S(1)}, u32[]{:S(2)}, u32[]{:S(2)}) collective-permute-start(bf16[2,2,2,16,1024]{4,3,2,1,0:T(8,128)(2,1)S(1)} %get-tuple-element.8), channel_id=1, source_target_pairs={{0,768},{256,512},{512,256},{768,0},{1,769},{257,513},{513,257},{7... | collective-permute-start | bytes 786440 | tf_op jit(solution)/shard_map/ppermute | solution.py:24
  160.3 4.2 %collective-permute-start.7 = (bf16[2,2,2,16,1024]{4,3,2,1,0:T(8,128)(2,1)S(1)}, bf16[2,2,2,16,1024]{4,3,2,1,0:T(8,128)(2,1)}, u32[]{:S(2)}, u32[]{:S(2)}) collective-permute-start(bf16[2,2,2,16,1024]{4,3,2,1,0:T(8,128)(2,1)S(1)} %get-tuple-element.9), channel_id=1, source_target_pairs={{0,512},{256,768},{512,0},{768,256},{1,513},{257,769},{513,1},{769... | collective-permute-start | bytes 786440 | tf_op jit(solution)/shard_map/ppermute | solution.py:24
  164.9 9.1 %collective-permute-done.8 = bf16[2,2,2,16,1024]{4,3,2,1,0:T(8,128)(2,1)S(1)} collective-permute-done((bf16[2,2,2,16,1024]{4,3,2,1,0:T(8,128)(2,1)S(1)}, bf16[2,2,2,16,1024]{4,3,2,1,0:T(8,128)(2,1)S(1)}, u32[]{:S(2)}, u32[]{:S(2)}) %collective-permute-start.8) | collective-permute-done | bytes 262176 | tf_op jit(solution)/shard_map/ppermute | solution.py:24
  175.2 3.9 %collective-permute-start.9 = (f32[2,2,16,1024]{3,2,1,0:T(8,128)S(1)}, f32[2,2,16,1024]{3,2,1,0:T(8,128)S(1)}, u32[]{:S(2)}, u32[]{:S(2)}) collective-permute-start(f32[2,2,16,1024]{3,2,1,0:T(8,128)S(1)} %dynamic-slice_bitcast_fusion), channel_id=1, source_target_pairs={{0,32},{32,0},{64,96},{96,64},{128,160},{160,128},{192,224},{224,1... | collective-permute-start | bytes 786440 | tf_op jit(solution)/shard_map/ppermute | solution.py:24
  179.9 4.2 %all-to-all-start.5 = ((bf16[4,16,1024]{2,1,0:T(8,128)(2,1)}), bf16[4,16,1024]{2,1,0:T(8,128)(2,1)S(1)}, u32[]{:S(2)}, u32[]{:S(2)}) async-start(bf16[4,16,1024]{2,1,0:T(8,128)(2,1)} %reduce_sum.90), calls=%async_computation.5 | async-start | bytes 262144 | tf_op jit(solution)/shard_map/all_to_all | solution.py:35
  185.0 4.2 %collective-permute-start.10 = (f32[2,16,1024]{2,1,0:T(8,128)S(1)}, f32[2,16,1024]{2,1,0:T(8,128)S(1)}, u32[]{:S(2)}, u32[]{:S(2)}) collective-permute-start(f32[2,16,1024]{2,1,0:T(8,128)S(1)} %dynamic-slice_bitcast_fusion.4), channel_id=1, source_target_pairs={{0,64},{32,96},{64,0},{96,32},{128,192},{160,224},{192,128},{224,1... | collective-permute-start | bytes 393224 | tf_op jit(solution)/shard_map/ppermute | solution.py:24
  189.2 13.3 %collective-permute-done.10 = f32[2,16,1024]{2,1,0:T(8,128)S(1)} collective-permute-done((f32[2,16,1024]{2,1,0:T(8,128)S(1)}, f32[2,16,1024]{2,1,0:T(8,128)S(1)}, u32[]{:S(2)}, u32[]{:S(2)}) %collective-permute-start.10) | collective-permute-done | bytes 131104 | tf_op jit(solution)/shard_map/ppermute | solution.py:24
  202.6 6.8 %collective-permute-start.11 = (f32[16,1024]{1,0:T(8,128)S(1)}, f32[16,1024]{1,0:T(8,128)S(1)}, u32[]{:S(2)}, u32[]{:S(2)}) collective-permute-start(f32[16,1024]{1,0:T(8,128)S(1)} %dynamic-slice_bitcast_fusion.5), channel_id=1, source_target_pairs={{0,128},{32,160},{64,192},{96,224},{128,0},{160,32},{192,64},{224,... | collective-permute-start | bytes 196616 | tf_op jit(solution)/shard_map/ppermute | solution.py:24
  209.4 4.5 %all-to-all-done.5 = bf16[4,16,1024]{2,1,0:T(8,128)(2,1)S(1)} async-done(((bf16[4,16,1024]{2,1,0:T(8,128)(2,1)}), bf16[4,16,1024]{2,1,0:T(8,128)(2,1)S(1)}, u32[]{:S(2)}, u32[]{:S(2)}) %all-to-all-start.5) | async-done | bytes 131104 | tf_op jit(solution)/shard_map/all_to_all | solution.py:35
  (67 shorter events, 12.7 us)
Async XLA Ops:
  0.6 34.0 %collective-permute-start = (bf16[16,1024]{1,0:T(8,128)(2,1)}, bf16[16,1024]{1,0:T(8,128)(2,1)S(1)}, u32[]{:S(2)}, u32[]{:S(2)}) collective-permute-start(bf16[16,1024]{1,0:T(8,128)(2,1)} %param.3), channel_id=1, source_target_pairs={{0,128},{32,160},{64,192},{96,224},{128,0},{160,32},{192,64},{224,... | collective-permute-start | bytes 98312 | tf_op jit(solution)/shard_map/ppermute | solution.py:24
  11.1 52.3 %all-to-all-start = ((bf16[4,16,1024]{2,1,0:T(8,128)(2,1)}), bf16[4,16,1024]{2,1,0:T(8,128)(2,1)S(1)}, u32[]{:S(2)}, u32[]{:S(2)}) async-start(bf16[4,16,1024]{2,1,0:T(8,128)(2,1)} %broadcast_in_dim.52), calls=%async_computation | async-start | bytes 262144 | tf_op jit(solution)/shard_map/all_to_all | solution.py:20
  35.5 11.5 %collective-permute-start.1 = (bf16[2,16,1024]{2,1,0:T(8,128)(2,1)S(1)}, bf16[2,16,1024]{2,1,0:T(8,128)(2,1)S(1)}, u32[]{:S(2)}, u32[]{:S(2)}) collective-permute-start(bf16[2,16,1024]{2,1,0:T(8,128)(2,1)S(1)} %pad_maximum_fusion.3), channel_id=1, source_target_pairs={{0,64},{32,96},{64,0},{96,32},{128,192},{160,224},{192,128},{224,1... | collective-permute-start | bytes 196616 | tf_op jit(solution)/shard_map/ppermute | solution.py:24
  47.0 8.6 %collective-permute-start.2 = (bf16[2,2,16,1024]{3,2,1,0:T(8,128)(2,1)S(1)}, bf16[2,2,16,1024]{3,2,1,0:T(8,128)(2,1)S(1)}, u32[]{:S(2)}, u32[]{:S(2)}) collective-permute-start(bf16[2,2,16,1024]{3,2,1,0:T(8,128)(2,1)S(1)} %pad_maximum_fusion.2), channel_id=1, source_target_pairs={{0,32},{32,0},{64,96},{96,64},{128,160},{160,128},{192,224},{224,1... | collective-permute-start | bytes 393224 | tf_op jit(solution)/shard_map/ppermute | solution.py:24
  64.6 22.9 %all-to-all-start.1 = ((bf16[8,4,16,1024]{3,2,1,0:T(8,128)(2,1)}), bf16[8,4,16,1024]{3,2,1,0:T(8,128)(2,1)S(1)}, u32[]{:S(2)}, u32[]{:S(2)}) async-start(bf16[8,4,16,1024]{3,2,1,0:T(8,128)(2,1)} %broadcast_in_dim.53), calls=%async_computation.1 | async-start | bytes 2097152 | tf_op jit(solution)/shard_map/all_to_all | solution.py:20
  69.4 11.9 %collective-permute-start.4 = (bf16[2,2,2,16,1024]{4,3,2,1,0:T(8,128)(2,1)S(1)}, bf16[2,2,2,16,1024]{4,3,2,1,0:T(8,128)(2,1)S(1)}, u32[]{:S(2)}, u32[]{:S(2)}) collective-permute-start(bf16[2,2,2,16,1024]{4,3,2,1,0:T(8,128)(2,1)S(1)} %pad_maximum_fusion.1), channel_id=1, source_target_pairs={{0,512},{256,768},{512,0},{768,256},{1,513},{257,769},{513,1},{769... | collective-permute-start | bytes 786440 | tf_op jit(solution)/shard_map/ppermute | solution.py:24
  74.5 12.3 %collective-permute-start.5 = (bf16[2,2,2,16,1024]{4,3,2,1,0:T(8,128)(2,1)S(1)}, bf16[2,2,2,16,1024]{4,3,2,1,0:T(8,128)(2,1)S(1)}, u32[]{:S(2)}, u32[]{:S(2)}) collective-permute-start(bf16[2,2,2,16,1024]{4,3,2,1,0:T(8,128)(2,1)S(1)} %pad_maximum_fusion.1), channel_id=1, source_target_pairs={{0,768},{256,512},{512,256},{768,0},{1,769},{257,513},{513,257},{7... | collective-permute-start | bytes 786440 | tf_op jit(solution)/shard_map/ppermute | solution.py:24
  77.5 9.7 %collective-permute-start.3 = (bf16[2,2,2,16,1024]{4,3,2,1,0:T(8,128)(2,1)S(1)}, bf16[2,2,2,16,1024]{4,3,2,1,0:T(8,128)(2,1)S(1)}, u32[]{:S(2)}, u32[]{:S(2)}) collective-permute-start(bf16[2,2,2,16,1024]{4,3,2,1,0:T(8,128)(2,1)S(1)} %pad_maximum_fusion.1), channel_id=1, source_target_pairs={{0,256},{256,0},{512,768},{768,512},{1,257},{257,1},{513,769},{769... | collective-permute-start | bytes 786440 | tf_op jit(solution)/shard_map/ppermute | solution.py:24
  87.5 1.0 copy-start
  89.7 12.5 %all-to-all-start.2 = ((f32[32,1,512]{2,1,0:T(1,128)}), f32[32,1,512]{2,1,0:T(1,128)S(1)}, u32[]{:S(2)}, u32[]{:S(2)}) async-start(f32[32,1,512]{2,1,0:T(1,128)} %all_to_all.26), calls=%async_computation.2 | async-start | bytes 131072 | tf_op jit(solution)/shard_map/all_to_all | solution.py:73
  103.3 38.8 %all-to-all-start.3 = ((f32[32,1,512]{2,1,0:T(1,128)}), f32[32,1,512]{2,1,0:T(1,128)S(1)}, u32[]{:S(2)}, u32[]{:S(2)}) async-start(f32[32,1,512]{2,1,0:T(1,128)} %all_to_all.28), calls=%async_computation.3 | async-start | bytes 131072 | tf_op jit(solution)/shard_map/all_to_all | solution.py:73
  144.0 1.2 copy-start.1
  146.9 32.1 %all-to-all-start.4 = ((bf16[8,4,16,1024]{3,2,1,0:T(8,128)(2,1)}), bf16[8,4,16,1024]{3,2,1,0:T(8,128)(2,1)S(1)}, u32[]{:S(2)}, u32[]{:S(2)}) async-start(bf16[8,4,16,1024]{3,2,1,0:T(8,128)(2,1)} %convolution_convert_fusion.1), calls=%async_computation.4 | async-start | bytes 2097152 | tf_op jit(solution)/shard_map/all_to_all | solution.py:35
  154.7 10.3 %collective-permute-start.6 = (bf16[2,2,2,16,1024]{4,3,2,1,0:T(8,128)(2,1)S(1)}, bf16[2,2,2,16,1024]{4,3,2,1,0:T(8,128)(2,1)S(1)}, u32[]{:S(2)}, u32[]{:S(2)}) collective-permute-start(bf16[2,2,2,16,1024]{4,3,2,1,0:T(8,128)(2,1)S(1)} %get-tuple-element.7), channel_id=1, source_target_pairs={{0,256},{256,0},{512,768},{768,512},{1,257},{257,1},{513,769},{769... | collective-permute-start | bytes 786440 | tf_op jit(solution)/shard_map/ppermute | solution.py:24
  157.2 16.8 %collective-permute-start.8 = (bf16[2,2,2,16,1024]{4,3,2,1,0:T(8,128)(2,1)S(1)}, bf16[2,2,2,16,1024]{4,3,2,1,0:T(8,128)(2,1)S(1)}, u32[]{:S(2)}, u32[]{:S(2)}) collective-permute-start(bf16[2,2,2,16,1024]{4,3,2,1,0:T(8,128)(2,1)S(1)} %get-tuple-element.8), channel_id=1, source_target_pairs={{0,768},{256,512},{512,256},{768,0},{1,769},{257,513},{513,257},{7... | collective-permute-start | bytes 786440 | tf_op jit(solution)/shard_map/ppermute | solution.py:24
  160.3 13.7 %collective-permute-start.7 = (bf16[2,2,2,16,1024]{4,3,2,1,0:T(8,128)(2,1)S(1)}, bf16[2,2,2,16,1024]{4,3,2,1,0:T(8,128)(2,1)}, u32[]{:S(2)}, u32[]{:S(2)}) collective-permute-start(bf16[2,2,2,16,1024]{4,3,2,1,0:T(8,128)(2,1)S(1)} %get-tuple-element.9), channel_id=1, source_target_pairs={{0,512},{256,768},{512,0},{768,256},{1,513},{257,769},{513,1},{769... | collective-permute-start | bytes 786440 | tf_op jit(solution)/shard_map/ppermute | solution.py:24
  175.2 9.8 %collective-permute-start.9 = (f32[2,2,16,1024]{3,2,1,0:T(8,128)S(1)}, f32[2,2,16,1024]{3,2,1,0:T(8,128)S(1)}, u32[]{:S(2)}, u32[]{:S(2)}) collective-permute-start(f32[2,2,16,1024]{3,2,1,0:T(8,128)S(1)} %dynamic-slice_bitcast_fusion), channel_id=1, source_target_pairs={{0,32},{32,0},{64,96},{96,64},{128,160},{160,128},{192,224},{224,1... | collective-permute-start | bytes 786440 | tf_op jit(solution)/shard_map/ppermute | solution.py:24
  179.9 34.0 %copy-start.2 = (bf16[16,1024]{1,0:T(8,128)(2,1)S(1)}, bf16[16,1024]{1,0:T(8,128)(2,1)}, u32[]{:S(2)}) copy-start(bf16[16,1024]{1,0:T(8,128)(2,1)} %param.2) | copy-start | bytes 98308
  179.9 34.0 %copy-start.3 = (bf16[16,1024]{1,0:T(8,128)(2,1)S(1)}, bf16[16,1024]{1,0:T(8,128)(2,1)}, u32[]{:S(2)}) copy-start(bf16[16,1024]{1,0:T(8,128)(2,1)} %param.3) | copy-start | bytes 98308
  179.9 34.0 %all-to-all-start.5 = ((bf16[4,16,1024]{2,1,0:T(8,128)(2,1)}), bf16[4,16,1024]{2,1,0:T(8,128)(2,1)S(1)}, u32[]{:S(2)}, u32[]{:S(2)}) async-start(bf16[4,16,1024]{2,1,0:T(8,128)(2,1)} %reduce_sum.90), calls=%async_computation.5 | async-start | bytes 262144 | tf_op jit(solution)/shard_map/all_to_all | solution.py:35
  185.0 17.6 %collective-permute-start.10 = (f32[2,16,1024]{2,1,0:T(8,128)S(1)}, f32[2,16,1024]{2,1,0:T(8,128)S(1)}, u32[]{:S(2)}, u32[]{:S(2)}) collective-permute-start(f32[2,16,1024]{2,1,0:T(8,128)S(1)} %dynamic-slice_bitcast_fusion.4), channel_id=1, source_target_pairs={{0,64},{32,96},{64,0},{96,32},{128,192},{160,224},{192,128},{224,1... | collective-permute-start | bytes 393224 | tf_op jit(solution)/shard_map/ppermute | solution.py:24
  202.6 11.3 %collective-permute-start.11 = (f32[16,1024]{1,0:T(8,128)S(1)}, f32[16,1024]{1,0:T(8,128)S(1)}, u32[]{:S(2)}, u32[]{:S(2)}) collective-permute-start(f32[16,1024]{1,0:T(8,128)S(1)} %dynamic-slice_bitcast_fusion.5), channel_id=1, source_target_pairs={{0,128},{32,160},{64,192},{96,224},{128,0},{160,32},{192,64},{224,... | collective-permute-start | bytes 196616 | tf_op jit(solution)/shard_map/ppermute | solution.py:24

commit v4 on v3

--- a/solution.py
+++ b/solution.py
@@ -1,3 +1,5 @@
+import functools
+
 import jax
 import jax.numpy as jnp
 from jax import lax
@@ -7,12 +9,9 @@
 
 fine = {"y": 4, "zl": 8, "zh": 4, "x": 4, "core": 2}
 chip = ("x", "core")
+blk = ("y", "zl")
 bits = (4, 2, 1)
 everything = ("y", "zl", "zh", "x", "core")
-
-
-def axes(axis):
-    return axis if isinstance(axis, tuple) else (axis,)
 
 
 def gather(rows, axis):
@@ -60,22 +59,25 @@
 def scatter_sum_by_halving(parts, axis, steps):
     for step in reversed(steps):
         upper = jnp.where((lax.axis_index(axis) & step) != 0, 1, 0)
-        given = swap(lax.dynamic_index_in_dim(parts, 1 - upper, 0, False), axis, step)
+        given = lax.dynamic_index_in_dim(parts, 1 - upper, 0, False)
+        if given.ndim > 2:
+            given = given.astype(jnp.bfloat16)
+        given = swap(given, axis, step).astype(jnp.float32)
         parts = lax.dynamic_index_in_dim(parts, upper, 0, False) + given
     return parts
 
 
-def lse_over(row, col, row_axis, col_axis):
-    n_row, n_col = lax.axis_size(row_axis), lax.axis_size(col_axis)
-    here, there = lax.axis_index(col_axis), lax.axis_index(row_axis)
-    same = (jnp.arange(n_col) == here)[:, None, None]
-    sent = jnp.broadcast_to(jnp.where(same, row, col), (n_col, n_row, row.shape[0]))
-    came = lax.all_to_all(sent.reshape(-1, row.shape[0]), axes(col_axis) + axes(row_axis), 0, 0)
-    came = came.reshape(sent.shape)
-    rows = lax.dynamic_index_in_dim(came, here, 0, False)
-    cols = lax.dynamic_index_in_dim(came, there, 1, False)
-    cols = jnp.where((jnp.arange(n_col) == here)[:, None], col, cols)
-    return lse(rows, 0), lse(cols, 0)
+def lse_of(*values):
+    top = functools.reduce(jnp.maximum, values)
+    return top + jnp.log(sum(jnp.exp(value - top) for value in values))
+
+
+def lse_rows_cols(row, col):
+    col = lse(gather(col, blk), 0)
+    row = lse_of(row, swap(row, "core", 1))
+    row = lse_of(row, *(swap(row, "x", step) for step in (1, 2, 3)))
+    row, col = lax.optimization_barrier((row, col))
+    return lse(gather(row, "zh"), 0), col
 
 
 def body(image_emb, text_emb):
@@ -85,8 +87,7 @@
     row_lanes, col_lanes = img_rows.shape[:-1], txt_cols.shape[:-1]
     img_rows, txt_cols = img_rows.reshape(-1, width), txt_cols.reshape(-1, width)
     scores = logit_scale * jnp.dot(img_rows, txt_cols.T, preferred_element_type=jnp.float32)
-    row_lse, col_lse = lse_over(lse(scores, 1), lse(scores, 0), chip, "y")
-    row_lse, col_lse = lse_over(row_lse, col_lse, "zh", "zl")
+    row_lse, col_lse = lse_rows_cols(lse(scores, 1), lse(scores, 0))
     weights = (
         0.5 * (jnp.exp(scores - row_lse[:, None]) + jnp.exp(scores - col_lse[None, :]))
     ).astype(jnp.bfloat16)

time: 217 us -> 225 us (1.037)
  the two profiles are of different devices: /device:TPU:4 before, /device:TPU:2 now
where the time goes in v4:
time: 225 us; the launch traced here: 224 us
  starting transfers between devices  121 us (54%)
  waiting for transfers between devices  85.9 us (38%)
  other arithmetic  6.6 us (3%)
  local copies, waits for them, and re-layouts  5.34 us (2%)
  matrix products  4.26 us (2%)
    ppermute x16, starting transfers between devices, swap(): lax.ppermute(value, axis, [(i, i ^ step) for i in range(lax.axis_size(axi...  59.8 us
    all_to_all x4, starting transfers between devices, gather(): return lax.all_to_all(copies, axis, 0, 0)  52 us
    ppermute x16, waiting for transfers between devices, swap(): lax.ppermute(value, axis, [(i, i ^ step) for i in range(lax.axis_size(axi...  46 us
    all_to_all x4, waiting for transfers between devices, gather(): return lax.all_to_all(copies, axis, 0, 0)  29.9 us
    all_to_all x2, waiting for transfers between devices, scatter_sum(): lax.all_to_all(parts.astype(jnp.bfloat16), axis, 0, 0).astype(jnp.float32)  10.1 us
    all_to_all x2, starting transfers between devices, scatter_sum(): lax.all_to_all(parts.astype(jnp.bfloat16), axis, 0, 0).astype(jnp.float32)  9.07 us
  transfers between devices with their start and end apart: 22, of which 13 were waited for; matrix products, arithmetic and copies ran while one was open for 3% of the time, Pallas kernels for 0%

profile of v4, /device:TPU:2, one launch (start us, length us, event | category | flops | bytes accessed | tf_op | source)
XLA Modules:
  0.0 224.1 jit_solution(7955636209008140879)
XLA Ops:
  0.6 9.1 %collective-permute-start = (bf16[16,1024]{1,0:T(8,128)(2,1)}, bf16[16,1024]{1,0:T(8,128)(2,1)S(1)}, u32[]{:S(2)}, u32[]{:S(2)}) collective-permute-start(bf16[16,1024]{1,0:T(8,128)(2,1)} %param.3), channel_id=1, source_target_pairs={{0,128},{32,160},{64,192},{96,224},{128,0},{160,32},{192,64},{224,... | collective-permute-start | bytes 98312 | tf_op jit(solution)/shard_map/ppermute | solution.py:23
  11.2 23.5 %all-to-all-start = ((bf16[4,16,1024]{2,1,0:T(8,128)(2,1)}), bf16[4,16,1024]{2,1,0:T(8,128)(2,1)S(1)}, u32[]{:S(2)}, u32[]{:S(2)}) async-start(bf16[4,16,1024]{2,1,0:T(8,128)(2,1)} %broadcast_in_dim.8), calls=%async_computation | async-start | bytes 262144 | tf_op jit(solution)/shard_map/all_to_all | solution.py:19
  35.5 3.4 %collective-permute-start.1 = (bf16[2,16,1024]{2,1,0:T(8,128)(2,1)S(1)}, bf16[2,16,1024]{2,1,0:T(8,128)(2,1)S(1)}, u32[]{:S(2)}, u32[]{:S(2)}) collective-permute-start(bf16[2,16,1024]{2,1,0:T(8,128)(2,1)S(1)} %pad_maximum_fusion.3), channel_id=1, source_target_pairs={{0,64},{32,96},{64,0},{96,32},{128,192},{160,224},{192,128},{224,1... | collective-permute-start | bytes 196616 | tf_op jit(solution)/shard_map/ppermute | solution.py:23
  38.9 8.1 %collective-permute-done.1 = bf16[2,16,1024]{2,1,0:T(8,128)(2,1)S(1)} collective-permute-done((bf16[2,16,1024]{2,1,0:T(8,128)(2,1)S(1)}, bf16[2,16,1024]{2,1,0:T(8,128)(2,1)S(1)}, u32[]{:S(2)}, u32[]{:S(2)}) %collective-permute-start.1) | collective-permute-done | bytes 65568 | tf_op jit(solution)/shard_map/ppermute | solution.py:23
  47.0 1.9 collective-permute-start.2
  49.0 6.7 %collective-permute-done.2 = bf16[2,2,16,1024]{3,2,1,0:T(8,128)(2,1)S(1)} collective-permute-done((bf16[2,2,16,1024]{3,2,1,0:T(8,128)(2,1)S(1)}, bf16[2,2,16,1024]{3,2,1,0:T(8,128)(2,1)S(1)}, u32[]{:S(2)}, u32[]{:S(2)}) %collective-permute-start.2) | collective-permute-done | bytes 131104 | tf_op jit(solution)/shard_map/ppermute | solution.py:23
  55.7 7.8 %all-to-all-done = bf16[4,16,1024]{2,1,0:T(8,128)(2,1)S(1)} async-done(((bf16[4,16,1024]{2,1,0:T(8,128)(2,1)}), bf16[4,16,1024]{2,1,0:T(8,128)(2,1)S(1)}, u32[]{:S(2)}, u32[]{:S(2)}) %all-to-all-start) | async-done | bytes 131104 | tf_op jit(solution)/shard_map/all_to_all | solution.py:19
  64.6 4.8 %all-to-all-start.1 = ((bf16[8,4,16,1024]{3,2,1,0:T(8,128)(2,1)}), bf16[8,4,16,1024]{3,2,1,0:T(8,128)(2,1)S(1)}, u32[]{:S(2)}, u32[]{:S(2)}) async-start(bf16[8,4,16,1024]{3,2,1,0:T(8,128)(2,1)} %broadcast_in_dim.9), calls=%async_computation.1 | async-start | bytes 2097152 | tf_op jit(solution)/shard_map/all_to_all | solution.py:19
  69.5 5.1 %collective-permute-start.4 = (bf16[2,2,2,16,1024]{4,3,2,1,0:T(8,128)(2,1)S(1)}, bf16[2,2,2,16,1024]{4,3,2,1,0:T(8,128)(2,1)S(1)}, u32[]{:S(2)}, u32[]{:S(2)}) collective-permute-start(bf16[2,2,2,16,1024]{4,3,2,1,0:T(8,128)(2,1)S(1)} %pad_maximum_fusion.1), channel_id=1, source_target_pairs={{0,512},{256,768},{512,0},{768,256},{1,513},{257,769},{513,1},{769... | collective-permute-start | bytes 786440 | tf_op jit(solution)/shard_map/ppermute | solution.py:23
  74.6 3.0 %collective-permute-start.5 = (bf16[2,2,2,16,1024]{4,3,2,1,0:T(8,128)(2,1)S(1)}, bf16[2,2,2,16,1024]{4,3,2,1,0:T(8,128)(2,1)S(1)}, u32[]{:S(2)}, u32[]{:S(2)}) collective-permute-start(bf16[2,2,2,16,1024]{4,3,2,1,0:T(8,128)(2,1)S(1)} %pad_maximum_fusion.1), channel_id=1, source_target_pairs={{0,768},{256,512},{512,256},{768,0},{1,769},{257,513},{513,257},{7... | collective-permute-start | bytes 786440 | tf_op jit(solution)/shard_map/ppermute | solution.py:23
  77.6 1.9 collective-permute-start.3
  79.5 1.8 collective-permute-done.4
  81.3 5.5 %collective-permute-done.5 = bf16[2,2,2,16,1024]{4,3,2,1,0:T(8,128)(2,1)S(1)} collective-permute-done((bf16[2,2,2,16,1024]{4,3,2,1,0:T(8,128)(2,1)S(1)}, bf16[2,2,2,16,1024]{4,3,2,1,0:T(8,128)(2,1)S(1)}, u32[]{:S(2)}, u32[]{:S(2)}) %collective-permute-start.5) | collective-permute-done | bytes 262176 | tf_op jit(solution)/shard_map/ppermute | solution.py:23
  89.6 9.5 %all-to-all-start.2 = ((f32[32,1,512]{2,1,0:T(1,128)}), f32[32,1,512]{2,1,0:T(1,128)S(1)}, u32[]{:S(2)}, u32[]{:S(2)}) async-start(f32[32,1,512]{2,1,0:T(1,128)} %broadcast_in_dim.10), calls=%async_computation.2 | async-start | bytes 131072 | tf_op jit(solution)/shard_map/all_to_all | solution.py:19
  99.1 1.9 collective-permute-start.6
  102.2 3.4 %collective-permute-start.9 = (f32[512]{0:T(512)S(1)}, f32[512]{0:T(512)S(1)}, u32[]{:S(2)}, u32[]{:S(2)}) collective-permute-start(f32[512]{0:T(512)S(1)} %log_add_fusion.4), channel_id=1, source_target_pairs={{0,6},{2,4},{4,2},{6,0},{1,7},{3,5},{5,3},{7,1},{8,14},{10,12},{12... | collective-permute-start | bytes 6152 | tf_op jit(solution)/shard_map/ppermute | solution.py:23
  105.6 2.9 %collective-permute-start.8 = (f32[512]{0:T(512)S(1)}, f32[512]{0:T(512)S(1)}, u32[]{:S(2)}, u32[]{:S(2)}) collective-permute-start(f32[512]{0:T(512)S(1)} %log_add_fusion.4), channel_id=1, source_target_pairs={{0,4},{2,6},{4,0},{6,2},{1,5},{3,7},{5,1},{7,3},{8,12},{10,14},{12... | collective-permute-start | bytes 6152 | tf_op jit(solution)/shard_map/ppermute | solution.py:23
  108.5 3.6 %collective-permute-start.7 = (f32[512]{0:T(512)S(1)}, f32[512]{0:T(512)S(1)}, u32[]{:S(2)}, u32[]{:S(2)}) collective-permute-start(f32[512]{0:T(512)S(1)} %log_add_fusion.4), channel_id=1, source_target_pairs={{0,2},{2,0},{4,6},{6,4},{1,3},{3,1},{5,7},{7,5},{8,10},{10,8},{12,... | collective-permute-start | bytes 6152 | tf_op jit(solution)/shard_map/ppermute | solution.py:23
  114.7 14.1 %all-to-all-start.3 = ((f32[4,1,512]{2,1,0:T(1,128)}), f32[4,1,512]{2,1,0:T(1,128)S(1)}, u32[]{:S(2)}, u32[]{:S(2)}) async-start(f32[4,1,512]{2,1,0:T(1,128)} %broadcast_in_dim.11), calls=%async_computation.3 | async-start | bytes 16384 | tf_op jit(solution)/shard_map/all_to_all | solution.py:19
  128.8 22.2 %all-to-all-done.3 = f32[4,1,512]{2,1,0:T(1,128)S(1)} async-done(((f32[4,1,512]{2,1,0:T(1,128)}), f32[4,1,512]{2,1,0:T(1,128)S(1)}, u32[]{:S(2)}, u32[]{:S(2)}) %all-to-all-start.3) | async-done | bytes 8224 | tf_op jit(solution)/shard_map/all_to_all | solution.py:19
  155.4 5.6 %all-to-all-start.4 = ((bf16[8,4,16,1024]{3,2,1,0:T(8,128)(2,1)}), bf16[8,4,16,1024]{3,2,1,0:T(8,128)(2,1)S(1)}, u32[]{:S(2)}, u32[]{:S(2)}) async-start(bf16[8,4,16,1024]{3,2,1,0:T(8,128)(2,1)} %convolution_convert_fusion.1), calls=%async_computation.4 | async-start | bytes 2097152 | tf_op jit(solution)/shard_map/all_to_all | solution.py:34
  161.0 1.8 convolution_convert_fusion
  162.9 3.7 %collective-permute-start.10 = (bf16[2,2,2,16,1024]{4,3,2,1,0:T(8,128)(2,1)S(1)}, bf16[2,2,2,16,1024]{4,3,2,1,0:T(8,128)(2,1)S(1)}, u32[]{:S(2)}, u32[]{:S(2)}) collective-permute-start(bf16[2,2,2,16,1024]{4,3,2,1,0:T(8,128)(2,1)S(1)} %get-tuple-element.11), channel_id=1, source_target_pairs={{0,256},{256,0},{512,768},{768,512},{1,257},{257,1},{513,769},{769... | collective-permute-start | bytes 786440 | tf_op jit(solution)/shard_map/ppermute | solution.py:23
  166.6 4.0 %collective-permute-start.12 = (bf16[2,2,2,16,1024]{4,3,2,1,0:T(8,128)(2,1)S(1)}, bf16[2,2,2,16,1024]{4,3,2,1,0:T(8,128)(2,1)S(1)}, u32[]{:S(2)}, u32[]{:S(2)}) collective-permute-start(bf16[2,2,2,16,1024]{4,3,2,1,0:T(8,128)(2,1)S(1)} %get-tuple-element.12), channel_id=1, source_target_pairs={{0,768},{256,512},{512,256},{768,0},{1,769},{257,513},{513,257},{7... | collective-permute-start | bytes 786440 | tf_op jit(solution)/shard_map/ppermute | solution.py:23
  170.6 2.6 %collective-permute-start.11 = (bf16[2,2,2,16,1024]{4,3,2,1,0:T(8,128)(2,1)S(1)}, bf16[2,2,2,16,1024]{4,3,2,1,0:T(8,128)(2,1)}, u32[]{:S(2)}, u32[]{:S(2)}) collective-permute-start(bf16[2,2,2,16,1024]{4,3,2,1,0:T(8,128)(2,1)S(1)} %get-tuple-element.13), channel_id=1, source_target_pairs={{0,512},{256,768},{512,0},{768,256},{1,513},{257,769},{513,1},{769... | collective-permute-start | bytes 786440 | tf_op jit(solution)/shard_map/ppermute | solution.py:23
  173.2 10.2 %collective-permute-done.12 = bf16[2,2,2,16,1024]{4,3,2,1,0:T(8,128)(2,1)S(1)} collective-permute-done((bf16[2,2,2,16,1024]{4,3,2,1,0:T(8,128)(2,1)S(1)}, bf16[2,2,2,16,1024]{4,3,2,1,0:T(8,128)(2,1)S(1)}, u32[]{:S(2)}, u32[]{:S(2)}) %collective-permute-start.12) | collective-permute-done | bytes 262176 | tf_op jit(solution)/shard_map/ppermute | solution.py:23
  184.5 3.4 %collective-permute-start.13 = (bf16[2,2,16,1024]{3,2,1,0:T(8,128)(2,1)S(1)}, bf16[2,2,16,1024]{3,2,1,0:T(8,128)(2,1)S(1)}, u32[]{:S(2)}, u32[]{:S(2)}) collective-permute-start(bf16[2,2,16,1024]{3,2,1,0:T(8,128)(2,1)S(1)} %fusion.2), channel_id=1, source_target_pairs={{0,32},{32,0},{64,96},{96,64},{128,160},{160,128},{192,224},{224,1... | collective-permute-start | bytes 393224 | tf_op jit(solution)/shard_map/ppermute | solution.py:23
  188.8 3.5 %all-to-all-start.5 = ((bf16[4,16,1024]{2,1,0:T(8,128)(2,1)}), bf16[4,16,1024]{2,1,0:T(8,128)(2,1)S(1)}, u32[]{:S(2)}, u32[]{:S(2)}) async-start(bf16[4,16,1024]{2,1,0:T(8,128)(2,1)} %reduce_sum.70), calls=%async_computation.5 | async-start | bytes 262144 | tf_op jit(solution)/shard_map/all_to_all | solution.py:34
  192.3 4.3 %collective-permute-start.14 = (bf16[2,16,1024]{2,1,0:T(8,128)(2,1)S(1)}, bf16[2,16,1024]{2,1,0:T(8,128)(2,1)S(1)}, u32[]{:S(2)}, u32[]{:S(2)}) collective-permute-start(bf16[2,16,1024]{2,1,0:T(8,128)(2,1)S(1)} %fusion.6), channel_id=1, source_target_pairs={{0,64},{32,96},{64,0},{96,32},{128,192},{160,224},{192,128},{224,1... | collective-permute-start | bytes 196616 | tf_op jit(solution)/shard_map/ppermute | solution.py:23
  196.6 10.1 %collective-permute-done.14 = bf16[2,16,1024]{2,1,0:T(8,128)(2,1)S(1)} collective-permute-done((bf16[2,16,1024]{2,1,0:T(8,128)(2,1)S(1)}, bf16[2,16,1024]{2,1,0:T(8,128)(2,1)S(1)}, u32[]{:S(2)}, u32[]{:S(2)}) %collective-permute-start.14) | collective-permute-done | bytes 65568 | tf_op jit(solution)/shard_map/ppermute | solution.py:23
  206.8 5.8 %collective-permute-start.15 = (f32[16,1024]{1,0:T(8,128)S(1)}, f32[16,1024]{1,0:T(8,128)S(1)}, u32[]{:S(2)}, u32[]{:S(2)}) collective-permute-start(f32[16,1024]{1,0:T(8,128)S(1)} %dynamic-slice_bitcast_fusion.3), channel_id=1, source_target_pairs={{0,128},{32,160},{64,192},{96,224},{128,0},{160,32},{192,64},{224,... | collective-permute-start | bytes 196616 | tf_op jit(solution)/shard_map/ppermute | solution.py:23
  212.6 10.1 %all-to-all-done.5 = bf16[4,16,1024]{2,1,0:T(8,128)(2,1)S(1)} async-done(((bf16[4,16,1024]{2,1,0:T(8,128)(2,1)}), bf16[4,16,1024]{2,1,0:T(8,128)(2,1)S(1)}, u32[]{:S(2)}, u32[]{:S(2)}) %all-to-all-start.5) | async-done | bytes 131104 | tf_op jit(solution)/shard_map/all_to_all | solution.py:34
  (61 shorter events, 17.9 us)
Async XLA Ops:
  0.6 34.1 %collective-permute-start = (bf16[16,1024]{1,0:T(8,128)(2,1)}, bf16[16,1024]{1,0:T(8,128)(2,1)S(1)}, u32[]{:S(2)}, u32[]{:S(2)}) collective-permute-start(bf16[16,1024]{1,0:T(8,128)(2,1)} %param.3), channel_id=1, source_target_pairs={{0,128},{32,160},{64,192},{96,224},{128,0},{160,32},{192,64},{224,... | collective-permute-start | bytes 98312 | tf_op jit(solution)/shard_map/ppermute | solution.py:23
  11.2 52.3 %all-to-all-start = ((bf16[4,16,1024]{2,1,0:T(8,128)(2,1)}), bf16[4,16,1024]{2,1,0:T(8,128)(2,1)S(1)}, u32[]{:S(2)}, u32[]{:S(2)}) async-start(bf16[4,16,1024]{2,1,0:T(8,128)(2,1)} %broadcast_in_dim.8), calls=%async_computation | async-start | bytes 262144 | tf_op jit(solution)/shard_map/all_to_all | solution.py:19
  35.5 11.5 %collective-permute-start.1 = (bf16[2,16,1024]{2,1,0:T(8,128)(2,1)S(1)}, bf16[2,16,1024]{2,1,0:T(8,128)(2,1)S(1)}, u32[]{:S(2)}, u32[]{:S(2)}) collective-permute-start(bf16[2,16,1024]{2,1,0:T(8,128)(2,1)S(1)} %pad_maximum_fusion.3), channel_id=1, source_target_pairs={{0,64},{32,96},{64,0},{96,32},{128,192},{160,224},{192,128},{224,1... | collective-permute-start | bytes 196616 | tf_op jit(solution)/shard_map/ppermute | solution.py:23
  47.0 8.6 %collective-permute-start.2 = (bf16[2,2,16,1024]{3,2,1,0:T(8,128)(2,1)S(1)}, bf16[2,2,16,1024]{3,2,1,0:T(8,128)(2,1)S(1)}, u32[]{:S(2)}, u32[]{:S(2)}) collective-permute-start(bf16[2,2,16,1024]{3,2,1,0:T(8,128)(2,1)S(1)} %pad_maximum_fusion.2), channel_id=1, source_target_pairs={{0,32},{32,0},{64,96},{96,64},{128,160},{160,128},{192,224},{224,1... | collective-permute-start | bytes 393224 | tf_op jit(solution)/shard_map/ppermute | solution.py:23
  64.6 22.9 %all-to-all-start.1 = ((bf16[8,4,16,1024]{3,2,1,0:T(8,128)(2,1)}), bf16[8,4,16,1024]{3,2,1,0:T(8,128)(2,1)S(1)}, u32[]{:S(2)}, u32[]{:S(2)}) async-start(bf16[8,4,16,1024]{3,2,1,0:T(8,128)(2,1)} %broadcast_in_dim.9), calls=%async_computation.1 | async-start | bytes 2097152 | tf_op jit(solution)/shard_map/all_to_all | solution.py:19
  69.5 11.9 %collective-permute-start.4 = (bf16[2,2,2,16,1024]{4,3,2,1,0:T(8,128)(2,1)S(1)}, bf16[2,2,2,16,1024]{4,3,2,1,0:T(8,128)(2,1)S(1)}, u32[]{:S(2)}, u32[]{:S(2)}) collective-permute-start(bf16[2,2,2,16,1024]{4,3,2,1,0:T(8,128)(2,1)S(1)} %pad_maximum_fusion.1), channel_id=1, source_target_pairs={{0,512},{256,768},{512,0},{768,256},{1,513},{257,769},{513,1},{769... | collective-permute-start | bytes 786440 | tf_op jit(solution)/shard_map/ppermute | solution.py:23
  74.6 12.3 %collective-permute-start.5 = (bf16[2,2,2,16,1024]{4,3,2,1,0:T(8,128)(2,1)S(1)}, bf16[2,2,2,16,1024]{4,3,2,1,0:T(8,128)(2,1)S(1)}, u32[]{:S(2)}, u32[]{:S(2)}) collective-permute-start(bf16[2,2,2,16,1024]{4,3,2,1,0:T(8,128)(2,1)S(1)} %pad_maximum_fusion.1), channel_id=1, source_target_pairs={{0,768},{256,512},{512,256},{768,0},{1,769},{257,513},{513,257},{7... | collective-permute-start | bytes 786440 | tf_op jit(solution)/shard_map/ppermute | solution.py:23
  77.6 9.7 %collective-permute-start.3 = (bf16[2,2,2,16,1024]{4,3,2,1,0:T(8,128)(2,1)S(1)}, bf16[2,2,2,16,1024]{4,3,2,1,0:T(8,128)(2,1)S(1)}, u32[]{:S(2)}, u32[]{:S(2)}) collective-permute-start(bf16[2,2,2,16,1024]{4,3,2,1,0:T(8,128)(2,1)S(1)} %pad_maximum_fusion.1), channel_id=1, source_target_pairs={{0,256},{256,0},{512,768},{768,512},{1,257},{257,1},{513,769},{769... | collective-permute-start | bytes 786440 | tf_op jit(solution)/shard_map/ppermute | solution.py:23
  87.5 1.0 copy-start
  89.6 24.4 %all-to-all-start.2 = ((f32[32,1,512]{2,1,0:T(1,128)}), f32[32,1,512]{2,1,0:T(1,128)S(1)}, u32[]{:S(2)}, u32[]{:S(2)}) async-start(f32[32,1,512]{2,1,0:T(1,128)} %broadcast_in_dim.10), calls=%async_computation.2 | async-start | bytes 131072 | tf_op jit(solution)/shard_map/all_to_all | solution.py:19
  99.1 3.1 %collective-permute-start.6 = (f32[512]{0:T(512)S(1)}, f32[512]{0:T(512)S(1)}, u32[]{:S(2)}, u32[]{:S(2)}) collective-permute-start(f32[512]{0:T(512)S(1)} %log_add_fusion.5), channel_id=1, source_target_pairs={{0,1},{1,0},{2,3},{3,2},{4,5},{5,4},{6,7},{7,6},{8,9},{9,8},{10,11... | collective-permute-start | bytes 6152 | tf_op jit(solution)/shard_map/ppermute | solution.py:23
  102.2 9.8 %collective-permute-start.9 = (f32[512]{0:T(512)S(1)}, f32[512]{0:T(512)S(1)}, u32[]{:S(2)}, u32[]{:S(2)}) collective-permute-start(f32[512]{0:T(512)S(1)} %log_add_fusion.4), channel_id=1, source_target_pairs={{0,6},{2,4},{4,2},{6,0},{1,7},{3,5},{5,3},{7,1},{8,14},{10,12},{12... | collective-permute-start | bytes 6152 | tf_op jit(solution)/shard_map/ppermute | solution.py:23
  105.6 7.0 %collective-permute-start.8 = (f32[512]{0:T(512)S(1)}, f32[512]{0:T(512)S(1)}, u32[]{:S(2)}, u32[]{:S(2)}) collective-permute-start(f32[512]{0:T(512)S(1)} %log_add_fusion.4), channel_id=1, source_target_pairs={{0,4},{2,6},{4,0},{6,2},{1,5},{3,7},{5,1},{7,3},{8,12},{10,14},{12... | collective-permute-start | bytes 6152 | tf_op jit(solution)/shard_map/ppermute | solution.py:23
  108.5 5.5 %collective-permute-start.7 = (f32[512]{0:T(512)S(1)}, f32[512]{0:T(512)S(1)}, u32[]{:S(2)}, u32[]{:S(2)}) collective-permute-start(f32[512]{0:T(512)S(1)} %log_add_fusion.4), channel_id=1, source_target_pairs={{0,2},{2,0},{4,6},{6,4},{1,3},{3,1},{5,7},{7,5},{8,10},{10,8},{12,... | collective-permute-start | bytes 6152 | tf_op jit(solution)/shard_map/ppermute | solution.py:23
  114.7 36.3 %all-to-all-start.3 = ((f32[4,1,512]{2,1,0:T(1,128)}), f32[4,1,512]{2,1,0:T(1,128)S(1)}, u32[]{:S(2)}, u32[]{:S(2)}) async-start(f32[4,1,512]{2,1,0:T(1,128)} %broadcast_in_dim.11), calls=%async_computation.3 | async-start | bytes 16384 | tf_op jit(solution)/shard_map/all_to_all | solution.py:19
  152.5 1.2 copy-start.1
  155.4 32.5 %all-to-all-start.4 = ((bf16[8,4,16,1024]{3,2,1,0:T(8,128)(2,1)}), bf16[8,4,16,1024]{3,2,1,0:T(8,128)(2,1)S(1)}, u32[]{:S(2)}, u32[]{:S(2)}) async-start(bf16[8,4,16,1024]{3,2,1,0:T(8,128)(2,1)} %convolution_convert_fusion.1), calls=%async_computation.4 | async-start | bytes 2097152 | tf_op jit(solution)/shard_map/all_to_all | solution.py:34
  162.9 10.3 %collective-permute-start.10 = (bf16[2,2,2,16,1024]{4,3,2,1,0:T(8,128)(2,1)S(1)}, bf16[2,2,2,16,1024]{4,3,2,1,0:T(8,128)(2,1)S(1)}, u32[]{:S(2)}, u32[]{:S(2)}) collective-permute-start(bf16[2,2,2,16,1024]{4,3,2,1,0:T(8,128)(2,1)S(1)} %get-tuple-element.11), channel_id=1, source_target_pairs={{0,256},{256,0},{512,768},{768,512},{1,257},{257,1},{513,769},{769... | collective-permute-start | bytes 786440 | tf_op jit(solution)/shard_map/ppermute | solution.py:23
  166.6 16.8 %collective-permute-start.12 = (bf16[2,2,2,16,1024]{4,3,2,1,0:T(8,128)(2,1)S(1)}, bf16[2,2,2,16,1024]{4,3,2,1,0:T(8,128)(2,1)S(1)}, u32[]{:S(2)}, u32[]{:S(2)}) collective-permute-start(bf16[2,2,2,16,1024]{4,3,2,1,0:T(8,128)(2,1)S(1)} %get-tuple-element.12), channel_id=1, source_target_pairs={{0,768},{256,512},{512,256},{768,0},{1,769},{257,513},{513,257},{7... | collective-permute-start | bytes 786440 | tf_op jit(solution)/shard_map/ppermute | solution.py:23
  170.6 12.8 %collective-permute-start.11 = (bf16[2,2,2,16,1024]{4,3,2,1,0:T(8,128)(2,1)S(1)}, bf16[2,2,2,16,1024]{4,3,2,1,0:T(8,128)(2,1)}, u32[]{:S(2)}, u32[]{:S(2)}) collective-permute-start(bf16[2,2,2,16,1024]{4,3,2,1,0:T(8,128)(2,1)S(1)} %get-tuple-element.13), channel_id=1, source_target_pairs={{0,512},{256,768},{512,0},{768,256},{1,513},{257,769},{513,1},{769... | collective-permute-start | bytes 786440 | tf_op jit(solution)/shard_map/ppermute | solution.py:23
  184.5 7.7 %collective-permute-start.13 = (bf16[2,2,16,1024]{3,2,1,0:T(8,128)(2,1)S(1)}, bf16[2,2,16,1024]{3,2,1,0:T(8,128)(2,1)S(1)}, u32[]{:S(2)}, u32[]{:S(2)}) collective-permute-start(bf16[2,2,16,1024]{3,2,1,0:T(8,128)(2,1)S(1)} %fusion.2), channel_id=1, source_target_pairs={{0,32},{32,0},{64,96},{96,64},{128,160},{160,128},{192,224},{224,1... | collective-permute-start | bytes 393224 | tf_op jit(solution)/shard_map/ppermute | solution.py:23
  188.8 33.9 %copy-start.2 = (bf16[16,1024]{1,0:T(8,128)(2,1)S(1)}, bf16[16,1024]{1,0:T(8,128)(2,1)}, u32[]{:S(2)}) copy-start(bf16[16,1024]{1,0:T(8,128)(2,1)} %param.2) | copy-start | bytes 98308
  188.8 34.0 %copy-start.3 = (bf16[16,1024]{1,0:T(8,128)(2,1)S(1)}, bf16[16,1024]{1,0:T(8,128)(2,1)}, u32[]{:S(2)}) copy-start(bf16[16,1024]{1,0:T(8,128)(2,1)} %param.3) | copy-start | bytes 98308
  188.8 33.9 %all-to-all-start.5 = ((bf16[4,16,1024]{2,1,0:T(8,128)(2,1)}), bf16[4,16,1024]{2,1,0:T(8,128)(2,1)S(1)}, u32[]{:S(2)}, u32[]{:S(2)}) async-start(bf16[4,16,1024]{2,1,0:T(8,128)(2,1)} %reduce_sum.70), calls=%async_computation.5 | async-start | bytes 262144 | tf_op jit(solution)/shard_map/all_to_all | solution.py:34
  192.3 14.4 %collective-permute-start.14 = (bf16[2,16,1024]{2,1,0:T(8,128)(2,1)S(1)}, bf16[2,16,1024]{2,1,0:T(8,128)(2,1)S(1)}, u32[]{:S(2)}, u32[]{:S(2)}) collective-permute-start(bf16[2,16,1024]{2,1,0:T(8,128)(2,1)S(1)} %fusion.6), channel_id=1, source_target_pairs={{0,64},{32,96},{64,0},{96,32},{128,192},{160,224},{192,128},{224,1... | collective-permute-start | bytes 196616 | tf_op jit(solution)/shard_map/ppermute | solution.py:23
  206.8 15.9 %collective-permute-start.15 = (f32[16,1024]{1,0:T(8,128)S(1)}, f32[16,1024]{1,0:T(8,128)S(1)}, u32[]{:S(2)}, u32[]{:S(2)}) collective-permute-start(f32[16,1024]{1,0:T(8,128)S(1)} %dynamic-slice_bitcast_fusion.3), channel_id=1, source_target_pairs={{0,128},{32,160},{64,192},{96,224},{128,0},{160,32},{192,64},{224,... | collective-permute-start | bytes 196616 | tf_op jit(solution)/shard_map/ppermute | solution.py:23

commit v5 on v4

--- a/solution.py
+++ b/solution.py
@@ -10,7 +10,7 @@
 fine = {"y": 4, "zl": 8, "zh": 4, "x": 4, "core": 2}
 chip = ("x", "core")
 blk = ("y", "zl")
-bits = (4, 2, 1)
+ring = ((1, 1), (3, 2))
 everything = ("y", "zl", "zh", "x", "core")
 
 
@@ -49,19 +49,17 @@
 
 
 def gather_by_doubling(rows, axis, steps):
-    for step in steps:
+    for step, bit in steps:
         other = swap(rows, axis, step)
-        upper = (lax.axis_index(axis) & step) != 0
+        upper = (lax.axis_index(axis) & bit) != 0
         rows = jnp.stack([jnp.where(upper, other, rows), jnp.where(upper, rows, other)])
     return rows
 
 
 def scatter_sum_by_halving(parts, axis, steps):
-    for step in reversed(steps):
-        upper = jnp.where((lax.axis_index(axis) & step) != 0, 1, 0)
-        given = lax.dynamic_index_in_dim(parts, 1 - upper, 0, False)
-        if given.ndim > 2:
-            given = given.astype(jnp.bfloat16)
+    for step, bit in reversed(steps):
+        upper = jnp.where((lax.axis_index(axis) & bit) != 0, 1, 0)
+        given = lax.dynamic_index_in_dim(parts, 1 - upper, 0, False).astype(jnp.bfloat16)
         given = swap(given, axis, step).astype(jnp.float32)
         parts = lax.dynamic_index_in_dim(parts, upper, 0, False) + given
     return parts
@@ -73,17 +71,21 @@
 
 
 def lse_rows_cols(row, col):
-    col = lse(gather(col, blk), 0)
-    row = lse_of(row, swap(row, "core", 1))
-    row = lse_of(row, *(swap(row, "x", step) for step in (1, 2, 3)))
+    row = lse(gather(row, chip), 0)
+    col = lse_of(col, *(swap(col, "y", step) for step in (1, 2, 3)))
     row, col = lax.optimization_barrier((row, col))
-    return lse(gather(row, "zh"), 0), col
+    for step, _ in ring:
+        row = lse_of(row, swap(row, "zh", step))
+    for step in (1, 2, 4):
+        col = lse_of(col, swap(col, "zl", step))
+    return row, col
 
 
 def body(image_emb, text_emb):
     own_rows, width = image_emb.shape
-    img_rows = gather(gather(image_emb, "zh"), chip)
-    txt_cols = gather_by_swaps(gather_by_doubling(text_emb, "zl", bits), "y")
+    img_rows = gather(gather_by_doubling(image_emb, "zh", ring), chip)
+    txt_cols = gather_by_swaps(gather(text_emb, "zl"), "y")
+    img_rows = img_rows.reshape(img_rows.shape[0], -1, own_rows, width)
     row_lanes, col_lanes = img_rows.shape[:-1], txt_cols.shape[:-1]
     img_rows, txt_cols = img_rows.reshape(-1, width), txt_cols.reshape(-1, width)
     scores = logit_scale * jnp.dot(img_rows, txt_cols.T, preferred_element_type=jnp.float32)
@@ -93,19 +95,18 @@
     ).astype(jnp.bfloat16)
     image_part = jnp.dot(weights, txt_cols, preferred_element_type=jnp.float32)
     image_part = image_part.reshape(row_lanes + (width,))
-    image_sum = scatter_sum(scatter_sum(image_part, chip), "zh")
+    image_sum = scatter_sum(image_part, chip).reshape(2, 2, own_rows, width)
+    image_sum = scatter_sum_by_halving(image_sum, "zh", ring)
     text_part = lax.dot_general(
         weights, img_rows, (((0,), (0,)), ((), ())), preferred_element_type=jnp.float32
     )
     text_part = text_part.reshape(col_lanes + (width,))
-    text_sum = scatter_sum_by_halving(scatter_sum_by_swaps(text_part, "y"), "zl", bits)
+    text_sum = scatter_sum(scatter_sum_by_swaps(text_part, "y"), "zl")
     grad_image = logit_scale * image_sum - logit_scale * text_emb.astype(jnp.float32)
     grad_text = logit_scale * text_sum - logit_scale * image_emb.astype(jnp.float32)
     own_row = lax.axis_index(chip) * row_lanes[1] + lax.axis_index("zh")
     own_row_lse = lax.dynamic_slice_in_dim(row_lse, own_row * own_rows, own_rows, 0)
-    zl = lax.axis_index("zl")
-    own_col = lax.axis_index("y") * 8 + (zl & 1) * 4 + (zl & 2) + (zl >> 2)
-    own_col_lse = lax.dynamic_slice_in_dim(col_lse, own_col * own_rows, own_rows, 0)
+    own_col_lse = lax.dynamic_slice_in_dim(col_lse, lax.axis_index(blk) * own_rows, own_rows, 0)
     diag = logit_scale * jnp.sum(
         image_emb.astype(jnp.float32) * text_emb.astype(jnp.float32), axis=1
     )

time: 225 us -> 219 us (0.973)
  the two profiles are of different devices: /device:TPU:2 before, /device:TPU:42 now
where the time goes in v5:
time: 219 us; the launch traced here: 218 us
  starting transfers between devices  162 us (74%)
  waiting for transfers between devices  39.9 us (18%)
  other arithmetic  5.7 us (3%)
  local copies, waits for them, and re-layouts  4.89 us (2%)
  matrix products  4.26 us (2%)
    ppermute x18, starting transfers between devices, swap(): lax.ppermute(value, axis, [(i, i ^ step) for i in range(lax.axis_size(axi...  125 us
    ppermute x18, waiting for transfers between devices, swap(): lax.ppermute(value, axis, [(i, i ^ step) for i in range(lax.axis_size(axi...  36 us
    all_to_all x3, starting transfers between devices, gather(): return lax.all_to_all(copies, axis, 0, 0)  22.3 us
    all_to_all x2, starting transfers between devices, scatter_sum(): lax.all_to_all(parts.astype(jnp.bfloat16), axis, 0, 0).astype(jnp.float32)  14.7 us
  transfers between devices with their start and end apart: 23, of which 11 were waited for; matrix products, arithmetic and copies ran while one was open for 3% of the time, Pallas kernels for 0%

profile of v5, /device:TPU:42, one launch (start us, length us, event | category | flops | bytes accessed | tf_op | source)
XLA Modules:
  0.0 217.8 jit_solution(15215880612253328854)
XLA Ops:
  2.1 12.6 %all-to-all-start.1 = ((bf16[8,16,1024]{2,1,0:T(8,128)(2,1)}), bf16[8,16,1024]{2,1,0:T(8,128)(2,1)S(1)}, u32[]{:S(2)}, u32[]{:S(2)}) async-start(bf16[8,16,1024]{2,1,0:T(8,128)(2,1)} %broadcast_in_dim.7), calls=%async_computation.1 | async-start | bytes 524288 | tf_op jit(solution)/shard_map/all_to_all | solution.py:19
  14.7 15.7 %collective-permute-start = (bf16[16,1024]{1,0:T(8,128)(2,1)}, bf16[16,1024]{1,0:T(8,128)(2,1)S(1)}, u32[]{:S(2)}, u32[]{:S(2)}) collective-permute-start(bf16[16,1024]{1,0:T(8,128)(2,1)} %param.2), channel_id=1, source_target_pairs={{0,8},{8,0},{16,24},{24,16},{1,9},{9,1},{17,25},{25,17},{2,10},{10... | collective-permute-start | bytes 98312 | tf_op jit(solution)/shard_map/ppermute | solution.py:23
  30.5 2.5 %collective-permute-done = bf16[16,1024]{1,0:T(8,128)(2,1)S(1)} collective-permute-done((bf16[16,1024]{1,0:T(8,128)(2,1)}, bf16[16,1024]{1,0:T(8,128)(2,1)S(1)}, u32[]{:S(2)}, u32[]{:S(2)}) %collective-permute-start) | collective-permute-done | bytes 32800 | tf_op jit(solution)/shard_map/ppermute | solution.py:23
  33.8 13.8 %collective-permute-start.1 = (bf16[2,16,1024]{2,1,0:T(8,128)(2,1)S(1)}, bf16[2,16,1024]{2,1,0:T(8,128)(2,1)S(1)}, u32[]{:S(2)}, u32[]{:S(2)}) collective-permute-start(bf16[2,16,1024]{2,1,0:T(8,128)(2,1)S(1)} %pad_maximum_fusion.2), channel_id=1, source_target_pairs={{0,24},{8,16},{16,8},{24,0},{1,25},{9,17},{17,9},{25,1},{2,26},{10... | collective-permute-start | bytes 196616 | tf_op jit(solution)/shard_map/ppermute | solution.py:23
  47.6 2.7 %collective-permute-done.1 = bf16[2,16,1024]{2,1,0:T(8,128)(2,1)S(1)} collective-permute-done((bf16[2,16,1024]{2,1,0:T(8,128)(2,1)S(1)}, bf16[2,16,1024]{2,1,0:T(8,128)(2,1)S(1)}, u32[]{:S(2)}, u32[]{:S(2)}) %collective-permute-start.1) | collective-permute-done | bytes 65568 | tf_op jit(solution)/shard_map/ppermute | solution.py:23
  51.4 4.8 %all-to-all-start = ((bf16[8,2,2,16,1024]{4,3,2,1,0:T(8,128)(2,1)}), bf16[8,2,2,16,1024]{4,3,2,1,0:T(8,128)(2,1)S(1)}, u32[]{:S(2)}, u32[]{:S(2)}) async-start(bf16[8,2,2,16,1024]{4,3,2,1,0:T(8,128)(2,1)} %broadcast_in_dim.6), calls=%async_computation | async-start | bytes 2097152 | tf_op jit(solution)/shard_map/all_to_all | solution.py:19
  56.3 3.5 %collective-permute-start.4 = (bf16[8,16,1024]{2,1,0:T(8,128)(2,1)S(1)}, bf16[8,16,1024]{2,1,0:T(8,128)(2,1)S(1)}, u32[]{:S(2)}, u32[]{:S(2)}) collective-permute-start(bf16[8,16,1024]{2,1,0:T(8,128)(2,1)S(1)} %all-to-all-done.1), channel_id=1, source_target_pairs={{0,768},{256,512},{512,256},{768,0},{1,769},{257,513},{513,257},{7... | collective-permute-start | bytes 786440 | tf_op jit(solution)/shard_map/ppermute | solution.py:23
  59.7 2.8 %collective-permute-start.3 = (bf16[8,16,1024]{2,1,0:T(8,128)(2,1)S(1)}, bf16[8,16,1024]{2,1,0:T(8,128)(2,1)S(1)}, u32[]{:S(2)}, u32[]{:S(2)}) collective-permute-start(bf16[8,16,1024]{2,1,0:T(8,128)(2,1)S(1)} %all-to-all-done.1), channel_id=1, source_target_pairs={{0,512},{256,768},{512,0},{768,256},{1,513},{257,769},{513,1},{769... | collective-permute-start | bytes 786440 | tf_op jit(solution)/shard_map/ppermute | solution.py:23
  62.6 3.5 %collective-permute-start.2 = (bf16[8,16,1024]{2,1,0:T(8,128)(2,1)S(1)}, bf16[8,16,1024]{2,1,0:T(8,128)(2,1)S(1)}, u32[]{:S(2)}, u32[]{:S(2)}) collective-permute-start(bf16[8,16,1024]{2,1,0:T(8,128)(2,1)S(1)} %all-to-all-done.1), channel_id=1, source_target_pairs={{0,256},{256,0},{512,768},{768,512},{1,257},{257,1},{513,769},{769... | collective-permute-start | bytes 786440 | tf_op jit(solution)/shard_map/ppermute | solution.py:23
  66.1 5.8 %collective-permute-done.4 = bf16[8,16,1024]{2,1,0:T(8,128)(2,1)S(1)} collective-permute-done((bf16[8,16,1024]{2,1,0:T(8,128)(2,1)S(1)}, bf16[8,16,1024]{2,1,0:T(8,128)(2,1)S(1)}, u32[]{:S(2)}, u32[]{:S(2)}) %collective-permute-start.4) | collective-permute-done | bytes 262176 | tf_op jit(solution)/shard_map/ppermute | solution.py:23
  72.3 3.5 %collective-permute-done.2 = bf16[8,16,1024]{2,1,0:T(8,128)(2,1)S(1)} collective-permute-done((bf16[8,16,1024]{2,1,0:T(8,128)(2,1)S(1)}, bf16[8,16,1024]{2,1,0:T(8,128)(2,1)S(1)}, u32[]{:S(2)}, u32[]{:S(2)}) %collective-permute-start.2) | collective-permute-done | bytes 262176 | tf_op jit(solution)/shard_map/ppermute | solution.py:23
  77.5 3.5 %collective-permute-start.7 = (f32[512]{0:T(512)S(1)}, f32[512]{0:T(512)S(1)}, u32[]{:S(2)}, u32[]{:S(2)}) collective-permute-start(f32[512]{0:T(512)S(1)} %log_add_fusion.6), channel_id=1, source_target_pairs={{0,768},{256,512},{512,256},{768,0},{1,769},{257,513},{513,257},{7... | collective-permute-start | bytes 6152 | tf_op jit(solution)/shard_map/ppermute | solution.py:23
  81.0 2.9 %collective-permute-start.6 = (f32[512]{0:T(512)S(1)}, f32[512]{0:T(512)S(1)}, u32[]{:S(2)}, u32[]{:S(2)}) collective-permute-start(f32[512]{0:T(512)S(1)} %log_add_fusion.6), channel_id=1, source_target_pairs={{0,512},{256,768},{512,0},{768,256},{1,513},{257,769},{513,1},{769... | collective-permute-start | bytes 6152 | tf_op jit(solution)/shard_map/ppermute | solution.py:23
  83.9 3.4 %collective-permute-start.5 = (f32[512]{0:T(512)S(1)}, f32[512]{0:T(512)S(1)}, u32[]{:S(2)}, u32[]{:S(2)}) collective-permute-start(f32[512]{0:T(512)S(1)} %log_add_fusion.6), channel_id=1, source_target_pairs={{0,256},{256,0},{512,768},{768,512},{1,257},{257,1},{513,769},{769... | collective-permute-start | bytes 6152 | tf_op jit(solution)/shard_map/ppermute | solution.py:23
  88.0 4.8 %all-to-all-start.2 = ((f32[8,1,512]{2,1,0:T(1,128)}), f32[8,1,512]{2,1,0:T(1,128)S(1)}, u32[]{:S(2)}, u32[]{:S(2)}) async-start(f32[8,1,512]{2,1,0:T(1,128)} %broadcast_in_dim.8), calls=%async_computation.2 | async-start | bytes 32768 | tf_op jit(solution)/shard_map/all_to_all | solution.py:19
  92.8 3.9 %all-to-all-done.2 = f32[8,1,512]{2,1,0:T(1,128)S(1)} async-done(((f32[8,1,512]{2,1,0:T(1,128)}), f32[8,1,512]{2,1,0:T(1,128)S(1)}, u32[]{:S(2)}, u32[]{:S(2)}) %all-to-all-start.2) | async-done | bytes 16416 | tf_op jit(solution)/shard_map/all_to_all | solution.py:19
  96.8 1.9 collective-permute-start.10
  98.7 13.8 %collective-permute-start.8 = (f32[512]{0:T(512)S(1)}, f32[512]{0:T(512)S(1)}, u32[]{:S(2)}, u32[]{:S(2)}) collective-permute-start(f32[512]{0:T(512)S(1)} %log_add_fusion.7), channel_id=1, source_target_pairs={{0,8},{8,0},{16,24},{24,16},{1,9},{9,1},{17,25},{25,17},{2,10},{10... | collective-permute-start | bytes 6152 | tf_op jit(solution)/shard_map/ppermute | solution.py:23
  112.5 2.3 %collective-permute-start.11 = (f32[512]{0:T(512)S(1)}, f32[512]{0:T(512)S(1)}, u32[]{:S(2)}, u32[]{:S(2)}) collective-permute-start(f32[512]{0:T(512)S(1)} %log_add_fusion.2), channel_id=1, source_target_pairs={{0,64},{32,96},{64,0},{96,32},{128,192},{160,224},{192,128},{224,1... | collective-permute-start | bytes 6152 | tf_op jit(solution)/shard_map/ppermute | solution.py:23
  114.8 10.7 %collective-permute-start.9 = (f32[512]{0:T(512)S(1)}, f32[512]{0:T(512)S(1)}, u32[]{:S(2)}, u32[]{:S(2)}) collective-permute-start(f32[512]{0:T(512)S(1)} %log_add_fusion.4), channel_id=1, source_target_pairs={{0,24},{8,16},{16,8},{24,0},{1,25},{9,17},{17,9},{25,1},{2,26},{10... | collective-permute-start | bytes 6152 | tf_op jit(solution)/shard_map/ppermute | solution.py:23
  125.6 11.1 %collective-permute-start.12 = (f32[512]{0:T(512)S(1)}, f32[512]{0:T(512)S(1)}, u32[]{:S(2)}, u32[]{:S(2)}) collective-permute-start(f32[512]{0:T(512)S(1)} %log_add_fusion.1), channel_id=1, source_target_pairs={{0,128},{32,160},{64,192},{96,224},{128,0},{160,32},{192,64},{224,... | collective-permute-start | bytes 6152 | tf_op jit(solution)/shard_map/ppermute | solution.py:23
  142.0 4.9 %all-to-all-start.3 = ((bf16[8,4,16,1024]{3,2,1,0:T(8,128)(2,1)}), bf16[8,4,16,1024]{3,2,1,0:T(8,128)(2,1)S(1)}, u32[]{:S(2)}, u32[]{:S(2)}) async-start(bf16[8,4,16,1024]{3,2,1,0:T(8,128)(2,1)} %convolution_convert_fusion.1), calls=%async_computation.3 | async-start | bytes 2097152 | tf_op jit(solution)/shard_map/all_to_all | solution.py:34
  148.8 2.4 %collective-permute-start.15 = (bf16[8,16,1024]{2,1,0:T(8,128)(2,1)S(1)}, bf16[8,16,1024]{2,1,0:T(8,128)(2,1)S(1)}, u32[]{:S(2)}, u32[]{:S(2)}) collective-permute-start(bf16[8,16,1024]{2,1,0:T(8,128)(2,1)S(1)} %get-tuple-element.11), channel_id=1, source_target_pairs={{0,256},{256,0},{512,768},{768,512},{1,257},{257,1},{513,769},{769... | collective-permute-start | bytes 786440 | tf_op jit(solution)/shard_map/ppermute | solution.py:23
  151.2 4.2 %collective-permute-start.17 = (bf16[8,16,1024]{2,1,0:T(8,128)(2,1)S(1)}, bf16[8,16,1024]{2,1,0:T(8,128)(2,1)S(1)}, u32[]{:S(2)}, u32[]{:S(2)}) collective-permute-start(bf16[8,16,1024]{2,1,0:T(8,128)(2,1)S(1)} %get-tuple-element.12), channel_id=1, source_target_pairs={{0,768},{256,512},{512,256},{768,0},{1,769},{257,513},{513,257},{7... | collective-permute-start | bytes 786440 | tf_op jit(solution)/shard_map/ppermute | solution.py:23
  155.5 3.1 %collective-permute-start.16 = (bf16[8,16,1024]{2,1,0:T(8,128)(2,1)S(1)}, bf16[8,16,1024]{2,1,0:T(8,128)(2,1)}, u32[]{:S(2)}, u32[]{:S(2)}) collective-permute-start(bf16[8,16,1024]{2,1,0:T(8,128)(2,1)S(1)} %get-tuple-element.13), channel_id=1, source_target_pairs={{0,512},{256,768},{512,0},{768,256},{1,513},{257,769},{513,1},{769... | collective-permute-start | bytes 786440 | tf_op jit(solution)/shard_map/ppermute | solution.py:23
  159.1 8.4 %collective-permute-done.17 = bf16[8,16,1024]{2,1,0:T(8,128)(2,1)S(1)} collective-permute-done((bf16[8,16,1024]{2,1,0:T(8,128)(2,1)S(1)}, bf16[8,16,1024]{2,1,0:T(8,128)(2,1)S(1)}, u32[]{:S(2)}, u32[]{:S(2)}) %collective-permute-start.17) | collective-permute-done | bytes 262176 | tf_op jit(solution)/shard_map/ppermute | solution.py:23
  167.4 1.8 fusion.2
  169.3 9.8 %all-to-all-start.4 = ((bf16[8,16,1024]{2,1,0:T(8,128)(2,1)}), bf16[8,16,1024]{2,1,0:T(8,128)(2,1)S(1)}, u32[]{:S(2)}, u32[]{:S(2)}) async-start(bf16[8,16,1024]{2,1,0:T(8,128)(2,1)} %fusion.2), calls=%async_computation.4 | async-start | bytes 524288 | tf_op jit(solution)/shard_map/all_to_all | solution.py:34
  179.2 7.0 %collective-permute-start.13 = (bf16[2,16,1024]{2,1,0:T(8,128)(2,1)S(1)}, bf16[2,16,1024]{2,1,0:T(8,128)(2,1)S(1)}, u32[]{:S(2)}, u32[]{:S(2)}) collective-permute-start(bf16[2,16,1024]{2,1,0:T(8,128)(2,1)S(1)} %fusion.6), channel_id=1, source_target_pairs={{0,24},{8,16},{16,8},{24,0},{1,25},{9,17},{17,9},{25,1},{2,26},{10... | collective-permute-start | bytes 196616 | tf_op jit(solution)/shard_map/ppermute | solution.py:23
  186.3 8.1 %collective-permute-done.13 = bf16[2,16,1024]{2,1,0:T(8,128)(2,1)S(1)} collective-permute-done((bf16[2,16,1024]{2,1,0:T(8,128)(2,1)S(1)}, bf16[2,16,1024]{2,1,0:T(8,128)(2,1)S(1)}, u32[]{:S(2)}, u32[]{:S(2)}) %collective-permute-start.13) | collective-permute-done | bytes 65568 | tf_op jit(solution)/shard_map/ppermute | solution.py:23
  194.4 19.3 %collective-permute-start.14 = (bf16[16,1024]{1,0:T(8,128)(2,1)S(1)}, bf16[16,1024]{1,0:T(8,128)(2,1)S(1)}, u32[]{:S(2)}, u32[]{:S(2)}) collective-permute-start(bf16[16,1024]{1,0:T(8,128)(2,1)S(1)} %fusion.8), channel_id=1, source_target_pairs={{0,8},{8,0},{16,24},{24,16},{1,9},{9,1},{17,25},{25,17},{2,10},{10... | collective-permute-start | bytes 98312 | tf_op jit(solution)/shard_map/ppermute | solution.py:23
  213.8 2.6 %collective-permute-done.14 = bf16[16,1024]{1,0:T(8,128)(2,1)S(1)} collective-permute-done((bf16[16,1024]{1,0:T(8,128)(2,1)S(1)}, bf16[16,1024]{1,0:T(8,128)(2,1)S(1)}, u32[]{:S(2)}, u32[]{:S(2)}) %collective-permute-start.14) | collective-permute-done | bytes 32800 | tf_op jit(solution)/shard_map/ppermute | solution.py:23
  (58 shorter events, 15.4 us)
Async XLA Ops:
  2.1 48.2 %all-to-all-start.1 = ((bf16[8,16,1024]{2,1,0:T(8,128)(2,1)}), bf16[8,16,1024]{2,1,0:T(8,128)(2,1)S(1)}, u32[]{:S(2)}, u32[]{:S(2)}) async-start(bf16[8,16,1024]{2,1,0:T(8,128)(2,1)} %broadcast_in_dim.7), calls=%async_computation.1 | async-start | bytes 524288 | tf_op jit(solution)/shard_map/all_to_all | solution.py:19
  14.7 18.3 %collective-permute-start = (bf16[16,1024]{1,0:T(8,128)(2,1)}, bf16[16,1024]{1,0:T(8,128)(2,1)S(1)}, u32[]{:S(2)}, u32[]{:S(2)}) collective-permute-start(bf16[16,1024]{1,0:T(8,128)(2,1)} %param.2), channel_id=1, source_target_pairs={{0,8},{8,0},{16,24},{24,16},{1,9},{9,1},{17,25},{25,17},{2,10},{10... | collective-permute-start | bytes 98312 | tf_op jit(solution)/shard_map/ppermute | solution.py:23
  33.8 16.5 %collective-permute-start.1 = (bf16[2,16,1024]{2,1,0:T(8,128)(2,1)S(1)}, bf16[2,16,1024]{2,1,0:T(8,128)(2,1)S(1)}, u32[]{:S(2)}, u32[]{:S(2)}) collective-permute-start(bf16[2,16,1024]{2,1,0:T(8,128)(2,1)S(1)} %pad_maximum_fusion.2), channel_id=1, source_target_pairs={{0,24},{8,16},{16,8},{24,0},{1,25},{9,17},{17,9},{25,1},{2,26},{10... | collective-permute-start | bytes 196616 | tf_op jit(solution)/shard_map/ppermute | solution.py:23
  51.4 24.7 %all-to-all-start = ((bf16[8,2,2,16,1024]{4,3,2,1,0:T(8,128)(2,1)}), bf16[8,2,2,16,1024]{4,3,2,1,0:T(8,128)(2,1)S(1)}, u32[]{:S(2)}, u32[]{:S(2)}) async-start(bf16[8,2,2,16,1024]{4,3,2,1,0:T(8,128)(2,1)} %broadcast_in_dim.6), calls=%async_computation | async-start | bytes 2097152 | tf_op jit(solution)/shard_map/all_to_all | solution.py:19
  56.3 15.6 %collective-permute-start.4 = (bf16[8,16,1024]{2,1,0:T(8,128)(2,1)S(1)}, bf16[8,16,1024]{2,1,0:T(8,128)(2,1)S(1)}, u32[]{:S(2)}, u32[]{:S(2)}) collective-permute-start(bf16[8,16,1024]{2,1,0:T(8,128)(2,1)S(1)} %all-to-all-done.1), channel_id=1, source_target_pairs={{0,768},{256,512},{512,256},{768,0},{1,769},{257,513},{513,257},{7... | collective-permute-start | bytes 786440 | tf_op jit(solution)/shard_map/ppermute | solution.py:23
  59.7 12.6 %collective-permute-start.3 = (bf16[8,16,1024]{2,1,0:T(8,128)(2,1)S(1)}, bf16[8,16,1024]{2,1,0:T(8,128)(2,1)S(1)}, u32[]{:S(2)}, u32[]{:S(2)}) collective-permute-start(bf16[8,16,1024]{2,1,0:T(8,128)(2,1)S(1)} %all-to-all-done.1), channel_id=1, source_target_pairs={{0,512},{256,768},{512,0},{768,256},{1,513},{257,769},{513,1},{769... | collective-permute-start | bytes 786440 | tf_op jit(solution)/shard_map/ppermute | solution.py:23
  62.6 13.3 %collective-permute-start.2 = (bf16[8,16,1024]{2,1,0:T(8,128)(2,1)S(1)}, bf16[8,16,1024]{2,1,0:T(8,128)(2,1)S(1)}, u32[]{:S(2)}, u32[]{:S(2)}) collective-permute-start(bf16[8,16,1024]{2,1,0:T(8,128)(2,1)S(1)} %all-to-all-done.1), channel_id=1, source_target_pairs={{0,256},{256,0},{512,768},{768,512},{1,257},{257,1},{513,769},{769... | collective-permute-start | bytes 786440 | tf_op jit(solution)/shard_map/ppermute | solution.py:23
  76.1 1.0 copy-start
  77.5 15.3 %collective-permute-start.7 = (f32[512]{0:T(512)S(1)}, f32[512]{0:T(512)S(1)}, u32[]{:S(2)}, u32[]{:S(2)}) collective-permute-start(f32[512]{0:T(512)S(1)} %log_add_fusion.6), channel_id=1, source_target_pairs={{0,768},{256,512},{512,256},{768,0},{1,769},{257,513},{513,257},{7... | collective-permute-start | bytes 6152 | tf_op jit(solution)/shard_map/ppermute | solution.py:23
  81.0 11.8 %collective-permute-start.6 = (f32[512]{0:T(512)S(1)}, f32[512]{0:T(512)S(1)}, u32[]{:S(2)}, u32[]{:S(2)}) collective-permute-start(f32[512]{0:T(512)S(1)} %log_add_fusion.6), channel_id=1, source_target_pairs={{0,512},{256,768},{512,0},{768,256},{1,513},{257,769},{513,1},{769... | collective-permute-start | bytes 6152 | tf_op jit(solution)/shard_map/ppermute | solution.py:23
  83.9 8.9 %collective-permute-start.5 = (f32[512]{0:T(512)S(1)}, f32[512]{0:T(512)S(1)}, u32[]{:S(2)}, u32[]{:S(2)}) collective-permute-start(f32[512]{0:T(512)S(1)} %log_add_fusion.6), channel_id=1, source_target_pairs={{0,256},{256,0},{512,768},{768,512},{1,257},{257,1},{513,769},{769... | collective-permute-start | bytes 6152 | tf_op jit(solution)/shard_map/ppermute | solution.py:23
  88.0 8.7 %all-to-all-start.2 = ((f32[8,1,512]{2,1,0:T(1,128)}), f32[8,1,512]{2,1,0:T(1,128)S(1)}, u32[]{:S(2)}, u32[]{:S(2)}) async-start(f32[8,1,512]{2,1,0:T(1,128)} %broadcast_in_dim.8), calls=%async_computation.2 | async-start | bytes 32768 | tf_op jit(solution)/shard_map/all_to_all | solution.py:19
  96.8 15.7 %collective-permute-start.10 = (f32[512]{0:T(512)S(1)}, f32[512]{0:T(512)S(1)}, u32[]{:S(2)}, u32[]{:S(2)}) collective-permute-start(f32[512]{0:T(512)S(1)} %log_add_fusion.5), channel_id=1, source_target_pairs={{0,32},{32,0},{64,96},{96,64},{128,160},{160,128},{192,224},{224,1... | collective-permute-start | bytes 6152 | tf_op jit(solution)/shard_map/ppermute | solution.py:23
  98.7 16.1 %collective-permute-start.8 = (f32[512]{0:T(512)S(1)}, f32[512]{0:T(512)S(1)}, u32[]{:S(2)}, u32[]{:S(2)}) collective-permute-start(f32[512]{0:T(512)S(1)} %log_add_fusion.7), channel_id=1, source_target_pairs={{0,8},{8,0},{16,24},{24,16},{1,9},{9,1},{17,25},{25,17},{2,10},{10... | collective-permute-start | bytes 6152 | tf_op jit(solution)/shard_map/ppermute | solution.py:23
  112.5 13.0 %collective-permute-start.11 = (f32[512]{0:T(512)S(1)}, f32[512]{0:T(512)S(1)}, u32[]{:S(2)}, u32[]{:S(2)}) collective-permute-start(f32[512]{0:T(512)S(1)} %log_add_fusion.2), channel_id=1, source_target_pairs={{0,64},{32,96},{64,0},{96,32},{128,192},{160,224},{192,128},{224,1... | collective-permute-start | bytes 6152 | tf_op jit(solution)/shard_map/ppermute | solution.py:23
  114.8 21.9 %collective-permute-start.9 = (f32[512]{0:T(512)S(1)}, f32[512]{0:T(512)S(1)}, u32[]{:S(2)}, u32[]{:S(2)}) collective-permute-start(f32[512]{0:T(512)S(1)} %log_add_fusion.4), channel_id=1, source_target_pairs={{0,24},{8,16},{16,8},{24,0},{1,25},{9,17},{17,9},{25,1},{2,26},{10... | collective-permute-start | bytes 6152 | tf_op jit(solution)/shard_map/ppermute | solution.py:23
  125.6 12.7 %collective-permute-start.12 = (f32[512]{0:T(512)S(1)}, f32[512]{0:T(512)S(1)}, u32[]{:S(2)}, u32[]{:S(2)}) collective-permute-start(f32[512]{0:T(512)S(1)} %log_add_fusion.1), channel_id=1, source_target_pairs={{0,128},{32,160},{64,192},{96,224},{128,0},{160,32},{192,64},{224,... | collective-permute-start | bytes 6152 | tf_op jit(solution)/shard_map/ppermute | solution.py:23
  138.9 1.4 copy-start.1
  142.0 27.2 %all-to-all-start.3 = ((bf16[8,4,16,1024]{3,2,1,0:T(8,128)(2,1)}), bf16[8,4,16,1024]{3,2,1,0:T(8,128)(2,1)S(1)}, u32[]{:S(2)}, u32[]{:S(2)}) async-start(bf16[8,4,16,1024]{3,2,1,0:T(8,128)(2,1)} %convolution_convert_fusion.1), calls=%async_computation.3 | async-start | bytes 2097152 | tf_op jit(solution)/shard_map/all_to_all | solution.py:34
  148.8 10.3 %collective-permute-start.15 = (bf16[8,16,1024]{2,1,0:T(8,128)(2,1)S(1)}, bf16[8,16,1024]{2,1,0:T(8,128)(2,1)S(1)}, u32[]{:S(2)}, u32[]{:S(2)}) collective-permute-start(bf16[8,16,1024]{2,1,0:T(8,128)(2,1)S(1)} %get-tuple-element.11), channel_id=1, source_target_pairs={{0,256},{256,0},{512,768},{768,512},{1,257},{257,1},{513,769},{769... | collective-permute-start | bytes 786440 | tf_op jit(solution)/shard_map/ppermute | solution.py:23
  151.2 16.2 %collective-permute-start.17 = (bf16[8,16,1024]{2,1,0:T(8,128)(2,1)S(1)}, bf16[8,16,1024]{2,1,0:T(8,128)(2,1)S(1)}, u32[]{:S(2)}, u32[]{:S(2)}) collective-permute-start(bf16[8,16,1024]{2,1,0:T(8,128)(2,1)S(1)} %get-tuple-element.12), channel_id=1, source_target_pairs={{0,768},{256,512},{512,256},{768,0},{1,769},{257,513},{513,257},{7... | collective-permute-start | bytes 786440 | tf_op jit(solution)/shard_map/ppermute | solution.py:23
  155.5 11.9 %collective-permute-start.16 = (bf16[8,16,1024]{2,1,0:T(8,128)(2,1)S(1)}, bf16[8,16,1024]{2,1,0:T(8,128)(2,1)}, u32[]{:S(2)}, u32[]{:S(2)}) collective-permute-start(bf16[8,16,1024]{2,1,0:T(8,128)(2,1)S(1)} %get-tuple-element.13), channel_id=1, source_target_pairs={{0,512},{256,768},{512,0},{768,256},{1,513},{257,769},{513,1},{769... | collective-permute-start | bytes 786440 | tf_op jit(solution)/shard_map/ppermute | solution.py:23
  169.3 44.4 %all-to-all-start.4 = ((bf16[8,16,1024]{2,1,0:T(8,128)(2,1)}), bf16[8,16,1024]{2,1,0:T(8,128)(2,1)S(1)}, u32[]{:S(2)}, u32[]{:S(2)}) async-start(bf16[8,16,1024]{2,1,0:T(8,128)(2,1)} %fusion.2), calls=%async_computation.4 | async-start | bytes 524288 | tf_op jit(solution)/shard_map/all_to_all | solution.py:34
  179.0 37.4 %copy-start.2 = (bf16[16,1024]{1,0:T(8,128)(2,1)S(1)}, bf16[16,1024]{1,0:T(8,128)(2,1)}, u32[]{:S(2)}) copy-start(bf16[16,1024]{1,0:T(8,128)(2,1)} %param.3) | copy-start | bytes 98308
  179.0 37.4 %copy-start.3 = (bf16[16,1024]{1,0:T(8,128)(2,1)S(1)}, bf16[16,1024]{1,0:T(8,128)(2,1)}, u32[]{:S(2)}) copy-start(bf16[16,1024]{1,0:T(8,128)(2,1)} %param.2) | copy-start | bytes 98308
  179.2 15.1 %collective-permute-start.13 = (bf16[2,16,1024]{2,1,0:T(8,128)(2,1)S(1)}, bf16[2,16,1024]{2,1,0:T(8,128)(2,1)S(1)}, u32[]{:S(2)}, u32[]{:S(2)}) collective-permute-start(bf16[2,16,1024]{2,1,0:T(8,128)(2,1)S(1)} %fusion.6), channel_id=1, source_target_pairs={{0,24},{8,16},{16,8},{24,0},{1,25},{9,17},{17,9},{25,1},{2,26},{10... | collective-permute-start | bytes 196616 | tf_op jit(solution)/shard_map/ppermute | solution.py:23
  194.4 22.0 %collective-permute-start.14 = (bf16[16,1024]{1,0:T(8,128)(2,1)S(1)}, bf16[16,1024]{1,0:T(8,128)(2,1)S(1)}, u32[]{:S(2)}, u32[]{:S(2)}) collective-permute-start(bf16[16,1024]{1,0:T(8,128)(2,1)S(1)} %fusion.8), channel_id=1, source_target_pairs={{0,8},{8,0},{16,24},{24,16},{1,9},{9,1},{17,25},{25,17},{2,10},{10... | collective-permute-start | bytes 98312 | tf_op jit(solution)/shard_map/ppermute | solution.py:23

commit v6 on v5

--- a/solution.py
+++ b/solution.py
@@ -9,6 +9,7 @@
 
 fine = {"y": 4, "zl": 8, "zh": 4, "x": 4, "core": 2}
 chip = ("x", "core")
+far = ("zh", "x")
 blk = ("y", "zl")
 ring = ((1, 1), (3, 2))
 everything = ("y", "zl", "zh", "x", "core")
@@ -65,20 +66,32 @@
     return parts
 
 
+def top_total(scores, dim):
+    top = jnp.max(scores, axis=dim, keepdims=True)
+    return jnp.squeeze(top, dim), jnp.sum(jnp.exp(scores - top), axis=dim)
+
+
+def combine(tops, totals):
+    top = functools.reduce(jnp.maximum, tops)
+    return top, sum(total * jnp.exp(each - top) for each, total in zip(tops, totals))
+
+
 def lse_of(*values):
     top = functools.reduce(jnp.maximum, values)
     return top + jnp.log(sum(jnp.exp(value - top) for value in values))
 
 
-def lse_rows_cols(row, col):
-    row = lse(gather(row, chip), 0)
+def lse_rows_cols(scores):
+    every = gather(jnp.stack(top_total(scores, 1)), far)
+    col = lse(scores, 0)
     col = lse_of(col, *(swap(col, "y", step) for step in (1, 2, 3)))
-    row, col = lax.optimization_barrier((row, col))
-    for step, _ in ring:
-        row = lse_of(row, swap(row, "zh", step))
-    for step in (1, 2, 4):
-        col = lse_of(col, swap(col, "zl", step))
-    return row, col
+    col = lse_of(col, *(swap(col, "zl", step) for step in (1, 2, 3)))
+    every, col = lax.optimization_barrier((every, col))
+    n = every.shape[0]
+    own = jnp.stack(combine([every[k, 0] for k in range(n)], [every[k, 1] for k in range(n)]))
+    other = swap(own, "core", 1)
+    top, total = combine((own[0], other[0]), (own[1], other[1]))
+    return top + jnp.log(total), lse_of(col, swap(col, "zl", 4))
 
 
 def body(image_emb, text_emb):
@@ -89,19 +102,22 @@
     row_lanes, col_lanes = img_rows.shape[:-1], txt_cols.shape[:-1]
     img_rows, txt_cols = img_rows.reshape(-1, width), txt_cols.reshape(-1, width)
     scores = logit_scale * jnp.dot(img_rows, txt_cols.T, preferred_element_type=jnp.float32)
-    row_lse, col_lse = lse_rows_cols(lse(scores, 1), lse(scores, 0))
+    row_lse, col_lse = lse_rows_cols(scores)
     weights = (
         0.5 * (jnp.exp(scores - row_lse[:, None]) + jnp.exp(scores - col_lse[None, :]))
     ).astype(jnp.bfloat16)
     image_part = jnp.dot(weights, txt_cols, preferred_element_type=jnp.float32)
     image_part = image_part.reshape(row_lanes + (width,))
-    image_sum = scatter_sum(image_part, chip).reshape(2, 2, own_rows, width)
-    image_sum = scatter_sum_by_halving(image_sum, "zh", ring)
     text_part = lax.dot_general(
         weights, img_rows, (((0,), (0,)), ((), ())), preferred_element_type=jnp.float32
     )
     text_part = text_part.reshape(col_lanes + (width,))
-    text_sum = scatter_sum(scatter_sum_by_swaps(text_part, "y"), "zl")
+    image_sum = scatter_sum(image_part, chip).reshape(2, 2, own_rows, width)
+    text_sum = scatter_sum_by_swaps(text_part, "y")
+    image_sum = scatter_sum_by_halving(image_sum, "zh", ring[1:])
+    image_sum, text_sum = lax.optimization_barrier((image_sum, text_sum))
+    image_sum = scatter_sum_by_halving(image_sum, "zh", ring[:1])
+    text_sum = scatter_sum(text_sum, "zl")
     grad_image = logit_scale * image_sum - logit_scale * text_emb.astype(jnp.float32)
     grad_text = logit_scale * text_sum - logit_scale * image_emb.astype(jnp.float32)
     own_row = lax.axis_index(chip) * row_lanes[1] + lax.axis_index("zh")

time: 219 us -> 220 us (level)
  the two profiles are of different devices: /device:TPU:42 before, /device:TPU:128 now
where the time goes in v6:
time: 220 us; the launch traced here: 219 us
  starting transfers between devices  140 us (64%)
  waiting for transfers between devices  64.1 us (29%)
  other arithmetic  5.76 us (3%)
  matrix products  4.46 us (2%)
  local copies, waits for them, and re-layouts  3.77 us (2%)
    ppermute x18, starting transfers between devices, swap(): lax.ppermute(value, axis, [(i, i ^ step) for i in range(lax.axis_size(axi...  88.8 us
    ppermute x18, waiting for transfers between devices, swap(): lax.ppermute(value, axis, [(i, i ^ step) for i in range(lax.axis_size(axi...  58.6 us
    all_to_all x3, starting transfers between devices, gather(): return lax.all_to_all(copies, axis, 0, 0)  33.1 us
    all_to_all x2, starting transfers between devices, scatter_sum(): lax.all_to_all(parts.astype(jnp.bfloat16), axis, 0, 0).astype(jnp.float32)  17.7 us
    all_to_all x2, waiting for transfers between devices, scatter_sum(): lax.all_to_all(parts.astype(jnp.bfloat16), axis, 0, 0).astype(jnp.float32)  5.47 us
  transfers between devices with their start and end apart: 23, of which 13 were waited for; matrix products, arithmetic and copies ran while one was open for 3% of the time, Pallas kernels for 0%

profile of v6, /device:TPU:128, one launch (start us, length us, event | category | flops | bytes accessed | tf_op | source)
XLA Modules:
  0.0 218.8 jit_solution(8173598320959412226)
XLA Ops:
  2.1 14.7 %all-to-all-start.1 = ((bf16[8,16,1024]{2,1,0:T(8,128)(2,1)}), bf16[8,16,1024]{2,1,0:T(8,128)(2,1)S(1)}, u32[]{:S(2)}, u32[]{:S(2)}) async-start(bf16[8,16,1024]{2,1,0:T(8,128)(2,1)} %broadcast_in_dim.7), calls=%async_computation.1 | async-start | bytes 524288 | tf_op jit(solution)/shard_map/all_to_all | solution.py:20
  16.8 12.3 %collective-permute-start = (bf16[16,1024]{1,0:T(8,128)(2,1)}, bf16[16,1024]{1,0:T(8,128)(2,1)S(1)}, u32[]{:S(2)}, u32[]{:S(2)}) collective-permute-start(bf16[16,1024]{1,0:T(8,128)(2,1)} %param.2), channel_id=1, source_target_pairs={{0,8},{8,0},{16,24},{24,16},{1,9},{9,1},{17,25},{25,17},{2,10},{10... | collective-permute-start | bytes 98312 | tf_op jit(solution)/shard_map/ppermute | solution.py:24
  29.1 12.5 %collective-permute-done = bf16[16,1024]{1,0:T(8,128)(2,1)S(1)} collective-permute-done((bf16[16,1024]{1,0:T(8,128)(2,1)}, bf16[16,1024]{1,0:T(8,128)(2,1)S(1)}, u32[]{:S(2)}, u32[]{:S(2)}) %collective-permute-start) | collective-permute-done | bytes 32800 | tf_op jit(solution)/shard_map/ppermute | solution.py:24
  42.3 6.9 %collective-permute-start.1 = (bf16[2,16,1024]{2,1,0:T(8,128)(2,1)S(1)}, bf16[2,16,1024]{2,1,0:T(8,128)(2,1)S(1)}, u32[]{:S(2)}, u32[]{:S(2)}) collective-permute-start(bf16[2,16,1024]{2,1,0:T(8,128)(2,1)S(1)} %pad_maximum_fusion.2), channel_id=1, source_target_pairs={{0,24},{8,16},{16,8},{24,0},{1,25},{9,17},{17,9},{25,1},{2,26},{10... | collective-permute-start | bytes 196616 | tf_op jit(solution)/shard_map/ppermute | solution.py:24
  49.3 7.9 %collective-permute-done.1 = bf16[2,16,1024]{2,1,0:T(8,128)(2,1)S(1)} collective-permute-done((bf16[2,16,1024]{2,1,0:T(8,128)(2,1)S(1)}, bf16[2,16,1024]{2,1,0:T(8,128)(2,1)S(1)}, u32[]{:S(2)}, u32[]{:S(2)}) %collective-permute-start.1) | collective-permute-done | bytes 65568 | tf_op jit(solution)/shard_map/ppermute | solution.py:24
  58.4 4.3 %all-to-all-start = ((bf16[8,2,2,16,1024]{4,3,2,1,0:T(8,128)(2,1)}), bf16[8,2,2,16,1024]{4,3,2,1,0:T(8,128)(2,1)S(1)}, u32[]{:S(2)}, u32[]{:S(2)}) async-start(bf16[8,2,2,16,1024]{4,3,2,1,0:T(8,128)(2,1)} %broadcast_in_dim.6), calls=%async_computation | async-start | bytes 2097152 | tf_op jit(solution)/shard_map/all_to_all | solution.py:20
  62.7 4.9 %collective-permute-start.4 = (bf16[8,16,1024]{2,1,0:T(8,128)(2,1)S(1)}, bf16[8,16,1024]{2,1,0:T(8,128)(2,1)S(1)}, u32[]{:S(2)}, u32[]{:S(2)}) collective-permute-start(bf16[8,16,1024]{2,1,0:T(8,128)(2,1)S(1)} %all-to-all-done.1), channel_id=1, source_target_pairs={{0,768},{256,512},{512,256},{768,0},{1,769},{257,513},{513,257},{7... | collective-permute-start | bytes 786440 | tf_op jit(solution)/shard_map/ppermute | solution.py:24
  67.6 2.5 %collective-permute-start.3 = (bf16[8,16,1024]{2,1,0:T(8,128)(2,1)S(1)}, bf16[8,16,1024]{2,1,0:T(8,128)(2,1)S(1)}, u32[]{:S(2)}, u32[]{:S(2)}) collective-permute-start(bf16[8,16,1024]{2,1,0:T(8,128)(2,1)S(1)} %all-to-all-done.1), channel_id=1, source_target_pairs={{0,512},{256,768},{512,0},{768,256},{1,513},{257,769},{513,1},{769... | collective-permute-start | bytes 786440 | tf_op jit(solution)/shard_map/ppermute | solution.py:24
  70.1 2.4 %collective-permute-start.2 = (bf16[8,16,1024]{2,1,0:T(8,128)(2,1)S(1)}, bf16[8,16,1024]{2,1,0:T(8,128)(2,1)S(1)}, u32[]{:S(2)}, u32[]{:S(2)}) collective-permute-start(bf16[8,16,1024]{2,1,0:T(8,128)(2,1)S(1)} %all-to-all-done.1), channel_id=1, source_target_pairs={{0,256},{256,0},{512,768},{768,512},{1,257},{257,1},{513,769},{769... | collective-permute-start | bytes 786440 | tf_op jit(solution)/shard_map/ppermute | solution.py:24
  72.5 7.6 %collective-permute-done.4 = bf16[8,16,1024]{2,1,0:T(8,128)(2,1)S(1)} collective-permute-done((bf16[8,16,1024]{2,1,0:T(8,128)(2,1)S(1)}, bf16[8,16,1024]{2,1,0:T(8,128)(2,1)S(1)}, u32[]{:S(2)}, u32[]{:S(2)}) %collective-permute-start.4) | collective-permute-done | bytes 262176 | tf_op jit(solution)/shard_map/ppermute | solution.py:24
  80.2 2.5 %collective-permute-done.2 = bf16[8,16,1024]{2,1,0:T(8,128)(2,1)S(1)} collective-permute-done((bf16[8,16,1024]{2,1,0:T(8,128)(2,1)S(1)}, bf16[8,16,1024]{2,1,0:T(8,128)(2,1)S(1)}, u32[]{:S(2)}, u32[]{:S(2)}) %collective-permute-start.2) | collective-permute-done | bytes 262176 | tf_op jit(solution)/shard_map/ppermute | solution.py:24
  85.0 14.0 %all-to-all-start.2 = ((f32[16,2,512]{2,1,0:T(2,128)}), f32[16,2,512]{2,1,0:T(2,128)S(1)}, u32[]{:S(2)}, u32[]{:S(2)}) async-start(f32[16,2,512]{2,1,0:T(2,128)} %broadcast_in_dim.8), calls=%async_computation.2 | async-start | bytes 131072 | tf_op jit(solution)/shard_map/all_to_all | solution.py:20
  99.1 4.8 %collective-permute-start.7 = (f32[512]{0:T(512)S(1)}, f32[512]{0:T(512)S(1)}, u32[]{:S(2)}, u32[]{:S(2)}) collective-permute-start(f32[512]{0:T(512)S(1)} %log_add_fusion.4), channel_id=1, source_target_pairs={{0,768},{256,512},{512,256},{768,0},{1,769},{257,513},{513,257},{7... | collective-permute-start | bytes 6152 | tf_op jit(solution)/shard_map/ppermute | solution.py:24
  103.9 2.5 %collective-permute-start.6 = (f32[512]{0:T(512)S(1)}, f32[512]{0:T(512)S(1)}, u32[]{:S(2)}, u32[]{:S(2)}) collective-permute-start(f32[512]{0:T(512)S(1)} %log_add_fusion.4), channel_id=1, source_target_pairs={{0,512},{256,768},{512,0},{768,256},{1,513},{257,769},{513,1},{769... | collective-permute-start | bytes 6152 | tf_op jit(solution)/shard_map/ppermute | solution.py:24
  106.5 2.4 %collective-permute-start.5 = (f32[512]{0:T(512)S(1)}, f32[512]{0:T(512)S(1)}, u32[]{:S(2)}, u32[]{:S(2)}) collective-permute-start(f32[512]{0:T(512)S(1)} %log_add_fusion.4), channel_id=1, source_target_pairs={{0,256},{256,0},{512,768},{768,512},{1,257},{257,1},{513,769},{769... | collective-permute-start | bytes 6152 | tf_op jit(solution)/shard_map/ppermute | solution.py:24
  108.9 2.0 collective-permute-done.6
  112.0 8.7 %collective-permute-start.10 = (f32[512]{0:T(512)S(1)}, f32[512]{0:T(512)S(1)}, u32[]{:S(2)}, u32[]{:S(2)}) collective-permute-start(f32[512]{0:T(512)S(1)} %log_add_fusion.3), channel_id=1, source_target_pairs={{0,96},{32,64},{64,32},{96,0},{128,224},{160,192},{192,160},{224,1... | collective-permute-start | bytes 6152 | tf_op jit(solution)/shard_map/ppermute | solution.py:24
  120.7 1.9 collective-permute-start.9
  122.6 2.5 %collective-permute-start.8 = (f32[512]{0:T(512)S(1)}, f32[512]{0:T(512)S(1)}, u32[]{:S(2)}, u32[]{:S(2)}) collective-permute-start(f32[512]{0:T(512)S(1)} %log_add_fusion.3), channel_id=1, source_target_pairs={{0,32},{32,0},{64,96},{96,64},{128,160},{160,128},{192,224},{224,1... | collective-permute-start | bytes 6152 | tf_op jit(solution)/shard_map/ppermute | solution.py:24
  125.1 2.0 collective-permute-done.9
  132.2 5.5 %collective-permute-done.12 = f32[512]{0:T(512)S(1)} collective-permute-done((f32[512]{0:T(512)S(1)}, f32[512]{0:T(512)S(1)}, u32[]{:S(2)}, u32[]{:S(2)}) %collective-permute-start.12) | collective-permute-done | bytes 2080 | tf_op jit(solution)/shard_map/ppermute | solution.py:24
  139.9 4.7 %all-to-all-start.3 = ((bf16[8,4,16,1024]{3,2,1,0:T(8,128)(2,1)}), bf16[8,4,16,1024]{3,2,1,0:T(8,128)(2,1)S(1)}, u32[]{:S(2)}, u32[]{:S(2)}) async-start(bf16[8,4,16,1024]{3,2,1,0:T(8,128)(2,1)} %convolution_convert_fusion.1), calls=%async_computation.3 | async-start | bytes 2097152 | tf_op jit(solution)/shard_map/all_to_all | solution.py:35
  145.1 1.9 convolution_convert_fusion
  147.1 2.4 %collective-permute-start.14 = (bf16[8,16,1024]{2,1,0:T(8,128)(2,1)S(1)}, bf16[8,16,1024]{2,1,0:T(8,128)(2,1)S(1)}, u32[]{:S(2)}, u32[]{:S(2)}) collective-permute-start(bf16[8,16,1024]{2,1,0:T(8,128)(2,1)S(1)} %get-tuple-element.17), channel_id=1, source_target_pairs={{0,256},{256,0},{512,768},{768,512},{1,257},{257,1},{513,769},{769... | collective-permute-start | bytes 786440 | tf_op jit(solution)/shard_map/ppermute | solution.py:24
  149.6 4.8 %collective-permute-start.16 = (bf16[8,16,1024]{2,1,0:T(8,128)(2,1)S(1)}, bf16[8,16,1024]{2,1,0:T(8,128)(2,1)S(1)}, u32[]{:S(2)}, u32[]{:S(2)}) collective-permute-start(bf16[8,16,1024]{2,1,0:T(8,128)(2,1)S(1)} %get-tuple-element.18), channel_id=1, source_target_pairs={{0,768},{256,512},{512,256},{768,0},{1,769},{257,513},{513,257},{7... | collective-permute-start | bytes 786440 | tf_op jit(solution)/shard_map/ppermute | solution.py:24
  154.4 2.5 %collective-permute-start.15 = (bf16[8,16,1024]{2,1,0:T(8,128)(2,1)S(1)}, bf16[8,16,1024]{2,1,0:T(8,128)(2,1)}, u32[]{:S(2)}, u32[]{:S(2)}) collective-permute-start(bf16[8,16,1024]{2,1,0:T(8,128)(2,1)S(1)} %get-tuple-element.19), channel_id=1, source_target_pairs={{0,512},{256,768},{512,0},{768,256},{1,513},{257,769},{513,1},{769... | collective-permute-start | bytes 786440 | tf_op jit(solution)/shard_map/ppermute | solution.py:24
  157.0 3.6 %all-to-all-done.3 = bf16[8,4,16,1024]{3,2,1,0:T(8,128)(2,1)S(1)} async-done(((bf16[8,4,16,1024]{3,2,1,0:T(8,128)(2,1)}), bf16[8,4,16,1024]{3,2,1,0:T(8,128)(2,1)S(1)}, u32[]{:S(2)}, u32[]{:S(2)}) %all-to-all-start.3) | async-done | bytes 1048608 | tf_op jit(solution)/shard_map/all_to_all | solution.py:35
  160.8 12.1 %collective-permute-start.13 = (bf16[2,16,1024]{2,1,0:T(8,128)(2,1)S(1)}, bf16[2,16,1024]{2,1,0:T(8,128)(2,1)S(1)}, u32[]{:S(2)}, u32[]{:S(2)}) collective-permute-start(bf16[2,16,1024]{2,1,0:T(8,128)(2,1)S(1)} %fusion.5), channel_id=1, source_target_pairs={{0,24},{8,16},{16,8},{24,0},{1,25},{9,17},{17,9},{25,1},{2,26},{10... | collective-permute-start | bytes 196616 | tf_op jit(solution)/shard_map/ppermute | solution.py:24
  174.7 6.1 %collective-permute-done.13 = bf16[2,16,1024]{2,1,0:T(8,128)(2,1)S(1)} collective-permute-done((bf16[2,16,1024]{2,1,0:T(8,128)(2,1)S(1)}, bf16[2,16,1024]{2,1,0:T(8,128)(2,1)S(1)}, u32[]{:S(2)}, u32[]{:S(2)}) %collective-permute-start.13) | collective-permute-done | bytes 65568 | tf_op jit(solution)/shard_map/ppermute | solution.py:24
  180.8 13.0 %all-to-all-start.4 = ((bf16[8,16,1024]{2,1,0:T(8,128)(2,1)}), bf16[8,16,1024]{2,1,0:T(8,128)(2,1)S(1)}, u32[]{:S(2)}, u32[]{:S(2)}) async-start(bf16[8,16,1024]{2,1,0:T(8,128)(2,1)} %fusion.1), calls=%async_computation.4 | async-start | bytes 524288 | tf_op jit(solution)/shard_map/all_to_all | solution.py:35
  193.9 11.1 %collective-permute-start.17 = (bf16[16,1024]{1,0:T(8,128)(2,1)S(1)}, bf16[16,1024]{1,0:T(8,128)(2,1)S(1)}, u32[]{:S(2)}, u32[]{:S(2)}) collective-permute-start(bf16[16,1024]{1,0:T(8,128)(2,1)S(1)} %fusion.7), channel_id=1, source_target_pairs={{0,8},{8,0},{16,24},{24,16},{1,9},{9,1},{17,25},{25,17},{2,10},{10... | collective-permute-start | bytes 98312 | tf_op jit(solution)/shard_map/ppermute | solution.py:24
  207.0 10.4 %collective-permute-done.17 = bf16[16,1024]{1,0:T(8,128)(2,1)S(1)} collective-permute-done((bf16[16,1024]{1,0:T(8,128)(2,1)S(1)}, bf16[16,1024]{1,0:T(8,128)(2,1)S(1)}, u32[]{:S(2)}, u32[]{:S(2)}) %collective-permute-start.17) | collective-permute-done | bytes 32800 | tf_op jit(solution)/shard_map/ppermute | solution.py:24
  (56 shorter events, 19.9 us)
Async XLA Ops:
  2.1 55.2 %all-to-all-start.1 = ((bf16[8,16,1024]{2,1,0:T(8,128)(2,1)}), bf16[8,16,1024]{2,1,0:T(8,128)(2,1)S(1)}, u32[]{:S(2)}, u32[]{:S(2)}) async-start(bf16[8,16,1024]{2,1,0:T(8,128)(2,1)} %broadcast_in_dim.7), calls=%async_computation.1 | async-start | bytes 524288 | tf_op jit(solution)/shard_map/all_to_all | solution.py:20
  16.8 24.7 %collective-permute-start = (bf16[16,1024]{1,0:T(8,128)(2,1)}, bf16[16,1024]{1,0:T(8,128)(2,1)S(1)}, u32[]{:S(2)}, u32[]{:S(2)}) collective-permute-start(bf16[16,1024]{1,0:T(8,128)(2,1)} %param.2), channel_id=1, source_target_pairs={{0,8},{8,0},{16,24},{24,16},{1,9},{9,1},{17,25},{25,17},{2,10},{10... | collective-permute-start | bytes 98312 | tf_op jit(solution)/shard_map/ppermute | solution.py:24
  42.3 14.9 %collective-permute-start.1 = (bf16[2,16,1024]{2,1,0:T(8,128)(2,1)S(1)}, bf16[2,16,1024]{2,1,0:T(8,128)(2,1)S(1)}, u32[]{:S(2)}, u32[]{:S(2)}) collective-permute-start(bf16[2,16,1024]{2,1,0:T(8,128)(2,1)S(1)} %pad_maximum_fusion.2), channel_id=1, source_target_pairs={{0,24},{8,16},{16,8},{24,0},{1,25},{9,17},{17,9},{25,1},{2,26},{10... | collective-permute-start | bytes 196616 | tf_op jit(solution)/shard_map/ppermute | solution.py:24
  58.4 24.6 %all-to-all-start = ((bf16[8,2,2,16,1024]{4,3,2,1,0:T(8,128)(2,1)}), bf16[8,2,2,16,1024]{4,3,2,1,0:T(8,128)(2,1)S(1)}, u32[]{:S(2)}, u32[]{:S(2)}) async-start(bf16[8,2,2,16,1024]{4,3,2,1,0:T(8,128)(2,1)} %broadcast_in_dim.6), calls=%async_computation | async-start | bytes 2097152 | tf_op jit(solution)/shard_map/all_to_all | solution.py:20
  62.7 17.5 %collective-permute-start.4 = (bf16[8,16,1024]{2,1,0:T(8,128)(2,1)S(1)}, bf16[8,16,1024]{2,1,0:T(8,128)(2,1)S(1)}, u32[]{:S(2)}, u32[]{:S(2)}) collective-permute-start(bf16[8,16,1024]{2,1,0:T(8,128)(2,1)S(1)} %all-to-all-done.1), channel_id=1, source_target_pairs={{0,768},{256,512},{512,256},{768,0},{1,769},{257,513},{513,257},{7... | collective-permute-start | bytes 786440 | tf_op jit(solution)/shard_map/ppermute | solution.py:24
  67.6 12.6 %collective-permute-start.3 = (bf16[8,16,1024]{2,1,0:T(8,128)(2,1)S(1)}, bf16[8,16,1024]{2,1,0:T(8,128)(2,1)S(1)}, u32[]{:S(2)}, u32[]{:S(2)}) collective-permute-start(bf16[8,16,1024]{2,1,0:T(8,128)(2,1)S(1)} %all-to-all-done.1), channel_id=1, source_target_pairs={{0,512},{256,768},{512,0},{768,256},{1,513},{257,769},{513,1},{769... | collective-permute-start | bytes 786440 | tf_op jit(solution)/shard_map/ppermute | solution.py:24
  70.1 12.6 %collective-permute-start.2 = (bf16[8,16,1024]{2,1,0:T(8,128)(2,1)S(1)}, bf16[8,16,1024]{2,1,0:T(8,128)(2,1)S(1)}, u32[]{:S(2)}, u32[]{:S(2)}) collective-permute-start(bf16[8,16,1024]{2,1,0:T(8,128)(2,1)S(1)} %all-to-all-done.1), channel_id=1, source_target_pairs={{0,256},{256,0},{512,768},{768,512},{1,257},{257,1},{513,769},{769... | collective-permute-start | bytes 786440 | tf_op jit(solution)/shard_map/ppermute | solution.py:24
  83.0 1.0 copy-start
  85.0 43.1 %all-to-all-start.2 = ((f32[16,2,512]{2,1,0:T(2,128)}), f32[16,2,512]{2,1,0:T(2,128)S(1)}, u32[]{:S(2)}, u32[]{:S(2)}) async-start(f32[16,2,512]{2,1,0:T(2,128)} %broadcast_in_dim.8), calls=%async_computation.2 | async-start | bytes 131072 | tf_op jit(solution)/shard_map/all_to_all | solution.py:20
  99.1 9.8 %collective-permute-start.7 = (f32[512]{0:T(512)S(1)}, f32[512]{0:T(512)S(1)}, u32[]{:S(2)}, u32[]{:S(2)}) collective-permute-start(f32[512]{0:T(512)S(1)} %log_add_fusion.4), channel_id=1, source_target_pairs={{0,768},{256,512},{512,256},{768,0},{1,769},{257,513},{513,257},{7... | collective-permute-start | bytes 6152 | tf_op jit(solution)/shard_map/ppermute | solution.py:24
  103.9 7.0 %collective-permute-start.6 = (f32[512]{0:T(512)S(1)}, f32[512]{0:T(512)S(1)}, u32[]{:S(2)}, u32[]{:S(2)}) collective-permute-start(f32[512]{0:T(512)S(1)} %log_add_fusion.4), channel_id=1, source_target_pairs={{0,512},{256,768},{512,0},{768,256},{1,513},{257,769},{513,1},{769... | collective-permute-start | bytes 6152 | tf_op jit(solution)/shard_map/ppermute | solution.py:24
  106.5 5.5 %collective-permute-start.5 = (f32[512]{0:T(512)S(1)}, f32[512]{0:T(512)S(1)}, u32[]{:S(2)}, u32[]{:S(2)}) collective-permute-start(f32[512]{0:T(512)S(1)} %log_add_fusion.4), channel_id=1, source_target_pairs={{0,256},{256,0},{512,768},{768,512},{1,257},{257,1},{513,769},{769... | collective-permute-start | bytes 6152 | tf_op jit(solution)/shard_map/ppermute | solution.py:24
  112.0 13.1 %collective-permute-start.10 = (f32[512]{0:T(512)S(1)}, f32[512]{0:T(512)S(1)}, u32[]{:S(2)}, u32[]{:S(2)}) collective-permute-start(f32[512]{0:T(512)S(1)} %log_add_fusion.3), channel_id=1, source_target_pairs={{0,96},{32,64},{64,32},{96,0},{128,224},{160,192},{192,160},{224,1... | collective-permute-start | bytes 6152 | tf_op jit(solution)/shard_map/ppermute | solution.py:24
  120.7 6.4 %collective-permute-start.9 = (f32[512]{0:T(512)S(1)}, f32[512]{0:T(512)S(1)}, u32[]{:S(2)}, u32[]{:S(2)}) collective-permute-start(f32[512]{0:T(512)S(1)} %log_add_fusion.3), channel_id=1, source_target_pairs={{0,64},{32,96},{64,0},{96,32},{128,192},{160,224},{192,128},{224,1... | collective-permute-start | bytes 6152 | tf_op jit(solution)/shard_map/ppermute | solution.py:24
  122.6 5.5 %collective-permute-start.8 = (f32[512]{0:T(512)S(1)}, f32[512]{0:T(512)S(1)}, u32[]{:S(2)}, u32[]{:S(2)}) collective-permute-start(f32[512]{0:T(512)S(1)} %log_add_fusion.3), channel_id=1, source_target_pairs={{0,32},{32,0},{64,96},{96,64},{128,160},{160,128},{192,224},{224,1... | collective-permute-start | bytes 6152 | tf_op jit(solution)/shard_map/ppermute | solution.py:24
  128.3 9.4 %collective-permute-start.12 = (f32[512]{0:T(512)S(1)}, f32[512]{0:T(512)S(1)}, u32[]{:S(2)}, u32[]{:S(2)}) collective-permute-start(f32[512]{0:T(512)S(1)} %log_add_fusion.2), channel_id=1, source_target_pairs={{0,128},{32,160},{64,192},{96,224},{128,0},{160,32},{192,64},{224,... | collective-permute-start | bytes 6152 | tf_op jit(solution)/shard_map/ppermute | solution.py:24
  130.3 7.5 %collective-permute-start.11 = (f32[2,512]{1,0:T(2,128)S(1)}, f32[2,512]{1,0:T(2,128)S(1)}, u32[]{:S(2)}, u32[]{:S(2)}) collective-permute-start(f32[2,512]{1,0:T(2,128)S(1)} %pad_maximum_fusion.4), channel_id=1, source_target_pairs={{0,1},{1,0},{2,3},{3,2},{4,5},{5,4},{6,7},{7,6},{8,9},{9,8},{10,11... | collective-permute-start | bytes 12296 | tf_op jit(solution)/shard_map/ppermute | solution.py:24
  139.9 20.7 %all-to-all-start.3 = ((bf16[8,4,16,1024]{3,2,1,0:T(8,128)(2,1)}), bf16[8,4,16,1024]{3,2,1,0:T(8,128)(2,1)S(1)}, u32[]{:S(2)}, u32[]{:S(2)}) async-start(bf16[8,4,16,1024]{3,2,1,0:T(8,128)(2,1)} %convolution_convert_fusion.1), calls=%async_computation.3 | async-start | bytes 2097152 | tf_op jit(solution)/shard_map/all_to_all | solution.py:35
  147.1 25.7 %collective-permute-start.14 = (bf16[8,16,1024]{2,1,0:T(8,128)(2,1)S(1)}, bf16[8,16,1024]{2,1,0:T(8,128)(2,1)S(1)}, u32[]{:S(2)}, u32[]{:S(2)}) collective-permute-start(bf16[8,16,1024]{2,1,0:T(8,128)(2,1)S(1)} %get-tuple-element.17), channel_id=1, source_target_pairs={{0,256},{256,0},{512,768},{768,512},{1,257},{257,1},{513,769},{769... | collective-permute-start | bytes 786440 | tf_op jit(solution)/shard_map/ppermute | solution.py:24
  149.6 23.3 %collective-permute-start.16 = (bf16[8,16,1024]{2,1,0:T(8,128)(2,1)S(1)}, bf16[8,16,1024]{2,1,0:T(8,128)(2,1)S(1)}, u32[]{:S(2)}, u32[]{:S(2)}) collective-permute-start(bf16[8,16,1024]{2,1,0:T(8,128)(2,1)S(1)} %get-tuple-element.18), channel_id=1, source_target_pairs={{0,768},{256,512},{512,256},{768,0},{1,769},{257,513},{513,257},{7... | collective-permute-start | bytes 786440 | tf_op jit(solution)/shard_map/ppermute | solution.py:24
  154.4 18.5 %collective-permute-start.15 = (bf16[8,16,1024]{2,1,0:T(8,128)(2,1)S(1)}, bf16[8,16,1024]{2,1,0:T(8,128)(2,1)}, u32[]{:S(2)}, u32[]{:S(2)}) collective-permute-start(bf16[8,16,1024]{2,1,0:T(8,128)(2,1)S(1)} %get-tuple-element.19), channel_id=1, source_target_pairs={{0,512},{256,768},{512,0},{768,256},{1,513},{257,769},{513,1},{769... | collective-permute-start | bytes 786440 | tf_op jit(solution)/shard_map/ppermute | solution.py:24
  160.7 56.6 %copy-start.1 = (bf16[16,1024]{1,0:T(8,128)(2,1)S(1)}, bf16[16,1024]{1,0:T(8,128)(2,1)}, u32[]{:S(2)}) copy-start(bf16[16,1024]{1,0:T(8,128)(2,1)} %param.3) | copy-start | bytes 98308
  160.7 56.6 %copy-start.2 = (bf16[16,1024]{1,0:T(8,128)(2,1)S(1)}, bf16[16,1024]{1,0:T(8,128)(2,1)}, u32[]{:S(2)}) copy-start(bf16[16,1024]{1,0:T(8,128)(2,1)} %param.2) | copy-start | bytes 98308
  160.8 20.1 %collective-permute-start.13 = (bf16[2,16,1024]{2,1,0:T(8,128)(2,1)S(1)}, bf16[2,16,1024]{2,1,0:T(8,128)(2,1)S(1)}, u32[]{:S(2)}, u32[]{:S(2)}) collective-permute-start(bf16[2,16,1024]{2,1,0:T(8,128)(2,1)S(1)} %fusion.5), channel_id=1, source_target_pairs={{0,24},{8,16},{16,8},{24,0},{1,25},{9,17},{17,9},{25,1},{2,26},{10... | collective-permute-start | bytes 196616 | tf_op jit(solution)/shard_map/ppermute | solution.py:24
  180.8 26.1 %all-to-all-start.4 = ((bf16[8,16,1024]{2,1,0:T(8,128)(2,1)}), bf16[8,16,1024]{2,1,0:T(8,128)(2,1)S(1)}, u32[]{:S(2)}, u32[]{:S(2)}) async-start(bf16[8,16,1024]{2,1,0:T(8,128)(2,1)} %fusion.1), calls=%async_computation.4 | async-start | bytes 524288 | tf_op jit(solution)/shard_map/all_to_all | solution.py:35
  193.9 23.5 %collective-permute-start.17 = (bf16[16,1024]{1,0:T(8,128)(2,1)S(1)}, bf16[16,1024]{1,0:T(8,128)(2,1)S(1)}, u32[]{:S(2)}, u32[]{:S(2)}) collective-permute-start(bf16[16,1024]{1,0:T(8,128)(2,1)S(1)} %fusion.7), channel_id=1, source_target_pairs={{0,8},{8,0},{16,24},{24,16},{1,9},{9,1},{17,25},{25,17},{2,10},{10... | collective-permute-start | bytes 98312 | tf_op jit(solution)/shard_map/ppermute | solution.py:24

commit v7 on v5

--- a/solution.py
+++ b/solution.py
@@ -70,15 +70,24 @@
     return top + jnp.log(sum(jnp.exp(value - top) for value in values))
 
 
-def lse_rows_cols(row, col):
-    row = lse(gather(row, chip), 0)
-    col = lse_of(col, *(swap(col, "y", step) for step in (1, 2, 3)))
-    row, col = lax.optimization_barrier((row, col))
-    for step, _ in ring:
-        row = lse_of(row, swap(row, "zh", step))
-    for step in (1, 2, 4):
-        col = lse_of(col, swap(col, "zl", step))
-    return row, col
+def lse_near(row, col):
+    n_y, n_chip = lax.axis_size("y"), lax.axis_size(chip)
+    y, own = lax.axis_index("y"), lax.axis_index(chip)
+    same = (jnp.arange(n_y) == y)[:, None]
+    sent = jnp.where(same, row, col)
+    sent = jnp.broadcast_to(sent[:, None], (n_y, n_chip, row.shape[0]))
+    came = lax.all_to_all(sent.reshape(-1, row.shape[0]), ("y",) + chip, 0, 0).reshape(sent.shape)
+    rows = lax.dynamic_index_in_dim(came, y, 0, False)
+    cols = jnp.where(same, col, lax.dynamic_index_in_dim(came, own, 1, False))
+    return lse(rows, 0), lse(cols, 0)
+
+
+def lse_rows_cols(scores):
+    row, col = lse_near(lse(scores, 1), lse(scores, 0))
+    cols = gather(col, "zl")
+    row = lse_of(row, swap(row, "zh", ring[0][0]))
+    row, cols = lax.optimization_barrier((row, cols))
+    return lse_of(row, swap(row, "zh", ring[1][0])), lse(cols, 0)
 
 
 def body(image_emb, text_emb):
@@ -89,18 +98,18 @@
     row_lanes, col_lanes = img_rows.shape[:-1], txt_cols.shape[:-1]
     img_rows, txt_cols = img_rows.reshape(-1, width), txt_cols.reshape(-1, width)
     scores = logit_scale * jnp.dot(img_rows, txt_cols.T, preferred_element_type=jnp.float32)
-    row_lse, col_lse = lse_rows_cols(lse(scores, 1), lse(scores, 0))
+    row_lse, col_lse = lse_rows_cols(scores)
     weights = (
         0.5 * (jnp.exp(scores - row_lse[:, None]) + jnp.exp(scores - col_lse[None, :]))
     ).astype(jnp.bfloat16)
     image_part = jnp.dot(weights, txt_cols, preferred_element_type=jnp.float32)
     image_part = image_part.reshape(row_lanes + (width,))
-    image_sum = scatter_sum(image_part, chip).reshape(2, 2, own_rows, width)
-    image_sum = scatter_sum_by_halving(image_sum, "zh", ring)
     text_part = lax.dot_general(
         weights, img_rows, (((0,), (0,)), ((), ())), preferred_element_type=jnp.float32
     )
     text_part = text_part.reshape(col_lanes + (width,))
+    image_sum = scatter_sum(image_part, chip).reshape(2, 2, own_rows, width)
+    image_sum = scatter_sum_by_halving(image_sum, "zh", ring)
     text_sum = scatter_sum(scatter_sum_by_swaps(text_part, "y"), "zl")
     grad_image = logit_scale * image_sum - logit_scale * text_emb.astype(jnp.float32)
     grad_text = logit_scale * text_sum - logit_scale * image_emb.astype(jnp.float32)

time: 219 us -> 218 us (level)
  the two profiles are of different devices: /device:TPU:42 before, /device:TPU:128 now
where the time goes in v7:
time: 218 us; the launch traced here: 217 us
  starting transfers between devices  120 us (55%)
  waiting for transfers between devices  82.1 us (38%)
  local copies, waits for them, and re-layouts  5.65 us (3%)
  other arithmetic  5.01 us (2%)
  matrix products  3.25 us (1%)
    ppermute x12, starting transfers between devices, swap(): lax.ppermute(value, axis, [(i, i ^ step) for i in range(lax.axis_size(axi...  70.3 us
    ppermute x12, waiting for transfers between devices, swap(): lax.ppermute(value, axis, [(i, i ^ step) for i in range(lax.axis_size(axi...  69.6 us
    all_to_all x3, starting transfers between devices, gather(): return lax.all_to_all(copies, axis, 0, 0)  30 us
    all_to_all x2, starting transfers between devices, scatter_sum(): lax.all_to_all(parts.astype(jnp.bfloat16), axis, 0, 0).astype(jnp.float32)  12.4 us
    all_to_all x1, waiting for transfers between devices, lse_near(): lax.all_to_all(sent.reshape(-1, row.shape[0]), ('y',) + chip, 0, 0)  7.45 us
    all_to_all x1, starting transfers between devices, lse_near(): lax.all_to_all(sent.reshape(-1, row.shape[0]), ('y',) + chip, 0, 0)  7.39 us
    all_to_all x3, waiting for transfers between devices, gather(): return lax.all_to_all(copies, axis, 0, 0)  5.11 us
  transfers between devices with their start and end apart: 18, of which 11 were waited for; matrix products, arithmetic and copies ran while one was open for 2% of the time, Pallas kernels for 0%

profile of v7, /device:TPU:128, one launch (start us, length us, event | category | flops | bytes accessed | tf_op | source)
XLA Modules:
  0.0 217.2 jit_solution(18055054709032271742)
XLA Ops:
  0.6 1.5 broadcast_in_dim.33
  2.1 14.7 %all-to-all-start.1 = ((bf16[8,16,1024]{2,1,0:T(8,128)(2,1)}), bf16[8,16,1024]{2,1,0:T(8,128)(2,1)S(1)}, u32[]{:S(2)}, u32[]{:S(2)}) async-start(bf16[8,16,1024]{2,1,0:T(8,128)(2,1)} %broadcast_in_dim.33), calls=%async_computation.1 | async-start | bytes 524288 | tf_op jit(solution)/shard_map/all_to_all | solution.py:19
  16.8 12.3 %collective-permute-start = (bf16[16,1024]{1,0:T(8,128)(2,1)}, bf16[16,1024]{1,0:T(8,128)(2,1)S(1)}, u32[]{:S(2)}, u32[]{:S(2)}) collective-permute-start(bf16[16,1024]{1,0:T(8,128)(2,1)} %param.2), channel_id=1, source_target_pairs={{0,8},{8,0},{16,24},{24,16},{1,9},{9,1},{17,25},{25,17},{2,10},{10... | collective-permute-start | bytes 98312 | tf_op jit(solution)/shard_map/ppermute | solution.py:23
  29.1 12.5 %collective-permute-done = bf16[16,1024]{1,0:T(8,128)(2,1)S(1)} collective-permute-done((bf16[16,1024]{1,0:T(8,128)(2,1)}, bf16[16,1024]{1,0:T(8,128)(2,1)S(1)}, u32[]{:S(2)}, u32[]{:S(2)}) %collective-permute-start) | collective-permute-done | bytes 32800 | tf_op jit(solution)/shard_map/ppermute | solution.py:23
  42.3 6.9 %collective-permute-start.1 = (bf16[2,16,1024]{2,1,0:T(8,128)(2,1)S(1)}, bf16[2,16,1024]{2,1,0:T(8,128)(2,1)S(1)}, u32[]{:S(2)}, u32[]{:S(2)}) collective-permute-start(bf16[2,16,1024]{2,1,0:T(8,128)(2,1)S(1)} %pad_maximum_fusion.2), channel_id=1, source_target_pairs={{0,24},{8,16},{16,8},{24,0},{1,25},{9,17},{17,9},{25,1},{2,26},{10... | collective-permute-start | bytes 196616 | tf_op jit(solution)/shard_map/ppermute | solution.py:23
  49.3 7.9 %collective-permute-done.1 = bf16[2,16,1024]{2,1,0:T(8,128)(2,1)S(1)} collective-permute-done((bf16[2,16,1024]{2,1,0:T(8,128)(2,1)S(1)}, bf16[2,16,1024]{2,1,0:T(8,128)(2,1)S(1)}, u32[]{:S(2)}, u32[]{:S(2)}) %collective-permute-start.1) | collective-permute-done | bytes 65568 | tf_op jit(solution)/shard_map/ppermute | solution.py:23
  57.3 1.2 broadcast_in_dim.28
  58.4 4.3 %all-to-all-start = ((bf16[8,2,2,16,1024]{4,3,2,1,0:T(8,128)(2,1)}), bf16[8,2,2,16,1024]{4,3,2,1,0:T(8,128)(2,1)S(1)}, u32[]{:S(2)}, u32[]{:S(2)}) async-start(bf16[8,2,2,16,1024]{4,3,2,1,0:T(8,128)(2,1)} %broadcast_in_dim.28), calls=%async_computation | async-start | bytes 2097152 | tf_op jit(solution)/shard_map/all_to_all | solution.py:19
  62.7 4.9 %collective-permute-start.4 = (bf16[8,16,1024]{2,1,0:T(8,128)(2,1)S(1)}, bf16[8,16,1024]{2,1,0:T(8,128)(2,1)S(1)}, u32[]{:S(2)}, u32[]{:S(2)}) collective-permute-start(bf16[8,16,1024]{2,1,0:T(8,128)(2,1)S(1)} %all-to-all-done.1), channel_id=1, source_target_pairs={{0,768},{256,512},{512,256},{768,0},{1,769},{257,513},{513,257},{7... | collective-permute-start | bytes 786440 | tf_op jit(solution)/shard_map/ppermute | solution.py:23
  67.6 2.5 %collective-permute-start.3 = (bf16[8,16,1024]{2,1,0:T(8,128)(2,1)S(1)}, bf16[8,16,1024]{2,1,0:T(8,128)(2,1)S(1)}, u32[]{:S(2)}, u32[]{:S(2)}) collective-permute-start(bf16[8,16,1024]{2,1,0:T(8,128)(2,1)S(1)} %all-to-all-done.1), channel_id=1, source_target_pairs={{0,512},{256,768},{512,0},{768,256},{1,513},{257,769},{513,1},{769... | collective-permute-start | bytes 786440 | tf_op jit(solution)/shard_map/ppermute | solution.py:23
  70.2 2.4 %collective-permute-start.2 = (bf16[8,16,1024]{2,1,0:T(8,128)(2,1)S(1)}, bf16[8,16,1024]{2,1,0:T(8,128)(2,1)S(1)}, u32[]{:S(2)}, u32[]{:S(2)}) collective-permute-start(bf16[8,16,1024]{2,1,0:T(8,128)(2,1)S(1)} %all-to-all-done.1), channel_id=1, source_target_pairs={{0,256},{256,0},{512,768},{768,512},{1,257},{257,1},{513,769},{769... | collective-permute-start | bytes 786440 | tf_op jit(solution)/shard_map/ppermute | solution.py:23
  72.6 7.6 %collective-permute-done.4 = bf16[8,16,1024]{2,1,0:T(8,128)(2,1)S(1)} collective-permute-done((bf16[8,16,1024]{2,1,0:T(8,128)(2,1)S(1)}, bf16[8,16,1024]{2,1,0:T(8,128)(2,1)S(1)}, u32[]{:S(2)}, u32[]{:S(2)}) %collective-permute-start.4) | collective-permute-done | bytes 262176 | tf_op jit(solution)/shard_map/ppermute | solution.py:23
  80.2 2.5 %collective-permute-done.2 = bf16[8,16,1024]{2,1,0:T(8,128)(2,1)S(1)} collective-permute-done((bf16[8,16,1024]{2,1,0:T(8,128)(2,1)S(1)}, bf16[8,16,1024]{2,1,0:T(8,128)(2,1)S(1)}, u32[]{:S(2)}, u32[]{:S(2)}) %collective-permute-start.2) | collective-permute-done | bytes 262176 | tf_op jit(solution)/shard_map/ppermute | solution.py:23
  85.2 7.4 %all-to-all-start.2 = ((f32[32,1,512]{2,1,0:T(1,128)}), f32[32,1,512]{2,1,0:T(1,128)S(1)}, u32[]{:S(2)}, u32[]{:S(2)}) async-start(f32[32,1,512]{2,1,0:T(1,128)} %all_to_all.26), calls=%async_computation.2 | async-start | bytes 131072 | tf_op jit(solution)/shard_map/all_to_all | solution.py:79
  92.6 7.5 %all-to-all-done.2 = f32[32,1,512]{2,1,0:T(1,128)S(1)} async-done(((f32[32,1,512]{2,1,0:T(1,128)}), f32[32,1,512]{2,1,0:T(1,128)S(1)}, u32[]{:S(2)}, u32[]{:S(2)}) %all-to-all-start.2) | async-done | bytes 65568 | tf_op jit(solution)/shard_map/all_to_all | solution.py:79
  100.4 4.4 %collective-permute-start.5 = (f32[512]{0:T(512)S(1)}, f32[512]{0:T(512)S(1)}, u32[]{:S(2)}, u32[]{:S(2)}) collective-permute-start(f32[512]{0:T(512)S(1)} %log_add_fusion.4), channel_id=1, source_target_pairs={{0,8},{8,0},{16,24},{24,16},{1,9},{9,1},{17,25},{25,17},{2,10},{10... | collective-permute-start | bytes 6152 | tf_op jit(solution)/shard_map/ppermute | solution.py:23
  105.4 11.0 %all-to-all-start.3 = ((f32[8,1,512]{2,1,0:T(1,128)}), f32[8,1,512]{2,1,0:T(1,128)S(1)}, u32[]{:S(2)}, u32[]{:S(2)}) async-start(f32[8,1,512]{2,1,0:T(1,128)} %broadcast_in_dim.38), calls=%async_computation.3 | async-start | bytes 32768 | tf_op jit(solution)/shard_map/all_to_all | solution.py:19
  116.5 5.1 %all-to-all-done.3 = f32[8,1,512]{2,1,0:T(1,128)S(1)} async-done(((f32[8,1,512]{2,1,0:T(1,128)}), f32[8,1,512]{2,1,0:T(1,128)S(1)}, u32[]{:S(2)}, u32[]{:S(2)}) %all-to-all-start.3) | async-done | bytes 16416 | tf_op jit(solution)/shard_map/all_to_all | solution.py:19
  121.6 12.4 %collective-permute-start.6 = (f32[512]{0:T(512)S(1)}, f32[512]{0:T(512)S(1)}, u32[]{:S(2)}, u32[]{:S(2)}) collective-permute-start(f32[512]{0:T(512)S(1)} %log_add_fusion.3), channel_id=1, source_target_pairs={{0,24},{8,16},{16,8},{24,0},{1,25},{9,17},{17,9},{25,1},{2,26},{10... | collective-permute-start | bytes 6152 | tf_op jit(solution)/shard_map/ppermute | solution.py:23
  134.1 1.7 collective-permute-done.6
  136.5 1.0 copy.9
  137.9 1.7 convolution_convert_fusion.1
  139.6 3.7 %all-to-all-start.4 = ((bf16[8,4,16,1024]{3,2,1,0:T(8,128)(2,1)}), bf16[8,4,16,1024]{3,2,1,0:T(8,128)(2,1)S(1)}, u32[]{:S(2)}, u32[]{:S(2)}) async-start(bf16[8,4,16,1024]{3,2,1,0:T(8,128)(2,1)} %convolution_convert_fusion.1), calls=%async_computation.4 | async-start | bytes 2097152 | tf_op jit(solution)/shard_map/all_to_all | solution.py:34
  144.1 2.6 %collective-permute-start.9 = (bf16[8,16,1024]{2,1,0:T(8,128)(2,1)S(1)}, bf16[8,16,1024]{2,1,0:T(8,128)(2,1)S(1)}, u32[]{:S(2)}, u32[]{:S(2)}) collective-permute-start(bf16[8,16,1024]{2,1,0:T(8,128)(2,1)S(1)} %get-tuple-element.11), channel_id=1, source_target_pairs={{0,256},{256,0},{512,768},{768,512},{1,257},{257,1},{513,769},{769... | collective-permute-start | bytes 786440 | tf_op jit(solution)/shard_map/ppermute | solution.py:23
  146.7 3.1 %collective-permute-start.11 = (bf16[8,16,1024]{2,1,0:T(8,128)(2,1)S(1)}, bf16[8,16,1024]{2,1,0:T(8,128)(2,1)S(1)}, u32[]{:S(2)}, u32[]{:S(2)}) collective-permute-start(bf16[8,16,1024]{2,1,0:T(8,128)(2,1)S(1)} %get-tuple-element.12), channel_id=1, source_target_pairs={{0,768},{256,512},{512,256},{768,0},{1,769},{257,513},{513,257},{7... | collective-permute-start | bytes 786440 | tf_op jit(solution)/shard_map/ppermute | solution.py:23
  149.8 4.2 %collective-permute-start.10 = (bf16[8,16,1024]{2,1,0:T(8,128)(2,1)S(1)}, bf16[8,16,1024]{2,1,0:T(8,128)(2,1)S(1)}, u32[]{:S(2)}, u32[]{:S(2)}) collective-permute-start(bf16[8,16,1024]{2,1,0:T(8,128)(2,1)S(1)} %get-tuple-element.13), channel_id=1, source_target_pairs={{0,512},{256,768},{512,0},{768,256},{1,513},{257,769},{513,1},{769... | collective-permute-start | bytes 786440 | tf_op jit(solution)/shard_map/ppermute | solution.py:23
  154.7 9.0 %collective-permute-done.11 = bf16[8,16,1024]{2,1,0:T(8,128)(2,1)S(1)} collective-permute-done((bf16[8,16,1024]{2,1,0:T(8,128)(2,1)S(1)}, bf16[8,16,1024]{2,1,0:T(8,128)(2,1)S(1)}, u32[]{:S(2)}, u32[]{:S(2)}) %collective-permute-start.11) | collective-permute-done | bytes 262176 | tf_op jit(solution)/shard_map/ppermute | solution.py:23
  164.6 8.7 %all-to-all-start.5 = ((bf16[8,16,1024]{2,1,0:T(8,128)(2,1)}), bf16[8,16,1024]{2,1,0:T(8,128)(2,1)S(1)}, u32[]{:S(2)}, u32[]{:S(2)}) async-start(bf16[8,16,1024]{2,1,0:T(8,128)(2,1)} %fusion.2), calls=%async_computation.5 | async-start | bytes 524288 | tf_op jit(solution)/shard_map/all_to_all | solution.py:34
  173.5 12.4 %collective-permute-start.7 = (bf16[2,16,1024]{2,1,0:T(8,128)(2,1)S(1)}, bf16[2,16,1024]{2,1,0:T(8,128)(2,1)S(1)}, u32[]{:S(2)}, u32[]{:S(2)}) collective-permute-start(bf16[2,16,1024]{2,1,0:T(8,128)(2,1)S(1)} %fusion.6), channel_id=1, source_target_pairs={{0,24},{8,16},{16,8},{24,0},{1,25},{9,17},{17,9},{25,1},{2,26},{10... | collective-permute-start | bytes 196616 | tf_op jit(solution)/shard_map/ppermute | solution.py:23
  186.0 15.2 %collective-permute-done.7 = bf16[2,16,1024]{2,1,0:T(8,128)(2,1)S(1)} collective-permute-done((bf16[2,16,1024]{2,1,0:T(8,128)(2,1)S(1)}, bf16[2,16,1024]{2,1,0:T(8,128)(2,1)S(1)}, u32[]{:S(2)}, u32[]{:S(2)}) %collective-permute-start.7) | collective-permute-done | bytes 65568 | tf_op jit(solution)/shard_map/ppermute | solution.py:23
  201.3 2.1 collective-permute-start.8
  203.5 12.3 %collective-permute-done.8 = bf16[16,1024]{1,0:T(8,128)(2,1)S(1)} collective-permute-done((bf16[16,1024]{1,0:T(8,128)(2,1)S(1)}, bf16[16,1024]{1,0:T(8,128)(2,1)S(1)}, u32[]{:S(2)}, u32[]{:S(2)}) %collective-permute-start.8) | collective-permute-done | bytes 32800 | tf_op jit(solution)/shard_map/ppermute | solution.py:23
  (58 shorter events, 9.3 us)
Async XLA Ops:
  2.1 55.2 %all-to-all-start.1 = ((bf16[8,16,1024]{2,1,0:T(8,128)(2,1)}), bf16[8,16,1024]{2,1,0:T(8,128)(2,1)S(1)}, u32[]{:S(2)}, u32[]{:S(2)}) async-start(bf16[8,16,1024]{2,1,0:T(8,128)(2,1)} %broadcast_in_dim.33), calls=%async_computation.1 | async-start | bytes 524288 | tf_op jit(solution)/shard_map/all_to_all | solution.py:19
  16.8 24.7 %collective-permute-start = (bf16[16,1024]{1,0:T(8,128)(2,1)}, bf16[16,1024]{1,0:T(8,128)(2,1)S(1)}, u32[]{:S(2)}, u32[]{:S(2)}) collective-permute-start(bf16[16,1024]{1,0:T(8,128)(2,1)} %param.2), channel_id=1, source_target_pairs={{0,8},{8,0},{16,24},{24,16},{1,9},{9,1},{17,25},{25,17},{2,10},{10... | collective-permute-start | bytes 98312 | tf_op jit(solution)/shard_map/ppermute | solution.py:23
  42.3 14.9 %collective-permute-start.1 = (bf16[2,16,1024]{2,1,0:T(8,128)(2,1)S(1)}, bf16[2,16,1024]{2,1,0:T(8,128)(2,1)S(1)}, u32[]{:S(2)}, u32[]{:S(2)}) collective-permute-start(bf16[2,16,1024]{2,1,0:T(8,128)(2,1)S(1)} %pad_maximum_fusion.2), channel_id=1, source_target_pairs={{0,24},{8,16},{16,8},{24,0},{1,25},{9,17},{17,9},{25,1},{2,26},{10... | collective-permute-start | bytes 196616 | tf_op jit(solution)/shard_map/ppermute | solution.py:23
  58.4 24.6 %all-to-all-start = ((bf16[8,2,2,16,1024]{4,3,2,1,0:T(8,128)(2,1)}), bf16[8,2,2,16,1024]{4,3,2,1,0:T(8,128)(2,1)S(1)}, u32[]{:S(2)}, u32[]{:S(2)}) async-start(bf16[8,2,2,16,1024]{4,3,2,1,0:T(8,128)(2,1)} %broadcast_in_dim.28), calls=%async_computation | async-start | bytes 2097152 | tf_op jit(solution)/shard_map/all_to_all | solution.py:19
  62.7 17.5 %collective-permute-start.4 = (bf16[8,16,1024]{2,1,0:T(8,128)(2,1)S(1)}, bf16[8,16,1024]{2,1,0:T(8,128)(2,1)S(1)}, u32[]{:S(2)}, u32[]{:S(2)}) collective-permute-start(bf16[8,16,1024]{2,1,0:T(8,128)(2,1)S(1)} %all-to-all-done.1), channel_id=1, source_target_pairs={{0,768},{256,512},{512,256},{768,0},{1,769},{257,513},{513,257},{7... | collective-permute-start | bytes 786440 | tf_op jit(solution)/shard_map/ppermute | solution.py:23
  67.6 12.6 %collective-permute-start.3 = (bf16[8,16,1024]{2,1,0:T(8,128)(2,1)S(1)}, bf16[8,16,1024]{2,1,0:T(8,128)(2,1)S(1)}, u32[]{:S(2)}, u32[]{:S(2)}) collective-permute-start(bf16[8,16,1024]{2,1,0:T(8,128)(2,1)S(1)} %all-to-all-done.1), channel_id=1, source_target_pairs={{0,512},{256,768},{512,0},{768,256},{1,513},{257,769},{513,1},{769... | collective-permute-start | bytes 786440 | tf_op jit(solution)/shard_map/ppermute | solution.py:23
  70.2 12.6 %collective-permute-start.2 = (bf16[8,16,1024]{2,1,0:T(8,128)(2,1)S(1)}, bf16[8,16,1024]{2,1,0:T(8,128)(2,1)S(1)}, u32[]{:S(2)}, u32[]{:S(2)}) collective-permute-start(bf16[8,16,1024]{2,1,0:T(8,128)(2,1)S(1)} %all-to-all-done.1), channel_id=1, source_target_pairs={{0,256},{256,0},{512,768},{768,512},{1,257},{257,1},{513,769},{769... | collective-permute-start | bytes 786440 | tf_op jit(solution)/shard_map/ppermute | solution.py:23
  83.0 1.0 copy-start
  85.2 14.9 %all-to-all-start.2 = ((f32[32,1,512]{2,1,0:T(1,128)}), f32[32,1,512]{2,1,0:T(1,128)S(1)}, u32[]{:S(2)}, u32[]{:S(2)}) async-start(f32[32,1,512]{2,1,0:T(1,128)} %all_to_all.26), calls=%async_computation.2 | async-start | bytes 131072 | tf_op jit(solution)/shard_map/all_to_all | solution.py:79
  100.4 16.1 %collective-permute-start.5 = (f32[512]{0:T(512)S(1)}, f32[512]{0:T(512)S(1)}, u32[]{:S(2)}, u32[]{:S(2)}) collective-permute-start(f32[512]{0:T(512)S(1)} %log_add_fusion.4), channel_id=1, source_target_pairs={{0,8},{8,0},{16,24},{24,16},{1,9},{9,1},{17,25},{25,17},{2,10},{10... | collective-permute-start | bytes 6152 | tf_op jit(solution)/shard_map/ppermute | solution.py:23
  105.4 16.1 %all-to-all-start.3 = ((f32[8,1,512]{2,1,0:T(1,128)}), f32[8,1,512]{2,1,0:T(1,128)S(1)}, u32[]{:S(2)}, u32[]{:S(2)}) async-start(f32[8,1,512]{2,1,0:T(1,128)} %broadcast_in_dim.38), calls=%async_computation.3 | async-start | bytes 32768 | tf_op jit(solution)/shard_map/all_to_all | solution.py:19
  121.6 14.2 %collective-permute-start.6 = (f32[512]{0:T(512)S(1)}, f32[512]{0:T(512)S(1)}, u32[]{:S(2)}, u32[]{:S(2)}) collective-permute-start(f32[512]{0:T(512)S(1)} %log_add_fusion.3), channel_id=1, source_target_pairs={{0,24},{8,16},{16,8},{24,0},{1,25},{9,17},{17,9},{25,1},{2,26},{10... | collective-permute-start | bytes 6152 | tf_op jit(solution)/shard_map/ppermute | solution.py:23
  136.5 1.4 copy-start.1
  139.6 3.7 %copy-start.2 = (bf16[512,512]{1,0:T(8,128)(2,1)S(1)}, bf16[512,512]{1,0:T(8,128)(2,1)}, u32[]{:S(2)}) copy-start(bf16[512,512]{1,0:T(8,128)(2,1)} %copy.9) | copy-start | bytes 1572868
  139.6 25.0 %all-to-all-start.4 = ((bf16[8,4,16,1024]{3,2,1,0:T(8,128)(2,1)}), bf16[8,4,16,1024]{3,2,1,0:T(8,128)(2,1)S(1)}, u32[]{:S(2)}, u32[]{:S(2)}) async-start(bf16[8,4,16,1024]{3,2,1,0:T(8,128)(2,1)} %convolution_convert_fusion.1), calls=%async_computation.4 | async-start | bytes 2097152 | tf_op jit(solution)/shard_map/all_to_all | solution.py:34
  144.1 10.5 %collective-permute-start.9 = (bf16[8,16,1024]{2,1,0:T(8,128)(2,1)S(1)}, bf16[8,16,1024]{2,1,0:T(8,128)(2,1)S(1)}, u32[]{:S(2)}, u32[]{:S(2)}) collective-permute-start(bf16[8,16,1024]{2,1,0:T(8,128)(2,1)S(1)} %get-tuple-element.11), channel_id=1, source_target_pairs={{0,256},{256,0},{512,768},{768,512},{1,257},{257,1},{513,769},{769... | collective-permute-start | bytes 786440 | tf_op jit(solution)/shard_map/ppermute | solution.py:23
  146.7 17.0 %collective-permute-start.11 = (bf16[8,16,1024]{2,1,0:T(8,128)(2,1)S(1)}, bf16[8,16,1024]{2,1,0:T(8,128)(2,1)S(1)}, u32[]{:S(2)}, u32[]{:S(2)}) collective-permute-start(bf16[8,16,1024]{2,1,0:T(8,128)(2,1)S(1)} %get-tuple-element.12), channel_id=1, source_target_pairs={{0,768},{256,512},{512,256},{768,0},{1,769},{257,513},{513,257},{7... | collective-permute-start | bytes 786440 | tf_op jit(solution)/shard_map/ppermute | solution.py:23
  149.8 13.9 %collective-permute-start.10 = (bf16[8,16,1024]{2,1,0:T(8,128)(2,1)S(1)}, bf16[8,16,1024]{2,1,0:T(8,128)(2,1)S(1)}, u32[]{:S(2)}, u32[]{:S(2)}) collective-permute-start(bf16[8,16,1024]{2,1,0:T(8,128)(2,1)S(1)} %get-tuple-element.13), channel_id=1, source_target_pairs={{0,512},{256,768},{512,0},{768,256},{1,513},{257,769},{513,1},{769... | collective-permute-start | bytes 786440 | tf_op jit(solution)/shard_map/ppermute | solution.py:23
  164.6 38.8 %all-to-all-start.5 = ((bf16[8,16,1024]{2,1,0:T(8,128)(2,1)}), bf16[8,16,1024]{2,1,0:T(8,128)(2,1)S(1)}, u32[]{:S(2)}, u32[]{:S(2)}) async-start(bf16[8,16,1024]{2,1,0:T(8,128)(2,1)} %fusion.2), calls=%async_computation.5 | async-start | bytes 524288 | tf_op jit(solution)/shard_map/all_to_all | solution.py:34
  173.3 42.5 %copy-start.3 = (bf16[16,1024]{1,0:T(8,128)(2,1)S(1)}, bf16[16,1024]{1,0:T(8,128)(2,1)}, u32[]{:S(2)}) copy-start(bf16[16,1024]{1,0:T(8,128)(2,1)} %param.3) | copy-start | bytes 98308
  173.3 42.5 %copy-start.4 = (bf16[16,1024]{1,0:T(8,128)(2,1)S(1)}, bf16[16,1024]{1,0:T(8,128)(2,1)}, u32[]{:S(2)}) copy-start(bf16[16,1024]{1,0:T(8,128)(2,1)} %param.2) | copy-start | bytes 98308
  173.5 27.7 %collective-permute-start.7 = (bf16[2,16,1024]{2,1,0:T(8,128)(2,1)S(1)}, bf16[2,16,1024]{2,1,0:T(8,128)(2,1)S(1)}, u32[]{:S(2)}, u32[]{:S(2)}) collective-permute-start(bf16[2,16,1024]{2,1,0:T(8,128)(2,1)S(1)} %fusion.6), channel_id=1, source_target_pairs={{0,24},{8,16},{16,8},{24,0},{1,25},{9,17},{17,9},{25,1},{2,26},{10... | collective-permute-start | bytes 196616 | tf_op jit(solution)/shard_map/ppermute | solution.py:23
  201.3 14.5 %collective-permute-start.8 = (bf16[16,1024]{1,0:T(8,128)(2,1)S(1)}, bf16[16,1024]{1,0:T(8,128)(2,1)S(1)}, u32[]{:S(2)}, u32[]{:S(2)}) collective-permute-start(bf16[16,1024]{1,0:T(8,128)(2,1)S(1)} %fusion.8), channel_id=1, source_target_pairs={{0,8},{8,0},{16,24},{24,16},{1,9},{9,1},{17,25},{25,17},{2,10},{10... | collective-permute-start | bytes 98312 | tf_op jit(solution)/shard_map/ppermute | solution.py:23

commit v8 on v5

--- a/solution.py
+++ b/solution.py
@@ -9,6 +9,7 @@
 
 fine = {"y": 4, "zl": 8, "zh": 4, "x": 4, "core": 2}
 chip = ("x", "core")
+dp = ("zh", "x", "core")
 blk = ("y", "zl")
 ring = ((1, 1), (3, 2))
 everything = ("y", "zl", "zh", "x", "core")
@@ -70,15 +71,15 @@
     return top + jnp.log(sum(jnp.exp(value - top) for value in values))
 
 
-def lse_rows_cols(row, col):
-    row = lse(gather(row, chip), 0)
-    col = lse_of(col, *(swap(col, "y", step) for step in (1, 2, 3)))
-    row, col = lax.optimization_barrier((row, col))
-    for step, _ in ring:
-        row = lse_of(row, swap(row, "zh", step))
-    for step in (1, 2, 4):
-        col = lse_of(col, swap(col, "zl", step))
-    return row, col
+def lse_rows_cols(scores):
+    cols, row = lax.optimization_barrier((gather(lse(scores, 0), blk), lse(scores, 1)))
+    return lse(gather(row, dp), 0), lse(cols, 0)
+
+
+def weighted(scores, row_lse, col_lse):
+    return (
+        0.5 * (jnp.exp(scores - row_lse[:, None]) + jnp.exp(scores - col_lse[None, :]))
+    ).astype(jnp.bfloat16)
 
 
 def body(image_emb, text_emb):
@@ -89,26 +90,27 @@
     row_lanes, col_lanes = img_rows.shape[:-1], txt_cols.shape[:-1]
     img_rows, txt_cols = img_rows.reshape(-1, width), txt_cols.reshape(-1, width)
     scores = logit_scale * jnp.dot(img_rows, txt_cols.T, preferred_element_type=jnp.float32)
-    row_lse, col_lse = lse_rows_cols(lse(scores, 1), lse(scores, 0))
-    weights = (
-        0.5 * (jnp.exp(scores - row_lse[:, None]) + jnp.exp(scores - col_lse[None, :]))
-    ).astype(jnp.bfloat16)
+    row_lse, col_lse = lse_rows_cols(scores)
+    weights = weighted(scores, row_lse, col_lse)
     image_part = jnp.dot(weights, txt_cols, preferred_element_type=jnp.float32)
-    image_part = image_part.reshape(row_lanes + (width,))
-    image_sum = scatter_sum(image_part, chip).reshape(2, 2, own_rows, width)
-    image_sum = scatter_sum_by_halving(image_sum, "zh", ring)
+    image_part = image_part.astype(jnp.bfloat16).reshape(row_lanes + (width,))
+    image_part, scores = lax.optimization_barrier((image_part, scores))
+    weights = weighted(scores, row_lse, col_lse)
     text_part = lax.dot_general(
         weights, img_rows, (((0,), (0,)), ((), ())), preferred_element_type=jnp.float32
     )
     text_part = text_part.reshape(col_lanes + (width,))
+    image_sum = scatter_sum(image_part, chip).reshape(2, 2, own_rows, width)
+    image_sum = scatter_sum_by_halving(image_sum, "zh", ring)
     text_sum = scatter_sum(scatter_sum_by_swaps(text_part, "y"), "zl")
     grad_image = logit_scale * image_sum - logit_scale * text_emb.astype(jnp.float32)
     grad_text = logit_scale * text_sum - logit_scale * image_emb.astype(jnp.float32)
     own_row = lax.axis_index(chip) * row_lanes[1] + lax.axis_index("zh")
     own_row_lse = lax.dynamic_slice_in_dim(row_lse, own_row * own_rows, own_rows, 0)
     own_col_lse = lax.dynamic_slice_in_dim(col_lse, lax.axis_index(blk) * own_rows, own_rows, 0)
+    image_own, text_own = lax.optimization_barrier((image_emb, text_emb))
     diag = logit_scale * jnp.sum(
-        image_emb.astype(jnp.float32) * text_emb.astype(jnp.float32), axis=1
+        image_own.astype(jnp.float32) * text_own.astype(jnp.float32), axis=1
     )
     row_loss = 0.5 * (own_row_lse + own_col_lse) - diag
     return (grad_image, grad_text, row_loss)

time: 219 us -> 234 us (1.068)
  the two profiles are of different devices: /device:TPU:42 before, /device:TPU:226 now
where the time goes in v8:
time: 234 us; the launch traced here: 233 us
  starting transfers between devices  111 us (47%)
  waiting for transfers between devices  106 us (45%)
  other arithmetic  6.03 us (3%)
  local copies, waits for them, and re-layouts  5.08 us (2%)
  matrix products  4.45 us (2%)
    ppermute x10, waiting for transfers between devices, swap(): lax.ppermute(value, axis, [(i, i ^ step) for i in range(lax.axis_size(axi...  75.5 us
    ppermute x10, starting transfers between devices, swap(): lax.ppermute(value, axis, [(i, i ^ step) for i in range(lax.axis_size(axi...  50.6 us
    all_to_all x4, starting transfers between devices, gather(): return lax.all_to_all(copies, axis, 0, 0)  43.5 us
    all_to_all x4, waiting for transfers between devices, gather(): return lax.all_to_all(copies, axis, 0, 0)  30.1 us
    all_to_all x2, starting transfers between devices, scatter_sum(): lax.all_to_all(parts.astype(jnp.bfloat16), axis, 0, 0).astype(jnp.float32)  16.6 us
  transfers between devices with their start and end apart: 16, of which 12 were waited for; matrix products, arithmetic and copies ran while one was open for 3% of the time, Pallas kernels for 0%

profile of v8, /device:TPU:226, one launch (start us, length us, event | category | flops | bytes accessed | tf_op | source)
XLA Modules:
  0.0 232.8 jit_solution(9343807400790016540)
XLA Ops:
  0.6 1.5 broadcast_in_dim.9
  2.1 9.9 %all-to-all-start.1 = ((bf16[8,16,1024]{2,1,0:T(8,128)(2,1)}), bf16[8,16,1024]{2,1,0:T(8,128)(2,1)S(1)}, u32[]{:S(2)}, u32[]{:S(2)}) async-start(bf16[8,16,1024]{2,1,0:T(8,128)(2,1)} %broadcast_in_dim.9), calls=%async_computation.1 | async-start | bytes 524288 | tf_op jit(solution)/shard_map/all_to_all | solution.py:20
  12.0 15.7 %collective-permute-start = (bf16[16,1024]{1,0:T(8,128)(2,1)}, bf16[16,1024]{1,0:T(8,128)(2,1)S(1)}, u32[]{:S(2)}, u32[]{:S(2)}) collective-permute-start(bf16[16,1024]{1,0:T(8,128)(2,1)} %param.2), channel_id=1, source_target_pairs={{0,8},{8,0},{16,24},{24,16},{1,9},{9,1},{17,25},{25,17},{2,10},{10... | collective-permute-start | bytes 98312 | tf_op jit(solution)/shard_map/ppermute | solution.py:24
  27.7 5.0 %collective-permute-done = bf16[16,1024]{1,0:T(8,128)(2,1)S(1)} collective-permute-done((bf16[16,1024]{1,0:T(8,128)(2,1)}, bf16[16,1024]{1,0:T(8,128)(2,1)S(1)}, u32[]{:S(2)}, u32[]{:S(2)}) %collective-permute-start) | collective-permute-done | bytes 32800 | tf_op jit(solution)/shard_map/ppermute | solution.py:24
  33.6 10.2 %collective-permute-start.1 = (bf16[2,16,1024]{2,1,0:T(8,128)(2,1)S(1)}, bf16[2,16,1024]{2,1,0:T(8,128)(2,1)S(1)}, u32[]{:S(2)}, u32[]{:S(2)}) collective-permute-start(bf16[2,16,1024]{2,1,0:T(8,128)(2,1)S(1)} %pad_maximum_fusion.2), channel_id=1, source_target_pairs={{0,24},{8,16},{16,8},{24,0},{1,25},{9,17},{17,9},{25,1},{2,26},{10... | collective-permute-start | bytes 196616 | tf_op jit(solution)/shard_map/ppermute | solution.py:24
  43.8 11.3 %collective-permute-done.1 = bf16[2,16,1024]{2,1,0:T(8,128)(2,1)S(1)} collective-permute-done((bf16[2,16,1024]{2,1,0:T(8,128)(2,1)S(1)}, bf16[2,16,1024]{2,1,0:T(8,128)(2,1)S(1)}, u32[]{:S(2)}, u32[]{:S(2)}) %collective-permute-start.1) | collective-permute-done | bytes 65568 | tf_op jit(solution)/shard_map/ppermute | solution.py:24
  55.2 1.1 broadcast_in_dim.8
  56.3 4.8 %all-to-all-start = ((bf16[8,2,2,16,1024]{4,3,2,1,0:T(8,128)(2,1)}), bf16[8,2,2,16,1024]{4,3,2,1,0:T(8,128)(2,1)S(1)}, u32[]{:S(2)}, u32[]{:S(2)}) async-start(bf16[8,2,2,16,1024]{4,3,2,1,0:T(8,128)(2,1)} %broadcast_in_dim.8), calls=%async_computation | async-start | bytes 2097152 | tf_op jit(solution)/shard_map/all_to_all | solution.py:20
  61.1 3.5 %collective-permute-start.2 = (bf16[8,16,1024]{2,1,0:T(8,128)(2,1)S(1)}, bf16[8,16,1024]{2,1,0:T(8,128)(2,1)S(1)}, u32[]{:S(2)}, u32[]{:S(2)}) collective-permute-start(bf16[8,16,1024]{2,1,0:T(8,128)(2,1)S(1)} %all-to-all-done.1), channel_id=1, source_target_pairs={{0,256},{256,0},{512,768},{768,512},{1,257},{257,1},{513,769},{769... | collective-permute-start | bytes 786440 | tf_op jit(solution)/shard_map/ppermute | solution.py:24
  64.6 4.8 %collective-permute-start.3 = (bf16[8,16,1024]{2,1,0:T(8,128)(2,1)S(1)}, bf16[8,16,1024]{2,1,0:T(8,128)(2,1)S(1)}, u32[]{:S(2)}, u32[]{:S(2)}) collective-permute-start(bf16[8,16,1024]{2,1,0:T(8,128)(2,1)S(1)} %all-to-all-done.1), channel_id=1, source_target_pairs={{0,512},{256,768},{512,0},{768,256},{1,513},{257,769},{513,1},{769... | collective-permute-start | bytes 786440 | tf_op jit(solution)/shard_map/ppermute | solution.py:24
  69.4 2.1 collective-permute-start.4
  72.2 7.4 %collective-permute-done.3 = bf16[8,16,1024]{2,1,0:T(8,128)(2,1)S(1)} collective-permute-done((bf16[8,16,1024]{2,1,0:T(8,128)(2,1)S(1)}, bf16[8,16,1024]{2,1,0:T(8,128)(2,1)S(1)}, u32[]{:S(2)}, u32[]{:S(2)}) %collective-permute-start.3) | collective-permute-done | bytes 262176 | tf_op jit(solution)/shard_map/ppermute | solution.py:24
  79.6 5.5 %collective-permute-done.4 = bf16[8,16,1024]{2,1,0:T(8,128)(2,1)S(1)} collective-permute-done((bf16[8,16,1024]{2,1,0:T(8,128)(2,1)S(1)}, bf16[8,16,1024]{2,1,0:T(8,128)(2,1)S(1)}, u32[]{:S(2)}, u32[]{:S(2)}) %collective-permute-start.4) | collective-permute-done | bytes 262176 | tf_op jit(solution)/shard_map/ppermute | solution.py:24
  87.2 10.1 %all-to-all-start.2 = ((f32[32,1,512]{2,1,0:T(1,128)}), f32[32,1,512]{2,1,0:T(1,128)S(1)}, u32[]{:S(2)}, u32[]{:S(2)}) async-start(f32[32,1,512]{2,1,0:T(1,128)} %broadcast_in_dim.10), calls=%async_computation.2 | async-start | bytes 131072 | tf_op jit(solution)/shard_map/all_to_all | solution.py:20
  97.3 6.0 %all-to-all-done.2 = f32[32,1,512]{2,1,0:T(1,128)S(1)} async-done(((f32[32,1,512]{2,1,0:T(1,128)}), f32[32,1,512]{2,1,0:T(1,128)S(1)}, u32[]{:S(2)}, u32[]{:S(2)}) %all-to-all-start.2) | async-done | bytes 65568 | tf_op jit(solution)/shard_map/all_to_all | solution.py:20
  104.0 18.7 %all-to-all-start.3 = ((f32[32,1,512]{2,1,0:T(1,128)}), f32[32,1,512]{2,1,0:T(1,128)S(1)}, u32[]{:S(2)}, u32[]{:S(2)}) async-start(f32[32,1,512]{2,1,0:T(1,128)} %broadcast_in_dim.11), calls=%async_computation.3 | async-start | bytes 131072 | tf_op jit(solution)/shard_map/all_to_all | solution.py:20
  122.8 24.0 %all-to-all-done.3 = f32[32,1,512]{2,1,0:T(1,128)S(1)} async-done(((f32[32,1,512]{2,1,0:T(1,128)}), f32[32,1,512]{2,1,0:T(1,128)S(1)}, u32[]{:S(2)}, u32[]{:S(2)}) %all-to-all-start.3) | async-done | bytes 65568 | tf_op jit(solution)/shard_map/all_to_all | solution.py:20
  147.0 1.9 convolution_convert_fusion.1
  149.2 1.0 copy.9
  150.2 5.2 %all-to-all-start.4 = ((bf16[8,4,16,1024]{3,2,1,0:T(8,128)(2,1)}), bf16[8,4,16,1024]{3,2,1,0:T(8,128)(2,1)S(1)}, u32[]{:S(2)}, u32[]{:S(2)}) async-start(bf16[8,4,16,1024]{3,2,1,0:T(8,128)(2,1)} %bitcast.66), calls=%async_computation.4 | async-start | bytes 2097152 | tf_op jit(solution)/shard_map/all_to_all | solution.py:35
  155.4 1.8 convolution_convert_fusion
  157.2 2.4 %collective-permute-start.7 = (bf16[8,16,1024]{2,1,0:T(8,128)(2,1)S(1)}, bf16[8,16,1024]{2,1,0:T(8,128)(2,1)S(1)}, u32[]{:S(2)}, u32[]{:S(2)}) collective-permute-start(bf16[8,16,1024]{2,1,0:T(8,128)(2,1)S(1)} %get-tuple-element.19), channel_id=1, source_target_pairs={{0,256},{256,0},{512,768},{768,512},{1,257},{257,1},{513,769},{769... | collective-permute-start | bytes 786440 | tf_op jit(solution)/shard_map/ppermute | solution.py:24
  159.7 3.9 %collective-permute-start.8 = (bf16[8,16,1024]{2,1,0:T(8,128)(2,1)S(1)}, bf16[8,16,1024]{2,1,0:T(8,128)(2,1)S(1)}, u32[]{:S(2)}, u32[]{:S(2)}) collective-permute-start(bf16[8,16,1024]{2,1,0:T(8,128)(2,1)S(1)} %get-tuple-element.21), channel_id=1, source_target_pairs={{0,512},{256,768},{512,0},{768,256},{1,513},{257,769},{513,1},{769... | collective-permute-start | bytes 786440 | tf_op jit(solution)/shard_map/ppermute | solution.py:24
  163.6 4.1 %collective-permute-start.9 = (bf16[8,16,1024]{2,1,0:T(8,128)(2,1)S(1)}, bf16[8,16,1024]{2,1,0:T(8,128)(2,1)}, u32[]{:S(2)}, u32[]{:S(2)}) collective-permute-start(bf16[8,16,1024]{2,1,0:T(8,128)(2,1)S(1)} %get-tuple-element.20), channel_id=1, source_target_pairs={{0,768},{256,512},{512,256},{768,0},{1,769},{257,513},{513,257},{7... | collective-permute-start | bytes 786440 | tf_op jit(solution)/shard_map/ppermute | solution.py:24
  168.3 5.4 %collective-permute-done.8 = bf16[8,16,1024]{2,1,0:T(8,128)(2,1)S(1)} collective-permute-done((bf16[8,16,1024]{2,1,0:T(8,128)(2,1)S(1)}, bf16[8,16,1024]{2,1,0:T(8,128)(2,1)S(1)}, u32[]{:S(2)}, u32[]{:S(2)}) %collective-permute-start.8) | collective-permute-done | bytes 262176 | tf_op jit(solution)/shard_map/ppermute | solution.py:24
  173.7 5.6 %collective-permute-done.9 = bf16[8,16,1024]{2,1,0:T(8,128)(2,1)} collective-permute-done((bf16[8,16,1024]{2,1,0:T(8,128)(2,1)S(1)}, bf16[8,16,1024]{2,1,0:T(8,128)(2,1)}, u32[]{:S(2)}, u32[]{:S(2)}) %collective-permute-start.9) | collective-permute-done | bytes 262176 | tf_op jit(solution)/shard_map/ppermute | solution.py:24
  179.3 1.8 fusion.3
  181.2 11.5 %all-to-all-start.5 = ((bf16[8,16,1024]{2,1,0:T(8,128)(2,1)}), bf16[8,16,1024]{2,1,0:T(8,128)(2,1)S(1)}, u32[]{:S(2)}, u32[]{:S(2)}) async-start(bf16[8,16,1024]{2,1,0:T(8,128)(2,1)} %fusion.3), calls=%async_computation.5 | async-start | bytes 524288 | tf_op jit(solution)/shard_map/all_to_all | solution.py:35
  192.8 1.9 collective-permute-start.5
  194.9 22.0 %collective-permute-done.5 = bf16[2,16,1024]{2,1,0:T(8,128)(2,1)S(1)} collective-permute-done((bf16[2,16,1024]{2,1,0:T(8,128)(2,1)S(1)}, bf16[2,16,1024]{2,1,0:T(8,128)(2,1)S(1)}, u32[]{:S(2)}, u32[]{:S(2)}) %collective-permute-start.5) | collective-permute-done | bytes 65568 | tf_op jit(solution)/shard_map/ppermute | solution.py:24
  217.0 1.9 collective-permute-start.6
  219.5 12.0 %collective-permute-done.6 = bf16[16,1024]{1,0:T(8,128)(2,1)S(1)} collective-permute-done((bf16[16,1024]{1,0:T(8,128)(2,1)S(1)}, bf16[16,1024]{1,0:T(8,128)(2,1)S(1)}, u32[]{:S(2)}, u32[]{:S(2)}) %collective-permute-start.6) | collective-permute-done | bytes 32800 | tf_op jit(solution)/shard_map/ppermute | solution.py:24
  (40 shorter events, 7.6 us)
Async XLA Ops:
  2.1 53.1 %all-to-all-start.1 = ((bf16[8,16,1024]{2,1,0:T(8,128)(2,1)}), bf16[8,16,1024]{2,1,0:T(8,128)(2,1)S(1)}, u32[]{:S(2)}, u32[]{:S(2)}) async-start(bf16[8,16,1024]{2,1,0:T(8,128)(2,1)} %broadcast_in_dim.9), calls=%async_computation.1 | async-start | bytes 524288 | tf_op jit(solution)/shard_map/all_to_all | solution.py:20
  12.0 20.8 %collective-permute-start = (bf16[16,1024]{1,0:T(8,128)(2,1)}, bf16[16,1024]{1,0:T(8,128)(2,1)S(1)}, u32[]{:S(2)}, u32[]{:S(2)}) collective-permute-start(bf16[16,1024]{1,0:T(8,128)(2,1)} %param.2), channel_id=1, source_target_pairs={{0,8},{8,0},{16,24},{24,16},{1,9},{9,1},{17,25},{25,17},{2,10},{10... | collective-permute-start | bytes 98312 | tf_op jit(solution)/shard_map/ppermute | solution.py:24
  33.6 21.6 %collective-permute-start.1 = (bf16[2,16,1024]{2,1,0:T(8,128)(2,1)S(1)}, bf16[2,16,1024]{2,1,0:T(8,128)(2,1)S(1)}, u32[]{:S(2)}, u32[]{:S(2)}) collective-permute-start(bf16[2,16,1024]{2,1,0:T(8,128)(2,1)S(1)} %pad_maximum_fusion.2), channel_id=1, source_target_pairs={{0,24},{8,16},{16,8},{24,0},{1,25},{9,17},{17,9},{25,1},{2,26},{10... | collective-permute-start | bytes 196616 | tf_op jit(solution)/shard_map/ppermute | solution.py:24
  56.3 29.0 %all-to-all-start = ((bf16[8,2,2,16,1024]{4,3,2,1,0:T(8,128)(2,1)}), bf16[8,2,2,16,1024]{4,3,2,1,0:T(8,128)(2,1)S(1)}, u32[]{:S(2)}, u32[]{:S(2)}) async-start(bf16[8,2,2,16,1024]{4,3,2,1,0:T(8,128)(2,1)} %broadcast_in_dim.8), calls=%async_computation | async-start | bytes 2097152 | tf_op jit(solution)/shard_map/all_to_all | solution.py:20
  61.1 11.0 %collective-permute-start.2 = (bf16[8,16,1024]{2,1,0:T(8,128)(2,1)S(1)}, bf16[8,16,1024]{2,1,0:T(8,128)(2,1)S(1)}, u32[]{:S(2)}, u32[]{:S(2)}) collective-permute-start(bf16[8,16,1024]{2,1,0:T(8,128)(2,1)S(1)} %all-to-all-done.1), channel_id=1, source_target_pairs={{0,256},{256,0},{512,768},{768,512},{1,257},{257,1},{513,769},{769... | collective-permute-start | bytes 786440 | tf_op jit(solution)/shard_map/ppermute | solution.py:24
  64.6 14.9 %collective-permute-start.3 = (bf16[8,16,1024]{2,1,0:T(8,128)(2,1)S(1)}, bf16[8,16,1024]{2,1,0:T(8,128)(2,1)S(1)}, u32[]{:S(2)}, u32[]{:S(2)}) collective-permute-start(bf16[8,16,1024]{2,1,0:T(8,128)(2,1)S(1)} %all-to-all-done.1), channel_id=1, source_target_pairs={{0,512},{256,768},{512,0},{768,256},{1,513},{257,769},{513,1},{769... | collective-permute-start | bytes 786440 | tf_op jit(solution)/shard_map/ppermute | solution.py:24
  69.4 15.6 %collective-permute-start.4 = (bf16[8,16,1024]{2,1,0:T(8,128)(2,1)S(1)}, bf16[8,16,1024]{2,1,0:T(8,128)(2,1)S(1)}, u32[]{:S(2)}, u32[]{:S(2)}) collective-permute-start(bf16[8,16,1024]{2,1,0:T(8,128)(2,1)S(1)} %all-to-all-done.1), channel_id=1, source_target_pairs={{0,768},{256,512},{512,256},{768,0},{1,769},{257,513},{513,257},{7... | collective-permute-start | bytes 786440 | tf_op jit(solution)/shard_map/ppermute | solution.py:24
  87.2 16.1 %all-to-all-start.2 = ((f32[32,1,512]{2,1,0:T(1,128)}), f32[32,1,512]{2,1,0:T(1,128)S(1)}, u32[]{:S(2)}, u32[]{:S(2)}) async-start(f32[32,1,512]{2,1,0:T(1,128)} %broadcast_in_dim.10), calls=%async_computation.2 | async-start | bytes 131072 | tf_op jit(solution)/shard_map/all_to_all | solution.py:20
  104.0 42.8 %all-to-all-start.3 = ((f32[32,1,512]{2,1,0:T(1,128)}), f32[32,1,512]{2,1,0:T(1,128)S(1)}, u32[]{:S(2)}, u32[]{:S(2)}) async-start(f32[32,1,512]{2,1,0:T(1,128)} %broadcast_in_dim.11), calls=%async_computation.3 | async-start | bytes 131072 | tf_op jit(solution)/shard_map/all_to_all | solution.py:20
  150.2 30.9 %all-to-all-start.4 = ((bf16[8,4,16,1024]{3,2,1,0:T(8,128)(2,1)}), bf16[8,4,16,1024]{3,2,1,0:T(8,128)(2,1)S(1)}, u32[]{:S(2)}, u32[]{:S(2)}) async-start(bf16[8,4,16,1024]{3,2,1,0:T(8,128)(2,1)} %bitcast.66), calls=%async_computation.4 | async-start | bytes 2097152 | tf_op jit(solution)/shard_map/all_to_all | solution.py:35
  157.2 11.0 %collective-permute-start.7 = (bf16[8,16,1024]{2,1,0:T(8,128)(2,1)S(1)}, bf16[8,16,1024]{2,1,0:T(8,128)(2,1)S(1)}, u32[]{:S(2)}, u32[]{:S(2)}) collective-permute-start(bf16[8,16,1024]{2,1,0:T(8,128)(2,1)S(1)} %get-tuple-element.19), channel_id=1, source_target_pairs={{0,256},{256,0},{512,768},{768,512},{1,257},{257,1},{513,769},{769... | collective-permute-start | bytes 786440 | tf_op jit(solution)/shard_map/ppermute | solution.py:24
  159.7 14.0 %collective-permute-start.8 = (bf16[8,16,1024]{2,1,0:T(8,128)(2,1)S(1)}, bf16[8,16,1024]{2,1,0:T(8,128)(2,1)S(1)}, u32[]{:S(2)}, u32[]{:S(2)}) collective-permute-start(bf16[8,16,1024]{2,1,0:T(8,128)(2,1)S(1)} %get-tuple-element.21), channel_id=1, source_target_pairs={{0,512},{256,768},{512,0},{768,256},{1,513},{257,769},{513,1},{769... | collective-permute-start | bytes 786440 | tf_op jit(solution)/shard_map/ppermute | solution.py:24
  163.6 15.7 %collective-permute-start.9 = (bf16[8,16,1024]{2,1,0:T(8,128)(2,1)S(1)}, bf16[8,16,1024]{2,1,0:T(8,128)(2,1)}, u32[]{:S(2)}, u32[]{:S(2)}) collective-permute-start(bf16[8,16,1024]{2,1,0:T(8,128)(2,1)S(1)} %get-tuple-element.20), channel_id=1, source_target_pairs={{0,768},{256,512},{512,256},{768,0},{1,769},{257,513},{513,257},{7... | collective-permute-start | bytes 786440 | tf_op jit(solution)/shard_map/ppermute | solution.py:24
  181.2 13.6 %copy-start = (bf16[16,1024]{1,0:T(8,128)(2,1)S(1)}, bf16[16,1024]{1,0:T(8,128)(2,1)}, u32[]{:S(2)}) copy-start(bf16[16,1024]{1,0:T(8,128)(2,1)} %param.3) | copy-start | bytes 98308
  181.2 13.6 %copy-start.1 = (bf16[16,1024]{1,0:T(8,128)(2,1)S(1)}, bf16[16,1024]{1,0:T(8,128)(2,1)}, u32[]{:S(2)}) copy-start(bf16[16,1024]{1,0:T(8,128)(2,1)} %param.2) | copy-start | bytes 98308
  181.2 51.0 %all-to-all-start.5 = ((bf16[8,16,1024]{2,1,0:T(8,128)(2,1)}), bf16[8,16,1024]{2,1,0:T(8,128)(2,1)S(1)}, u32[]{:S(2)}, u32[]{:S(2)}) async-start(bf16[8,16,1024]{2,1,0:T(8,128)(2,1)} %fusion.3), calls=%async_computation.5 | async-start | bytes 524288 | tf_op jit(solution)/shard_map/all_to_all | solution.py:35
  192.8 24.1 %collective-permute-start.5 = (bf16[2,16,1024]{2,1,0:T(8,128)(2,1)S(1)}, bf16[2,16,1024]{2,1,0:T(8,128)(2,1)S(1)}, u32[]{:S(2)}, u32[]{:S(2)}) collective-permute-start(bf16[2,16,1024]{2,1,0:T(8,128)(2,1)S(1)} %fusion.7), channel_id=1, source_target_pairs={{0,24},{8,16},{16,8},{24,0},{1,25},{9,17},{17,9},{25,1},{2,26},{10... | collective-permute-start | bytes 196616 | tf_op jit(solution)/shard_map/ppermute | solution.py:24
  217.0 14.5 %collective-permute-start.6 = (bf16[16,1024]{1,0:T(8,128)(2,1)S(1)}, bf16[16,1024]{1,0:T(8,128)(2,1)S(1)}, u32[]{:S(2)}, u32[]{:S(2)}) collective-permute-start(bf16[16,1024]{1,0:T(8,128)(2,1)S(1)} %fusion.12), channel_id=1, source_target_pairs={{0,8},{8,0},{16,24},{24,16},{1,9},{9,1},{17,25},{25,17},{2,10},{10... | collective-permute-start | bytes 98312 | tf_op jit(solution)/shard_map/ppermute | solution.py:24

commit v9 on v7

--- a/solution.py
+++ b/solution.py
@@ -71,23 +71,22 @@
 
 
 def lse_near(row, col):
-    n_y, n_chip = lax.axis_size("y"), lax.axis_size(chip)
-    y, own = lax.axis_index("y"), lax.axis_index(chip)
-    same = (jnp.arange(n_y) == y)[:, None]
+    n_zl, n_chip = lax.axis_size("zl"), lax.axis_size(chip)
+    zl, own = lax.axis_index("zl"), lax.axis_index(chip)
+    same = (jnp.arange(n_zl) == zl)[:, None]
     sent = jnp.where(same, row, col)
-    sent = jnp.broadcast_to(sent[:, None], (n_y, n_chip, row.shape[0]))
-    came = lax.all_to_all(sent.reshape(-1, row.shape[0]), ("y",) + chip, 0, 0).reshape(sent.shape)
-    rows = lax.dynamic_index_in_dim(came, y, 0, False)
+    sent = jnp.broadcast_to(sent[:, None], (n_zl, n_chip, row.shape[0]))
+    came = lax.all_to_all(sent.reshape(-1, row.shape[0]), ("zl",) + chip, 0, 0).reshape(sent.shape)
+    rows = lax.dynamic_index_in_dim(came, zl, 0, False)
     cols = jnp.where(same, col, lax.dynamic_index_in_dim(came, own, 1, False))
     return lse(rows, 0), lse(cols, 0)
 
 
 def lse_rows_cols(scores):
     row, col = lse_near(lse(scores, 1), lse(scores, 0))
-    cols = gather(col, "zl")
-    row = lse_of(row, swap(row, "zh", ring[0][0]))
-    row, cols = lax.optimization_barrier((row, cols))
-    return lse_of(row, swap(row, "zh", ring[1][0])), lse(cols, 0)
+    for step, _ in ring:
+        row = lse_of(row, swap(row, "zh", step))
+    return row, lse_of(col, *(swap(col, "y", step) for step in (1, 2, 3)))
 
 
 def body(image_emb, text_emb):
@@ -116,8 +115,9 @@
     own_row = lax.axis_index(chip) * row_lanes[1] + lax.axis_index("zh")
     own_row_lse = lax.dynamic_slice_in_dim(row_lse, own_row * own_rows, own_rows, 0)
     own_col_lse = lax.dynamic_slice_in_dim(col_lse, lax.axis_index(blk) * own_rows, own_rows, 0)
+    image_own, text_own = lax.optimization_barrier((image_emb, text_emb))
     diag = logit_scale * jnp.sum(
-        image_emb.astype(jnp.float32) * text_emb.astype(jnp.float32), axis=1
+        image_own.astype(jnp.float32) * text_own.astype(jnp.float32), axis=1
     )
     row_loss = 0.5 * (own_row_lse + own_col_lse) - diag
     return (grad_image, grad_text, row_loss)

time: 218 us -> 224 us (1.028)
  starting transfers between devices: 120 us -> 128 us
  waiting for transfers between devices: 82.1 us -> 77.5 us
    ppermute x12 -> x15, starting transfers between devices: 70.3 us -> 83.9 us  [swap(): lax.ppermute(value, axis, [(i, i ^ step) for i in range(lax.axis_size(axi...]
    all_to_all x3 -> x2, starting transfers between devices: 30 us -> 19 us  [gather(): return lax.all_to_all(copies, axis, 0, 0)]
    all_to_all x3 -> x2, waiting for transfers between devices: 5.11 us -> 0.01 us  [gather(): return lax.all_to_all(copies, axis, 0, 0)]
    all_to_all x1, starting transfers between devices: 7.39 us -> 12.5 us  [lse_near(): lax.all_to_all(sent.reshape(-1, row.shape[0]), ('zl',) + chip, 0, 0)]
    all_to_all x1, waiting for transfers between devices: 7.45 us -> 9.86 us  [lse_near(): lax.all_to_all(sent.reshape(-1, row.shape[0]), ('zl',) + chip, 0, 0)]
    ppermute x12 -> x15, waiting for transfers between devices: 69.6 us -> 67.6 us  [swap(): lax.ppermute(value, axis, [(i, i ^ step) for i in range(lax.axis_size(axi...]
  transfers between devices with their start and end apart: 18 -> 20, of which waited for: 11 -> 10; matrix products, arithmetic and copies ran while one was open for 2% -> 3% of each run, Pallas kernels for 0% -> 0%
where the time goes in v9:
time: 224 us; the launch traced here: 223 us
  starting transfers between devices  128 us (57%)
  waiting for transfers between devices  77.5 us (35%)
  other arithmetic  6.53 us (3%)
  local copies, waits for them, and re-layouts  5.09 us (2%)
  matrix products  4.26 us (2%)
    ppermute x15, starting transfers between devices, swap(): lax.ppermute(value, axis, [(i, i ^ step) for i in range(lax.axis_size(axi...  83.9 us
    ppermute x15, waiting for transfers between devices, swap(): lax.ppermute(value, axis, [(i, i ^ step) for i in range(lax.axis_size(axi...  67.6 us
    all_to_all x2, starting transfers between devices, gather(): return lax.all_to_all(copies, axis, 0, 0)  19 us
    all_to_all x2, starting transfers between devices, scatter_sum(): lax.all_to_all(parts.astype(jnp.bfloat16), axis, 0, 0).astype(jnp.float32)  12.7 us
    all_to_all x1, starting transfers between devices, lse_near(): lax.all_to_all(sent.reshape(-1, row.shape[0]), ('zl',) + chip, 0, 0)  12.5 us
    all_to_all x1, waiting for transfers between devices, lse_near(): lax.all_to_all(sent.reshape(-1, row.shape[0]), ('zl',) + chip, 0, 0)  9.86 us
  transfers between devices with their start and end apart: 20, of which 10 were waited for; matrix products, arithmetic and copies ran while one was open for 3% of the time, Pallas kernels for 0%

profile of v9, /device:TPU:128, one launch (start us, length us, event | category | flops | bytes accessed | tf_op | source)
XLA Modules:
  0.0 222.6 jit_solution(11869465739453623528)
XLA Ops:
  2.1 14.7 %all-to-all-start.1 = ((bf16[8,16,1024]{2,1,0:T(8,128)(2,1)}), bf16[8,16,1024]{2,1,0:T(8,128)(2,1)S(1)}, u32[]{:S(2)}, u32[]{:S(2)}) async-start(bf16[8,16,1024]{2,1,0:T(8,128)(2,1)} %broadcast_in_dim.27), calls=%async_computation.1 | async-start | bytes 524288 | tf_op jit(solution)/shard_map/all_to_all | solution.py:19
  16.8 12.3 %collective-permute-start = (bf16[16,1024]{1,0:T(8,128)(2,1)}, bf16[16,1024]{1,0:T(8,128)(2,1)S(1)}, u32[]{:S(2)}, u32[]{:S(2)}) collective-permute-start(bf16[16,1024]{1,0:T(8,128)(2,1)} %param.2), channel_id=1, source_target_pairs={{0,8},{8,0},{16,24},{24,16},{1,9},{9,1},{17,25},{25,17},{2,10},{10... | collective-permute-start | bytes 98312 | tf_op jit(solution)/shard_map/ppermute | solution.py:23
  29.1 12.5 %collective-permute-done = bf16[16,1024]{1,0:T(8,128)(2,1)S(1)} collective-permute-done((bf16[16,1024]{1,0:T(8,128)(2,1)}, bf16[16,1024]{1,0:T(8,128)(2,1)S(1)}, u32[]{:S(2)}, u32[]{:S(2)}) %collective-permute-start) | collective-permute-done | bytes 32800 | tf_op jit(solution)/shard_map/ppermute | solution.py:23
  42.3 6.9 %collective-permute-start.1 = (bf16[2,16,1024]{2,1,0:T(8,128)(2,1)S(1)}, bf16[2,16,1024]{2,1,0:T(8,128)(2,1)S(1)}, u32[]{:S(2)}, u32[]{:S(2)}) collective-permute-start(bf16[2,16,1024]{2,1,0:T(8,128)(2,1)S(1)} %pad_maximum_fusion.2), channel_id=1, source_target_pairs={{0,24},{8,16},{16,8},{24,0},{1,25},{9,17},{17,9},{25,1},{2,26},{10... | collective-permute-start | bytes 196616 | tf_op jit(solution)/shard_map/ppermute | solution.py:23
  49.3 7.9 %collective-permute-done.1 = bf16[2,16,1024]{2,1,0:T(8,128)(2,1)S(1)} collective-permute-done((bf16[2,16,1024]{2,1,0:T(8,128)(2,1)S(1)}, bf16[2,16,1024]{2,1,0:T(8,128)(2,1)S(1)}, u32[]{:S(2)}, u32[]{:S(2)}) %collective-permute-start.1) | collective-permute-done | bytes 65568 | tf_op jit(solution)/shard_map/ppermute | solution.py:23
  58.4 4.3 %all-to-all-start = ((bf16[8,2,2,16,1024]{4,3,2,1,0:T(8,128)(2,1)}), bf16[8,2,2,16,1024]{4,3,2,1,0:T(8,128)(2,1)S(1)}, u32[]{:S(2)}, u32[]{:S(2)}) async-start(bf16[8,2,2,16,1024]{4,3,2,1,0:T(8,128)(2,1)} %broadcast_in_dim.26), calls=%async_computation | async-start | bytes 2097152 | tf_op jit(solution)/shard_map/all_to_all | solution.py:19
  62.7 4.9 %collective-permute-start.4 = (bf16[8,16,1024]{2,1,0:T(8,128)(2,1)S(1)}, bf16[8,16,1024]{2,1,0:T(8,128)(2,1)S(1)}, u32[]{:S(2)}, u32[]{:S(2)}) collective-permute-start(bf16[8,16,1024]{2,1,0:T(8,128)(2,1)S(1)} %all-to-all-done.1), channel_id=1, source_target_pairs={{0,768},{256,512},{512,256},{768,0},{1,769},{257,513},{513,257},{7... | collective-permute-start | bytes 786440 | tf_op jit(solution)/shard_map/ppermute | solution.py:23
  67.6 2.5 %collective-permute-start.3 = (bf16[8,16,1024]{2,1,0:T(8,128)(2,1)S(1)}, bf16[8,16,1024]{2,1,0:T(8,128)(2,1)S(1)}, u32[]{:S(2)}, u32[]{:S(2)}) collective-permute-start(bf16[8,16,1024]{2,1,0:T(8,128)(2,1)S(1)} %all-to-all-done.1), channel_id=1, source_target_pairs={{0,512},{256,768},{512,0},{768,256},{1,513},{257,769},{513,1},{769... | collective-permute-start | bytes 786440 | tf_op jit(solution)/shard_map/ppermute | solution.py:23
  70.2 2.4 %collective-permute-start.2 = (bf16[8,16,1024]{2,1,0:T(8,128)(2,1)S(1)}, bf16[8,16,1024]{2,1,0:T(8,128)(2,1)S(1)}, u32[]{:S(2)}, u32[]{:S(2)}) collective-permute-start(bf16[8,16,1024]{2,1,0:T(8,128)(2,1)S(1)} %all-to-all-done.1), channel_id=1, source_target_pairs={{0,256},{256,0},{512,768},{768,512},{1,257},{257,1},{513,769},{769... | collective-permute-start | bytes 786440 | tf_op jit(solution)/shard_map/ppermute | solution.py:23
  72.6 7.6 %collective-permute-done.4 = bf16[8,16,1024]{2,1,0:T(8,128)(2,1)S(1)} collective-permute-done((bf16[8,16,1024]{2,1,0:T(8,128)(2,1)S(1)}, bf16[8,16,1024]{2,1,0:T(8,128)(2,1)S(1)}, u32[]{:S(2)}, u32[]{:S(2)}) %collective-permute-start.4) | collective-permute-done | bytes 262176 | tf_op jit(solution)/shard_map/ppermute | solution.py:23
  80.2 2.5 %collective-permute-done.2 = bf16[8,16,1024]{2,1,0:T(8,128)(2,1)S(1)} collective-permute-done((bf16[8,16,1024]{2,1,0:T(8,128)(2,1)S(1)}, bf16[8,16,1024]{2,1,0:T(8,128)(2,1)S(1)}, u32[]{:S(2)}, u32[]{:S(2)}) %collective-permute-start.2) | collective-permute-done | bytes 262176 | tf_op jit(solution)/shard_map/ppermute | solution.py:23
  85.3 12.5 %all-to-all-start.2 = ((f32[64,1,512]{2,1,0:T(1,128)}), f32[64,1,512]{2,1,0:T(1,128)S(1)}, u32[]{:S(2)}, u32[]{:S(2)}) async-start(f32[64,1,512]{2,1,0:T(1,128)} %all_to_all.20), calls=%async_computation.2 | async-start | bytes 262144 | tf_op jit(solution)/shard_map/all_to_all | solution.py:79
  97.8 9.9 %all-to-all-done.2 = f32[64,1,512]{2,1,0:T(1,128)S(1)} async-done(((f32[64,1,512]{2,1,0:T(1,128)}), f32[64,1,512]{2,1,0:T(1,128)S(1)}, u32[]{:S(2)}, u32[]{:S(2)}) %all-to-all-start.2) | async-done | bytes 131104 | tf_op jit(solution)/shard_map/all_to_all | solution.py:79
  107.9 6.3 %collective-permute-start.5 = (f32[512]{0:T(512)S(1)}, f32[512]{0:T(512)S(1)}, u32[]{:S(2)}, u32[]{:S(2)}) collective-permute-start(f32[512]{0:T(512)S(1)} %log_add_fusion.4), channel_id=1, source_target_pairs={{0,8},{8,0},{16,24},{24,16},{1,9},{9,1},{17,25},{25,17},{2,10},{10... | collective-permute-start | bytes 6152 | tf_op jit(solution)/shard_map/ppermute | solution.py:23
  114.2 4.8 %collective-permute-start.9 = (f32[512]{0:T(512)S(1)}, f32[512]{0:T(512)S(1)}, u32[]{:S(2)}, u32[]{:S(2)}) collective-permute-start(f32[512]{0:T(512)S(1)} %log_add_fusion.1), channel_id=1, source_target_pairs={{0,768},{256,512},{512,256},{768,0},{1,769},{257,513},{513,257},{7... | collective-permute-start | bytes 6152 | tf_op jit(solution)/shard_map/ppermute | solution.py:23
  119.0 2.5 %collective-permute-start.8 = (f32[512]{0:T(512)S(1)}, f32[512]{0:T(512)S(1)}, u32[]{:S(2)}, u32[]{:S(2)}) collective-permute-start(f32[512]{0:T(512)S(1)} %log_add_fusion.1), channel_id=1, source_target_pairs={{0,512},{256,768},{512,0},{768,256},{1,513},{257,769},{513,1},{769... | collective-permute-start | bytes 6152 | tf_op jit(solution)/shard_map/ppermute | solution.py:23
  121.6 2.4 %collective-permute-start.7 = (f32[512]{0:T(512)S(1)}, f32[512]{0:T(512)S(1)}, u32[]{:S(2)}, u32[]{:S(2)}) collective-permute-start(f32[512]{0:T(512)S(1)} %log_add_fusion.1), channel_id=1, source_target_pairs={{0,256},{256,0},{512,768},{768,512},{1,257},{257,1},{513,769},{769... | collective-permute-start | bytes 6152 | tf_op jit(solution)/shard_map/ppermute | solution.py:23
  124.1 12.4 %collective-permute-start.6 = (f32[512]{0:T(512)S(1)}, f32[512]{0:T(512)S(1)}, u32[]{:S(2)}, u32[]{:S(2)}) collective-permute-start(f32[512]{0:T(512)S(1)} %log_add_fusion.3), channel_id=1, source_target_pairs={{0,24},{8,16},{16,8},{24,0},{1,25},{9,17},{17,9},{25,1},{2,26},{10... | collective-permute-start | bytes 6152 | tf_op jit(solution)/shard_map/ppermute | solution.py:23
  136.6 1.7 collective-permute-done.6
  140.4 1.7 convolution_convert_fusion.1
  142.0 3.6 %all-to-all-start.3 = ((bf16[8,4,16,1024]{3,2,1,0:T(8,128)(2,1)}), bf16[8,4,16,1024]{3,2,1,0:T(8,128)(2,1)S(1)}, u32[]{:S(2)}, u32[]{:S(2)}) async-start(bf16[8,4,16,1024]{3,2,1,0:T(8,128)(2,1)} %convolution_convert_fusion.1), calls=%async_computation.3 | async-start | bytes 2097152 | tf_op jit(solution)/shard_map/all_to_all | solution.py:34
  145.6 1.8 convolution_convert_fusion
  147.4 3.4 %collective-permute-start.12 = (bf16[8,16,1024]{2,1,0:T(8,128)(2,1)S(1)}, bf16[8,16,1024]{2,1,0:T(8,128)(2,1)S(1)}, u32[]{:S(2)}, u32[]{:S(2)}) collective-permute-start(bf16[8,16,1024]{2,1,0:T(8,128)(2,1)S(1)} %get-tuple-element.11), channel_id=1, source_target_pairs={{0,256},{256,0},{512,768},{768,512},{1,257},{257,1},{513,769},{769... | collective-permute-start | bytes 786440 | tf_op jit(solution)/shard_map/ppermute | solution.py:23
  150.9 4.1 %collective-permute-start.14 = (bf16[8,16,1024]{2,1,0:T(8,128)(2,1)S(1)}, bf16[8,16,1024]{2,1,0:T(8,128)(2,1)S(1)}, u32[]{:S(2)}, u32[]{:S(2)}) collective-permute-start(bf16[8,16,1024]{2,1,0:T(8,128)(2,1)S(1)} %get-tuple-element.12), channel_id=1, source_target_pairs={{0,768},{256,512},{512,256},{768,0},{1,769},{257,513},{513,257},{7... | collective-permute-start | bytes 786440 | tf_op jit(solution)/shard_map/ppermute | solution.py:23
  155.0 2.6 %collective-permute-start.13 = (bf16[8,16,1024]{2,1,0:T(8,128)(2,1)S(1)}, bf16[8,16,1024]{2,1,0:T(8,128)(2,1)}, u32[]{:S(2)}, u32[]{:S(2)}) collective-permute-start(bf16[8,16,1024]{2,1,0:T(8,128)(2,1)S(1)} %get-tuple-element.13), channel_id=1, source_target_pairs={{0,512},{256,768},{512,0},{768,256},{1,513},{257,769},{513,1},{769... | collective-permute-start | bytes 786440 | tf_op jit(solution)/shard_map/ppermute | solution.py:23
  158.0 10.0 %collective-permute-done.14 = bf16[8,16,1024]{2,1,0:T(8,128)(2,1)S(1)} collective-permute-done((bf16[8,16,1024]{2,1,0:T(8,128)(2,1)S(1)}, bf16[8,16,1024]{2,1,0:T(8,128)(2,1)S(1)}, u32[]{:S(2)}, u32[]{:S(2)}) %collective-permute-start.14) | collective-permute-done | bytes 262176 | tf_op jit(solution)/shard_map/ppermute | solution.py:23
  167.9 1.8 fusion.2
  169.8 9.2 %all-to-all-start.4 = ((bf16[8,16,1024]{2,1,0:T(8,128)(2,1)}), bf16[8,16,1024]{2,1,0:T(8,128)(2,1)S(1)}, u32[]{:S(2)}, u32[]{:S(2)}) async-start(bf16[8,16,1024]{2,1,0:T(8,128)(2,1)} %fusion.2), calls=%async_computation.4 | async-start | bytes 524288 | tf_op jit(solution)/shard_map/all_to_all | solution.py:34
  179.2 12.4 %collective-permute-start.10 = (bf16[2,16,1024]{2,1,0:T(8,128)(2,1)S(1)}, bf16[2,16,1024]{2,1,0:T(8,128)(2,1)S(1)}, u32[]{:S(2)}, u32[]{:S(2)}) collective-permute-start(bf16[2,16,1024]{2,1,0:T(8,128)(2,1)S(1)} %fusion.3), channel_id=1, source_target_pairs={{0,24},{8,16},{16,8},{24,0},{1,25},{9,17},{17,9},{25,1},{2,26},{10... | collective-permute-start | bytes 196616 | tf_op jit(solution)/shard_map/ppermute | solution.py:23
  191.8 14.9 %collective-permute-done.10 = bf16[2,16,1024]{2,1,0:T(8,128)(2,1)S(1)} collective-permute-done((bf16[2,16,1024]{2,1,0:T(8,128)(2,1)S(1)}, bf16[2,16,1024]{2,1,0:T(8,128)(2,1)S(1)}, u32[]{:S(2)}, u32[]{:S(2)}) %collective-permute-start.10) | collective-permute-done | bytes 65568 | tf_op jit(solution)/shard_map/ppermute | solution.py:23
  206.7 3.8 %collective-permute-start.11 = (bf16[16,1024]{1,0:T(8,128)(2,1)S(1)}, bf16[16,1024]{1,0:T(8,128)(2,1)S(1)}, u32[]{:S(2)}, u32[]{:S(2)}) collective-permute-start(bf16[16,1024]{1,0:T(8,128)(2,1)S(1)} %fusion.6), channel_id=1, source_target_pairs={{0,8},{8,0},{16,24},{24,16},{1,9},{9,1},{17,25},{25,17},{2,10},{10... | collective-permute-start | bytes 98312 | tf_op jit(solution)/shard_map/ppermute | solution.py:23
  211.1 10.1 %collective-permute-done.11 = bf16[16,1024]{1,0:T(8,128)(2,1)S(1)} collective-permute-done((bf16[16,1024]{1,0:T(8,128)(2,1)S(1)}, bf16[16,1024]{1,0:T(8,128)(2,1)S(1)}, u32[]{:S(2)}, u32[]{:S(2)}) %collective-permute-start.11) | collective-permute-done | bytes 32800 | tf_op jit(solution)/shard_map/ppermute | solution.py:23
  (58 shorter events, 11.0 us)
Async XLA Ops:
  2.1 55.2 %all-to-all-start.1 = ((bf16[8,16,1024]{2,1,0:T(8,128)(2,1)}), bf16[8,16,1024]{2,1,0:T(8,128)(2,1)S(1)}, u32[]{:S(2)}, u32[]{:S(2)}) async-start(bf16[8,16,1024]{2,1,0:T(8,128)(2,1)} %broadcast_in_dim.27), calls=%async_computation.1 | async-start | bytes 524288 | tf_op jit(solution)/shard_map/all_to_all | solution.py:19
  16.8 24.7 %collective-permute-start = (bf16[16,1024]{1,0:T(8,128)(2,1)}, bf16[16,1024]{1,0:T(8,128)(2,1)S(1)}, u32[]{:S(2)}, u32[]{:S(2)}) collective-permute-start(bf16[16,1024]{1,0:T(8,128)(2,1)} %param.2), channel_id=1, source_target_pairs={{0,8},{8,0},{16,24},{24,16},{1,9},{9,1},{17,25},{25,17},{2,10},{10... | collective-permute-start | bytes 98312 | tf_op jit(solution)/shard_map/ppermute | solution.py:23
  42.3 14.9 %collective-permute-start.1 = (bf16[2,16,1024]{2,1,0:T(8,128)(2,1)S(1)}, bf16[2,16,1024]{2,1,0:T(8,128)(2,1)S(1)}, u32[]{:S(2)}, u32[]{:S(2)}) collective-permute-start(bf16[2,16,1024]{2,1,0:T(8,128)(2,1)S(1)} %pad_maximum_fusion.2), channel_id=1, source_target_pairs={{0,24},{8,16},{16,8},{24,0},{1,25},{9,17},{17,9},{25,1},{2,26},{10... | collective-permute-start | bytes 196616 | tf_op jit(solution)/shard_map/ppermute | solution.py:23
  58.4 24.6 %all-to-all-start = ((bf16[8,2,2,16,1024]{4,3,2,1,0:T(8,128)(2,1)}), bf16[8,2,2,16,1024]{4,3,2,1,0:T(8,128)(2,1)S(1)}, u32[]{:S(2)}, u32[]{:S(2)}) async-start(bf16[8,2,2,16,1024]{4,3,2,1,0:T(8,128)(2,1)} %broadcast_in_dim.26), calls=%async_computation | async-start | bytes 2097152 | tf_op jit(solution)/shard_map/all_to_all | solution.py:19
  62.7 17.5 %collective-permute-start.4 = (bf16[8,16,1024]{2,1,0:T(8,128)(2,1)S(1)}, bf16[8,16,1024]{2,1,0:T(8,128)(2,1)S(1)}, u32[]{:S(2)}, u32[]{:S(2)}) collective-permute-start(bf16[8,16,1024]{2,1,0:T(8,128)(2,1)S(1)} %all-to-all-done.1), channel_id=1, source_target_pairs={{0,768},{256,512},{512,256},{768,0},{1,769},{257,513},{513,257},{7... | collective-permute-start | bytes 786440 | tf_op jit(solution)/shard_map/ppermute | solution.py:23
  67.6 12.6 %collective-permute-start.3 = (bf16[8,16,1024]{2,1,0:T(8,128)(2,1)S(1)}, bf16[8,16,1024]{2,1,0:T(8,128)(2,1)S(1)}, u32[]{:S(2)}, u32[]{:S(2)}) collective-permute-start(bf16[8,16,1024]{2,1,0:T(8,128)(2,1)S(1)} %all-to-all-done.1), channel_id=1, source_target_pairs={{0,512},{256,768},{512,0},{768,256},{1,513},{257,769},{513,1},{769... | collective-permute-start | bytes 786440 | tf_op jit(solution)/shard_map/ppermute | solution.py:23
  70.2 12.6 %collective-permute-start.2 = (bf16[8,16,1024]{2,1,0:T(8,128)(2,1)S(1)}, bf16[8,16,1024]{2,1,0:T(8,128)(2,1)S(1)}, u32[]{:S(2)}, u32[]{:S(2)}) collective-permute-start(bf16[8,16,1024]{2,1,0:T(8,128)(2,1)S(1)} %all-to-all-done.1), channel_id=1, source_target_pairs={{0,256},{256,0},{512,768},{768,512},{1,257},{257,1},{513,769},{769... | collective-permute-start | bytes 786440 | tf_op jit(solution)/shard_map/ppermute | solution.py:23
  83.0 1.0 copy-start
  85.3 22.4 %all-to-all-start.2 = ((f32[64,1,512]{2,1,0:T(1,128)}), f32[64,1,512]{2,1,0:T(1,128)S(1)}, u32[]{:S(2)}, u32[]{:S(2)}) async-start(f32[64,1,512]{2,1,0:T(1,128)} %all_to_all.20), calls=%async_computation.2 | async-start | bytes 262144 | tf_op jit(solution)/shard_map/all_to_all | solution.py:79
  107.9 16.1 %collective-permute-start.5 = (f32[512]{0:T(512)S(1)}, f32[512]{0:T(512)S(1)}, u32[]{:S(2)}, u32[]{:S(2)}) collective-permute-start(f32[512]{0:T(512)S(1)} %log_add_fusion.4), channel_id=1, source_target_pairs={{0,8},{8,0},{16,24},{24,16},{1,9},{9,1},{17,25},{25,17},{2,10},{10... | collective-permute-start | bytes 6152 | tf_op jit(solution)/shard_map/ppermute | solution.py:23
  114.2 22.3 %collective-permute-start.9 = (f32[512]{0:T(512)S(1)}, f32[512]{0:T(512)S(1)}, u32[]{:S(2)}, u32[]{:S(2)}) collective-permute-start(f32[512]{0:T(512)S(1)} %log_add_fusion.1), channel_id=1, source_target_pairs={{0,768},{256,512},{512,256},{768,0},{1,769},{257,513},{513,257},{7... | collective-permute-start | bytes 6152 | tf_op jit(solution)/shard_map/ppermute | solution.py:23
  119.0 17.5 %collective-permute-start.8 = (f32[512]{0:T(512)S(1)}, f32[512]{0:T(512)S(1)}, u32[]{:S(2)}, u32[]{:S(2)}) collective-permute-start(f32[512]{0:T(512)S(1)} %log_add_fusion.1), channel_id=1, source_target_pairs={{0,512},{256,768},{512,0},{768,256},{1,513},{257,769},{513,1},{769... | collective-permute-start | bytes 6152 | tf_op jit(solution)/shard_map/ppermute | solution.py:23
  121.6 14.9 %collective-permute-start.7 = (f32[512]{0:T(512)S(1)}, f32[512]{0:T(512)S(1)}, u32[]{:S(2)}, u32[]{:S(2)}) collective-permute-start(f32[512]{0:T(512)S(1)} %log_add_fusion.1), channel_id=1, source_target_pairs={{0,256},{256,0},{512,768},{768,512},{1,257},{257,1},{513,769},{769... | collective-permute-start | bytes 6152 | tf_op jit(solution)/shard_map/ppermute | solution.py:23
  124.1 14.2 %collective-permute-start.6 = (f32[512]{0:T(512)S(1)}, f32[512]{0:T(512)S(1)}, u32[]{:S(2)}, u32[]{:S(2)}) collective-permute-start(f32[512]{0:T(512)S(1)} %log_add_fusion.3), channel_id=1, source_target_pairs={{0,24},{8,16},{16,8},{24,0},{1,25},{9,17},{17,9},{25,1},{2,26},{10... | collective-permute-start | bytes 6152 | tf_op jit(solution)/shard_map/ppermute | solution.py:23
  138.9 1.4 copy-start.1
  142.0 27.7 %all-to-all-start.3 = ((bf16[8,4,16,1024]{3,2,1,0:T(8,128)(2,1)}), bf16[8,4,16,1024]{3,2,1,0:T(8,128)(2,1)S(1)}, u32[]{:S(2)}, u32[]{:S(2)}) async-start(bf16[8,4,16,1024]{3,2,1,0:T(8,128)(2,1)} %convolution_convert_fusion.1), calls=%async_computation.3 | async-start | bytes 2097152 | tf_op jit(solution)/shard_map/all_to_all | solution.py:34
  147.4 10.5 %collective-permute-start.12 = (bf16[8,16,1024]{2,1,0:T(8,128)(2,1)S(1)}, bf16[8,16,1024]{2,1,0:T(8,128)(2,1)S(1)}, u32[]{:S(2)}, u32[]{:S(2)}) collective-permute-start(bf16[8,16,1024]{2,1,0:T(8,128)(2,1)S(1)} %get-tuple-element.11), channel_id=1, source_target_pairs={{0,256},{256,0},{512,768},{768,512},{1,257},{257,1},{513,769},{769... | collective-permute-start | bytes 786440 | tf_op jit(solution)/shard_map/ppermute | solution.py:23
  150.9 17.1 %collective-permute-start.14 = (bf16[8,16,1024]{2,1,0:T(8,128)(2,1)S(1)}, bf16[8,16,1024]{2,1,0:T(8,128)(2,1)S(1)}, u32[]{:S(2)}, u32[]{:S(2)}) collective-permute-start(bf16[8,16,1024]{2,1,0:T(8,128)(2,1)S(1)} %get-tuple-element.12), channel_id=1, source_target_pairs={{0,768},{256,512},{512,256},{768,0},{1,769},{257,513},{513,257},{7... | collective-permute-start | bytes 786440 | tf_op jit(solution)/shard_map/ppermute | solution.py:23
  155.0 13.0 %collective-permute-start.13 = (bf16[8,16,1024]{2,1,0:T(8,128)(2,1)S(1)}, bf16[8,16,1024]{2,1,0:T(8,128)(2,1)}, u32[]{:S(2)}, u32[]{:S(2)}) collective-permute-start(bf16[8,16,1024]{2,1,0:T(8,128)(2,1)S(1)} %get-tuple-element.13), channel_id=1, source_target_pairs={{0,512},{256,768},{512,0},{768,256},{1,513},{257,769},{513,1},{769... | collective-permute-start | bytes 786440 | tf_op jit(solution)/shard_map/ppermute | solution.py:23
  169.8 21.8 %copy-start.2 = (bf16[16,1024]{1,0:T(8,128)(2,1)S(1)}, bf16[16,1024]{1,0:T(8,128)(2,1)}, u32[]{:S(2)}) copy-start(bf16[16,1024]{1,0:T(8,128)(2,1)} %param.3) | copy-start | bytes 98308
  169.8 21.9 %copy-start.3 = (bf16[16,1024]{1,0:T(8,128)(2,1)S(1)}, bf16[16,1024]{1,0:T(8,128)(2,1)}, u32[]{:S(2)}) copy-start(bf16[16,1024]{1,0:T(8,128)(2,1)} %param.2) | copy-start | bytes 98308
  169.8 52.1 %all-to-all-start.4 = ((bf16[8,16,1024]{2,1,0:T(8,128)(2,1)}), bf16[8,16,1024]{2,1,0:T(8,128)(2,1)S(1)}, u32[]{:S(2)}, u32[]{:S(2)}) async-start(bf16[8,16,1024]{2,1,0:T(8,128)(2,1)} %fusion.2), calls=%async_computation.4 | async-start | bytes 524288 | tf_op jit(solution)/shard_map/all_to_all | solution.py:34
  179.2 27.5 %collective-permute-start.10 = (bf16[2,16,1024]{2,1,0:T(8,128)(2,1)S(1)}, bf16[2,16,1024]{2,1,0:T(8,128)(2,1)S(1)}, u32[]{:S(2)}, u32[]{:S(2)}) collective-permute-start(bf16[2,16,1024]{2,1,0:T(8,128)(2,1)S(1)} %fusion.3), channel_id=1, source_target_pairs={{0,24},{8,16},{16,8},{24,0},{1,25},{9,17},{17,9},{25,1},{2,26},{10... | collective-permute-start | bytes 196616 | tf_op jit(solution)/shard_map/ppermute | solution.py:23
  206.7 14.5 %collective-permute-start.11 = (bf16[16,1024]{1,0:T(8,128)(2,1)S(1)}, bf16[16,1024]{1,0:T(8,128)(2,1)S(1)}, u32[]{:S(2)}, u32[]{:S(2)}) collective-permute-start(bf16[16,1024]{1,0:T(8,128)(2,1)S(1)} %fusion.6), channel_id=1, source_target_pairs={{0,8},{8,0},{16,24},{24,16},{1,9},{9,1},{17,25},{25,17},{2,10},{10... | collective-permute-start | bytes 98312 | tf_op jit(solution)/shard_map/ppermute | solution.py:23

commit v10 on v7

--- a/solution.py
+++ b/solution.py
@@ -43,22 +43,41 @@
     return sum(part.astype(jnp.float32) for part in came)
 
 
+def gather_ring(rows):
+    me, half = lax.axis_index("zh"), rows.shape[-1] // 2
+    first = gather_by_doubling(rows[:, :half], "zh", me, ring)
+    second = gather_by_doubling(rows[:, half:], "zh", me ^ (me >> 1), ring[::-1])
+    first = first.reshape((-1,) + first.shape[2:])
+    second = jnp.stack([second[0, 0], second[1, 0], second[1, 1], second[0, 1]])
+    return jnp.concatenate([first, second], axis=-1)
+
+
+def scatter_sum_ring(parts):
+    me, half = lax.axis_index("zh"), parts.shape[-1] // 2
+    first, second = parts[:, :, :half], parts[:, :, half:]
+    first = jnp.stack([jnp.stack([first[0], first[1]]), jnp.stack([first[2], first[3]])])
+    second = jnp.stack([jnp.stack([second[0], second[3]]), jnp.stack([second[1], second[2]])])
+    first = scatter_sum_by_halving(first, "zh", me, ring)
+    second = scatter_sum_by_halving(second, "zh", me ^ (me >> 1), ring[::-1])
+    return jnp.concatenate([first, second], axis=-1)
+
+
 def lse(values, dim):
     top = jnp.max(values, axis=dim, keepdims=True)
     return jnp.squeeze(top, dim) + jnp.log(jnp.sum(jnp.exp(values - top), axis=dim))
 
 
-def gather_by_doubling(rows, axis, steps):
+def gather_by_doubling(rows, axis, code, steps):
     for step, bit in steps:
         other = swap(rows, axis, step)
-        upper = (lax.axis_index(axis) & bit) != 0
+        upper = (code & bit) != 0
         rows = jnp.stack([jnp.where(upper, other, rows), jnp.where(upper, rows, other)])
     return rows
 
 
-def scatter_sum_by_halving(parts, axis, steps):
+def scatter_sum_by_halving(parts, axis, code, steps):
     for step, bit in reversed(steps):
-        upper = jnp.where((lax.axis_index(axis) & bit) != 0, 1, 0)
+        upper = jnp.where((code & bit) != 0, 1, 0)
         given = lax.dynamic_index_in_dim(parts, 1 - upper, 0, False).astype(jnp.bfloat16)
         given = swap(given, axis, step).astype(jnp.float32)
         parts = lax.dynamic_index_in_dim(parts, upper, 0, False) + given
@@ -92,7 +111,7 @@
 
 def body(image_emb, text_emb):
     own_rows, width = image_emb.shape
-    img_rows = gather(gather_by_doubling(image_emb, "zh", ring), chip)
+    img_rows = gather(gather_ring(image_emb), chip)
     txt_cols = gather_by_swaps(gather(text_emb, "zl"), "y")
     img_rows = img_rows.reshape(img_rows.shape[0], -1, own_rows, width)
     row_lanes, col_lanes = img_rows.shape[:-1], txt_cols.shape[:-1]
@@ -108,16 +127,16 @@
         weights, img_rows, (((0,), (0,)), ((), ())), preferred_element_type=jnp.float32
     )
     text_part = text_part.reshape(col_lanes + (width,))
-    image_sum = scatter_sum(image_part, chip).reshape(2, 2, own_rows, width)
-    image_sum = scatter_sum_by_halving(image_sum, "zh", ring)
+    image_sum = scatter_sum_ring(scatter_sum(image_part, chip))
     text_sum = scatter_sum(scatter_sum_by_swaps(text_part, "y"), "zl")
     grad_image = logit_scale * image_sum - logit_scale * text_emb.astype(jnp.float32)
     grad_text = logit_scale * text_sum - logit_scale * image_emb.astype(jnp.float32)
     own_row = lax.axis_index(chip) * row_lanes[1] + lax.axis_index("zh")
     own_row_lse = lax.dynamic_slice_in_dim(row_lse, own_row * own_rows, own_rows, 0)
     own_col_lse = lax.dynamic_slice_in_dim(col_lse, lax.axis_index(blk) * own_rows, own_rows, 0)
+    image_own, text_own = lax.optimization_barrier((image_emb, text_emb))
     diag = logit_scale * jnp.sum(
-        image_emb.astype(jnp.float32) * text_emb.astype(jnp.float32), axis=1
+        image_own.astype(jnp.float32) * text_own.astype(jnp.float32), axis=1
     )
     row_loss = 0.5 * (own_row_lse + own_col_lse) - diag
     return (grad_image, grad_text, row_loss)

time: 218 us -> 235 us (1.078)
  starting transfers between devices: 120 us -> 149 us
  waiting for transfers between devices: 82.1 us -> 65.6 us
    ppermute x12 -> x16, starting transfers between devices: 70.3 us -> 100 us  [swap(): lax.ppermute(value, axis, [(i, i ^ step) for i in range(lax.axis_size(axi...]
    ppermute x12 -> x16, waiting for transfers between devices: 69.6 us -> 53.1 us  [swap(): lax.ppermute(value, axis, [(i, i ^ step) for i in range(lax.axis_size(axi...]
  transfers between devices with their start and end apart: 18 -> 22, of which waited for: 11 -> 14; matrix products, arithmetic and copies ran while one was open for 2% -> 4% of each run, Pallas kernels for 0% -> 0%
where the time goes in v10:
time: 235 us; the launch traced here: 234 us
  starting transfers between devices  149 us (63%)
  waiting for transfers between devices  65.6 us (28%)
  local copies, waits for them, and re-layouts  7.11 us (3%)
  other arithmetic  6.67 us (3%)
  matrix products  4.26 us (2%)
    ppermute x16, starting transfers between devices, swap(): lax.ppermute(value, axis, [(i, i ^ step) for i in range(lax.axis_size(axi...  100 us
    ppermute x16, waiting for transfers between devices, swap(): lax.ppermute(value, axis, [(i, i ^ step) for i in range(lax.axis_size(axi...  53.1 us
    all_to_all x3, starting transfers between devices, gather(): return lax.all_to_all(copies, axis, 0, 0)  28.8 us
    all_to_all x2, starting transfers between devices, scatter_sum(): lax.all_to_all(parts.astype(jnp.bfloat16), axis, 0, 0).astype(jnp.float32)  12.3 us
    all_to_all x1, waiting for transfers between devices, lse_near(): lax.all_to_all(sent.reshape(-1, row.shape[0]), ('y',) + chip, 0, 0)  7.45 us
    all_to_all x1, starting transfers between devices, lse_near(): lax.all_to_all(sent.reshape(-1, row.shape[0]), ('y',) + chip, 0, 0)  7.4 us
    all_to_all x3, waiting for transfers between devices, gather(): return lax.all_to_all(copies, axis, 0, 0)  5.11 us
  transfers between devices with their start and end apart: 22, of which 14 were waited for; matrix products, arithmetic and copies ran while one was open for 4% of the time, Pallas kernels for 0%

profile of v10, /device:TPU:128, one launch (start us, length us, event | category | flops | bytes accessed | tf_op | source)
XLA Modules:
  0.0 233.5 jit_solution(8470458691959176277)
XLA Ops:
  2.1 14.7 %all-to-all-start.1 = ((bf16[8,16,1024]{2,1,0:T(8,128)(2,1)}), bf16[8,16,1024]{2,1,0:T(8,128)(2,1)S(1)}, u32[]{:S(2)}, u32[]{:S(2)}) async-start(bf16[8,16,1024]{2,1,0:T(8,128)(2,1)} %broadcast_in_dim.33), calls=%async_computation.1 | async-start | bytes 524288 | tf_op jit(solution)/shard_map/all_to_all | solution.py:19
  17.6 12.3 %collective-permute-start = (bf16[16,512]{1,0:T(8,128)(2,1)S(1)}, bf16[16,512]{1,0:T(8,128)(2,1)S(1)}, u32[]{:S(2)}, u32[]{:S(2)}) collective-permute-start(bf16[16,512]{1,0:T(8,128)(2,1)S(1)} %get-tuple-element.37), channel_id=1, source_target_pairs={{0,8},{8,0},{16,24},{24,16},{1,9},{9,1},{17,25},{25,17},{2,10},{10... | collective-permute-start | bytes 49160 | tf_op jit(solution)/shard_map/ppermute | solution.py:23
  29.8 8.2 %collective-permute-start.2 = (bf16[16,512]{1,0:T(8,128)(2,1)S(1)}, bf16[16,512]{1,0:T(8,128)(2,1)S(1)}, u32[]{:S(2)}, u32[]{:S(2)}) collective-permute-start(bf16[16,512]{1,0:T(8,128)(2,1)S(1)} %get-tuple-element.38), channel_id=1, source_target_pairs={{0,24},{8,16},{16,8},{24,0},{1,25},{9,17},{17,9},{25,1},{2,26},{10... | collective-permute-start | bytes 49160 | tf_op jit(solution)/shard_map/ppermute | solution.py:23
  38.1 3.3 %collective-permute-done = bf16[16,512]{1,0:T(8,128)(2,1)S(1)} collective-permute-done((bf16[16,512]{1,0:T(8,128)(2,1)S(1)}, bf16[16,512]{1,0:T(8,128)(2,1)S(1)}, u32[]{:S(2)}, u32[]{:S(2)}) %collective-permute-start) | collective-permute-done | bytes 16416 | tf_op jit(solution)/shard_map/ppermute | solution.py:23
  41.4 3.3 %collective-permute-done.2 = bf16[16,512]{1,0:T(8,128)(2,1)S(1)} collective-permute-done((bf16[16,512]{1,0:T(8,128)(2,1)S(1)}, bf16[16,512]{1,0:T(8,128)(2,1)S(1)}, u32[]{:S(2)}, u32[]{:S(2)}) %collective-permute-start.2) | collective-permute-done | bytes 16416 | tf_op jit(solution)/shard_map/ppermute | solution.py:23
  45.5 3.9 %collective-permute-start.3 = (bf16[2,16,512]{2,1,0:T(8,128)(2,1)S(1)}, bf16[2,16,512]{2,1,0:T(8,128)(2,1)S(1)}, u32[]{:S(2)}, u32[]{:S(2)}) collective-permute-start(bf16[2,16,512]{2,1,0:T(8,128)(2,1)S(1)} %pad_maximum_fusion.3), channel_id=1, source_target_pairs={{0,8},{8,0},{16,24},{24,16},{1,9},{9,1},{17,25},{25,17},{2,10},{10... | collective-permute-start | bytes 98312 | tf_op jit(solution)/shard_map/ppermute | solution.py:23
  49.3 10.5 %collective-permute-start.1 = (bf16[2,16,512]{2,1,0:T(8,128)(2,1)S(1)}, bf16[2,16,512]{2,1,0:T(8,128)(2,1)S(1)}, u32[]{:S(2)}, u32[]{:S(2)}) collective-permute-start(bf16[2,16,512]{2,1,0:T(8,128)(2,1)S(1)} %pad_maximum_fusion.2), channel_id=1, source_target_pairs={{0,24},{8,16},{16,8},{24,0},{1,25},{9,17},{17,9},{25,1},{2,26},{10... | collective-permute-start | bytes 98312 | tf_op jit(solution)/shard_map/ppermute | solution.py:23
  60.0 5.0 %collective-permute-done.1 = bf16[2,16,512]{2,1,0:T(8,128)(2,1)S(1)} collective-permute-done((bf16[2,16,512]{2,1,0:T(8,128)(2,1)S(1)}, bf16[2,16,512]{2,1,0:T(8,128)(2,1)S(1)}, u32[]{:S(2)}, u32[]{:S(2)}) %collective-permute-start.1) | collective-permute-done | bytes 32800 | tf_op jit(solution)/shard_map/ppermute | solution.py:23
  66.3 3.9 %all-to-all-start = ((bf16[8,4,16,1024]{3,2,1,0:T(8,128)(2,1)}), bf16[8,4,16,1024]{3,2,1,0:T(8,128)(2,1)S(1)}, u32[]{:S(2)}, u32[]{:S(2)}) async-start(bf16[8,4,16,1024]{3,2,1,0:T(8,128)(2,1)} %broadcast_in_dim.28), calls=%async_computation | async-start | bytes 2097152 | tf_op jit(solution)/shard_map/all_to_all | solution.py:19
  70.2 4.9 %collective-permute-start.6 = (bf16[8,16,1024]{2,1,0:T(8,128)(2,1)S(1)}, bf16[8,16,1024]{2,1,0:T(8,128)(2,1)S(1)}, u32[]{:S(2)}, u32[]{:S(2)}) collective-permute-start(bf16[8,16,1024]{2,1,0:T(8,128)(2,1)S(1)} %all-to-all-done.1), channel_id=1, source_target_pairs={{0,768},{256,512},{512,256},{768,0},{1,769},{257,513},{513,257},{7... | collective-permute-start | bytes 786440 | tf_op jit(solution)/shard_map/ppermute | solution.py:23
  75.1 2.5 %collective-permute-start.5 = (bf16[8,16,1024]{2,1,0:T(8,128)(2,1)S(1)}, bf16[8,16,1024]{2,1,0:T(8,128)(2,1)S(1)}, u32[]{:S(2)}, u32[]{:S(2)}) collective-permute-start(bf16[8,16,1024]{2,1,0:T(8,128)(2,1)S(1)} %all-to-all-done.1), channel_id=1, source_target_pairs={{0,512},{256,768},{512,0},{768,256},{1,513},{257,769},{513,1},{769... | collective-permute-start | bytes 786440 | tf_op jit(solution)/shard_map/ppermute | solution.py:23
  80.1 7.6 %collective-permute-done.6 = bf16[8,16,1024]{2,1,0:T(8,128)(2,1)S(1)} collective-permute-done((bf16[8,16,1024]{2,1,0:T(8,128)(2,1)S(1)}, bf16[8,16,1024]{2,1,0:T(8,128)(2,1)S(1)}, u32[]{:S(2)}, u32[]{:S(2)}) %collective-permute-start.6) | collective-permute-done | bytes 262176 | tf_op jit(solution)/shard_map/ppermute | solution.py:23
  87.7 2.5 %collective-permute-done.4 = bf16[8,16,1024]{2,1,0:T(8,128)(2,1)S(1)} collective-permute-done((bf16[8,16,1024]{2,1,0:T(8,128)(2,1)S(1)}, bf16[8,16,1024]{2,1,0:T(8,128)(2,1)S(1)}, u32[]{:S(2)}, u32[]{:S(2)}) %collective-permute-start.4) | collective-permute-done | bytes 262176 | tf_op jit(solution)/shard_map/ppermute | solution.py:23
  92.7 7.4 %all-to-all-start.2 = ((f32[32,1,512]{2,1,0:T(1,128)}), f32[32,1,512]{2,1,0:T(1,128)S(1)}, u32[]{:S(2)}, u32[]{:S(2)}) async-start(f32[32,1,512]{2,1,0:T(1,128)} %all_to_all.26), calls=%async_computation.2 | async-start | bytes 131072 | tf_op jit(solution)/shard_map/all_to_all | solution.py:98
  100.1 7.5 %all-to-all-done.2 = f32[32,1,512]{2,1,0:T(1,128)S(1)} async-done(((f32[32,1,512]{2,1,0:T(1,128)}), f32[32,1,512]{2,1,0:T(1,128)S(1)}, u32[]{:S(2)}, u32[]{:S(2)}) %all-to-all-start.2) | async-done | bytes 65568 | tf_op jit(solution)/shard_map/all_to_all | solution.py:98
  107.8 10.2 %collective-permute-start.7 = (f32[512]{0:T(512)S(1)}, f32[512]{0:T(512)S(1)}, u32[]{:S(2)}, u32[]{:S(2)}) collective-permute-start(f32[512]{0:T(512)S(1)} %log_add_fusion.4), channel_id=1, source_target_pairs={{0,8},{8,0},{16,24},{24,16},{1,9},{9,1},{17,25},{25,17},{2,10},{10... | collective-permute-start | bytes 6152 | tf_op jit(solution)/shard_map/ppermute | solution.py:23
  118.7 10.1 %all-to-all-start.3 = ((f32[8,1,512]{2,1,0:T(1,128)}), f32[8,1,512]{2,1,0:T(1,128)S(1)}, u32[]{:S(2)}, u32[]{:S(2)}) async-start(f32[8,1,512]{2,1,0:T(1,128)} %broadcast_in_dim.38), calls=%async_computation.3 | async-start | bytes 32768 | tf_op jit(solution)/shard_map/all_to_all | solution.py:19
  128.8 5.1 %all-to-all-done.3 = f32[8,1,512]{2,1,0:T(1,128)S(1)} async-done(((f32[8,1,512]{2,1,0:T(1,128)}), f32[8,1,512]{2,1,0:T(1,128)S(1)}, u32[]{:S(2)}, u32[]{:S(2)}) %all-to-all-start.3) | async-done | bytes 16416 | tf_op jit(solution)/shard_map/all_to_all | solution.py:19
  133.9 9.3 %collective-permute-start.8 = (f32[512]{0:T(512)S(1)}, f32[512]{0:T(512)S(1)}, u32[]{:S(2)}, u32[]{:S(2)}) collective-permute-start(f32[512]{0:T(512)S(1)} %log_add_fusion.3), channel_id=1, source_target_pairs={{0,24},{8,16},{16,8},{24,0},{1,25},{9,17},{17,9},{25,1},{2,26},{10... | collective-permute-start | bytes 6152 | tf_op jit(solution)/shard_map/ppermute | solution.py:23
  143.2 4.9 %collective-permute-done.8 = f32[512]{0:T(512)S(1)} collective-permute-done((f32[512]{0:T(512)S(1)}, f32[512]{0:T(512)S(1)}, u32[]{:S(2)}, u32[]{:S(2)}) %collective-permute-start.8) | collective-permute-done | bytes 2080 | tf_op jit(solution)/shard_map/ppermute | solution.py:23
  151.9 3.6 %all-to-all-start.4 = ((bf16[8,4,16,1024]{3,2,1,0:T(8,128)(2,1)}), bf16[8,4,16,1024]{3,2,1,0:T(8,128)(2,1)S(1)}, u32[]{:S(2)}, u32[]{:S(2)}) async-start(bf16[8,4,16,1024]{3,2,1,0:T(8,128)(2,1)} %convolution_convert_fusion.1), calls=%async_computation.4 | async-start | bytes 2097152 | tf_op jit(solution)/shard_map/all_to_all | solution.py:34
  158.1 2.5 %collective-permute-start.13 = (bf16[8,16,1024]{2,1,0:T(8,128)(2,1)}, bf16[8,16,1024]{2,1,0:T(8,128)(2,1)S(1)}, u32[]{:S(2)}, u32[]{:S(2)}) collective-permute-start(bf16[8,16,1024]{2,1,0:T(8,128)(2,1)} %get-tuple-element.15), channel_id=1, source_target_pairs={{0,256},{256,0},{512,768},{768,512},{1,257},{257,1},{513,769},{769... | collective-permute-start | bytes 786440 | tf_op jit(solution)/shard_map/ppermute | solution.py:23
  160.6 3.1 %collective-permute-start.15 = (bf16[8,16,1024]{2,1,0:T(8,128)(2,1)S(1)}, bf16[8,16,1024]{2,1,0:T(8,128)(2,1)S(1)}, u32[]{:S(2)}, u32[]{:S(2)}) collective-permute-start(bf16[8,16,1024]{2,1,0:T(8,128)(2,1)S(1)} %get-tuple-element.16), channel_id=1, source_target_pairs={{0,768},{256,512},{512,256},{768,0},{1,769},{257,513},{513,257},{7... | collective-permute-start | bytes 786440 | tf_op jit(solution)/shard_map/ppermute | solution.py:23
  163.7 4.2 %collective-permute-start.14 = (bf16[8,16,1024]{2,1,0:T(8,128)(2,1)S(1)}, bf16[8,16,1024]{2,1,0:T(8,128)(2,1)}, u32[]{:S(2)}, u32[]{:S(2)}) collective-permute-start(bf16[8,16,1024]{2,1,0:T(8,128)(2,1)S(1)} %get-tuple-element.17), channel_id=1, source_target_pairs={{0,512},{256,768},{512,0},{768,256},{1,513},{257,769},{513,1},{769... | collective-permute-start | bytes 786440 | tf_op jit(solution)/shard_map/ppermute | solution.py:23
  168.8 8.9 %collective-permute-done.15 = bf16[8,16,1024]{2,1,0:T(8,128)(2,1)S(1)} collective-permute-done((bf16[8,16,1024]{2,1,0:T(8,128)(2,1)S(1)}, bf16[8,16,1024]{2,1,0:T(8,128)(2,1)S(1)}, u32[]{:S(2)}, u32[]{:S(2)}) %collective-permute-start.15) | collective-permute-done | bytes 262176 | tf_op jit(solution)/shard_map/ppermute | solution.py:23
  179.5 8.7 %all-to-all-start.5 = ((bf16[8,16,1024]{2,1,0:T(8,128)(2,1)}), bf16[8,16,1024]{2,1,0:T(8,128)(2,1)S(1)}, u32[]{:S(2)}, u32[]{:S(2)}) async-start(bf16[8,16,1024]{2,1,0:T(8,128)(2,1)} %fusion.2), calls=%async_computation.5 | async-start | bytes 524288 | tf_op jit(solution)/shard_map/all_to_all | solution.py:34
  188.5 9.3 %collective-permute-start.9 = (bf16[2,16,512]{2,1,0:T(8,128)(2,1)S(1)}, bf16[2,16,512]{2,1,0:T(8,128)(2,1)S(1)}, u32[]{:S(2)}, u32[]{:S(2)}) collective-permute-start(bf16[2,16,512]{2,1,0:T(8,128)(2,1)S(1)} %fusion.14), channel_id=1, source_target_pairs={{0,24},{8,16},{16,8},{24,0},{1,25},{9,17},{17,9},{25,1},{2,26},{10... | collective-permute-start | bytes 98312 | tf_op jit(solution)/shard_map/ppermute | solution.py:23
  197.8 5.1 %collective-permute-start.11 = (bf16[2,16,512]{2,1,0:T(8,128)(2,1)S(1)}, bf16[2,16,512]{2,1,0:T(8,128)(2,1)S(1)}, u32[]{:S(2)}, u32[]{:S(2)}) collective-permute-start(bf16[2,16,512]{2,1,0:T(8,128)(2,1)S(1)} %fusion.15), channel_id=1, source_target_pairs={{0,8},{8,0},{16,24},{24,16},{1,9},{9,1},{17,25},{25,17},{2,10},{10... | collective-permute-start | bytes 98312 | tf_op jit(solution)/shard_map/ppermute | solution.py:23
  202.9 5.6 %collective-permute-done.9 = bf16[2,16,512]{2,1,0:T(8,128)(2,1)S(1)} collective-permute-done((bf16[2,16,512]{2,1,0:T(8,128)(2,1)S(1)}, bf16[2,16,512]{2,1,0:T(8,128)(2,1)S(1)}, u32[]{:S(2)}, u32[]{:S(2)}) %collective-permute-start.9) | collective-permute-done | bytes 32800 | tf_op jit(solution)/shard_map/ppermute | solution.py:23
  208.6 9.2 %collective-permute-start.10 = (bf16[16,512]{1,0:T(8,128)(2,1)S(1)}, bf16[16,512]{1,0:T(8,128)(2,1)S(1)}, u32[]{:S(2)}, u32[]{:S(2)}) collective-permute-start(bf16[16,512]{1,0:T(8,128)(2,1)S(1)} %fusion.16), channel_id=1, source_target_pairs={{0,8},{8,0},{16,24},{24,16},{1,9},{9,1},{17,25},{25,17},{2,10},{10... | collective-permute-start | bytes 49160 | tf_op jit(solution)/shard_map/ppermute | solution.py:23
  217.8 2.8 %collective-permute-start.12 = (bf16[16,512]{1,0:T(8,128)(2,1)S(1)}, bf16[16,512]{1,0:T(8,128)(2,1)S(1)}, u32[]{:S(2)}, u32[]{:S(2)}) collective-permute-start(bf16[16,512]{1,0:T(8,128)(2,1)S(1)} %fusion.17), channel_id=1, source_target_pairs={{0,24},{8,16},{16,8},{24,0},{1,25},{9,17},{17,9},{25,1},{2,26},{10... | collective-permute-start | bytes 49160 | tf_op jit(solution)/shard_map/ppermute | solution.py:23
  222.9 9.3 %collective-permute-done.12 = bf16[16,512]{1,0:T(8,128)(2,1)S(1)} collective-permute-done((bf16[16,512]{1,0:T(8,128)(2,1)S(1)}, bf16[16,512]{1,0:T(8,128)(2,1)S(1)}, u32[]{:S(2)}, u32[]{:S(2)}) %collective-permute-start.12) | collective-permute-done | bytes 16416 | tf_op jit(solution)/shard_map/ppermute | solution.py:23
  (80 shorter events, 23.0 us)
Async XLA Ops:
  2.1 63.0 %all-to-all-start.1 = ((bf16[8,16,1024]{2,1,0:T(8,128)(2,1)}), bf16[8,16,1024]{2,1,0:T(8,128)(2,1)S(1)}, u32[]{:S(2)}, u32[]{:S(2)}) async-start(bf16[8,16,1024]{2,1,0:T(8,128)(2,1)} %broadcast_in_dim.33), calls=%async_computation.1 | async-start | bytes 524288 | tf_op jit(solution)/shard_map/all_to_all | solution.py:19
  17.6 23.8 %collective-permute-start = (bf16[16,512]{1,0:T(8,128)(2,1)S(1)}, bf16[16,512]{1,0:T(8,128)(2,1)S(1)}, u32[]{:S(2)}, u32[]{:S(2)}) collective-permute-start(bf16[16,512]{1,0:T(8,128)(2,1)S(1)} %get-tuple-element.37), channel_id=1, source_target_pairs={{0,8},{8,0},{16,24},{24,16},{1,9},{9,1},{17,25},{25,17},{2,10},{10... | collective-permute-start | bytes 49160 | tf_op jit(solution)/shard_map/ppermute | solution.py:23
  29.8 14.9 %collective-permute-start.2 = (bf16[16,512]{1,0:T(8,128)(2,1)S(1)}, bf16[16,512]{1,0:T(8,128)(2,1)S(1)}, u32[]{:S(2)}, u32[]{:S(2)}) collective-permute-start(bf16[16,512]{1,0:T(8,128)(2,1)S(1)} %get-tuple-element.38), channel_id=1, source_target_pairs={{0,24},{8,16},{16,8},{24,0},{1,25},{9,17},{17,9},{25,1},{2,26},{10... | collective-permute-start | bytes 49160 | tf_op jit(solution)/shard_map/ppermute | solution.py:23
  45.5 14.6 %collective-permute-start.3 = (bf16[2,16,512]{2,1,0:T(8,128)(2,1)S(1)}, bf16[2,16,512]{2,1,0:T(8,128)(2,1)S(1)}, u32[]{:S(2)}, u32[]{:S(2)}) collective-permute-start(bf16[2,16,512]{2,1,0:T(8,128)(2,1)S(1)} %pad_maximum_fusion.3), channel_id=1, source_target_pairs={{0,8},{8,0},{16,24},{24,16},{1,9},{9,1},{17,25},{25,17},{2,10},{10... | collective-permute-start | bytes 98312 | tf_op jit(solution)/shard_map/ppermute | solution.py:23
  49.3 15.7 %collective-permute-start.1 = (bf16[2,16,512]{2,1,0:T(8,128)(2,1)S(1)}, bf16[2,16,512]{2,1,0:T(8,128)(2,1)S(1)}, u32[]{:S(2)}, u32[]{:S(2)}) collective-permute-start(bf16[2,16,512]{2,1,0:T(8,128)(2,1)S(1)} %pad_maximum_fusion.2), channel_id=1, source_target_pairs={{0,24},{8,16},{16,8},{24,0},{1,25},{9,17},{17,9},{25,1},{2,26},{10... | collective-permute-start | bytes 98312 | tf_op jit(solution)/shard_map/ppermute | solution.py:23
  66.3 24.2 %all-to-all-start = ((bf16[8,4,16,1024]{3,2,1,0:T(8,128)(2,1)}), bf16[8,4,16,1024]{3,2,1,0:T(8,128)(2,1)S(1)}, u32[]{:S(2)}, u32[]{:S(2)}) async-start(bf16[8,4,16,1024]{3,2,1,0:T(8,128)(2,1)} %broadcast_in_dim.28), calls=%async_computation | async-start | bytes 2097152 | tf_op jit(solution)/shard_map/all_to_all | solution.py:19
  70.2 17.5 %collective-permute-start.6 = (bf16[8,16,1024]{2,1,0:T(8,128)(2,1)S(1)}, bf16[8,16,1024]{2,1,0:T(8,128)(2,1)S(1)}, u32[]{:S(2)}, u32[]{:S(2)}) collective-permute-start(bf16[8,16,1024]{2,1,0:T(8,128)(2,1)S(1)} %all-to-all-done.1), channel_id=1, source_target_pairs={{0,768},{256,512},{512,256},{768,0},{1,769},{257,513},{513,257},{7... | collective-permute-start | bytes 786440 | tf_op jit(solution)/shard_map/ppermute | solution.py:23
  75.1 12.6 %collective-permute-start.5 = (bf16[8,16,1024]{2,1,0:T(8,128)(2,1)S(1)}, bf16[8,16,1024]{2,1,0:T(8,128)(2,1)S(1)}, u32[]{:S(2)}, u32[]{:S(2)}) collective-permute-start(bf16[8,16,1024]{2,1,0:T(8,128)(2,1)S(1)} %all-to-all-done.1), channel_id=1, source_target_pairs={{0,512},{256,768},{512,0},{768,256},{1,513},{257,769},{513,1},{769... | collective-permute-start | bytes 786440 | tf_op jit(solution)/shard_map/ppermute | solution.py:23
  77.7 12.6 %collective-permute-start.4 = (bf16[8,16,1024]{2,1,0:T(8,128)(2,1)S(1)}, bf16[8,16,1024]{2,1,0:T(8,128)(2,1)S(1)}, u32[]{:S(2)}, u32[]{:S(2)}) collective-permute-start(bf16[8,16,1024]{2,1,0:T(8,128)(2,1)S(1)} %all-to-all-done.1), channel_id=1, source_target_pairs={{0,256},{256,0},{512,768},{768,512},{1,257},{257,1},{513,769},{769... | collective-permute-start | bytes 786440 | tf_op jit(solution)/shard_map/ppermute | solution.py:23
  90.5 1.0 copy-start
  92.7 14.9 %all-to-all-start.2 = ((f32[32,1,512]{2,1,0:T(1,128)}), f32[32,1,512]{2,1,0:T(1,128)S(1)}, u32[]{:S(2)}, u32[]{:S(2)}) async-start(f32[32,1,512]{2,1,0:T(1,128)} %all_to_all.26), calls=%async_computation.2 | async-start | bytes 131072 | tf_op jit(solution)/shard_map/all_to_all | solution.py:98
  107.8 20.9 %collective-permute-start.7 = (f32[512]{0:T(512)S(1)}, f32[512]{0:T(512)S(1)}, u32[]{:S(2)}, u32[]{:S(2)}) collective-permute-start(f32[512]{0:T(512)S(1)} %log_add_fusion.4), channel_id=1, source_target_pairs={{0,8},{8,0},{16,24},{24,16},{1,9},{9,1},{17,25},{25,17},{2,10},{10... | collective-permute-start | bytes 6152 | tf_op jit(solution)/shard_map/ppermute | solution.py:23
  118.7 15.2 %all-to-all-start.3 = ((f32[8,1,512]{2,1,0:T(1,128)}), f32[8,1,512]{2,1,0:T(1,128)S(1)}, u32[]{:S(2)}, u32[]{:S(2)}) async-start(f32[8,1,512]{2,1,0:T(1,128)} %broadcast_in_dim.38), calls=%async_computation.3 | async-start | bytes 32768 | tf_op jit(solution)/shard_map/all_to_all | solution.py:19
  133.9 14.2 %collective-permute-start.8 = (f32[512]{0:T(512)S(1)}, f32[512]{0:T(512)S(1)}, u32[]{:S(2)}, u32[]{:S(2)}) collective-permute-start(f32[512]{0:T(512)S(1)} %log_add_fusion.3), channel_id=1, source_target_pairs={{0,24},{8,16},{16,8},{24,0},{1,25},{9,17},{17,9},{25,1},{2,26},{10... | collective-permute-start | bytes 6152 | tf_op jit(solution)/shard_map/ppermute | solution.py:23
  148.8 1.4 copy-start.1
  151.9 27.6 %all-to-all-start.4 = ((bf16[8,4,16,1024]{3,2,1,0:T(8,128)(2,1)}), bf16[8,4,16,1024]{3,2,1,0:T(8,128)(2,1)S(1)}, u32[]{:S(2)}, u32[]{:S(2)}) async-start(bf16[8,4,16,1024]{3,2,1,0:T(8,128)(2,1)} %convolution_convert_fusion.1), calls=%async_computation.4 | async-start | bytes 2097152 | tf_op jit(solution)/shard_map/all_to_all | solution.py:34
  157.2 10.7 %copy-start.2 = (bf16[16,1024]{1,0:T(8,128)(2,1)S(1)}, bf16[16,1024]{1,0:T(8,128)(2,1)}, u32[]{:S(2)}) copy-start(bf16[16,1024]{1,0:T(8,128)(2,1)} %param.2) | copy-start | bytes 98308
  157.3 10.7 %copy-start.3 = (bf16[16,1024]{1,0:T(8,128)(2,1)S(1)}, bf16[16,1024]{1,0:T(8,128)(2,1)}, u32[]{:S(2)}) copy-start(bf16[16,1024]{1,0:T(8,128)(2,1)} %param.3) | copy-start | bytes 98308
  158.1 10.7 %collective-permute-start.13 = (bf16[8,16,1024]{2,1,0:T(8,128)(2,1)}, bf16[8,16,1024]{2,1,0:T(8,128)(2,1)S(1)}, u32[]{:S(2)}, u32[]{:S(2)}) collective-permute-start(bf16[8,16,1024]{2,1,0:T(8,128)(2,1)} %get-tuple-element.15), channel_id=1, source_target_pairs={{0,256},{256,0},{512,768},{768,512},{1,257},{257,1},{513,769},{769... | collective-permute-start | bytes 786440 | tf_op jit(solution)/shard_map/ppermute | solution.py:23
  160.6 17.1 %collective-permute-start.15 = (bf16[8,16,1024]{2,1,0:T(8,128)(2,1)S(1)}, bf16[8,16,1024]{2,1,0:T(8,128)(2,1)S(1)}, u32[]{:S(2)}, u32[]{:S(2)}) collective-permute-start(bf16[8,16,1024]{2,1,0:T(8,128)(2,1)S(1)} %get-tuple-element.16), channel_id=1, source_target_pairs={{0,768},{256,512},{512,256},{768,0},{1,769},{257,513},{513,257},{7... | collective-permute-start | bytes 786440 | tf_op jit(solution)/shard_map/ppermute | solution.py:23
  163.7 14.0 %collective-permute-start.14 = (bf16[8,16,1024]{2,1,0:T(8,128)(2,1)S(1)}, bf16[8,16,1024]{2,1,0:T(8,128)(2,1)}, u32[]{:S(2)}, u32[]{:S(2)}) collective-permute-start(bf16[8,16,1024]{2,1,0:T(8,128)(2,1)S(1)} %get-tuple-element.17), channel_id=1, source_target_pairs={{0,512},{256,768},{512,0},{768,256},{1,513},{257,769},{513,1},{769... | collective-permute-start | bytes 786440 | tf_op jit(solution)/shard_map/ppermute | solution.py:23
  179.5 53.3 %all-to-all-start.5 = ((bf16[8,16,1024]{2,1,0:T(8,128)(2,1)}), bf16[8,16,1024]{2,1,0:T(8,128)(2,1)S(1)}, u32[]{:S(2)}, u32[]{:S(2)}) async-start(bf16[8,16,1024]{2,1,0:T(8,128)(2,1)} %fusion.2), calls=%async_computation.5 | async-start | bytes 524288 | tf_op jit(solution)/shard_map/all_to_all | solution.py:34
  188.5 20.0 %collective-permute-start.9 = (bf16[2,16,512]{2,1,0:T(8,128)(2,1)S(1)}, bf16[2,16,512]{2,1,0:T(8,128)(2,1)S(1)}, u32[]{:S(2)}, u32[]{:S(2)}) collective-permute-start(bf16[2,16,512]{2,1,0:T(8,128)(2,1)S(1)} %fusion.14), channel_id=1, source_target_pairs={{0,24},{8,16},{16,8},{24,0},{1,25},{9,17},{17,9},{25,1},{2,26},{10... | collective-permute-start | bytes 98312 | tf_op jit(solution)/shard_map/ppermute | solution.py:23
  197.8 19.9 %collective-permute-start.11 = (bf16[2,16,512]{2,1,0:T(8,128)(2,1)S(1)}, bf16[2,16,512]{2,1,0:T(8,128)(2,1)S(1)}, u32[]{:S(2)}, u32[]{:S(2)}) collective-permute-start(bf16[2,16,512]{2,1,0:T(8,128)(2,1)S(1)} %fusion.15), channel_id=1, source_target_pairs={{0,8},{8,0},{16,24},{24,16},{1,9},{9,1},{17,25},{25,17},{2,10},{10... | collective-permute-start | bytes 98312 | tf_op jit(solution)/shard_map/ppermute | solution.py:23
  208.6 14.3 %collective-permute-start.10 = (bf16[16,512]{1,0:T(8,128)(2,1)S(1)}, bf16[16,512]{1,0:T(8,128)(2,1)S(1)}, u32[]{:S(2)}, u32[]{:S(2)}) collective-permute-start(bf16[16,512]{1,0:T(8,128)(2,1)S(1)} %fusion.16), channel_id=1, source_target_pairs={{0,8},{8,0},{16,24},{24,16},{1,9},{9,1},{17,25},{25,17},{2,10},{10... | collective-permute-start | bytes 49160 | tf_op jit(solution)/shard_map/ppermute | solution.py:23
  217.8 14.3 %collective-permute-start.12 = (bf16[16,512]{1,0:T(8,128)(2,1)S(1)}, bf16[16,512]{1,0:T(8,128)(2,1)S(1)}, u32[]{:S(2)}, u32[]{:S(2)}) collective-permute-start(bf16[16,512]{1,0:T(8,128)(2,1)S(1)} %fusion.17), channel_id=1, source_target_pairs={{0,24},{8,16},{16,8},{24,0},{1,25},{9,17},{17,9},{25,1},{2,26},{10... | collective-permute-start | bytes 49160 | tf_op jit(solution)/shard_map/ppermute | solution.py:23

commit v11 on v8

--- a/solution.py
+++ b/solution.py
@@ -71,31 +71,33 @@
     return top + jnp.log(sum(jnp.exp(value - top) for value in values))
 
 
-def lse_rows_cols(scores):
-    cols, row = lax.optimization_barrier((gather(lse(scores, 0), blk), lse(scores, 1)))
-    return lse(gather(row, dp), 0), lse(cols, 0)
+def lse_rows(scores):
+    return lse(gather(lse(scores, 1), dp), 0)
 
 
-def weighted(scores, row_lse, col_lse):
-    return (
-        0.5 * (jnp.exp(scores - row_lse[:, None]) + jnp.exp(scores - col_lse[None, :]))
-    ).astype(jnp.bfloat16)
+def lse_cols(scores):
+    col = lse(scores, 0)
+    col = lse_of(col, *(swap(col, "y", step) for step in (1, 2, 3)))
+    col = lse_of(col, *(swap(col, "zl", step) for step in (1, 2, 3)))
+    return lse_of(col, swap(col, "zl", 4))
 
 
 def body(image_emb, text_emb):
     own_rows, width = image_emb.shape
-    img_rows = gather(gather_by_doubling(image_emb, "zh", ring), chip)
-    txt_cols = gather_by_swaps(gather(text_emb, "zl"), "y")
+    img_rows = gather_by_doubling(image_emb, "zh", ring[:1])
+    img_rows, txt_cols = lax.optimization_barrier((img_rows, text_emb))
+    img_rows = gather(gather_by_doubling(img_rows, "zh", ring[1:]), chip)
+    txt_cols = gather_by_swaps(gather(txt_cols, "zl"), "y")
     img_rows = img_rows.reshape(img_rows.shape[0], -1, own_rows, width)
     row_lanes, col_lanes = img_rows.shape[:-1], txt_cols.shape[:-1]
     img_rows, txt_cols = img_rows.reshape(-1, width), txt_cols.reshape(-1, width)
     scores = logit_scale * jnp.dot(img_rows, txt_cols.T, preferred_element_type=jnp.float32)
-    row_lse, col_lse = lse_rows_cols(scores)
-    weights = weighted(scores, row_lse, col_lse)
+    row_lse, col_lse = lse_rows(scores), lse_cols(scores)
+    weights = (
+        0.5 * (jnp.exp(scores - row_lse[:, None]) + jnp.exp(scores - col_lse[None, :]))
+    ).astype(jnp.bfloat16)
     image_part = jnp.dot(weights, txt_cols, preferred_element_type=jnp.float32)
-    image_part = image_part.astype(jnp.bfloat16).reshape(row_lanes + (width,))
-    image_part, scores = lax.optimization_barrier((image_part, scores))
-    weights = weighted(scores, row_lse, col_lse)
+    image_part = image_part.reshape(row_lanes + (width,))
     text_part = lax.dot_general(
         weights, img_rows, (((0,), (0,)), ((), ())), preferred_element_type=jnp.float32
     )

time: 234 us -> 221 us (0.944)
  the two profiles are of different devices: /device:TPU:226 before, /device:TPU:98 now
where the time goes in v11:
time: 221 us; the launch traced here: 220 us
  starting transfers between devices  146 us (66%)
  waiting for transfers between devices  57.6 us (26%)
  other arithmetic  6.33 us (3%)
  local copies, waits for them, and re-layouts  4.96 us (2%)
  matrix products  4.27 us (2%)
    ppermute x17, starting transfers between devices, swap(): lax.ppermute(value, axis, [(i, i ^ step) for i in range(lax.axis_size(axi...  96.8 us
    ppermute x17, waiting for transfers between devices, swap(): lax.ppermute(value, axis, [(i, i ^ step) for i in range(lax.axis_size(axi...  55.4 us
    all_to_all x3, starting transfers between devices, gather(): return lax.all_to_all(copies, axis, 0, 0)  34.7 us
    all_to_all x2, starting transfers between devices, scatter_sum(): lax.all_to_all(parts.astype(jnp.bfloat16), axis, 0, 0).astype(jnp.float32)  14.6 us
  transfers between devices with their start and end apart: 22, of which 12 were waited for; matrix products, arithmetic and copies ran while one was open for 3% of the time, Pallas kernels for 0%

profile of v11, /device:TPU:98, one launch (start us, length us, event | category | flops | bytes accessed | tf_op | source)
XLA Modules:
  0.0 220.2 jit_solution(12585309082643705003)
XLA Ops:
  0.6 15.7 %collective-permute-start = (bf16[16,1024]{1,0:T(8,128)(2,1)}, bf16[16,1024]{1,0:T(8,128)(2,1)S(1)}, u32[]{:S(2)}, u32[]{:S(2)}) collective-permute-start(bf16[16,1024]{1,0:T(8,128)(2,1)} %param.2), channel_id=1, source_target_pairs={{0,8},{8,0},{16,24},{24,16},{1,9},{9,1},{17,25},{25,17},{2,10},{10... | collective-permute-start | bytes 98312 | tf_op jit(solution)/shard_map/ppermute | solution.py:24
  16.4 2.1 collective-permute-done
  20.7 12.5 %all-to-all-start.1 = ((bf16[8,16,1024]{2,1,0:T(8,128)(2,1)}), bf16[8,16,1024]{2,1,0:T(8,128)(2,1)S(1)}, u32[]{:S(2)}, u32[]{:S(2)}) async-start(bf16[8,16,1024]{2,1,0:T(8,128)(2,1)} %broadcast_in_dim.7), calls=%async_computation.1 | async-start | bytes 524288 | tf_op jit(solution)/shard_map/all_to_all | solution.py:20
  33.3 13.4 %collective-permute-start.1 = (bf16[2,16,1024]{2,1,0:T(8,128)(2,1)S(1)}, bf16[2,16,1024]{2,1,0:T(8,128)(2,1)S(1)}, u32[]{:S(2)}, u32[]{:S(2)}) collective-permute-start(bf16[2,16,1024]{2,1,0:T(8,128)(2,1)S(1)} %pad_maximum_fusion.2), channel_id=1, source_target_pairs={{0,24},{8,16},{16,8},{24,0},{1,25},{9,17},{17,9},{25,1},{2,26},{10... | collective-permute-start | bytes 196616 | tf_op jit(solution)/shard_map/ppermute | solution.py:24
  46.7 12.0 %collective-permute-done.1 = bf16[2,16,1024]{2,1,0:T(8,128)(2,1)S(1)} collective-permute-done((bf16[2,16,1024]{2,1,0:T(8,128)(2,1)S(1)}, bf16[2,16,1024]{2,1,0:T(8,128)(2,1)S(1)}, u32[]{:S(2)}, u32[]{:S(2)}) %collective-permute-start.1) | collective-permute-done | bytes 65568 | tf_op jit(solution)/shard_map/ppermute | solution.py:24
  59.9 4.8 %all-to-all-start = ((bf16[8,2,2,16,1024]{4,3,2,1,0:T(8,128)(2,1)}), bf16[8,2,2,16,1024]{4,3,2,1,0:T(8,128)(2,1)S(1)}, u32[]{:S(2)}, u32[]{:S(2)}) async-start(bf16[8,2,2,16,1024]{4,3,2,1,0:T(8,128)(2,1)} %broadcast_in_dim.6), calls=%async_computation | async-start | bytes 2097152 | tf_op jit(solution)/shard_map/all_to_all | solution.py:20
  64.7 4.9 %collective-permute-start.4 = (bf16[8,16,1024]{2,1,0:T(8,128)(2,1)S(1)}, bf16[8,16,1024]{2,1,0:T(8,128)(2,1)S(1)}, u32[]{:S(2)}, u32[]{:S(2)}) collective-permute-start(bf16[8,16,1024]{2,1,0:T(8,128)(2,1)S(1)} %all-to-all-done.1), channel_id=1, source_target_pairs={{0,768},{256,512},{512,256},{768,0},{1,769},{257,513},{513,257},{7... | collective-permute-start | bytes 786440 | tf_op jit(solution)/shard_map/ppermute | solution.py:24
  69.7 2.5 %collective-permute-start.3 = (bf16[8,16,1024]{2,1,0:T(8,128)(2,1)S(1)}, bf16[8,16,1024]{2,1,0:T(8,128)(2,1)S(1)}, u32[]{:S(2)}, u32[]{:S(2)}) collective-permute-start(bf16[8,16,1024]{2,1,0:T(8,128)(2,1)S(1)} %all-to-all-done.1), channel_id=1, source_target_pairs={{0,512},{256,768},{512,0},{768,256},{1,513},{257,769},{513,1},{769... | collective-permute-start | bytes 786440 | tf_op jit(solution)/shard_map/ppermute | solution.py:24
  72.2 2.4 %collective-permute-start.2 = (bf16[8,16,1024]{2,1,0:T(8,128)(2,1)S(1)}, bf16[8,16,1024]{2,1,0:T(8,128)(2,1)S(1)}, u32[]{:S(2)}, u32[]{:S(2)}) collective-permute-start(bf16[8,16,1024]{2,1,0:T(8,128)(2,1)S(1)} %all-to-all-done.1), channel_id=1, source_target_pairs={{0,256},{256,0},{512,768},{768,512},{1,257},{257,1},{513,769},{769... | collective-permute-start | bytes 786440 | tf_op jit(solution)/shard_map/ppermute | solution.py:24
  74.6 6.9 %collective-permute-done.4 = bf16[8,16,1024]{2,1,0:T(8,128)(2,1)S(1)} collective-permute-done((bf16[8,16,1024]{2,1,0:T(8,128)(2,1)S(1)}, bf16[8,16,1024]{2,1,0:T(8,128)(2,1)S(1)}, u32[]{:S(2)}, u32[]{:S(2)}) %collective-permute-start.4) | collective-permute-done | bytes 262176 | tf_op jit(solution)/shard_map/ppermute | solution.py:24
  82.2 2.2 collective-permute-done.2
  86.0 4.8 %collective-permute-start.7 = (f32[512]{0:T(512)S(1)}, f32[512]{0:T(512)S(1)}, u32[]{:S(2)}, u32[]{:S(2)}) collective-permute-start(f32[512]{0:T(512)S(1)} %log_add_fusion.3), channel_id=1, source_target_pairs={{0,768},{256,512},{512,256},{768,0},{1,769},{257,513},{513,257},{7... | collective-permute-start | bytes 6152 | tf_op jit(solution)/shard_map/ppermute | solution.py:24
  90.9 2.5 %collective-permute-start.6 = (f32[512]{0:T(512)S(1)}, f32[512]{0:T(512)S(1)}, u32[]{:S(2)}, u32[]{:S(2)}) collective-permute-start(f32[512]{0:T(512)S(1)} %log_add_fusion.3), channel_id=1, source_target_pairs={{0,512},{256,768},{512,0},{768,256},{1,513},{257,769},{513,1},{769... | collective-permute-start | bytes 6152 | tf_op jit(solution)/shard_map/ppermute | solution.py:24
  93.4 2.4 %collective-permute-start.5 = (f32[512]{0:T(512)S(1)}, f32[512]{0:T(512)S(1)}, u32[]{:S(2)}, u32[]{:S(2)}) collective-permute-start(f32[512]{0:T(512)S(1)} %log_add_fusion.3), channel_id=1, source_target_pairs={{0,256},{256,0},{512,768},{768,512},{1,257},{257,1},{513,769},{769... | collective-permute-start | bytes 6152 | tf_op jit(solution)/shard_map/ppermute | solution.py:24
  96.6 17.3 %all-to-all-start.2 = ((f32[32,1,512]{2,1,0:T(1,128)}), f32[32,1,512]{2,1,0:T(1,128)S(1)}, u32[]{:S(2)}, u32[]{:S(2)}) async-start(f32[32,1,512]{2,1,0:T(1,128)} %broadcast_in_dim.8), calls=%async_computation.2 | async-start | bytes 131072 | tf_op jit(solution)/shard_map/all_to_all | solution.py:20
  113.9 1.9 collective-permute-start.10
  115.9 1.9 collective-permute-start.9
  117.8 6.3 %collective-permute-start.8 = (f32[512]{0:T(512)S(1)}, f32[512]{0:T(512)S(1)}, u32[]{:S(2)}, u32[]{:S(2)}) collective-permute-start(f32[512]{0:T(512)S(1)} %log_add_fusion.2), channel_id=1, source_target_pairs={{0,32},{32,0},{64,96},{96,64},{128,160},{160,128},{192,224},{224,1... | collective-permute-start | bytes 6152 | tf_op jit(solution)/shard_map/ppermute | solution.py:24
  125.6 6.7 %collective-permute-start.11 = (f32[512]{0:T(512)S(1)}, f32[512]{0:T(512)S(1)}, u32[]{:S(2)}, u32[]{:S(2)}) collective-permute-start(f32[512]{0:T(512)S(1)} %log_add_fusion.1), channel_id=1, source_target_pairs={{0,128},{32,160},{64,192},{96,224},{128,0},{160,32},{192,64},{224,... | collective-permute-start | bytes 6152 | tf_op jit(solution)/shard_map/ppermute | solution.py:24
  132.4 2.6 %collective-permute-done.11 = f32[512]{0:T(512)S(1)} collective-permute-done((f32[512]{0:T(512)S(1)}, f32[512]{0:T(512)S(1)}, u32[]{:S(2)}, u32[]{:S(2)}) %collective-permute-start.11) | collective-permute-done | bytes 2080 | tf_op jit(solution)/shard_map/ppermute | solution.py:24
  135.0 2.1 all-to-all-done.2
  141.1 4.9 %all-to-all-start.3 = ((bf16[8,4,16,1024]{3,2,1,0:T(8,128)(2,1)}), bf16[8,4,16,1024]{3,2,1,0:T(8,128)(2,1)S(1)}, u32[]{:S(2)}, u32[]{:S(2)}) async-start(bf16[8,4,16,1024]{3,2,1,0:T(8,128)(2,1)} %convolution_convert_fusion.1), calls=%async_computation.3 | async-start | bytes 2097152 | tf_op jit(solution)/shard_map/all_to_all | solution.py:35
  147.9 3.4 %collective-permute-start.14 = (bf16[8,16,1024]{2,1,0:T(8,128)(2,1)S(1)}, bf16[8,16,1024]{2,1,0:T(8,128)(2,1)S(1)}, u32[]{:S(2)}, u32[]{:S(2)}) collective-permute-start(bf16[8,16,1024]{2,1,0:T(8,128)(2,1)S(1)} %get-tuple-element.15), channel_id=1, source_target_pairs={{0,256},{256,0},{512,768},{768,512},{1,257},{257,1},{513,769},{769... | collective-permute-start | bytes 786440 | tf_op jit(solution)/shard_map/ppermute | solution.py:24
  151.3 4.1 %collective-permute-start.16 = (bf16[8,16,1024]{2,1,0:T(8,128)(2,1)S(1)}, bf16[8,16,1024]{2,1,0:T(8,128)(2,1)S(1)}, u32[]{:S(2)}, u32[]{:S(2)}) collective-permute-start(bf16[8,16,1024]{2,1,0:T(8,128)(2,1)S(1)} %get-tuple-element.16), channel_id=1, source_target_pairs={{0,768},{256,512},{512,256},{768,0},{1,769},{257,513},{513,257},{7... | collective-permute-start | bytes 786440 | tf_op jit(solution)/shard_map/ppermute | solution.py:24
  155.4 2.6 %collective-permute-start.15 = (bf16[8,16,1024]{2,1,0:T(8,128)(2,1)S(1)}, bf16[8,16,1024]{2,1,0:T(8,128)(2,1)}, u32[]{:S(2)}, u32[]{:S(2)}) collective-permute-start(bf16[8,16,1024]{2,1,0:T(8,128)(2,1)S(1)} %get-tuple-element.17), channel_id=1, source_target_pairs={{0,512},{256,768},{512,0},{768,256},{1,513},{257,769},{513,1},{769... | collective-permute-start | bytes 786440 | tf_op jit(solution)/shard_map/ppermute | solution.py:24
  158.1 10.0 %collective-permute-done.16 = bf16[8,16,1024]{2,1,0:T(8,128)(2,1)S(1)} collective-permute-done((bf16[8,16,1024]{2,1,0:T(8,128)(2,1)S(1)}, bf16[8,16,1024]{2,1,0:T(8,128)(2,1)S(1)}, u32[]{:S(2)}, u32[]{:S(2)}) %collective-permute-start.16) | collective-permute-done | bytes 262176 | tf_op jit(solution)/shard_map/ppermute | solution.py:24
  168.1 1.8 fusion.2
  169.9 9.6 %all-to-all-start.4 = ((bf16[8,16,1024]{2,1,0:T(8,128)(2,1)}), bf16[8,16,1024]{2,1,0:T(8,128)(2,1)S(1)}, u32[]{:S(2)}, u32[]{:S(2)}) async-start(bf16[8,16,1024]{2,1,0:T(8,128)(2,1)} %fusion.2), calls=%async_computation.4 | async-start | bytes 524288 | tf_op jit(solution)/shard_map/all_to_all | solution.py:35
  179.7 9.9 %collective-permute-start.12 = (bf16[2,16,1024]{2,1,0:T(8,128)(2,1)S(1)}, bf16[2,16,1024]{2,1,0:T(8,128)(2,1)S(1)}, u32[]{:S(2)}, u32[]{:S(2)}) collective-permute-start(bf16[2,16,1024]{2,1,0:T(8,128)(2,1)S(1)} %fusion.3), channel_id=1, source_target_pairs={{0,24},{8,16},{16,8},{24,0},{1,25},{9,17},{17,9},{25,1},{2,26},{10... | collective-permute-start | bytes 196616 | tf_op jit(solution)/shard_map/ppermute | solution.py:24
  189.8 13.9 %collective-permute-done.12 = bf16[2,16,1024]{2,1,0:T(8,128)(2,1)S(1)} collective-permute-done((bf16[2,16,1024]{2,1,0:T(8,128)(2,1)S(1)}, bf16[2,16,1024]{2,1,0:T(8,128)(2,1)S(1)}, u32[]{:S(2)}, u32[]{:S(2)}) %collective-permute-start.12) | collective-permute-done | bytes 65568 | tf_op jit(solution)/shard_map/ppermute | solution.py:24
  203.7 11.1 %collective-permute-start.13 = (bf16[16,1024]{1,0:T(8,128)(2,1)S(1)}, bf16[16,1024]{1,0:T(8,128)(2,1)S(1)}, u32[]{:S(2)}, u32[]{:S(2)}) collective-permute-start(bf16[16,1024]{1,0:T(8,128)(2,1)S(1)} %fusion.8), channel_id=1, source_target_pairs={{0,8},{8,0},{16,24},{24,16},{1,9},{9,1},{17,25},{25,17},{2,10},{10... | collective-permute-start | bytes 98312 | tf_op jit(solution)/shard_map/ppermute | solution.py:24
  215.4 3.4 %collective-permute-done.13 = bf16[16,1024]{1,0:T(8,128)(2,1)S(1)} collective-permute-done((bf16[16,1024]{1,0:T(8,128)(2,1)S(1)}, bf16[16,1024]{1,0:T(8,128)(2,1)S(1)}, u32[]{:S(2)}, u32[]{:S(2)}) %collective-permute-start.13) | collective-permute-done | bytes 32800 | tf_op jit(solution)/shard_map/ppermute | solution.py:24
  (55 shorter events, 16.1 us)
Async XLA Ops:
  0.6 17.8 %collective-permute-start = (bf16[16,1024]{1,0:T(8,128)(2,1)}, bf16[16,1024]{1,0:T(8,128)(2,1)S(1)}, u32[]{:S(2)}, u32[]{:S(2)}) collective-permute-start(bf16[16,1024]{1,0:T(8,128)(2,1)} %param.2), channel_id=1, source_target_pairs={{0,8},{8,0},{16,24},{24,16},{1,9},{9,1},{17,25},{25,17},{2,10},{10... | collective-permute-start | bytes 98312 | tf_op jit(solution)/shard_map/ppermute | solution.py:24
  20.7 38.0 %all-to-all-start.1 = ((bf16[8,16,1024]{2,1,0:T(8,128)(2,1)}), bf16[8,16,1024]{2,1,0:T(8,128)(2,1)S(1)}, u32[]{:S(2)}, u32[]{:S(2)}) async-start(bf16[8,16,1024]{2,1,0:T(8,128)(2,1)} %broadcast_in_dim.7), calls=%async_computation.1 | async-start | bytes 524288 | tf_op jit(solution)/shard_map/all_to_all | solution.py:20
  33.3 25.4 %collective-permute-start.1 = (bf16[2,16,1024]{2,1,0:T(8,128)(2,1)S(1)}, bf16[2,16,1024]{2,1,0:T(8,128)(2,1)S(1)}, u32[]{:S(2)}, u32[]{:S(2)}) collective-permute-start(bf16[2,16,1024]{2,1,0:T(8,128)(2,1)S(1)} %pad_maximum_fusion.2), channel_id=1, source_target_pairs={{0,24},{8,16},{16,8},{24,0},{1,25},{9,17},{17,9},{25,1},{2,26},{10... | collective-permute-start | bytes 196616 | tf_op jit(solution)/shard_map/ppermute | solution.py:24
  59.9 24.8 %all-to-all-start = ((bf16[8,2,2,16,1024]{4,3,2,1,0:T(8,128)(2,1)}), bf16[8,2,2,16,1024]{4,3,2,1,0:T(8,128)(2,1)S(1)}, u32[]{:S(2)}, u32[]{:S(2)}) async-start(bf16[8,2,2,16,1024]{4,3,2,1,0:T(8,128)(2,1)} %broadcast_in_dim.6), calls=%async_computation | async-start | bytes 2097152 | tf_op jit(solution)/shard_map/all_to_all | solution.py:20
  64.7 16.8 %collective-permute-start.4 = (bf16[8,16,1024]{2,1,0:T(8,128)(2,1)S(1)}, bf16[8,16,1024]{2,1,0:T(8,128)(2,1)S(1)}, u32[]{:S(2)}, u32[]{:S(2)}) collective-permute-start(bf16[8,16,1024]{2,1,0:T(8,128)(2,1)S(1)} %all-to-all-done.1), channel_id=1, source_target_pairs={{0,768},{256,512},{512,256},{768,0},{1,769},{257,513},{513,257},{7... | collective-permute-start | bytes 786440 | tf_op jit(solution)/shard_map/ppermute | solution.py:24
  69.7 12.6 %collective-permute-start.3 = (bf16[8,16,1024]{2,1,0:T(8,128)(2,1)S(1)}, bf16[8,16,1024]{2,1,0:T(8,128)(2,1)S(1)}, u32[]{:S(2)}, u32[]{:S(2)}) collective-permute-start(bf16[8,16,1024]{2,1,0:T(8,128)(2,1)S(1)} %all-to-all-done.1), channel_id=1, source_target_pairs={{0,512},{256,768},{512,0},{768,256},{1,513},{257,769},{513,1},{769... | collective-permute-start | bytes 786440 | tf_op jit(solution)/shard_map/ppermute | solution.py:24
  72.2 12.2 %collective-permute-start.2 = (bf16[8,16,1024]{2,1,0:T(8,128)(2,1)S(1)}, bf16[8,16,1024]{2,1,0:T(8,128)(2,1)S(1)}, u32[]{:S(2)}, u32[]{:S(2)}) collective-permute-start(bf16[8,16,1024]{2,1,0:T(8,128)(2,1)S(1)} %all-to-all-done.1), channel_id=1, source_target_pairs={{0,256},{256,0},{512,768},{768,512},{1,257},{257,1},{513,769},{769... | collective-permute-start | bytes 786440 | tf_op jit(solution)/shard_map/ppermute | solution.py:24
  84.7 1.0 copy-start
  86.0 27.8 %collective-permute-start.7 = (f32[512]{0:T(512)S(1)}, f32[512]{0:T(512)S(1)}, u32[]{:S(2)}, u32[]{:S(2)}) collective-permute-start(f32[512]{0:T(512)S(1)} %log_add_fusion.3), channel_id=1, source_target_pairs={{0,768},{256,512},{512,256},{768,0},{1,769},{257,513},{513,257},{7... | collective-permute-start | bytes 6152 | tf_op jit(solution)/shard_map/ppermute | solution.py:24
  90.9 23.0 %collective-permute-start.6 = (f32[512]{0:T(512)S(1)}, f32[512]{0:T(512)S(1)}, u32[]{:S(2)}, u32[]{:S(2)}) collective-permute-start(f32[512]{0:T(512)S(1)} %log_add_fusion.3), channel_id=1, source_target_pairs={{0,512},{256,768},{512,0},{768,256},{1,513},{257,769},{513,1},{769... | collective-permute-start | bytes 6152 | tf_op jit(solution)/shard_map/ppermute | solution.py:24
  93.4 20.4 %collective-permute-start.5 = (f32[512]{0:T(512)S(1)}, f32[512]{0:T(512)S(1)}, u32[]{:S(2)}, u32[]{:S(2)}) collective-permute-start(f32[512]{0:T(512)S(1)} %log_add_fusion.3), channel_id=1, source_target_pairs={{0,256},{256,0},{512,768},{768,512},{1,257},{257,1},{513,769},{769... | collective-permute-start | bytes 6152 | tf_op jit(solution)/shard_map/ppermute | solution.py:24
  96.6 40.6 %all-to-all-start.2 = ((f32[32,1,512]{2,1,0:T(1,128)}), f32[32,1,512]{2,1,0:T(1,128)S(1)}, u32[]{:S(2)}, u32[]{:S(2)}) async-start(f32[32,1,512]{2,1,0:T(1,128)} %broadcast_in_dim.8), calls=%async_computation.2 | async-start | bytes 131072 | tf_op jit(solution)/shard_map/all_to_all | solution.py:20
  113.9 10.1 %collective-permute-start.10 = (f32[512]{0:T(512)S(1)}, f32[512]{0:T(512)S(1)}, u32[]{:S(2)}, u32[]{:S(2)}) collective-permute-start(f32[512]{0:T(512)S(1)} %log_add_fusion.2), channel_id=1, source_target_pairs={{0,96},{32,64},{64,32},{96,0},{128,224},{160,192},{192,160},{224,1... | collective-permute-start | bytes 6152 | tf_op jit(solution)/shard_map/ppermute | solution.py:24
  115.9 8.2 %collective-permute-start.9 = (f32[512]{0:T(512)S(1)}, f32[512]{0:T(512)S(1)}, u32[]{:S(2)}, u32[]{:S(2)}) collective-permute-start(f32[512]{0:T(512)S(1)} %log_add_fusion.2), channel_id=1, source_target_pairs={{0,64},{32,96},{64,0},{96,32},{128,192},{160,224},{192,128},{224,1... | collective-permute-start | bytes 6152 | tf_op jit(solution)/shard_map/ppermute | solution.py:24
  117.8 7.8 %collective-permute-start.8 = (f32[512]{0:T(512)S(1)}, f32[512]{0:T(512)S(1)}, u32[]{:S(2)}, u32[]{:S(2)}) collective-permute-start(f32[512]{0:T(512)S(1)} %log_add_fusion.2), channel_id=1, source_target_pairs={{0,32},{32,0},{64,96},{96,64},{128,160},{160,128},{192,224},{224,1... | collective-permute-start | bytes 6152 | tf_op jit(solution)/shard_map/ppermute | solution.py:24
  125.6 9.4 %collective-permute-start.11 = (f32[512]{0:T(512)S(1)}, f32[512]{0:T(512)S(1)}, u32[]{:S(2)}, u32[]{:S(2)}) collective-permute-start(f32[512]{0:T(512)S(1)} %log_add_fusion.1), channel_id=1, source_target_pairs={{0,128},{32,160},{64,192},{96,224},{128,0},{160,32},{192,64},{224,... | collective-permute-start | bytes 6152 | tf_op jit(solution)/shard_map/ppermute | solution.py:24
  138.0 1.4 copy-start.1
  141.1 28.8 %all-to-all-start.3 = ((bf16[8,4,16,1024]{3,2,1,0:T(8,128)(2,1)}), bf16[8,4,16,1024]{3,2,1,0:T(8,128)(2,1)S(1)}, u32[]{:S(2)}, u32[]{:S(2)}) async-start(bf16[8,4,16,1024]{3,2,1,0:T(8,128)(2,1)} %convolution_convert_fusion.1), calls=%async_computation.3 | async-start | bytes 2097152 | tf_op jit(solution)/shard_map/all_to_all | solution.py:35
  147.9 10.3 %collective-permute-start.14 = (bf16[8,16,1024]{2,1,0:T(8,128)(2,1)S(1)}, bf16[8,16,1024]{2,1,0:T(8,128)(2,1)S(1)}, u32[]{:S(2)}, u32[]{:S(2)}) collective-permute-start(bf16[8,16,1024]{2,1,0:T(8,128)(2,1)S(1)} %get-tuple-element.15), channel_id=1, source_target_pairs={{0,256},{256,0},{512,768},{768,512},{1,257},{257,1},{513,769},{769... | collective-permute-start | bytes 786440 | tf_op jit(solution)/shard_map/ppermute | solution.py:24
  151.3 16.8 %collective-permute-start.16 = (bf16[8,16,1024]{2,1,0:T(8,128)(2,1)S(1)}, bf16[8,16,1024]{2,1,0:T(8,128)(2,1)S(1)}, u32[]{:S(2)}, u32[]{:S(2)}) collective-permute-start(bf16[8,16,1024]{2,1,0:T(8,128)(2,1)S(1)} %get-tuple-element.16), channel_id=1, source_target_pairs={{0,768},{256,512},{512,256},{768,0},{1,769},{257,513},{513,257},{7... | collective-permute-start | bytes 786440 | tf_op jit(solution)/shard_map/ppermute | solution.py:24
  155.4 12.7 %collective-permute-start.15 = (bf16[8,16,1024]{2,1,0:T(8,128)(2,1)S(1)}, bf16[8,16,1024]{2,1,0:T(8,128)(2,1)}, u32[]{:S(2)}, u32[]{:S(2)}) collective-permute-start(bf16[8,16,1024]{2,1,0:T(8,128)(2,1)S(1)} %get-tuple-element.17), channel_id=1, source_target_pairs={{0,512},{256,768},{512,0},{768,256},{1,513},{257,769},{513,1},{769... | collective-permute-start | bytes 786440 | tf_op jit(solution)/shard_map/ppermute | solution.py:24
  169.9 19.7 %copy-start.2 = (bf16[16,1024]{1,0:T(8,128)(2,1)S(1)}, bf16[16,1024]{1,0:T(8,128)(2,1)}, u32[]{:S(2)}) copy-start(bf16[16,1024]{1,0:T(8,128)(2,1)} %param.3) | copy-start | bytes 98308
  169.9 19.7 %copy-start.3 = (bf16[16,1024]{1,0:T(8,128)(2,1)S(1)}, bf16[16,1024]{1,0:T(8,128)(2,1)}, u32[]{:S(2)}) copy-start(bf16[16,1024]{1,0:T(8,128)(2,1)} %param.2) | copy-start | bytes 98308
  169.9 49.6 %all-to-all-start.4 = ((bf16[8,16,1024]{2,1,0:T(8,128)(2,1)}), bf16[8,16,1024]{2,1,0:T(8,128)(2,1)S(1)}, u32[]{:S(2)}, u32[]{:S(2)}) async-start(bf16[8,16,1024]{2,1,0:T(8,128)(2,1)} %fusion.2), calls=%async_computation.4 | async-start | bytes 524288 | tf_op jit(solution)/shard_map/all_to_all | solution.py:35
  179.7 23.9 %collective-permute-start.12 = (bf16[2,16,1024]{2,1,0:T(8,128)(2,1)S(1)}, bf16[2,16,1024]{2,1,0:T(8,128)(2,1)S(1)}, u32[]{:S(2)}, u32[]{:S(2)}) collective-permute-start(bf16[2,16,1024]{2,1,0:T(8,128)(2,1)S(1)} %fusion.3), channel_id=1, source_target_pairs={{0,24},{8,16},{16,8},{24,0},{1,25},{9,17},{17,9},{25,1},{2,26},{10... | collective-permute-start | bytes 196616 | tf_op jit(solution)/shard_map/ppermute | solution.py:24
  203.7 15.1 %collective-permute-start.13 = (bf16[16,1024]{1,0:T(8,128)(2,1)S(1)}, bf16[16,1024]{1,0:T(8,128)(2,1)S(1)}, u32[]{:S(2)}, u32[]{:S(2)}) collective-permute-start(bf16[16,1024]{1,0:T(8,128)(2,1)S(1)} %fusion.8), channel_id=1, source_target_pairs={{0,8},{8,0},{16,24},{24,16},{1,9},{9,1},{17,25},{25,17},{2,10},{10... | collective-permute-start | bytes 98312 | tf_op jit(solution)/shard_map/ppermute | solution.py:24

commit v12 on v3

--- a/solution.py
+++ b/solution.py
@@ -7,7 +7,8 @@
 
 fine = {"y": 4, "zl": 8, "zh": 4, "x": 4, "core": 2}
 chip = ("x", "core")
-bits = (4, 2, 1)
+blk = ("y", "zl")
+ring = ((1, 1), (3, 2))
 everything = ("y", "zl", "zh", "x", "core")
 
 
@@ -50,17 +51,18 @@
 
 
 def gather_by_doubling(rows, axis, steps):
-    for step in steps:
+    for step, bit in steps:
         other = swap(rows, axis, step)
-        upper = (lax.axis_index(axis) & step) != 0
+        upper = (lax.axis_index(axis) & bit) != 0
         rows = jnp.stack([jnp.where(upper, other, rows), jnp.where(upper, rows, other)])
     return rows
 
 
 def scatter_sum_by_halving(parts, axis, steps):
-    for step in reversed(steps):
-        upper = jnp.where((lax.axis_index(axis) & step) != 0, 1, 0)
-        given = swap(lax.dynamic_index_in_dim(parts, 1 - upper, 0, False), axis, step)
+    for step, bit in reversed(steps):
+        upper = jnp.where((lax.axis_index(axis) & bit) != 0, 1, 0)
+        given = lax.dynamic_index_in_dim(parts, 1 - upper, 0, False).astype(jnp.bfloat16)
+        given = swap(given, axis, step).astype(jnp.float32)
         parts = lax.dynamic_index_in_dim(parts, upper, 0, False) + given
     return parts
 
@@ -80,8 +82,9 @@
 
 def body(image_emb, text_emb):
     own_rows, width = image_emb.shape
-    img_rows = gather(gather(image_emb, "zh"), chip)
-    txt_cols = gather_by_swaps(gather_by_doubling(text_emb, "zl", bits), "y")
+    img_rows = gather(gather_by_doubling(image_emb, "zh", ring), chip)
+    txt_cols = gather_by_swaps(gather(text_emb, "zl"), "y")
+    img_rows = img_rows.reshape(img_rows.shape[0], -1, own_rows, width)
     row_lanes, col_lanes = img_rows.shape[:-1], txt_cols.shape[:-1]
     img_rows, txt_cols = img_rows.reshape(-1, width), txt_cols.reshape(-1, width)
     scores = logit_scale * jnp.dot(img_rows, txt_cols.T, preferred_element_type=jnp.float32)
@@ -92,21 +95,21 @@
     ).astype(jnp.bfloat16)
     image_part = jnp.dot(weights, txt_cols, preferred_element_type=jnp.float32)
     image_part = image_part.reshape(row_lanes + (width,))
-    image_sum = scatter_sum(scatter_sum(image_part, chip), "zh")
     text_part = lax.dot_general(
         weights, img_rows, (((0,), (0,)), ((), ())), preferred_element_type=jnp.float32
     )
     text_part = text_part.reshape(col_lanes + (width,))
-    text_sum = scatter_sum_by_halving(scatter_sum_by_swaps(text_part, "y"), "zl", bits)
+    image_sum = scatter_sum(image_part, chip).reshape(2, 2, own_rows, width)
+    image_sum = scatter_sum_by_halving(image_sum, "zh", ring)
+    text_sum = scatter_sum(scatter_sum_by_swaps(text_part, "y"), "zl")
     grad_image = logit_scale * image_sum - logit_scale * text_emb.astype(jnp.float32)
     grad_text = logit_scale * text_sum - logit_scale * image_emb.astype(jnp.float32)
     own_row = lax.axis_index(chip) * row_lanes[1] + lax.axis_index("zh")
     own_row_lse = lax.dynamic_slice_in_dim(row_lse, own_row * own_rows, own_rows, 0)
-    zl = lax.axis_index("zl")
-    own_col = lax.axis_index("y") * 8 + (zl & 1) * 4 + (zl & 2) + (zl >> 2)
-    own_col_lse = lax.dynamic_slice_in_dim(col_lse, own_col * own_rows, own_rows, 0)
+    own_col_lse = lax.dynamic_slice_in_dim(col_lse, lax.axis_index(blk) * own_rows, own_rows, 0)
+    image_own, text_own = lax.optimization_barrier((image_emb, text_emb))
     diag = logit_scale * jnp.sum(
-        image_emb.astype(jnp.float32) * text_emb.astype(jnp.float32), axis=1
+        image_own.astype(jnp.float32) * text_own.astype(jnp.float32), axis=1
     )
     row_loss = 0.5 * (own_row_lse + own_col_lse) - diag
     return (grad_image, grad_text, row_loss)

time: 217 us -> 215 us (level)
  the two profiles are of different devices: /device:TPU:4 before, /device:TPU:98 now
where the time goes in v12:
time: 215 us; the launch traced here: 214 us
  starting transfers between devices  116 us (54%)
  waiting for transfers between devices  81.7 us (38%)
  other arithmetic  6.03 us (3%)
  local copies, waits for them, and re-layouts  5.81 us (3%)
  matrix products  3.24 us (2%)
    ppermute x10, starting transfers between devices, swap(): lax.ppermute(value, axis, [(i, i ^ step) for i in range(lax.axis_size(axi...  62.4 us
    ppermute x10, waiting for transfers between devices, swap(): lax.ppermute(value, axis, [(i, i ^ step) for i in range(lax.axis_size(axi...  53.3 us
    all_to_all x2, waiting for transfers between devices, lse_over(): lax.all_to_all(sent.reshape(-1, row.shape[0]), axes(col_axis) + axes(row_...  28.3 us
    all_to_all x2, starting transfers between devices, lse_over(): lax.all_to_all(sent.reshape(-1, row.shape[0]), axes(col_axis) + axes(row_...  26.3 us
    all_to_all x2, starting transfers between devices, gather(): return lax.all_to_all(copies, axis, 0, 0)  16.6 us
    all_to_all x2, starting transfers between devices, scatter_sum(): lax.all_to_all(parts.astype(jnp.bfloat16), axis, 0, 0).astype(jnp.float32)  11.1 us
  transfers between devices with their start and end apart: 16, of which 11 were waited for; matrix products, arithmetic and copies ran while one was open for 2% of the time, Pallas kernels for 0%

profile of v12, /device:TPU:98, one launch (start us, length us, event | category | flops | bytes accessed | tf_op | source)
XLA Modules:
  0.0 214.3 jit_solution(11246637947072279859)
XLA Ops:
  0.6 1.5 broadcast_in_dim.53
  2.1 11.7 %all-to-all-start.1 = ((bf16[8,16,1024]{2,1,0:T(8,128)(2,1)}), bf16[8,16,1024]{2,1,0:T(8,128)(2,1)S(1)}, u32[]{:S(2)}, u32[]{:S(2)}) async-start(bf16[8,16,1024]{2,1,0:T(8,128)(2,1)} %broadcast_in_dim.53), calls=%async_computation.1 | async-start | bytes 524288 | tf_op jit(solution)/shard_map/all_to_all | solution.py:21
  13.8 15.7 %collective-permute-start = (bf16[16,1024]{1,0:T(8,128)(2,1)}, bf16[16,1024]{1,0:T(8,128)(2,1)S(1)}, u32[]{:S(2)}, u32[]{:S(2)}) collective-permute-start(bf16[16,1024]{1,0:T(8,128)(2,1)} %param.2), channel_id=1, source_target_pairs={{0,8},{8,0},{16,24},{24,16},{1,9},{9,1},{17,25},{25,17},{2,10},{10... | collective-permute-start | bytes 98312 | tf_op jit(solution)/shard_map/ppermute | solution.py:25
  29.6 5.2 %collective-permute-done = bf16[16,1024]{1,0:T(8,128)(2,1)S(1)} collective-permute-done((bf16[16,1024]{1,0:T(8,128)(2,1)}, bf16[16,1024]{1,0:T(8,128)(2,1)S(1)}, u32[]{:S(2)}, u32[]{:S(2)}) %collective-permute-start) | collective-permute-done | bytes 32800 | tf_op jit(solution)/shard_map/ppermute | solution.py:25
  34.8 0.8 select_bitcast_fusion.7
  35.5 15.3 %collective-permute-start.1 = (bf16[2,16,1024]{2,1,0:T(8,128)(2,1)S(1)}, bf16[2,16,1024]{2,1,0:T(8,128)(2,1)S(1)}, u32[]{:S(2)}, u32[]{:S(2)}) collective-permute-start(bf16[2,16,1024]{2,1,0:T(8,128)(2,1)S(1)} %pad_maximum_fusion.2), channel_id=1, source_target_pairs={{0,24},{8,16},{16,8},{24,0},{1,25},{9,17},{17,9},{25,1},{2,26},{10... | collective-permute-start | bytes 196616 | tf_op jit(solution)/shard_map/ppermute | solution.py:25
  50.9 3.6 %collective-permute-done.1 = bf16[2,16,1024]{2,1,0:T(8,128)(2,1)S(1)} collective-permute-done((bf16[2,16,1024]{2,1,0:T(8,128)(2,1)S(1)}, bf16[2,16,1024]{2,1,0:T(8,128)(2,1)S(1)}, u32[]{:S(2)}, u32[]{:S(2)}) %collective-permute-start.1) | collective-permute-done | bytes 65568 | tf_op jit(solution)/shard_map/ppermute | solution.py:25
  54.5 1.2 broadcast_in_dim.52
  55.7 4.8 %all-to-all-start = ((bf16[8,2,2,16,1024]{4,3,2,1,0:T(8,128)(2,1)}), bf16[8,2,2,16,1024]{4,3,2,1,0:T(8,128)(2,1)S(1)}, u32[]{:S(2)}, u32[]{:S(2)}) async-start(bf16[8,2,2,16,1024]{4,3,2,1,0:T(8,128)(2,1)} %broadcast_in_dim.52), calls=%async_computation | async-start | bytes 2097152 | tf_op jit(solution)/shard_map/all_to_all | solution.py:21
  60.5 4.9 %collective-permute-start.4 = (bf16[8,16,1024]{2,1,0:T(8,128)(2,1)S(1)}, bf16[8,16,1024]{2,1,0:T(8,128)(2,1)S(1)}, u32[]{:S(2)}, u32[]{:S(2)}) collective-permute-start(bf16[8,16,1024]{2,1,0:T(8,128)(2,1)S(1)} %all-to-all-done.1), channel_id=1, source_target_pairs={{0,768},{256,512},{512,256},{768,0},{1,769},{257,513},{513,257},{7... | collective-permute-start | bytes 786440 | tf_op jit(solution)/shard_map/ppermute | solution.py:25
  65.4 2.5 %collective-permute-start.3 = (bf16[8,16,1024]{2,1,0:T(8,128)(2,1)S(1)}, bf16[8,16,1024]{2,1,0:T(8,128)(2,1)S(1)}, u32[]{:S(2)}, u32[]{:S(2)}) collective-permute-start(bf16[8,16,1024]{2,1,0:T(8,128)(2,1)S(1)} %all-to-all-done.1), channel_id=1, source_target_pairs={{0,512},{256,768},{512,0},{768,256},{1,513},{257,769},{513,1},{769... | collective-permute-start | bytes 786440 | tf_op jit(solution)/shard_map/ppermute | solution.py:25
  68.0 2.4 %collective-permute-start.2 = (bf16[8,16,1024]{2,1,0:T(8,128)(2,1)S(1)}, bf16[8,16,1024]{2,1,0:T(8,128)(2,1)S(1)}, u32[]{:S(2)}, u32[]{:S(2)}) collective-permute-start(bf16[8,16,1024]{2,1,0:T(8,128)(2,1)S(1)} %all-to-all-done.1), channel_id=1, source_target_pairs={{0,256},{256,0},{512,768},{768,512},{1,257},{257,1},{513,769},{769... | collective-permute-start | bytes 786440 | tf_op jit(solution)/shard_map/ppermute | solution.py:25
  70.4 6.9 %collective-permute-done.4 = bf16[8,16,1024]{2,1,0:T(8,128)(2,1)S(1)} collective-permute-done((bf16[8,16,1024]{2,1,0:T(8,128)(2,1)S(1)}, bf16[8,16,1024]{2,1,0:T(8,128)(2,1)S(1)}, u32[]{:S(2)}, u32[]{:S(2)}) %collective-permute-start.4) | collective-permute-done | bytes 262176 | tf_op jit(solution)/shard_map/ppermute | solution.py:25
  78.0 2.2 %collective-permute-done.2 = bf16[8,16,1024]{2,1,0:T(8,128)(2,1)S(1)} collective-permute-done((bf16[8,16,1024]{2,1,0:T(8,128)(2,1)S(1)}, bf16[8,16,1024]{2,1,0:T(8,128)(2,1)S(1)}, u32[]{:S(2)}, u32[]{:S(2)}) %collective-permute-start.2) | collective-permute-done | bytes 262176 | tf_op jit(solution)/shard_map/ppermute | solution.py:25
  80.5 0.8 fusion.13
  82.6 7.5 %all-to-all-start.2 = ((f32[32,1,512]{2,1,0:T(1,128)}), f32[32,1,512]{2,1,0:T(1,128)S(1)}, u32[]{:S(2)}, u32[]{:S(2)}) async-start(f32[32,1,512]{2,1,0:T(1,128)} %all_to_all.26), calls=%async_computation.2 | async-start | bytes 131072 | tf_op jit(solution)/shard_map/all_to_all | solution.py:75
  90.2 6.3 %all-to-all-done.2 = f32[32,1,512]{2,1,0:T(1,128)S(1)} async-done(((f32[32,1,512]{2,1,0:T(1,128)}), f32[32,1,512]{2,1,0:T(1,128)S(1)}, u32[]{:S(2)}, u32[]{:S(2)}) %all-to-all-start.2) | async-done | bytes 65568 | tf_op jit(solution)/shard_map/all_to_all | solution.py:75
  97.6 18.8 %all-to-all-start.3 = ((f32[32,1,512]{2,1,0:T(1,128)}), f32[32,1,512]{2,1,0:T(1,128)S(1)}, u32[]{:S(2)}, u32[]{:S(2)}) async-start(f32[32,1,512]{2,1,0:T(1,128)} %all_to_all.28), calls=%async_computation.3 | async-start | bytes 131072 | tf_op jit(solution)/shard_map/all_to_all | solution.py:75
  116.4 22.1 %all-to-all-done.3 = f32[32,1,512]{2,1,0:T(1,128)S(1)} async-done(((f32[32,1,512]{2,1,0:T(1,128)}), f32[32,1,512]{2,1,0:T(1,128)S(1)}, u32[]{:S(2)}, u32[]{:S(2)}) %all-to-all-start.3) | async-done | bytes 65568 | tf_op jit(solution)/shard_map/all_to_all | solution.py:75
  139.6 1.0 copy.7
  141.0 1.7 convolution_convert_fusion.1
  142.7 5.0 %all-to-all-start.4 = ((bf16[8,4,16,1024]{3,2,1,0:T(8,128)(2,1)}), bf16[8,4,16,1024]{3,2,1,0:T(8,128)(2,1)S(1)}, u32[]{:S(2)}, u32[]{:S(2)}) async-start(bf16[8,4,16,1024]{3,2,1,0:T(8,128)(2,1)} %convolution_convert_fusion.1), calls=%async_computation.4 | async-start | bytes 2097152 | tf_op jit(solution)/shard_map/all_to_all | solution.py:36
  148.6 2.5 %collective-permute-start.7 = (bf16[8,16,1024]{2,1,0:T(8,128)(2,1)S(1)}, bf16[8,16,1024]{2,1,0:T(8,128)(2,1)S(1)}, u32[]{:S(2)}, u32[]{:S(2)}) collective-permute-start(bf16[8,16,1024]{2,1,0:T(8,128)(2,1)S(1)} %get-tuple-element.11), channel_id=1, source_target_pairs={{0,256},{256,0},{512,768},{768,512},{1,257},{257,1},{513,769},{769... | collective-permute-start | bytes 786440 | tf_op jit(solution)/shard_map/ppermute | solution.py:25
  151.1 3.1 %collective-permute-start.9 = (bf16[8,16,1024]{2,1,0:T(8,128)(2,1)S(1)}, bf16[8,16,1024]{2,1,0:T(8,128)(2,1)S(1)}, u32[]{:S(2)}, u32[]{:S(2)}) collective-permute-start(bf16[8,16,1024]{2,1,0:T(8,128)(2,1)S(1)} %get-tuple-element.12), channel_id=1, source_target_pairs={{0,768},{256,512},{512,256},{768,0},{1,769},{257,513},{513,257},{7... | collective-permute-start | bytes 786440 | tf_op jit(solution)/shard_map/ppermute | solution.py:25
  154.2 4.2 %collective-permute-start.8 = (bf16[8,16,1024]{2,1,0:T(8,128)(2,1)S(1)}, bf16[8,16,1024]{2,1,0:T(8,128)(2,1)S(1)}, u32[]{:S(2)}, u32[]{:S(2)}) collective-permute-start(bf16[8,16,1024]{2,1,0:T(8,128)(2,1)S(1)} %get-tuple-element.13), channel_id=1, source_target_pairs={{0,512},{256,768},{512,0},{768,256},{1,513},{257,769},{513,1},{769... | collective-permute-start | bytes 786440 | tf_op jit(solution)/shard_map/ppermute | solution.py:25
  158.8 9.1 %collective-permute-done.9 = bf16[8,16,1024]{2,1,0:T(8,128)(2,1)S(1)} collective-permute-done((bf16[8,16,1024]{2,1,0:T(8,128)(2,1)S(1)}, bf16[8,16,1024]{2,1,0:T(8,128)(2,1)S(1)}, u32[]{:S(2)}, u32[]{:S(2)}) %collective-permute-start.9) | collective-permute-done | bytes 262176 | tf_op jit(solution)/shard_map/ppermute | solution.py:25
  167.9 0.9 fusion.2
  168.8 6.1 %all-to-all-start.5 = ((bf16[8,16,1024]{2,1,0:T(8,128)(2,1)}), bf16[8,16,1024]{2,1,0:T(8,128)(2,1)S(1)}, u32[]{:S(2)}, u32[]{:S(2)}) async-start(bf16[8,16,1024]{2,1,0:T(8,128)(2,1)} %fusion.2), calls=%async_computation.5 | async-start | bytes 524288 | tf_op jit(solution)/shard_map/all_to_all | solution.py:36
  175.1 8.5 %collective-permute-start.5 = (bf16[2,16,1024]{2,1,0:T(8,128)(2,1)S(1)}, bf16[2,16,1024]{2,1,0:T(8,128)(2,1)S(1)}, u32[]{:S(2)}, u32[]{:S(2)}) collective-permute-start(bf16[2,16,1024]{2,1,0:T(8,128)(2,1)S(1)} %fusion.3), channel_id=1, source_target_pairs={{0,24},{8,16},{16,8},{24,0},{1,25},{9,17},{17,9},{25,1},{2,26},{10... | collective-permute-start | bytes 196616 | tf_op jit(solution)/shard_map/ppermute | solution.py:25
  183.8 13.9 %collective-permute-done.5 = bf16[2,16,1024]{2,1,0:T(8,128)(2,1)S(1)} collective-permute-done((bf16[2,16,1024]{2,1,0:T(8,128)(2,1)S(1)}, bf16[2,16,1024]{2,1,0:T(8,128)(2,1)S(1)}, u32[]{:S(2)}, u32[]{:S(2)}) %collective-permute-start.5) | collective-permute-done | bytes 65568 | tf_op jit(solution)/shard_map/ppermute | solution.py:25
  197.7 3.3 %collective-permute-start.6 = (bf16[16,1024]{1,0:T(8,128)(2,1)S(1)}, bf16[16,1024]{1,0:T(8,128)(2,1)S(1)}, u32[]{:S(2)}, u32[]{:S(2)}) collective-permute-start(bf16[16,1024]{1,0:T(8,128)(2,1)S(1)} %fusion.6), channel_id=1, source_target_pairs={{0,8},{8,0},{16,24},{24,16},{1,9},{9,1},{17,25},{25,17},{2,10},{10... | collective-permute-start | bytes 98312 | tf_op jit(solution)/shard_map/ppermute | solution.py:25
  201.6 11.3 %collective-permute-done.6 = bf16[16,1024]{1,0:T(8,128)(2,1)S(1)} collective-permute-done((bf16[16,1024]{1,0:T(8,128)(2,1)S(1)}, bf16[16,1024]{1,0:T(8,128)(2,1)S(1)}, u32[]{:S(2)}, u32[]{:S(2)}) %collective-permute-start.6) | collective-permute-done | bytes 32800 | tf_op jit(solution)/shard_map/ppermute | solution.py:25
  (62 shorter events, 8.4 us)
Async XLA Ops:
  2.1 52.4 %all-to-all-start.1 = ((bf16[8,16,1024]{2,1,0:T(8,128)(2,1)}), bf16[8,16,1024]{2,1,0:T(8,128)(2,1)S(1)}, u32[]{:S(2)}, u32[]{:S(2)}) async-start(bf16[8,16,1024]{2,1,0:T(8,128)(2,1)} %broadcast_in_dim.53), calls=%async_computation.1 | async-start | bytes 524288 | tf_op jit(solution)/shard_map/all_to_all | solution.py:21
  13.8 20.9 %collective-permute-start = (bf16[16,1024]{1,0:T(8,128)(2,1)}, bf16[16,1024]{1,0:T(8,128)(2,1)S(1)}, u32[]{:S(2)}, u32[]{:S(2)}) collective-permute-start(bf16[16,1024]{1,0:T(8,128)(2,1)} %param.2), channel_id=1, source_target_pairs={{0,8},{8,0},{16,24},{24,16},{1,9},{9,1},{17,25},{25,17},{2,10},{10... | collective-permute-start | bytes 98312 | tf_op jit(solution)/shard_map/ppermute | solution.py:25
  35.5 18.9 %collective-permute-start.1 = (bf16[2,16,1024]{2,1,0:T(8,128)(2,1)S(1)}, bf16[2,16,1024]{2,1,0:T(8,128)(2,1)S(1)}, u32[]{:S(2)}, u32[]{:S(2)}) collective-permute-start(bf16[2,16,1024]{2,1,0:T(8,128)(2,1)S(1)} %pad_maximum_fusion.2), channel_id=1, source_target_pairs={{0,24},{8,16},{16,8},{24,0},{1,25},{9,17},{17,9},{25,1},{2,26},{10... | collective-permute-start | bytes 196616 | tf_op jit(solution)/shard_map/ppermute | solution.py:25
  55.7 24.8 %all-to-all-start = ((bf16[8,2,2,16,1024]{4,3,2,1,0:T(8,128)(2,1)}), bf16[8,2,2,16,1024]{4,3,2,1,0:T(8,128)(2,1)S(1)}, u32[]{:S(2)}, u32[]{:S(2)}) async-start(bf16[8,2,2,16,1024]{4,3,2,1,0:T(8,128)(2,1)} %broadcast_in_dim.52), calls=%async_computation | async-start | bytes 2097152 | tf_op jit(solution)/shard_map/all_to_all | solution.py:21
  60.5 16.8 %collective-permute-start.4 = (bf16[8,16,1024]{2,1,0:T(8,128)(2,1)S(1)}, bf16[8,16,1024]{2,1,0:T(8,128)(2,1)S(1)}, u32[]{:S(2)}, u32[]{:S(2)}) collective-permute-start(bf16[8,16,1024]{2,1,0:T(8,128)(2,1)S(1)} %all-to-all-done.1), channel_id=1, source_target_pairs={{0,768},{256,512},{512,256},{768,0},{1,769},{257,513},{513,257},{7... | collective-permute-start | bytes 786440 | tf_op jit(solution)/shard_map/ppermute | solution.py:25
  65.4 12.6 %collective-permute-start.3 = (bf16[8,16,1024]{2,1,0:T(8,128)(2,1)S(1)}, bf16[8,16,1024]{2,1,0:T(8,128)(2,1)S(1)}, u32[]{:S(2)}, u32[]{:S(2)}) collective-permute-start(bf16[8,16,1024]{2,1,0:T(8,128)(2,1)S(1)} %all-to-all-done.1), channel_id=1, source_target_pairs={{0,512},{256,768},{512,0},{768,256},{1,513},{257,769},{513,1},{769... | collective-permute-start | bytes 786440 | tf_op jit(solution)/shard_map/ppermute | solution.py:25
  68.0 12.2 %collective-permute-start.2 = (bf16[8,16,1024]{2,1,0:T(8,128)(2,1)S(1)}, bf16[8,16,1024]{2,1,0:T(8,128)(2,1)S(1)}, u32[]{:S(2)}, u32[]{:S(2)}) collective-permute-start(bf16[8,16,1024]{2,1,0:T(8,128)(2,1)S(1)} %all-to-all-done.1), channel_id=1, source_target_pairs={{0,256},{256,0},{512,768},{768,512},{1,257},{257,1},{513,769},{769... | collective-permute-start | bytes 786440 | tf_op jit(solution)/shard_map/ppermute | solution.py:25
  80.5 1.0 copy-start
  82.6 13.8 %all-to-all-start.2 = ((f32[32,1,512]{2,1,0:T(1,128)}), f32[32,1,512]{2,1,0:T(1,128)S(1)}, u32[]{:S(2)}, u32[]{:S(2)}) async-start(f32[32,1,512]{2,1,0:T(1,128)} %all_to_all.26), calls=%async_computation.2 | async-start | bytes 131072 | tf_op jit(solution)/shard_map/all_to_all | solution.py:75
  97.6 40.9 %all-to-all-start.3 = ((f32[32,1,512]{2,1,0:T(1,128)}), f32[32,1,512]{2,1,0:T(1,128)S(1)}, u32[]{:S(2)}, u32[]{:S(2)}) async-start(f32[32,1,512]{2,1,0:T(1,128)} %all_to_all.28), calls=%async_computation.3 | async-start | bytes 131072 | tf_op jit(solution)/shard_map/all_to_all | solution.py:75
  139.6 1.4 copy-start.1
  142.7 5.0 %copy-start.2 = (bf16[512,512]{1,0:T(8,128)(2,1)S(1)}, bf16[512,512]{1,0:T(8,128)(2,1)}, u32[]{:S(2)}) copy-start(bf16[512,512]{1,0:T(8,128)(2,1)} %copy.7) | copy-start | bytes 1572868
  142.7 26.1 %all-to-all-start.4 = ((bf16[8,4,16,1024]{3,2,1,0:T(8,128)(2,1)}), bf16[8,4,16,1024]{3,2,1,0:T(8,128)(2,1)S(1)}, u32[]{:S(2)}, u32[]{:S(2)}) async-start(bf16[8,4,16,1024]{3,2,1,0:T(8,128)(2,1)} %convolution_convert_fusion.1), calls=%async_computation.4 | async-start | bytes 2097152 | tf_op jit(solution)/shard_map/all_to_all | solution.py:36
  148.6 10.3 %collective-permute-start.7 = (bf16[8,16,1024]{2,1,0:T(8,128)(2,1)S(1)}, bf16[8,16,1024]{2,1,0:T(8,128)(2,1)S(1)}, u32[]{:S(2)}, u32[]{:S(2)}) collective-permute-start(bf16[8,16,1024]{2,1,0:T(8,128)(2,1)S(1)} %get-tuple-element.11), channel_id=1, source_target_pairs={{0,256},{256,0},{512,768},{768,512},{1,257},{257,1},{513,769},{769... | collective-permute-start | bytes 786440 | tf_op jit(solution)/shard_map/ppermute | solution.py:25
  151.1 16.8 %collective-permute-start.9 = (bf16[8,16,1024]{2,1,0:T(8,128)(2,1)S(1)}, bf16[8,16,1024]{2,1,0:T(8,128)(2,1)S(1)}, u32[]{:S(2)}, u32[]{:S(2)}) collective-permute-start(bf16[8,16,1024]{2,1,0:T(8,128)(2,1)S(1)} %get-tuple-element.12), channel_id=1, source_target_pairs={{0,768},{256,512},{512,256},{768,0},{1,769},{257,513},{513,257},{7... | collective-permute-start | bytes 786440 | tf_op jit(solution)/shard_map/ppermute | solution.py:25
  154.2 13.7 %collective-permute-start.8 = (bf16[8,16,1024]{2,1,0:T(8,128)(2,1)S(1)}, bf16[8,16,1024]{2,1,0:T(8,128)(2,1)S(1)}, u32[]{:S(2)}, u32[]{:S(2)}) collective-permute-start(bf16[8,16,1024]{2,1,0:T(8,128)(2,1)S(1)} %get-tuple-element.13), channel_id=1, source_target_pairs={{0,512},{256,768},{512,0},{768,256},{1,513},{257,769},{513,1},{769... | collective-permute-start | bytes 786440 | tf_op jit(solution)/shard_map/ppermute | solution.py:25
  168.8 14.8 %copy-start.3 = (bf16[16,1024]{1,0:T(8,128)(2,1)S(1)}, bf16[16,1024]{1,0:T(8,128)(2,1)}, u32[]{:S(2)}) copy-start(bf16[16,1024]{1,0:T(8,128)(2,1)} %param.3) | copy-start | bytes 98308
  168.8 14.9 %copy-start.4 = (bf16[16,1024]{1,0:T(8,128)(2,1)S(1)}, bf16[16,1024]{1,0:T(8,128)(2,1)}, u32[]{:S(2)}) copy-start(bf16[16,1024]{1,0:T(8,128)(2,1)} %param.2) | copy-start | bytes 98308
  168.8 44.8 %all-to-all-start.5 = ((bf16[8,16,1024]{2,1,0:T(8,128)(2,1)}), bf16[8,16,1024]{2,1,0:T(8,128)(2,1)S(1)}, u32[]{:S(2)}, u32[]{:S(2)}) async-start(bf16[8,16,1024]{2,1,0:T(8,128)(2,1)} %fusion.2), calls=%async_computation.5 | async-start | bytes 524288 | tf_op jit(solution)/shard_map/all_to_all | solution.py:36
  175.1 22.6 %collective-permute-start.5 = (bf16[2,16,1024]{2,1,0:T(8,128)(2,1)S(1)}, bf16[2,16,1024]{2,1,0:T(8,128)(2,1)S(1)}, u32[]{:S(2)}, u32[]{:S(2)}) collective-permute-start(bf16[2,16,1024]{2,1,0:T(8,128)(2,1)S(1)} %fusion.3), channel_id=1, source_target_pairs={{0,24},{8,16},{16,8},{24,0},{1,25},{9,17},{17,9},{25,1},{2,26},{10... | collective-permute-start | bytes 196616 | tf_op jit(solution)/shard_map/ppermute | solution.py:25
  197.7 15.2 %collective-permute-start.6 = (bf16[16,1024]{1,0:T(8,128)(2,1)S(1)}, bf16[16,1024]{1,0:T(8,128)(2,1)S(1)}, u32[]{:S(2)}, u32[]{:S(2)}) collective-permute-start(bf16[16,1024]{1,0:T(8,128)(2,1)S(1)} %fusion.6), channel_id=1, source_target_pairs={{0,8},{8,0},{16,24},{24,16},{1,9},{9,1},{17,25},{25,17},{2,10},{10... | collective-permute-start | bytes 98312 | tf_op jit(solution)/shard_map/ppermute | solution.py:25

commit v13 on v12

--- a/solution.py
+++ b/solution.py
@@ -37,12 +37,9 @@
     )
 
 
-def scatter_sum_by_swaps(parts, axis):
+def pieces(parts, axis):
     me = lax.axis_index(axis)
-    parts = parts.astype(jnp.bfloat16)
-    own = [lax.dynamic_index_in_dim(parts, me ^ p, 0, False) for p in range(parts.shape[0])]
-    came = own[:1] + [swap(own[p], axis, p) for p in range(1, parts.shape[0])]
-    return sum(part.astype(jnp.float32) for part in came)
+    return [lax.dynamic_index_in_dim(parts, me ^ p, 0, False) for p in range(parts.shape[0])]
 
 
 def lse(values, dim):
@@ -100,8 +97,12 @@
     )
     text_part = text_part.reshape(col_lanes + (width,))
     image_sum = scatter_sum(image_part, chip).reshape(2, 2, own_rows, width)
+    own, near, opposite, other = pieces(text_part.astype(jnp.bfloat16), "y")
+    came = [own, swap(opposite, "y", 2), swap(other, "y", 3)]
+    image_sum, near = lax.optimization_barrier((image_sum, near))
+    came.append(swap(near, "y", 1))
+    text_sum = scatter_sum(sum(part.astype(jnp.float32) for part in came), "zl")
     image_sum = scatter_sum_by_halving(image_sum, "zh", ring)
-    text_sum = scatter_sum(scatter_sum_by_swaps(text_part, "y"), "zl")
     grad_image = logit_scale * image_sum - logit_scale * text_emb.astype(jnp.float32)
     grad_text = logit_scale * text_sum - logit_scale * image_emb.astype(jnp.float32)
     own_row = lax.axis_index(chip) * row_lanes[1] + lax.axis_index("zh")

time: 215 us -> 218 us (1.014)
  the two profiles are of different devices: /device:TPU:98 before, /device:TPU:128 now
where the time goes in v13:
time: 218 us; the launch traced here: 217 us
  starting transfers between devices  104 us (48%)
  waiting for transfers between devices  96 us (44%)
  other arithmetic  6.01 us (3%)
  local copies, waits for them, and re-layouts  5.36 us (2%)
  matrix products  4.47 us (2%)
    ppermute x10, waiting for transfers between devices, swap(): lax.ppermute(value, axis, [(i, i ^ step) for i in range(lax.axis_size(axi...  62.5 us
    ppermute x10, starting transfers between devices, swap(): lax.ppermute(value, axis, [(i, i ^ step) for i in range(lax.axis_size(axi...  50.7 us
    all_to_all x2, waiting for transfers between devices, lse_over(): lax.all_to_all(sent.reshape(-1, row.shape[0]), axes(col_axis) + axes(row_...  28.1 us
    all_to_all x2, starting transfers between devices, lse_over(): lax.all_to_all(sent.reshape(-1, row.shape[0]), axes(col_axis) + axes(row_...  23 us
    all_to_all x2, starting transfers between devices, gather(): return lax.all_to_all(copies, axis, 0, 0)  19 us
    all_to_all x2, starting transfers between devices, scatter_sum(): lax.all_to_all(parts.astype(jnp.bfloat16), axis, 0, 0).astype(jnp.float32)  11 us
    all_to_all x2, waiting for transfers between devices, scatter_sum(): lax.all_to_all(parts.astype(jnp.bfloat16), axis, 0, 0).astype(jnp.float32)  5.44 us
  transfers between devices with their start and end apart: 16, of which 11 were waited for; matrix products, arithmetic and copies ran while one was open for 3% of the time, Pallas kernels for 0%

profile of v13, /device:TPU:128, one launch (start us, length us, event | category | flops | bytes accessed | tf_op | source)
XLA Modules:
  0.0 216.7 jit_solution(5381393660206093603)
XLA Ops:
  0.6 1.5 broadcast_in_dim.53
  2.1 14.7 %all-to-all-start.1 = ((bf16[8,16,1024]{2,1,0:T(8,128)(2,1)}), bf16[8,16,1024]{2,1,0:T(8,128)(2,1)S(1)}, u32[]{:S(2)}, u32[]{:S(2)}) async-start(bf16[8,16,1024]{2,1,0:T(8,128)(2,1)} %broadcast_in_dim.53), calls=%async_computation.1 | async-start | bytes 524288 | tf_op jit(solution)/shard_map/all_to_all | solution.py:21
  16.8 12.3 %collective-permute-start = (bf16[16,1024]{1,0:T(8,128)(2,1)}, bf16[16,1024]{1,0:T(8,128)(2,1)S(1)}, u32[]{:S(2)}, u32[]{:S(2)}) collective-permute-start(bf16[16,1024]{1,0:T(8,128)(2,1)} %param.2), channel_id=1, source_target_pairs={{0,8},{8,0},{16,24},{24,16},{1,9},{9,1},{17,25},{25,17},{2,10},{10... | collective-permute-start | bytes 98312 | tf_op jit(solution)/shard_map/ppermute | solution.py:25
  29.1 12.5 %collective-permute-done = bf16[16,1024]{1,0:T(8,128)(2,1)S(1)} collective-permute-done((bf16[16,1024]{1,0:T(8,128)(2,1)}, bf16[16,1024]{1,0:T(8,128)(2,1)S(1)}, u32[]{:S(2)}, u32[]{:S(2)}) %collective-permute-start) | collective-permute-done | bytes 32800 | tf_op jit(solution)/shard_map/ppermute | solution.py:25
  42.3 6.9 %collective-permute-start.1 = (bf16[2,16,1024]{2,1,0:T(8,128)(2,1)S(1)}, bf16[2,16,1024]{2,1,0:T(8,128)(2,1)S(1)}, u32[]{:S(2)}, u32[]{:S(2)}) collective-permute-start(bf16[2,16,1024]{2,1,0:T(8,128)(2,1)S(1)} %pad_maximum_fusion.2), channel_id=1, source_target_pairs={{0,24},{8,16},{16,8},{24,0},{1,25},{9,17},{17,9},{25,1},{2,26},{10... | collective-permute-start | bytes 196616 | tf_op jit(solution)/shard_map/ppermute | solution.py:25
  49.3 7.9 %collective-permute-done.1 = bf16[2,16,1024]{2,1,0:T(8,128)(2,1)S(1)} collective-permute-done((bf16[2,16,1024]{2,1,0:T(8,128)(2,1)S(1)}, bf16[2,16,1024]{2,1,0:T(8,128)(2,1)S(1)}, u32[]{:S(2)}, u32[]{:S(2)}) %collective-permute-start.1) | collective-permute-done | bytes 65568 | tf_op jit(solution)/shard_map/ppermute | solution.py:25
  57.3 1.1 broadcast_in_dim.52
  58.4 4.3 %all-to-all-start = ((bf16[8,2,2,16,1024]{4,3,2,1,0:T(8,128)(2,1)}), bf16[8,2,2,16,1024]{4,3,2,1,0:T(8,128)(2,1)S(1)}, u32[]{:S(2)}, u32[]{:S(2)}) async-start(bf16[8,2,2,16,1024]{4,3,2,1,0:T(8,128)(2,1)} %broadcast_in_dim.52), calls=%async_computation | async-start | bytes 2097152 | tf_op jit(solution)/shard_map/all_to_all | solution.py:21
  62.7 4.9 %collective-permute-start.4 = (bf16[8,16,1024]{2,1,0:T(8,128)(2,1)S(1)}, bf16[8,16,1024]{2,1,0:T(8,128)(2,1)S(1)}, u32[]{:S(2)}, u32[]{:S(2)}) collective-permute-start(bf16[8,16,1024]{2,1,0:T(8,128)(2,1)S(1)} %all-to-all-done.1), channel_id=1, source_target_pairs={{0,768},{256,512},{512,256},{768,0},{1,769},{257,513},{513,257},{7... | collective-permute-start | bytes 786440 | tf_op jit(solution)/shard_map/ppermute | solution.py:25
  67.6 2.5 %collective-permute-start.3 = (bf16[8,16,1024]{2,1,0:T(8,128)(2,1)S(1)}, bf16[8,16,1024]{2,1,0:T(8,128)(2,1)S(1)}, u32[]{:S(2)}, u32[]{:S(2)}) collective-permute-start(bf16[8,16,1024]{2,1,0:T(8,128)(2,1)S(1)} %all-to-all-done.1), channel_id=1, source_target_pairs={{0,512},{256,768},{512,0},{768,256},{1,513},{257,769},{513,1},{769... | collective-permute-start | bytes 786440 | tf_op jit(solution)/shard_map/ppermute | solution.py:25
  70.1 2.4 %collective-permute-start.2 = (bf16[8,16,1024]{2,1,0:T(8,128)(2,1)S(1)}, bf16[8,16,1024]{2,1,0:T(8,128)(2,1)S(1)}, u32[]{:S(2)}, u32[]{:S(2)}) collective-permute-start(bf16[8,16,1024]{2,1,0:T(8,128)(2,1)S(1)} %all-to-all-done.1), channel_id=1, source_target_pairs={{0,256},{256,0},{512,768},{768,512},{1,257},{257,1},{513,769},{769... | collective-permute-start | bytes 786440 | tf_op jit(solution)/shard_map/ppermute | solution.py:25
  72.6 7.6 %collective-permute-done.4 = bf16[8,16,1024]{2,1,0:T(8,128)(2,1)S(1)} collective-permute-done((bf16[8,16,1024]{2,1,0:T(8,128)(2,1)S(1)}, bf16[8,16,1024]{2,1,0:T(8,128)(2,1)S(1)}, u32[]{:S(2)}, u32[]{:S(2)}) %collective-permute-start.4) | collective-permute-done | bytes 262176 | tf_op jit(solution)/shard_map/ppermute | solution.py:25
  80.2 2.5 %collective-permute-done.2 = bf16[8,16,1024]{2,1,0:T(8,128)(2,1)S(1)} collective-permute-done((bf16[8,16,1024]{2,1,0:T(8,128)(2,1)S(1)}, bf16[8,16,1024]{2,1,0:T(8,128)(2,1)S(1)}, u32[]{:S(2)}, u32[]{:S(2)}) %collective-permute-start.2) | collective-permute-done | bytes 262176 | tf_op jit(solution)/shard_map/ppermute | solution.py:25
  85.2 7.4 %all-to-all-start.2 = ((f32[32,1,512]{2,1,0:T(1,128)}), f32[32,1,512]{2,1,0:T(1,128)S(1)}, u32[]{:S(2)}, u32[]{:S(2)}) async-start(f32[32,1,512]{2,1,0:T(1,128)} %all_to_all.26), calls=%async_computation.2 | async-start | bytes 131072 | tf_op jit(solution)/shard_map/all_to_all | solution.py:72
  92.6 7.5 %all-to-all-done.2 = f32[32,1,512]{2,1,0:T(1,128)S(1)} async-done(((f32[32,1,512]{2,1,0:T(1,128)}), f32[32,1,512]{2,1,0:T(1,128)S(1)}, u32[]{:S(2)}, u32[]{:S(2)}) %all-to-all-start.2) | async-done | bytes 65568 | tf_op jit(solution)/shard_map/all_to_all | solution.py:72
  101.2 15.6 %all-to-all-start.3 = ((f32[32,1,512]{2,1,0:T(1,128)}), f32[32,1,512]{2,1,0:T(1,128)S(1)}, u32[]{:S(2)}, u32[]{:S(2)}) async-start(f32[32,1,512]{2,1,0:T(1,128)} %all_to_all.28), calls=%async_computation.3 | async-start | bytes 131072 | tf_op jit(solution)/shard_map/all_to_all | solution.py:72
  116.8 20.6 %all-to-all-done.3 = f32[32,1,512]{2,1,0:T(1,128)S(1)} async-done(((f32[32,1,512]{2,1,0:T(1,128)}), f32[32,1,512]{2,1,0:T(1,128)S(1)}, u32[]{:S(2)}, u32[]{:S(2)}) %all-to-all-start.3) | async-done | bytes 65568 | tf_op jit(solution)/shard_map/all_to_all | solution.py:72
  138.3 1.7 convolution_convert_fusion.1
  140.0 3.6 %all-to-all-start.4 = ((bf16[8,4,16,1024]{3,2,1,0:T(8,128)(2,1)}), bf16[8,4,16,1024]{3,2,1,0:T(8,128)(2,1)S(1)}, u32[]{:S(2)}, u32[]{:S(2)}) async-start(bf16[8,4,16,1024]{3,2,1,0:T(8,128)(2,1)} %convolution_convert_fusion.1), calls=%async_computation.4 | async-start | bytes 2097152 | tf_op jit(solution)/shard_map/all_to_all | solution.py:36
  144.1 1.9 convolution_convert_fusion
  146.9 3.2 %collective-permute-start.7 = (bf16[8,16,1024]{2,1,0:T(8,128)(2,1)}, bf16[8,16,1024]{2,1,0:T(8,128)(2,1)S(1)}, u32[]{:S(2)}, u32[]{:S(2)}) collective-permute-start(bf16[8,16,1024]{2,1,0:T(8,128)(2,1)} %get-tuple-element.15), channel_id=1, source_target_pairs={{0,512},{256,768},{512,0},{768,256},{1,513},{257,769},{513,1},{769... | collective-permute-start | bytes 786440 | tf_op jit(solution)/shard_map/ppermute | solution.py:25
  150.0 4.0 %collective-permute-start.8 = (bf16[8,16,1024]{2,1,0:T(8,128)(2,1)S(1)}, bf16[8,16,1024]{2,1,0:T(8,128)(2,1)S(1)}, u32[]{:S(2)}, u32[]{:S(2)}) collective-permute-start(bf16[8,16,1024]{2,1,0:T(8,128)(2,1)S(1)} %get-tuple-element.16), channel_id=1, source_target_pairs={{0,768},{256,512},{512,256},{768,0},{1,769},{257,513},{513,257},{7... | collective-permute-start | bytes 786440 | tf_op jit(solution)/shard_map/ppermute | solution.py:25
  154.0 5.4 %all-to-all-done.4 = bf16[8,4,16,1024]{3,2,1,0:T(8,128)(2,1)S(1)} async-done(((bf16[8,4,16,1024]{3,2,1,0:T(8,128)(2,1)}), bf16[8,4,16,1024]{3,2,1,0:T(8,128)(2,1)S(1)}, u32[]{:S(2)}, u32[]{:S(2)}) %all-to-all-start.4) | async-done | bytes 1048608 | tf_op jit(solution)/shard_map/all_to_all | solution.py:36
  159.6 2.5 %collective-permute-start.9 = (bf16[8,16,1024]{2,1,0:T(8,128)(2,1)S(1)}, bf16[8,16,1024]{2,1,0:T(8,128)(2,1)S(1)}, u32[]{:S(2)}, u32[]{:S(2)}) collective-permute-start(bf16[8,16,1024]{2,1,0:T(8,128)(2,1)S(1)} %get-tuple-element.8), channel_id=1, source_target_pairs={{0,256},{256,0},{512,768},{768,512},{1,257},{257,1},{513,769},{769... | collective-permute-start | bytes 786440 | tf_op jit(solution)/shard_map/ppermute | solution.py:25
  162.2 2.5 %collective-permute-done.8 = bf16[8,16,1024]{2,1,0:T(8,128)(2,1)S(1)} collective-permute-done((bf16[8,16,1024]{2,1,0:T(8,128)(2,1)S(1)}, bf16[8,16,1024]{2,1,0:T(8,128)(2,1)S(1)}, u32[]{:S(2)}, u32[]{:S(2)}) %collective-permute-start.8) | collective-permute-done | bytes 262176 | tf_op jit(solution)/shard_map/ppermute | solution.py:25
  164.7 4.7 %collective-permute-done.9 = bf16[8,16,1024]{2,1,0:T(8,128)(2,1)S(1)} collective-permute-done((bf16[8,16,1024]{2,1,0:T(8,128)(2,1)S(1)}, bf16[8,16,1024]{2,1,0:T(8,128)(2,1)S(1)}, u32[]{:S(2)}, u32[]{:S(2)}) %collective-permute-start.9) | collective-permute-done | bytes 262176 | tf_op jit(solution)/shard_map/ppermute | solution.py:25
  169.4 0.9 fusion.2
  170.2 7.5 %all-to-all-start.5 = ((bf16[8,16,1024]{2,1,0:T(8,128)(2,1)}), bf16[8,16,1024]{2,1,0:T(8,128)(2,1)S(1)}, u32[]{:S(2)}, u32[]{:S(2)}) async-start(bf16[8,16,1024]{2,1,0:T(8,128)(2,1)} %fusion.2), calls=%async_computation.5 | async-start | bytes 524288 | tf_op jit(solution)/shard_map/all_to_all | solution.py:36
  177.7 8.5 %collective-permute-start.5 = (bf16[2,16,1024]{2,1,0:T(8,128)(2,1)S(1)}, bf16[2,16,1024]{2,1,0:T(8,128)(2,1)S(1)}, u32[]{:S(2)}, u32[]{:S(2)}) collective-permute-start(bf16[2,16,1024]{2,1,0:T(8,128)(2,1)S(1)} %fusion.3), channel_id=1, source_target_pairs={{0,24},{8,16},{16,8},{24,0},{1,25},{9,17},{17,9},{25,1},{2,26},{10... | collective-permute-start | bytes 196616 | tf_op jit(solution)/shard_map/ppermute | solution.py:25
  186.4 14.5 %collective-permute-done.5 = bf16[2,16,1024]{2,1,0:T(8,128)(2,1)S(1)} collective-permute-done((bf16[2,16,1024]{2,1,0:T(8,128)(2,1)S(1)}, bf16[2,16,1024]{2,1,0:T(8,128)(2,1)S(1)}, u32[]{:S(2)}, u32[]{:S(2)}) %collective-permute-start.5) | collective-permute-done | bytes 65568 | tf_op jit(solution)/shard_map/ppermute | solution.py:25
  200.9 3.6 %collective-permute-start.6 = (bf16[16,1024]{1,0:T(8,128)(2,1)S(1)}, bf16[16,1024]{1,0:T(8,128)(2,1)S(1)}, u32[]{:S(2)}, u32[]{:S(2)}) collective-permute-start(bf16[16,1024]{1,0:T(8,128)(2,1)S(1)} %fusion.6), channel_id=1, source_target_pairs={{0,8},{8,0},{16,24},{24,16},{1,9},{9,1},{17,25},{25,17},{2,10},{10... | collective-permute-start | bytes 98312 | tf_op jit(solution)/shard_map/ppermute | solution.py:25
  205.1 10.3 %collective-permute-done.6 = bf16[16,1024]{1,0:T(8,128)(2,1)S(1)} collective-permute-done((bf16[16,1024]{1,0:T(8,128)(2,1)S(1)}, bf16[16,1024]{1,0:T(8,128)(2,1)S(1)}, u32[]{:S(2)}, u32[]{:S(2)}) %collective-permute-start.6) | collective-permute-done | bytes 32800 | tf_op jit(solution)/shard_map/ppermute | solution.py:25
  (58 shorter events, 8.8 us)
Async XLA Ops:
  2.1 55.2 %all-to-all-start.1 = ((bf16[8,16,1024]{2,1,0:T(8,128)(2,1)}), bf16[8,16,1024]{2,1,0:T(8,128)(2,1)S(1)}, u32[]{:S(2)}, u32[]{:S(2)}) async-start(bf16[8,16,1024]{2,1,0:T(8,128)(2,1)} %broadcast_in_dim.53), calls=%async_computation.1 | async-start | bytes 524288 | tf_op jit(solution)/shard_map/all_to_all | solution.py:21
  16.8 24.7 %collective-permute-start = (bf16[16,1024]{1,0:T(8,128)(2,1)}, bf16[16,1024]{1,0:T(8,128)(2,1)S(1)}, u32[]{:S(2)}, u32[]{:S(2)}) collective-permute-start(bf16[16,1024]{1,0:T(8,128)(2,1)} %param.2), channel_id=1, source_target_pairs={{0,8},{8,0},{16,24},{24,16},{1,9},{9,1},{17,25},{25,17},{2,10},{10... | collective-permute-start | bytes 98312 | tf_op jit(solution)/shard_map/ppermute | solution.py:25
  42.3 14.9 %collective-permute-start.1 = (bf16[2,16,1024]{2,1,0:T(8,128)(2,1)S(1)}, bf16[2,16,1024]{2,1,0:T(8,128)(2,1)S(1)}, u32[]{:S(2)}, u32[]{:S(2)}) collective-permute-start(bf16[2,16,1024]{2,1,0:T(8,128)(2,1)S(1)} %pad_maximum_fusion.2), channel_id=1, source_target_pairs={{0,24},{8,16},{16,8},{24,0},{1,25},{9,17},{17,9},{25,1},{2,26},{10... | collective-permute-start | bytes 196616 | tf_op jit(solution)/shard_map/ppermute | solution.py:25
  58.4 24.6 %all-to-all-start = ((bf16[8,2,2,16,1024]{4,3,2,1,0:T(8,128)(2,1)}), bf16[8,2,2,16,1024]{4,3,2,1,0:T(8,128)(2,1)S(1)}, u32[]{:S(2)}, u32[]{:S(2)}) async-start(bf16[8,2,2,16,1024]{4,3,2,1,0:T(8,128)(2,1)} %broadcast_in_dim.52), calls=%async_computation | async-start | bytes 2097152 | tf_op jit(solution)/shard_map/all_to_all | solution.py:21
  62.7 17.5 %collective-permute-start.4 = (bf16[8,16,1024]{2,1,0:T(8,128)(2,1)S(1)}, bf16[8,16,1024]{2,1,0:T(8,128)(2,1)S(1)}, u32[]{:S(2)}, u32[]{:S(2)}) collective-permute-start(bf16[8,16,1024]{2,1,0:T(8,128)(2,1)S(1)} %all-to-all-done.1), channel_id=1, source_target_pairs={{0,768},{256,512},{512,256},{768,0},{1,769},{257,513},{513,257},{7... | collective-permute-start | bytes 786440 | tf_op jit(solution)/shard_map/ppermute | solution.py:25
  67.6 12.6 %collective-permute-start.3 = (bf16[8,16,1024]{2,1,0:T(8,128)(2,1)S(1)}, bf16[8,16,1024]{2,1,0:T(8,128)(2,1)S(1)}, u32[]{:S(2)}, u32[]{:S(2)}) collective-permute-start(bf16[8,16,1024]{2,1,0:T(8,128)(2,1)S(1)} %all-to-all-done.1), channel_id=1, source_target_pairs={{0,512},{256,768},{512,0},{768,256},{1,513},{257,769},{513,1},{769... | collective-permute-start | bytes 786440 | tf_op jit(solution)/shard_map/ppermute | solution.py:25
  70.1 12.6 %collective-permute-start.2 = (bf16[8,16,1024]{2,1,0:T(8,128)(2,1)S(1)}, bf16[8,16,1024]{2,1,0:T(8,128)(2,1)S(1)}, u32[]{:S(2)}, u32[]{:S(2)}) collective-permute-start(bf16[8,16,1024]{2,1,0:T(8,128)(2,1)S(1)} %all-to-all-done.1), channel_id=1, source_target_pairs={{0,256},{256,0},{512,768},{768,512},{1,257},{257,1},{513,769},{769... | collective-permute-start | bytes 786440 | tf_op jit(solution)/shard_map/ppermute | solution.py:25
  83.0 1.0 copy-start
  85.2 14.9 %all-to-all-start.2 = ((f32[32,1,512]{2,1,0:T(1,128)}), f32[32,1,512]{2,1,0:T(1,128)S(1)}, u32[]{:S(2)}, u32[]{:S(2)}) async-start(f32[32,1,512]{2,1,0:T(1,128)} %all_to_all.26), calls=%async_computation.2 | async-start | bytes 131072 | tf_op jit(solution)/shard_map/all_to_all | solution.py:72
  101.2 36.2 %all-to-all-start.3 = ((f32[32,1,512]{2,1,0:T(1,128)}), f32[32,1,512]{2,1,0:T(1,128)S(1)}, u32[]{:S(2)}, u32[]{:S(2)}) async-start(f32[32,1,512]{2,1,0:T(1,128)} %all_to_all.28), calls=%async_computation.3 | async-start | bytes 131072 | tf_op jit(solution)/shard_map/all_to_all | solution.py:72
  140.0 19.4 %all-to-all-start.4 = ((bf16[8,4,16,1024]{3,2,1,0:T(8,128)(2,1)}), bf16[8,4,16,1024]{3,2,1,0:T(8,128)(2,1)S(1)}, u32[]{:S(2)}, u32[]{:S(2)}) async-start(bf16[8,4,16,1024]{3,2,1,0:T(8,128)(2,1)} %convolution_convert_fusion.1), calls=%async_computation.4 | async-start | bytes 2097152 | tf_op jit(solution)/shard_map/all_to_all | solution.py:36
  146.9 15.3 %collective-permute-start.7 = (bf16[8,16,1024]{2,1,0:T(8,128)(2,1)}, bf16[8,16,1024]{2,1,0:T(8,128)(2,1)S(1)}, u32[]{:S(2)}, u32[]{:S(2)}) collective-permute-start(bf16[8,16,1024]{2,1,0:T(8,128)(2,1)} %get-tuple-element.15), channel_id=1, source_target_pairs={{0,512},{256,768},{512,0},{768,256},{1,513},{257,769},{513,1},{769... | collective-permute-start | bytes 786440 | tf_op jit(solution)/shard_map/ppermute | solution.py:25
  150.0 14.6 %collective-permute-start.8 = (bf16[8,16,1024]{2,1,0:T(8,128)(2,1)S(1)}, bf16[8,16,1024]{2,1,0:T(8,128)(2,1)S(1)}, u32[]{:S(2)}, u32[]{:S(2)}) collective-permute-start(bf16[8,16,1024]{2,1,0:T(8,128)(2,1)S(1)} %get-tuple-element.16), channel_id=1, source_target_pairs={{0,768},{256,512},{512,256},{768,0},{1,769},{257,513},{513,257},{7... | collective-permute-start | bytes 786440 | tf_op jit(solution)/shard_map/ppermute | solution.py:25
  159.6 26.6 %copy-start.1 = (bf16[16,1024]{1,0:T(8,128)(2,1)S(1)}, bf16[16,1024]{1,0:T(8,128)(2,1)}, u32[]{:S(2)}) copy-start(bf16[16,1024]{1,0:T(8,128)(2,1)} %param.3) | copy-start | bytes 98308
  159.6 26.6 %copy-start.2 = (bf16[16,1024]{1,0:T(8,128)(2,1)S(1)}, bf16[16,1024]{1,0:T(8,128)(2,1)}, u32[]{:S(2)}) copy-start(bf16[16,1024]{1,0:T(8,128)(2,1)} %param.2) | copy-start | bytes 98308
  159.6 9.7 %collective-permute-start.9 = (bf16[8,16,1024]{2,1,0:T(8,128)(2,1)S(1)}, bf16[8,16,1024]{2,1,0:T(8,128)(2,1)S(1)}, u32[]{:S(2)}, u32[]{:S(2)}) collective-permute-start(bf16[8,16,1024]{2,1,0:T(8,128)(2,1)S(1)} %get-tuple-element.8), channel_id=1, source_target_pairs={{0,256},{256,0},{512,768},{768,512},{1,257},{257,1},{513,769},{769... | collective-permute-start | bytes 786440 | tf_op jit(solution)/shard_map/ppermute | solution.py:25
  170.2 45.8 %all-to-all-start.5 = ((bf16[8,16,1024]{2,1,0:T(8,128)(2,1)}), bf16[8,16,1024]{2,1,0:T(8,128)(2,1)S(1)}, u32[]{:S(2)}, u32[]{:S(2)}) async-start(bf16[8,16,1024]{2,1,0:T(8,128)(2,1)} %fusion.2), calls=%async_computation.5 | async-start | bytes 524288 | tf_op jit(solution)/shard_map/all_to_all | solution.py:36
  177.7 23.1 %collective-permute-start.5 = (bf16[2,16,1024]{2,1,0:T(8,128)(2,1)S(1)}, bf16[2,16,1024]{2,1,0:T(8,128)(2,1)S(1)}, u32[]{:S(2)}, u32[]{:S(2)}) collective-permute-start(bf16[2,16,1024]{2,1,0:T(8,128)(2,1)S(1)} %fusion.3), channel_id=1, source_target_pairs={{0,24},{8,16},{16,8},{24,0},{1,25},{9,17},{17,9},{25,1},{2,26},{10... | collective-permute-start | bytes 196616 | tf_op jit(solution)/shard_map/ppermute | solution.py:25
  200.9 14.5 %collective-permute-start.6 = (bf16[16,1024]{1,0:T(8,128)(2,1)S(1)}, bf16[16,1024]{1,0:T(8,128)(2,1)S(1)}, u32[]{:S(2)}, u32[]{:S(2)}) collective-permute-start(bf16[16,1024]{1,0:T(8,128)(2,1)S(1)} %fusion.6), channel_id=1, source_target_pairs={{0,8},{8,0},{16,24},{24,16},{1,9},{9,1},{17,25},{25,17},{2,10},{10... | collective-permute-start | bytes 98312 | tf_op jit(solution)/shard_map/ppermute | solution.py:25

commit v14 on v12

--- a/solution.py
+++ b/solution.py
@@ -95,9 +95,11 @@
     ).astype(jnp.bfloat16)
     image_part = jnp.dot(weights, txt_cols, preferred_element_type=jnp.float32)
     image_part = image_part.reshape(row_lanes + (width,))
-    text_part = lax.dot_general(
-        weights, img_rows, (((0,), (0,)), ((), ())), preferred_element_type=jnp.float32
-    )
+    turned = logit_scale * jnp.dot(txt_cols, img_rows.T, preferred_element_type=jnp.float32)
+    turned = (
+        0.5 * (jnp.exp(turned - row_lse[None, :]) + jnp.exp(turned - col_lse[:, None]))
+    ).astype(jnp.bfloat16)
+    text_part = jnp.dot(turned, img_rows, preferred_element_type=jnp.float32)
     text_part = text_part.reshape(col_lanes + (width,))
     image_sum = scatter_sum(image_part, chip).reshape(2, 2, own_rows, width)
     image_sum = scatter_sum_by_halving(image_sum, "zh", ring)

time: 215 us -> 214 us (level)
  the two profiles are of different devices: /device:TPU:98 before, /device:TPU:128 now
where the time goes in v14:
time: 214 us; the launch traced here: 213 us
  starting transfers between devices  104 us (49%)
  waiting for transfers between devices  94 us (44%)
  other arithmetic  5.71 us (3%)
  local copies, waits for them, and re-layouts  4.21 us (2%)
  matrix products  4.18 us (2%)
    ppermute x10, waiting for transfers between devices, swap(): lax.ppermute(value, axis, [(i, i ^ step) for i in range(lax.axis_size(axi...  65.9 us
    ppermute x10, starting transfers between devices, swap(): lax.ppermute(value, axis, [(i, i ^ step) for i in range(lax.axis_size(axi...  50.9 us
    all_to_all x2, waiting for transfers between devices, lse_over(): lax.all_to_all(sent.reshape(-1, row.shape[0]), axes(col_axis) + axes(row_...  28.1 us
    all_to_all x2, starting transfers between devices, lse_over(): lax.all_to_all(sent.reshape(-1, row.shape[0]), axes(col_axis) + axes(row_...  23 us
    all_to_all x2, starting transfers between devices, gather(): return lax.all_to_all(copies, axis, 0, 0)  19 us
    all_to_all x2, starting transfers between devices, scatter_sum(): lax.all_to_all(parts.astype(jnp.bfloat16), axis, 0, 0).astype(jnp.float32)  11.1 us
  transfers between devices with their start and end apart: 16, of which 10 were waited for; matrix products, arithmetic and copies ran while one was open for 2% of the time, Pallas kernels for 0%

profile of v14, /device:TPU:128, one launch (start us, length us, event | category | flops | bytes accessed | tf_op | source)
XLA Modules:
  0.0 213.2 jit_solution(6257771802632464552)
XLA Ops:
  0.6 1.5 broadcast_in_dim.53
  2.1 14.7 %all-to-all-start.1 = ((bf16[8,16,1024]{2,1,0:T(8,128)(2,1)}), bf16[8,16,1024]{2,1,0:T(8,128)(2,1)S(1)}, u32[]{:S(2)}, u32[]{:S(2)}) async-start(bf16[8,16,1024]{2,1,0:T(8,128)(2,1)} %broadcast_in_dim.53), calls=%async_computation.1 | async-start | bytes 524288 | tf_op jit(solution)/shard_map/all_to_all | solution.py:21
  16.8 12.3 %collective-permute-start = (bf16[16,1024]{1,0:T(8,128)(2,1)}, bf16[16,1024]{1,0:T(8,128)(2,1)S(1)}, u32[]{:S(2)}, u32[]{:S(2)}) collective-permute-start(bf16[16,1024]{1,0:T(8,128)(2,1)} %param.2), channel_id=1, source_target_pairs={{0,8},{8,0},{16,24},{24,16},{1,9},{9,1},{17,25},{25,17},{2,10},{10... | collective-permute-start | bytes 98312 | tf_op jit(solution)/shard_map/ppermute | solution.py:25
  29.1 12.5 %collective-permute-done = bf16[16,1024]{1,0:T(8,128)(2,1)S(1)} collective-permute-done((bf16[16,1024]{1,0:T(8,128)(2,1)}, bf16[16,1024]{1,0:T(8,128)(2,1)S(1)}, u32[]{:S(2)}, u32[]{:S(2)}) %collective-permute-start) | collective-permute-done | bytes 32800 | tf_op jit(solution)/shard_map/ppermute | solution.py:25
  41.6 0.8 select_bitcast_fusion.7
  42.3 6.9 %collective-permute-start.1 = (bf16[2,16,1024]{2,1,0:T(8,128)(2,1)S(1)}, bf16[2,16,1024]{2,1,0:T(8,128)(2,1)S(1)}, u32[]{:S(2)}, u32[]{:S(2)}) collective-permute-start(bf16[2,16,1024]{2,1,0:T(8,128)(2,1)S(1)} %pad_maximum_fusion.2), channel_id=1, source_target_pairs={{0,24},{8,16},{16,8},{24,0},{1,25},{9,17},{17,9},{25,1},{2,26},{10... | collective-permute-start | bytes 196616 | tf_op jit(solution)/shard_map/ppermute | solution.py:25
  49.3 7.9 %collective-permute-done.1 = bf16[2,16,1024]{2,1,0:T(8,128)(2,1)S(1)} collective-permute-done((bf16[2,16,1024]{2,1,0:T(8,128)(2,1)S(1)}, bf16[2,16,1024]{2,1,0:T(8,128)(2,1)S(1)}, u32[]{:S(2)}, u32[]{:S(2)}) %collective-permute-start.1) | collective-permute-done | bytes 65568 | tf_op jit(solution)/shard_map/ppermute | solution.py:25
  57.3 1.1 broadcast_in_dim.52
  58.4 4.3 %all-to-all-start = ((bf16[8,2,2,16,1024]{4,3,2,1,0:T(8,128)(2,1)}), bf16[8,2,2,16,1024]{4,3,2,1,0:T(8,128)(2,1)S(1)}, u32[]{:S(2)}, u32[]{:S(2)}) async-start(bf16[8,2,2,16,1024]{4,3,2,1,0:T(8,128)(2,1)} %broadcast_in_dim.52), calls=%async_computation | async-start | bytes 2097152 | tf_op jit(solution)/shard_map/all_to_all | solution.py:21
  62.7 4.9 %collective-permute-start.4 = (bf16[8,16,1024]{2,1,0:T(8,128)(2,1)S(1)}, bf16[8,16,1024]{2,1,0:T(8,128)(2,1)S(1)}, u32[]{:S(2)}, u32[]{:S(2)}) collective-permute-start(bf16[8,16,1024]{2,1,0:T(8,128)(2,1)S(1)} %all-to-all-done.1), channel_id=1, source_target_pairs={{0,768},{256,512},{512,256},{768,0},{1,769},{257,513},{513,257},{7... | collective-permute-start | bytes 786440 | tf_op jit(solution)/shard_map/ppermute | solution.py:25
  67.6 2.5 %collective-permute-start.3 = (bf16[8,16,1024]{2,1,0:T(8,128)(2,1)S(1)}, bf16[8,16,1024]{2,1,0:T(8,128)(2,1)S(1)}, u32[]{:S(2)}, u32[]{:S(2)}) collective-permute-start(bf16[8,16,1024]{2,1,0:T(8,128)(2,1)S(1)} %all-to-all-done.1), channel_id=1, source_target_pairs={{0,512},{256,768},{512,0},{768,256},{1,513},{257,769},{513,1},{769... | collective-permute-start | bytes 786440 | tf_op jit(solution)/shard_map/ppermute | solution.py:25
  70.1 2.4 %collective-permute-start.2 = (bf16[8,16,1024]{2,1,0:T(8,128)(2,1)S(1)}, bf16[8,16,1024]{2,1,0:T(8,128)(2,1)S(1)}, u32[]{:S(2)}, u32[]{:S(2)}) collective-permute-start(bf16[8,16,1024]{2,1,0:T(8,128)(2,1)S(1)} %all-to-all-done.1), channel_id=1, source_target_pairs={{0,256},{256,0},{512,768},{768,512},{1,257},{257,1},{513,769},{769... | collective-permute-start | bytes 786440 | tf_op jit(solution)/shard_map/ppermute | solution.py:25
  72.6 7.6 %collective-permute-done.4 = bf16[8,16,1024]{2,1,0:T(8,128)(2,1)S(1)} collective-permute-done((bf16[8,16,1024]{2,1,0:T(8,128)(2,1)S(1)}, bf16[8,16,1024]{2,1,0:T(8,128)(2,1)S(1)}, u32[]{:S(2)}, u32[]{:S(2)}) %collective-permute-start.4) | collective-permute-done | bytes 262176 | tf_op jit(solution)/shard_map/ppermute | solution.py:25
  80.2 2.5 %collective-permute-done.2 = bf16[8,16,1024]{2,1,0:T(8,128)(2,1)S(1)} collective-permute-done((bf16[8,16,1024]{2,1,0:T(8,128)(2,1)S(1)}, bf16[8,16,1024]{2,1,0:T(8,128)(2,1)S(1)}, u32[]{:S(2)}, u32[]{:S(2)}) %collective-permute-start.2) | collective-permute-done | bytes 262176 | tf_op jit(solution)/shard_map/ppermute | solution.py:25
  83.0 0.8 fusion.13
  85.0 7.4 %all-to-all-start.2 = ((f32[32,1,512]{2,1,0:T(1,128)}), f32[32,1,512]{2,1,0:T(1,128)S(1)}, u32[]{:S(2)}, u32[]{:S(2)}) async-start(f32[32,1,512]{2,1,0:T(1,128)} %all_to_all.26), calls=%async_computation.2 | async-start | bytes 131072 | tf_op jit(solution)/shard_map/all_to_all | solution.py:75
  92.4 7.5 %all-to-all-done.2 = f32[32,1,512]{2,1,0:T(1,128)S(1)} async-done(((f32[32,1,512]{2,1,0:T(1,128)}), f32[32,1,512]{2,1,0:T(1,128)S(1)}, u32[]{:S(2)}, u32[]{:S(2)}) %all-to-all-start.2) | async-done | bytes 65568 | tf_op jit(solution)/shard_map/all_to_all | solution.py:75
  101.0 15.6 %all-to-all-start.3 = ((f32[32,1,512]{2,1,0:T(1,128)}), f32[32,1,512]{2,1,0:T(1,128)S(1)}, u32[]{:S(2)}, u32[]{:S(2)}) async-start(f32[32,1,512]{2,1,0:T(1,128)} %all_to_all.28), calls=%async_computation.3 | async-start | bytes 131072 | tf_op jit(solution)/shard_map/all_to_all | solution.py:75
  116.7 20.6 %all-to-all-done.3 = f32[32,1,512]{2,1,0:T(1,128)S(1)} async-done(((f32[32,1,512]{2,1,0:T(1,128)}), f32[32,1,512]{2,1,0:T(1,128)S(1)}, u32[]{:S(2)}, u32[]{:S(2)}) %all-to-all-start.3) | async-done | bytes 65568 | tf_op jit(solution)/shard_map/all_to_all | solution.py:75
  138.1 0.9 multiply_convert_fusion
  139.0 1.7 convolution_convert_fusion.1
  140.7 3.6 %all-to-all-start.4 = ((bf16[8,4,16,1024]{3,2,1,0:T(8,128)(2,1)}), bf16[8,4,16,1024]{3,2,1,0:T(8,128)(2,1)S(1)}, u32[]{:S(2)}, u32[]{:S(2)}) async-start(bf16[8,4,16,1024]{3,2,1,0:T(8,128)(2,1)} %convolution_convert_fusion.1), calls=%async_computation.4 | async-start | bytes 2097152 | tf_op jit(solution)/shard_map/all_to_all | solution.py:36
  145.1 2.5 %collective-permute-start.7 = (bf16[8,16,1024]{2,1,0:T(8,128)(2,1)S(1)}, bf16[8,16,1024]{2,1,0:T(8,128)(2,1)S(1)}, u32[]{:S(2)}, u32[]{:S(2)}) collective-permute-start(bf16[8,16,1024]{2,1,0:T(8,128)(2,1)S(1)} %get-tuple-element.11), channel_id=1, source_target_pairs={{0,256},{256,0},{512,768},{768,512},{1,257},{257,1},{513,769},{769... | collective-permute-start | bytes 786440 | tf_op jit(solution)/shard_map/ppermute | solution.py:25
  147.6 3.1 %collective-permute-start.9 = (bf16[8,16,1024]{2,1,0:T(8,128)(2,1)S(1)}, bf16[8,16,1024]{2,1,0:T(8,128)(2,1)S(1)}, u32[]{:S(2)}, u32[]{:S(2)}) collective-permute-start(bf16[8,16,1024]{2,1,0:T(8,128)(2,1)S(1)} %get-tuple-element.12), channel_id=1, source_target_pairs={{0,768},{256,512},{512,256},{768,0},{1,769},{257,513},{513,257},{7... | collective-permute-start | bytes 786440 | tf_op jit(solution)/shard_map/ppermute | solution.py:25
  150.7 4.2 %collective-permute-start.8 = (bf16[8,16,1024]{2,1,0:T(8,128)(2,1)S(1)}, bf16[8,16,1024]{2,1,0:T(8,128)(2,1)S(1)}, u32[]{:S(2)}, u32[]{:S(2)}) collective-permute-start(bf16[8,16,1024]{2,1,0:T(8,128)(2,1)S(1)} %get-tuple-element.13), channel_id=1, source_target_pairs={{0,512},{256,768},{512,0},{768,256},{1,513},{257,769},{513,1},{769... | collective-permute-start | bytes 786440 | tf_op jit(solution)/shard_map/ppermute | solution.py:25
  155.6 9.1 %collective-permute-done.9 = bf16[8,16,1024]{2,1,0:T(8,128)(2,1)S(1)} collective-permute-done((bf16[8,16,1024]{2,1,0:T(8,128)(2,1)S(1)}, bf16[8,16,1024]{2,1,0:T(8,128)(2,1)S(1)}, u32[]{:S(2)}, u32[]{:S(2)}) %collective-permute-start.9) | collective-permute-done | bytes 262176 | tf_op jit(solution)/shard_map/ppermute | solution.py:25
  164.7 0.9 fusion.2
  165.6 7.6 %all-to-all-start.5 = ((bf16[8,16,1024]{2,1,0:T(8,128)(2,1)}), bf16[8,16,1024]{2,1,0:T(8,128)(2,1)S(1)}, u32[]{:S(2)}, u32[]{:S(2)}) async-start(bf16[8,16,1024]{2,1,0:T(8,128)(2,1)} %fusion.2), calls=%async_computation.5 | async-start | bytes 524288 | tf_op jit(solution)/shard_map/all_to_all | solution.py:36
  173.4 8.5 %collective-permute-start.5 = (bf16[2,16,1024]{2,1,0:T(8,128)(2,1)S(1)}, bf16[2,16,1024]{2,1,0:T(8,128)(2,1)S(1)}, u32[]{:S(2)}, u32[]{:S(2)}) collective-permute-start(bf16[2,16,1024]{2,1,0:T(8,128)(2,1)S(1)} %fusion.3), channel_id=1, source_target_pairs={{0,24},{8,16},{16,8},{24,0},{1,25},{9,17},{17,9},{25,1},{2,26},{10... | collective-permute-start | bytes 196616 | tf_op jit(solution)/shard_map/ppermute | solution.py:25
  182.0 14.9 %collective-permute-done.5 = bf16[2,16,1024]{2,1,0:T(8,128)(2,1)S(1)} collective-permute-done((bf16[2,16,1024]{2,1,0:T(8,128)(2,1)S(1)}, bf16[2,16,1024]{2,1,0:T(8,128)(2,1)S(1)}, u32[]{:S(2)}, u32[]{:S(2)}) %collective-permute-start.5) | collective-permute-done | bytes 65568 | tf_op jit(solution)/shard_map/ppermute | solution.py:25
  196.9 3.6 %collective-permute-start.6 = (bf16[16,1024]{1,0:T(8,128)(2,1)S(1)}, bf16[16,1024]{1,0:T(8,128)(2,1)S(1)}, u32[]{:S(2)}, u32[]{:S(2)}) collective-permute-start(bf16[16,1024]{1,0:T(8,128)(2,1)S(1)} %fusion.6), channel_id=1, source_target_pairs={{0,8},{8,0},{16,24},{24,16},{1,9},{9,1},{17,25},{25,17},{2,10},{10... | collective-permute-start | bytes 98312 | tf_op jit(solution)/shard_map/ppermute | solution.py:25
  201.1 10.7 %collective-permute-done.6 = bf16[16,1024]{1,0:T(8,128)(2,1)S(1)} collective-permute-done((bf16[16,1024]{1,0:T(8,128)(2,1)S(1)}, bf16[16,1024]{1,0:T(8,128)(2,1)S(1)}, u32[]{:S(2)}, u32[]{:S(2)}) %collective-permute-start.6) | collective-permute-done | bytes 32800 | tf_op jit(solution)/shard_map/ppermute | solution.py:25
  (55 shorter events, 7.1 us)
Async XLA Ops:
  2.1 55.2 %all-to-all-start.1 = ((bf16[8,16,1024]{2,1,0:T(8,128)(2,1)}), bf16[8,16,1024]{2,1,0:T(8,128)(2,1)S(1)}, u32[]{:S(2)}, u32[]{:S(2)}) async-start(bf16[8,16,1024]{2,1,0:T(8,128)(2,1)} %broadcast_in_dim.53), calls=%async_computation.1 | async-start | bytes 524288 | tf_op jit(solution)/shard_map/all_to_all | solution.py:21
  16.8 24.7 %collective-permute-start = (bf16[16,1024]{1,0:T(8,128)(2,1)}, bf16[16,1024]{1,0:T(8,128)(2,1)S(1)}, u32[]{:S(2)}, u32[]{:S(2)}) collective-permute-start(bf16[16,1024]{1,0:T(8,128)(2,1)} %param.2), channel_id=1, source_target_pairs={{0,8},{8,0},{16,24},{24,16},{1,9},{9,1},{17,25},{25,17},{2,10},{10... | collective-permute-start | bytes 98312 | tf_op jit(solution)/shard_map/ppermute | solution.py:25
  42.3 14.9 %collective-permute-start.1 = (bf16[2,16,1024]{2,1,0:T(8,128)(2,1)S(1)}, bf16[2,16,1024]{2,1,0:T(8,128)(2,1)S(1)}, u32[]{:S(2)}, u32[]{:S(2)}) collective-permute-start(bf16[2,16,1024]{2,1,0:T(8,128)(2,1)S(1)} %pad_maximum_fusion.2), channel_id=1, source_target_pairs={{0,24},{8,16},{16,8},{24,0},{1,25},{9,17},{17,9},{25,1},{2,26},{10... | collective-permute-start | bytes 196616 | tf_op jit(solution)/shard_map/ppermute | solution.py:25
  58.4 24.6 %all-to-all-start = ((bf16[8,2,2,16,1024]{4,3,2,1,0:T(8,128)(2,1)}), bf16[8,2,2,16,1024]{4,3,2,1,0:T(8,128)(2,1)S(1)}, u32[]{:S(2)}, u32[]{:S(2)}) async-start(bf16[8,2,2,16,1024]{4,3,2,1,0:T(8,128)(2,1)} %broadcast_in_dim.52), calls=%async_computation | async-start | bytes 2097152 | tf_op jit(solution)/shard_map/all_to_all | solution.py:21
  62.7 17.5 %collective-permute-start.4 = (bf16[8,16,1024]{2,1,0:T(8,128)(2,1)S(1)}, bf16[8,16,1024]{2,1,0:T(8,128)(2,1)S(1)}, u32[]{:S(2)}, u32[]{:S(2)}) collective-permute-start(bf16[8,16,1024]{2,1,0:T(8,128)(2,1)S(1)} %all-to-all-done.1), channel_id=1, source_target_pairs={{0,768},{256,512},{512,256},{768,0},{1,769},{257,513},{513,257},{7... | collective-permute-start | bytes 786440 | tf_op jit(solution)/shard_map/ppermute | solution.py:25
  67.6 12.6 %collective-permute-start.3 = (bf16[8,16,1024]{2,1,0:T(8,128)(2,1)S(1)}, bf16[8,16,1024]{2,1,0:T(8,128)(2,1)S(1)}, u32[]{:S(2)}, u32[]{:S(2)}) collective-permute-start(bf16[8,16,1024]{2,1,0:T(8,128)(2,1)S(1)} %all-to-all-done.1), channel_id=1, source_target_pairs={{0,512},{256,768},{512,0},{768,256},{1,513},{257,769},{513,1},{769... | collective-permute-start | bytes 786440 | tf_op jit(solution)/shard_map/ppermute | solution.py:25
  70.1 12.6 %collective-permute-start.2 = (bf16[8,16,1024]{2,1,0:T(8,128)(2,1)S(1)}, bf16[8,16,1024]{2,1,0:T(8,128)(2,1)S(1)}, u32[]{:S(2)}, u32[]{:S(2)}) collective-permute-start(bf16[8,16,1024]{2,1,0:T(8,128)(2,1)S(1)} %all-to-all-done.1), channel_id=1, source_target_pairs={{0,256},{256,0},{512,768},{768,512},{1,257},{257,1},{513,769},{769... | collective-permute-start | bytes 786440 | tf_op jit(solution)/shard_map/ppermute | solution.py:25
  85.0 14.9 %all-to-all-start.2 = ((f32[32,1,512]{2,1,0:T(1,128)}), f32[32,1,512]{2,1,0:T(1,128)S(1)}, u32[]{:S(2)}, u32[]{:S(2)}) async-start(f32[32,1,512]{2,1,0:T(1,128)} %all_to_all.26), calls=%async_computation.2 | async-start | bytes 131072 | tf_op jit(solution)/shard_map/all_to_all | solution.py:75
  101.0 36.2 %all-to-all-start.3 = ((f32[32,1,512]{2,1,0:T(1,128)}), f32[32,1,512]{2,1,0:T(1,128)S(1)}, u32[]{:S(2)}, u32[]{:S(2)}) async-start(f32[32,1,512]{2,1,0:T(1,128)} %all_to_all.28), calls=%async_computation.3 | async-start | bytes 131072 | tf_op jit(solution)/shard_map/all_to_all | solution.py:75
  140.7 24.9 %all-to-all-start.4 = ((bf16[8,4,16,1024]{3,2,1,0:T(8,128)(2,1)}), bf16[8,4,16,1024]{3,2,1,0:T(8,128)(2,1)S(1)}, u32[]{:S(2)}, u32[]{:S(2)}) async-start(bf16[8,4,16,1024]{3,2,1,0:T(8,128)(2,1)} %convolution_convert_fusion.1), calls=%async_computation.4 | async-start | bytes 2097152 | tf_op jit(solution)/shard_map/all_to_all | solution.py:36
  145.1 10.5 %collective-permute-start.7 = (bf16[8,16,1024]{2,1,0:T(8,128)(2,1)S(1)}, bf16[8,16,1024]{2,1,0:T(8,128)(2,1)S(1)}, u32[]{:S(2)}, u32[]{:S(2)}) collective-permute-start(bf16[8,16,1024]{2,1,0:T(8,128)(2,1)S(1)} %get-tuple-element.11), channel_id=1, source_target_pairs={{0,256},{256,0},{512,768},{768,512},{1,257},{257,1},{513,769},{769... | collective-permute-start | bytes 786440 | tf_op jit(solution)/shard_map/ppermute | solution.py:25
  147.6 17.1 %collective-permute-start.9 = (bf16[8,16,1024]{2,1,0:T(8,128)(2,1)S(1)}, bf16[8,16,1024]{2,1,0:T(8,128)(2,1)S(1)}, u32[]{:S(2)}, u32[]{:S(2)}) collective-permute-start(bf16[8,16,1024]{2,1,0:T(8,128)(2,1)S(1)} %get-tuple-element.12), channel_id=1, source_target_pairs={{0,768},{256,512},{512,256},{768,0},{1,769},{257,513},{513,257},{7... | collective-permute-start | bytes 786440 | tf_op jit(solution)/shard_map/ppermute | solution.py:25
  150.7 14.0 %collective-permute-start.8 = (bf16[8,16,1024]{2,1,0:T(8,128)(2,1)S(1)}, bf16[8,16,1024]{2,1,0:T(8,128)(2,1)S(1)}, u32[]{:S(2)}, u32[]{:S(2)}) collective-permute-start(bf16[8,16,1024]{2,1,0:T(8,128)(2,1)S(1)} %get-tuple-element.13), channel_id=1, source_target_pairs={{0,512},{256,768},{512,0},{768,256},{1,513},{257,769},{513,1},{769... | collective-permute-start | bytes 786440 | tf_op jit(solution)/shard_map/ppermute | solution.py:25
  165.6 16.3 %copy-start = (bf16[16,1024]{1,0:T(8,128)(2,1)S(1)}, bf16[16,1024]{1,0:T(8,128)(2,1)}, u32[]{:S(2)}) copy-start(bf16[16,1024]{1,0:T(8,128)(2,1)} %param.3) | copy-start | bytes 98308
  165.6 16.3 %copy-start.1 = (bf16[16,1024]{1,0:T(8,128)(2,1)S(1)}, bf16[16,1024]{1,0:T(8,128)(2,1)}, u32[]{:S(2)}) copy-start(bf16[16,1024]{1,0:T(8,128)(2,1)} %param.2) | copy-start | bytes 98308
  165.6 46.9 %all-to-all-start.5 = ((bf16[8,16,1024]{2,1,0:T(8,128)(2,1)}), bf16[8,16,1024]{2,1,0:T(8,128)(2,1)S(1)}, u32[]{:S(2)}, u32[]{:S(2)}) async-start(bf16[8,16,1024]{2,1,0:T(8,128)(2,1)} %fusion.2), calls=%async_computation.5 | async-start | bytes 524288 | tf_op jit(solution)/shard_map/all_to_all | solution.py:36
  173.4 23.5 %collective-permute-start.5 = (bf16[2,16,1024]{2,1,0:T(8,128)(2,1)S(1)}, bf16[2,16,1024]{2,1,0:T(8,128)(2,1)S(1)}, u32[]{:S(2)}, u32[]{:S(2)}) collective-permute-start(bf16[2,16,1024]{2,1,0:T(8,128)(2,1)S(1)} %fusion.3), channel_id=1, source_target_pairs={{0,24},{8,16},{16,8},{24,0},{1,25},{9,17},{17,9},{25,1},{2,26},{10... | collective-permute-start | bytes 196616 | tf_op jit(solution)/shard_map/ppermute | solution.py:25
  196.9 14.9 %collective-permute-start.6 = (bf16[16,1024]{1,0:T(8,128)(2,1)S(1)}, bf16[16,1024]{1,0:T(8,128)(2,1)S(1)}, u32[]{:S(2)}, u32[]{:S(2)}) collective-permute-start(bf16[16,1024]{1,0:T(8,128)(2,1)S(1)} %fusion.6), channel_id=1, source_target_pairs={{0,8},{8,0},{16,24},{24,16},{1,9},{9,1},{17,25},{25,17},{2,10},{10... | collective-permute-start | bytes 98312 | tf_op jit(solution)/shard_map/ppermute | solution.py:25
